TPU v7x, 32 devices: a whole 2x2x4 slice. The times are simulated.
32 devices in a mesh: expert: 16 (over z, y, x), tensor: 2 (over core).
Axes of the slice: x: 2, y: 2, z: 4, core: 2. Of those that a mesh axis runs over, the one named last changes fastest.
Arguments:
- tokens: bfloat16 [16384, 1024], P('expert'), may hold values from -6 to 6
- segment_ids: int32 [16384], P('expert'), may hold values from 0 to 7, as said below
- router_logits: float32 [16384, 16], P('expert'), may hold values from -3 to 3
- expert_ids: int32 [16384, 8], P('expert'), may hold values from 0 to 15, all different within a row; in each aligned block of 1024 rows (0 to 1023, 1024 to 2047, ...) at most 768 rows name the same one
- gain_attn: float32 [1024], replicated, may hold values from 0.1 to 1.9
- w_query: bfloat16 [1024, 1024], P(None, 'tensor'), may hold values from -0.1875 to 0.1875
- key_matrix: bfloat16 [1024, 512], P(None, 'tensor'), may hold values from -0.1875 to 0.1875
- value_matrix: bfloat16 [1024, 512], P(None, 'tensor'), may hold values from -0.1875 to 0.1875
- w_out: bfloat16 [1024, 1024], P('tensor'), may hold values from -0.75 to 0.75
- gain_mlp: float32 [1024], replicated, may hold values from 0.1 to 1.9
- w_gate: bfloat16 [16, 1024, 512], P('expert', None, 'tensor'), may hold values from -0.1875 to 0.1875
- w_up: bfloat16 [16, 1024, 512], P('expert', None, 'tensor'), may hold values from -0.1875 to 0.1875
- w_down: bfloat16 [16, 512, 1024], P('expert', 'tensor'), may hold values from -0.75 to 0.75
- out_grad: float32 [16384, 1024], P('expert', 'tensor'), may hold values from -6 to 6
Outputs:
- block_out: bfloat16 [16384, 1024], P('expert', 'tensor')
- grad_tokens: float32 [16384, 1024], P('expert', 'tensor')
- grad_logits: float32 [16384, 16], P('expert')
- grad_gain_attn: float32 [1024], P('tensor')
- grad_query: float32 [1024, 1024], P(None, 'tensor')
- grad_key: float32 [1024, 512], P(None, 'tensor')
- grad_value: float32 [1024, 512], P(None, 'tensor')
- grad_out: float32 [1024, 1024], P('tensor')
- grad_gain_mlp: float32 [1024], P('tensor')
- grad_gate: float32 [16, 1024, 512], P('expert', None, 'tensor')
- grad_up: float32 [16, 1024, 512], P('expert', None, 'tensor')
- grad_down: float32 [16, 512, 1024], P('expert', 'tensor')
Inputs may be any that keep to these rules, and one draw needn't show every extreme that they name: `segment_ids`: within each block of 1024 rows the ids start at 0 and rise by 0 or 1 from row to row; a run of equal ids is one sequence; a block holds 1 to 8 sequences; some block holds a single sequence of 1024 tokens and some block holds eight. `expert_ids`: each row names 8 different experts; within the rows of one index of the expert axis no expert is named by more than 768 rows.
All inputs are finite; a program needn't handle non-finite values.
Results may differ from a plain program's by a relative error of at most 0.023.
Values may be sent and summed in bfloat16 or wider, within the bound.
No kernel may reach another device: no remote copies, remote signals or barrier semaphores. Data moves between devices by JAX's collectives and lax.ppermute only.
A program may use at most 448 MiB of HBM per device.

v0:
```python
import jax
import jax.numpy as jnp
from jax import lax
from jax.sharding import PartitionSpec as P

HEAD_SIZE = 64


EPS = 1e-06
THETA = 10000.0
NEG = -1e30


def positions(segment_row):
    row_index = jnp.arange(segment_row.shape[0], dtype=jnp.int32)
    before = jnp.concatenate([segment_row[:1] - 1, segment_row[:-1]])
    starts = lax.cummax(jnp.where(segment_row != before, row_index, 0), axis=0)
    return row_index - starts


def rope_tables(places, head_dim):
    half_dim = head_dim // 2
    freq_row = jnp.power(THETA, -2.0 * jnp.arange(half_dim, dtype=jnp.float32) / head_dim)
    angles = places.astype(jnp.float32)[:, None] * freq_row[None, :]
    return (jnp.cos(angles), jnp.sin(angles))


def rotate_pairs(value_rows, cosine_table, sine_table):
    half_dim = value_rows.shape[-1] // 2
    first = value_rows[..., :half_dim]
    second = value_rows[..., half_dim:]
    cos_b = cosine_table[:, None, :]
    sin_b = sine_table[:, None, :]
    return jnp.concatenate(
        [first * cos_b - second * sin_b, second * cos_b + first * sin_b], axis=-1
    )


def body(
    tokens,
    segment_ids,
    router_logits,
    expert_ids,
    gain_attn,
    w_query,
    key_matrix,
    value_matrix,
    w_out,
    gain_mlp,
    w_gate,
    w_up,
    w_down,
    out_grad,
):
    tok_count, model_width = tokens.shape
    col_width = out_grad.shape[1]
    col_start = lax.axis_index("tensor") * col_width
    head_dim = HEAD_SIZE
    q_heads = w_query.shape[1] // head_dim
    kv_heads = key_matrix.shape[1] // head_dim
    query_group_size = q_heads // kv_heads
    score_scale = head_dim ** (-0.5)
    block_rows = min(512, tok_count)
    top_k = expert_ids.shape[1]
    n_experts = router_logits.shape[1]
    capacity = min(tok_count, tok_count * top_k * 3 // (2 * n_experts))

    def to_expert(x_cols):
        got_cols = lax.all_to_all(x_cols, "expert", split_axis=0, concat_axis=0, tiled=True)
        return lax.all_gather(got_cols, "tensor", axis=2, tiled=True).reshape(-1, model_width)

    def part_sum(terms):
        return lax.psum_scatter(
            terms.reshape(n_experts, capacity, model_width),
            "tensor",
            scatter_dimension=2,
            tiled=True,
        ).astype(jnp.bfloat16)

    def home_back(cols):
        return lax.all_to_all(cols, "expert", split_axis=0, concat_axis=0, tiled=True).reshape(
            -1, col_width
        )

    x_full = tokens.astype(jnp.float32)
    places = positions(segment_ids)
    cosine_table, sine_table = rope_tables(places, head_dim)
    inv_one = lax.rsqrt(jnp.mean(x_full * x_full, axis=1, keepdims=True) + EPS)
    normed_one = x_full * inv_one
    attn_in = (normed_one * gain_attn).astype(jnp.bfloat16)
    q_pre = jnp.dot(attn_in, w_query, preferred_element_type=jnp.float32)
    key_projected = jnp.dot(attn_in, key_matrix, preferred_element_type=jnp.float32)
    v_pre = jnp.dot(attn_in, value_matrix, preferred_element_type=jnp.float32)
    queries = (
        rotate_pairs(q_pre.reshape(tok_count, q_heads, head_dim), cosine_table, sine_table)
        .astype(jnp.bfloat16)
        .reshape(tok_count, kv_heads, query_group_size, head_dim)
    )
    rotated_keys = rotate_pairs(
        key_projected.reshape(tok_count, kv_heads, head_dim), cosine_table, sine_table
    ).astype(jnp.bfloat16)
    value_rows = v_pre.reshape(tok_count, kv_heads, head_dim).astype(jnp.bfloat16)
    key_index = jnp.arange(tok_count)

    def block_scores(row_start, q_block):
        row_index = row_start + jnp.arange(block_rows)
        same_seq = segment_ids[row_start : row_start + block_rows][:, None] == segment_ids[None, :]
        allowed = same_seq & (row_index[:, None] >= key_index[None, :])
        raw = jnp.einsum(
            "qhgd,shd->hgqs", q_block, rotated_keys, preferred_element_type=jnp.float32
        )
        return jnp.where(allowed[None, None], raw * score_scale, NEG)

    attn_rows = []
    log_sums = []
    for row_start in range(0, tok_count, block_rows):
        scores = block_scores(row_start, queries[row_start : row_start + block_rows])
        row_peak = jnp.max(scores, axis=-1, keepdims=True)
        exp_scores = jnp.exp(scores - row_peak)
        row_total = jnp.sum(exp_scores, axis=-1, keepdims=True)
        prob_rows = exp_scores / row_total
        log_sums.append(row_peak + jnp.log(row_total))
        attn_rows.append(
            jnp.einsum(
                "hgqs,shd->qhgd",
                prob_rows.astype(jnp.bfloat16),
                value_rows,
                preferred_element_type=jnp.float32,
            )
        )
    attn_vals = (
        jnp.concatenate(attn_rows, axis=0)
        .reshape(tok_count, q_heads * head_dim)
        .astype(jnp.bfloat16)
    )
    attn_part = jnp.dot(attn_vals, w_out, preferred_element_type=jnp.float32)
    mixed = x_full + lax.psum(attn_part, "tensor")
    inv_two = lax.rsqrt(jnp.mean(mixed * mixed, axis=1, keepdims=True) + EPS)
    normed_two = mixed * inv_two
    mlp_in = (normed_two * gain_mlp).astype(jnp.bfloat16)
    chosen = jnp.take_along_axis(router_logits, expert_ids, axis=1)
    gates = jax.nn.softmax(chosen, axis=1)
    flat_ids = expert_ids.reshape(-1)
    expert_range = jnp.arange(n_experts, dtype=jnp.int32)
    onehot = (flat_ids[:, None] == expert_range[None, :]).astype(jnp.int32)
    rank_run = jnp.cumsum(onehot, axis=0) - 1
    dest_slot = flat_ids * capacity + jnp.sum(rank_run * onehot, axis=1)
    slot_count = n_experts * capacity
    pair_of_slot = (
        jnp.zeros((slot_count,), jnp.int32)
        .at[dest_slot]
        .set(jnp.arange(tok_count * top_k, dtype=jnp.int32))
    )
    slot_filled = jnp.zeros((slot_count,), jnp.bool_).at[dest_slot].set(True)
    token_of_slot = pair_of_slot // top_k
    send_rows = jnp.where(
        slot_filled[:, None], mlp_in[token_of_slot], jnp.zeros((), jnp.bfloat16)
    ).reshape(n_experts, capacity, model_width)
    expert_rows = to_expert(lax.dynamic_slice_in_dim(send_rows, col_start, col_width, 2))
    gate_w, up_w, down_w = (w_gate[0], w_up[0], w_down[0])
    gate_pre = jnp.dot(expert_rows, gate_w, preferred_element_type=jnp.float32)
    up_pre = jnp.dot(expert_rows, up_w, preferred_element_type=jnp.float32)
    gate_sig = jax.nn.sigmoid(gate_pre)
    gate_silu = gate_pre * gate_sig
    hidden_act = (gate_silu * up_pre).astype(jnp.bfloat16)
    out_terms = jnp.dot(hidden_act, down_w, preferred_element_type=jnp.float32)
    back_out = home_back(part_sum(out_terms))
    pair_out = back_out[dest_slot].reshape(tok_count, top_k, col_width).astype(jnp.float32)
    expert_sum = jnp.sum(pair_out * gates[:, :, None], axis=1)
    mixed_cols = lax.dynamic_slice_in_dim(mixed, col_start, col_width, 1)
    block_out = (mixed_cols + expert_sum).astype(jnp.bfloat16)
    gate_part = jnp.sum(pair_out * out_grad[:, None, :], axis=2)
    slot_gate = gates.reshape(-1)[pair_of_slot]
    d_slots = (
        jnp.where(slot_filled[:, None], slot_gate[:, None] * out_grad[token_of_slot], 0.0)
        .astype(jnp.bfloat16)
        .reshape(n_experts, capacity, col_width)
    )
    grad_rows = to_expert(d_slots)
    down_local = jnp.einsum("rf,rd->fd", hidden_act, grad_rows, preferred_element_type=jnp.float32)
    d_hidden = jnp.einsum("rd,fd->rf", grad_rows, down_w, preferred_element_type=jnp.float32)
    d_gate = (d_hidden * up_pre * gate_sig * (1.0 + gate_pre * (1.0 - gate_sig))).astype(
        jnp.bfloat16
    )
    d_up = (d_hidden * gate_silu).astype(jnp.bfloat16)
    gate_local = jnp.einsum("rd,rf->df", expert_rows, d_gate, preferred_element_type=jnp.float32)
    up_local = jnp.einsum("rd,rf->df", expert_rows, d_up, preferred_element_type=jnp.float32)
    row_terms = jnp.einsum(
        "rf,df->rd", d_gate, gate_w, preferred_element_type=jnp.float32
    ) + jnp.einsum("rf,df->rd", d_up, up_w, preferred_element_type=jnp.float32)
    back_grads = home_back(part_sum(row_terms))
    grad_gate, grad_up, grad_down = (gate_local[None], up_local[None], down_local[None])
    d_mlp_in = jnp.sum(
        back_grads[dest_slot].reshape(tok_count, top_k, col_width).astype(jnp.float32), axis=1
    )
    gain_two_cols = lax.dynamic_slice_in_dim(gain_mlp, col_start, col_width, 0)
    normed_two_cols = lax.dynamic_slice_in_dim(normed_two, col_start, col_width, 1)
    scaled_two = d_mlp_in * gain_two_cols
    dot_part = jnp.sum(scaled_two * normed_two_cols, axis=1)
    gate_dots, norm_dots = (
        lax.psum(gate_part.astype(jnp.bfloat16), "tensor").astype(jnp.float32),
        lax.psum(dot_part.astype(jnp.bfloat16), "tensor").astype(jnp.float32),
    )
    d_mixed = out_grad + inv_two * (
        scaled_two - normed_two_cols * (norm_dots / model_width)[:, None]
    )
    gain_two_grad = jnp.sum(d_mlp_in * normed_two_cols, axis=0)
    d_chosen = gates * (gate_dots - jnp.sum(gates * gate_dots, axis=1, keepdims=True))
    onehot_pick = (expert_ids[:, :, None] == expert_range[None, None, :]).astype(jnp.float32)
    grad_logits = jnp.sum(d_chosen[:, :, None] * onehot_pick, axis=1)
    dy_full = lax.all_gather(d_mixed.astype(jnp.bfloat16), "tensor", axis=1, tiled=True)
    out_w_grad = jnp.einsum("tc,td->cd", attn_vals, dy_full, preferred_element_type=jnp.float32)
    d_attn = (
        jnp.einsum("td,cd->tc", dy_full, w_out, preferred_element_type=jnp.float32)
        .astype(jnp.bfloat16)
        .reshape(tok_count, kv_heads, query_group_size, head_dim)
    )
    d_keys = jnp.zeros((tok_count, kv_heads, head_dim), jnp.float32)
    d_values = jnp.zeros((tok_count, kv_heads, head_dim), jnp.float32)
    d_query_rows = []
    for block_index, row_start in enumerate(range(0, tok_count, block_rows)):
        q_block = queries[row_start : row_start + block_rows]
        g_block = d_attn[row_start : row_start + block_rows]
        scores = block_scores(row_start, q_block)
        prob_rows = jnp.exp(scores - log_sums[block_index])
        d_values = d_values + jnp.einsum(
            "hgqs,qhgd->shd",
            prob_rows.astype(jnp.bfloat16),
            g_block,
            preferred_element_type=jnp.float32,
        )
        d_probs = jnp.einsum(
            "qhgd,shd->hgqs", g_block, value_rows, preferred_element_type=jnp.float32
        )
        d_scores = prob_rows * (d_probs - jnp.sum(d_probs * prob_rows, axis=-1, keepdims=True))
        d_scaled = (d_scores * score_scale).astype(jnp.bfloat16)
        d_query_rows.append(
            jnp.einsum("hgqs,shd->qhgd", d_scaled, rotated_keys, preferred_element_type=jnp.float32)
        )
        d_keys = d_keys + jnp.einsum(
            "hgqs,qhgd->shd", d_scaled, q_block, preferred_element_type=jnp.float32
        )
    d_query = (
        rotate_pairs(
            jnp.concatenate(d_query_rows, axis=0).reshape(tok_count, q_heads, head_dim),
            cosine_table,
            -sine_table,
        )
        .astype(jnp.bfloat16)
        .reshape(tok_count, q_heads * head_dim)
    )
    d_key = (
        rotate_pairs(d_keys, cosine_table, -sine_table)
        .astype(jnp.bfloat16)
        .reshape(tok_count, kv_heads * head_dim)
    )
    d_value = d_values.astype(jnp.bfloat16).reshape(tok_count, kv_heads * head_dim)
    query_grad = jnp.einsum("td,tc->dc", attn_in, d_query, preferred_element_type=jnp.float32)
    key_grad = jnp.einsum("td,tc->dc", attn_in, d_key, preferred_element_type=jnp.float32)
    value_grad = jnp.einsum("td,tc->dc", attn_in, d_value, preferred_element_type=jnp.float32)
    in_terms = jnp.einsum("tc,dc->td", d_query, w_query, preferred_element_type=jnp.float32)
    in_terms = in_terms + jnp.einsum(
        "tc,dc->td", d_key, key_matrix, preferred_element_type=jnp.float32
    )
    in_terms = in_terms + jnp.einsum(
        "tc,dc->td", d_value, value_matrix, preferred_element_type=jnp.float32
    )
    d_attn_in = lax.psum(in_terms.astype(jnp.bfloat16), "tensor").astype(jnp.float32)
    scaled_one = d_attn_in * gain_attn
    one_dots = jnp.mean(scaled_one * normed_one, axis=1, keepdims=True)
    d_norm_one = inv_one * (scaled_one - normed_one * one_dots)
    grad_tokens = d_mixed + lax.dynamic_slice_in_dim(d_norm_one, col_start, col_width, 1)
    gain_one_grad = lax.dynamic_slice_in_dim(
        jnp.sum(d_attn_in * normed_one, axis=0), col_start, col_width, 0
    )
    grad_query, grad_key, grad_value, grad_out, grad_gain_attn, grad_gain_mlp = (
        lax.psum(query_grad.astype(jnp.bfloat16), "expert").astype(jnp.float32),
        lax.psum(key_grad.astype(jnp.bfloat16), "expert").astype(jnp.float32),
        lax.psum(value_grad.astype(jnp.bfloat16), "expert").astype(jnp.float32),
        lax.psum(out_w_grad.astype(jnp.bfloat16), "expert").astype(jnp.float32),
        lax.psum(gain_one_grad.astype(jnp.bfloat16), "expert").astype(jnp.float32),
        lax.psum(gain_two_grad.astype(jnp.bfloat16), "expert").astype(jnp.float32),
    )
    return (
        block_out,
        grad_tokens,
        grad_logits,
        grad_gain_attn,
        grad_query,
        grad_key,
        grad_value,
        grad_out,
        grad_gain_mlp,
        grad_gate,
        grad_up,
        grad_down,
    )


def solution(mesh):
    return jax.shard_map(
        body,
        mesh=mesh,
        in_specs=(
            P("expert", None),
            P("expert"),
            P("expert", None),
            P("expert", None),
            P(),
            P(None, "tensor"),
            P(None, "tensor"),
            P(None, "tensor"),
            P("tensor", None),
            P(),
            P("expert", None, "tensor"),
            P("expert", None, "tensor"),
            P("expert", "tensor", None),
            P("expert", "tensor"),
        ),
        out_specs=(
            P("expert", "tensor"),
            P("expert", "tensor"),
            P("expert", None),
            P("tensor"),
            P(None, "tensor"),
            P(None, "tensor"),
            P(None, "tensor"),
            P("tensor", None),
            P("tensor"),
            P("expert", None, "tensor"),
            P("expert", None, "tensor"),
            P("expert", "tensor", None),
        ),
        check_vma=False,
    )
```

profile of v0, /device:TPU:0, one launch (start us, length us, event | category | flops | bytes accessed | tf_op | source)
XLA Modules:
  0.0 2134.1 jit_solution(17130223782028919859)
XLA Ops:
  13.7 2.6 convolution_convert_fusion.5
  16.3 2.8 fusion.96
  23.6 7.4 fusion.100
  31.0 8.1 fusion.11
  39.1 7.4 fusion.56
  46.6 7.2 fusion.101
  53.8 8.1 fusion.10
  61.9 7.6 fusion.55
  70.6 3.3 fusion.102
  80.7 10.0 reduce-window.19
  94.2 34.6 %scatter_custom_fusion = pred[12288]{0:T(1024)(128)(4,1)S(1)} fusion(s32[8192]{0:T(1024)S(1)} %bitcast.275, pred[8192]{0:T(1024)(128)(4,1)S(1)} %broadcast.306, pred[]{:T(512)} %constant.82.clone.1), kind=kCustom, calls=%fused_computation.170 | custom fusion | bytes 12289 | tf_op jit(solution)/shard_map/scatter | solution.py:154
  128.9 30.5 %scatter_custom_fusion.1 = s32[12288]{0:T(1024)S(1)} fusion(s32[8192]{0:T(1024)S(1)} %bitcast.276, s32[8192]{0:T(1024)S(1)} %iota.57, s32[]{:T(128)} %constant.33.clone.1), kind=kCustom, calls=%fused_computation.168 | custom fusion | bytes 49156 | tf_op jit(solution)/shard_map/scatter | solution.py:152
  160.1 2.8 multiply_reduce_fusion.1
  167.3 52.5 %gather_fusion = bf16[12288,1024]{1,0:T(8,128)(2,1)} fusion(bf16[1024,1024]{1,0:T(8,128)(2,1)S(1)} %get-tuple-element.28, s32[12288]{0:T(1024)S(1)} %get-tuple-element.50), kind=kCustom, calls=%fused_computation | custom fusion | bytes 50380800 | tf_op jit(solution)/shard_map/gather | solution.py:157
  219.9 11.6 dynamic-slice_select_fusion
  231.4 8.5 all-to-all-start
  240.5 66.0 %gather_fusion.5 = f32[8192]{0:T(1024)S(1)} fusion(f32[1024,16]{0,1:T(8,128)S(1)} %copy-done.1, s32[8192]{0:T(1024)S(1)} %reshape.490), kind=kCustom, calls=%fused_computation.5 | custom fusion | bytes 131072 | tf_op jit(solution)/shard_map/jit(take_along_axis)/gather | solution.py:141
  307.1 170.1 %all-to-all-done = bf16[16,768,512]{2,1,0:T(8,128)(2,1)} async-done(((bf16[16,768,512]{2,1,0:T(8,128)(2,1)}), bf16[16,768,512]{2,1,0:T(8,128)(2,1)}, u32[]{:S(2)}, u32[]{:S(2)}) %all-to-all-start) | async-done | bytes 12582944 | tf_op jit(solution)/shard_map/all_to_all | solution.py:69
  478.3 68.0 %gather_fusion.2 = f32[12288]{0:T(1024)S(1)} fusion(f32[8192]{0:T(1024)S(1)} %div.79, s32[12288]{0:T(1024)S(1)} %copy-done.46), kind=kCustom, calls=%fused_computation.2 | custom fusion | bytes 147456 | tf_op jit(solution)/shard_map/gather | solution.py:173
  546.4 48.4 %gather_fusion.3 = f32[12288,512]{1,0:T(8,128)} fusion(f32[1024,512]{1,0:T(8,128)S(1)} %copy-done.2, s32[12288]{0:T(1024)S(1)} %copy-done.40), kind=kCustom, calls=%fused_computation.3 | custom fusion | bytes 50380800 | tf_op jit(solution)/shard_map/gather | solution.py:175
  594.8 9.0 select_convert_fusion
  603.8 326.9 %all_to_all.20 = bf16[16,768,512]{2,1,0:T(8,128)(2,1)} all-to-all(bf16[16,768,512]{2,1,0:T(8,128)(2,1)S(1)} %select_convert_fusion), channel_id=1, replica_groups=mesh['expert'=16,'tensor'=2] {'expert'}, dimensions={0} | all-to-all | bytes 25165824 | tf_op jit(solution)/shard_map/all_to_all | solution.py:69
  931.8 22.1 %fusion.65 = f32[12288,256]{1,0:T(8,128)} fusion(bf16[12288,1024]{1,0:T(8,128)(2,1)} %bitcast.290, bf16[1,1024,256]{2,1,0:T(8,128)(2,1)S(1)} %copy-done.31), kind=kOutput, calls=%fused_computation.127 | convolution fusion | flops 6442450944 | bytes 38273024 | tf_op jit(solution)/shard_map/dot_general | solution.py:162
  953.8 17.6 fusion.69
  971.4 26.6 %multiply_convert_fusion = (bf16[12288,256]{1,0:T(8,128)(2,1)}, bf16[12288,256]{1,0:T(8,128)(2,1)}, bf16[12288,256]{1,0:T(8,128)(2,1)}) fusion(f32[12288,256]{1,0:T(8,128)} %fusion.69, f32[12288,256]{1,0:T(8,128)} %fusion.65, bf16[12288,1024]{1,0:T(8,128)(2,1)} %bitcast.248, bf16[1,256,1024]{2,1,0:T(8,128)(2,1)S(1)} %copy-done.32), kind=kOutput, calls=%fused_computation.40 | convolution fusion | flops 6489636864 | bytes 69730304 | tf_op jit(solution)/shard_map/rd,fd->rf/dot_general | solution.py:181
  998.0 22.3 %fusion.67 = f32[12288,1024]{1,0:T(8,128)} fusion(bf16[12288,256]{1,0:T(8,128)(2,1)} %get-tuple-element.33, bf16[1,1024,256]{2,1,0:T(8,128)(2,1)S(1)} %copy-done.30), kind=kOutput, calls=%fused_computation.129 | convolution fusion | flops 6442450944 | bytes 57147392 | tf_op jit(solution)/shard_map/rf,df->rd/dot_general | solution.py:188
  1020.3 34.0 %convolution_add_fusion = f32[12288,1024]{1,0:T(8,128)} fusion(f32[12288,1024]{1,0:T(8,128)} %fusion.67, bf16[12288,256]{1,0:T(8,128)(2,1)} %get-tuple-element.32, bf16[1,1024,256]{2,1,0:T(8,128)(2,1)S(1)} %copy-done.31), kind=kOutput, calls=%fused_computation.11 | convolution fusion | flops 6455033856 | bytes 107479040 | tf_op jit(solution)/shard_map/rf,df->rd/dot_general | solution.py:190
  1054.4 34.3 %fusion.60 = f32[16,768,1024]{2,1,0:T(8,128)} fusion(bf16[16,768,256]{2,1,0:T(8,128)(2,1)} %bitcast.247, bf16[1,256,1024]{2,1,0:T(8,128)(2,1)S(1)} %copy-done.32), kind=kOutput, calls=%fused_computation.122 | convolution fusion | flops 6442450944 | bytes 57147392 | tf_op jit(solution)/shard_map/dot_general | solution.py:166
  1088.7 29.0 %reduce-scatter.5.cloned.1.call-done = f32[16,768,512]{2,1,0:T(8,128)} async-done(((f32[16,768,1024]{2,1,0:T(8,128)}), f32[16,768,512]{2,1,0:T(8,128)}) %reduce-scatter.5.cloned.1.call-update) | async-done | bytes 25165840 | tf_op jit(solution)/shard_map/reduce_scatter | solution.py:73
  1117.7 14.3 convert_element_type.184
  1132.0 7.1 all-to-all-start.3
  1139.1 45.4 %reduce-scatter.3.cloned.1.call-done = f32[16,768,512]{2,1,0:T(8,128)} async-done(((f32[16,768,1024]{2,1,0:T(8,128)}), f32[16,768,512]{2,1,0:T(8,128)}) %reduce-scatter.3.cloned.1.call-update) | async-done | bytes 25165840 | tf_op jit(solution)/shard_map/reduce_scatter | solution.py:73
  1184.5 13.2 convert_element_type.177
  1197.8 178.9 %all-to-all-done.3 = bf16[16,768,512]{2,1,0:T(8,128)(2,1)} async-done(((bf16[16,768,512]{2,1,0:T(8,128)(2,1)}), bf16[16,768,512]{2,1,0:T(8,128)(2,1)}, u32[]{:S(2)}, u32[]{:S(2)}) %all-to-all-start.3) | async-done | bytes 12582944 | tf_op jit(solution)/shard_map/all_to_all | solution.py:81
  1376.7 54.8 %all-to-all-start.1 = ((bf16[16,768,512]{2,1,0:T(8,128)(2,1)}), bf16[16,768,512]{2,1,0:T(8,128)(2,1)}, u32[]{:S(2)}, u32[]{:S(2)}) async-start(bf16[16,768,512]{2,1,0:T(8,128)(2,1)} %convert_element_type.177), calls=%async_computation.2 | async-start | bytes 25165824 | tf_op jit(solution)/shard_map/all_to_all | solution.py:81
  1431.7 40.2 %gather_fusion.4 = bf16[8192,512]{1,0:T(8,128)(2,1)} fusion(bf16[12288,512]{1,0:T(8,128)(2,1)} %bitcast.35, s32[8192]{0:T(1024)S(1)} %broadcast_clamp_fusion), kind=kCustom, calls=%fused_computation.4 | custom fusion | bytes 16809984 | tf_op jit(solution)/shard_map/gather | solution.py:194
  1471.9 10.2 convert_reduce_fusion
  1482.2 183.7 %all-to-all-done.1 = bf16[16,768,512]{2,1,0:T(8,128)(2,1)} async-done(((bf16[16,768,512]{2,1,0:T(8,128)(2,1)}), bf16[16,768,512]{2,1,0:T(8,128)(2,1)}, u32[]{:S(2)}, u32[]{:S(2)}) %all-to-all-start.1) | async-done | bytes 12582944 | tf_op jit(solution)/shard_map/all_to_all | solution.py:81
  1665.8 40.1 %gather_fusion.1 = bf16[8192,512]{1,0:T(8,128)(2,1)} fusion(bf16[12288,512]{1,0:T(8,128)(2,1)} %bitcast.29, s32[8192]{0:T(1024)S(1)} %broadcast_clamp_fusion), kind=kCustom, calls=%fused_computation.1 | custom fusion | bytes 16809984 | tf_op jit(solution)/shard_map/gather | solution.py:168
  1705.9 11.5 fusion.3
  1717.5 2.7 multiply_reduce_fusion.2
  1720.2 3.8 all-reduce.2
  1724.1 4.4 fusion.97
  1728.6 14.2 convolution_bitcast_fusion
  1742.8 46.6 %all-gather.8.cloned.1.call-done = bf16[1024,1024]{1,0:T(8,128)(2,1)} async-done(((bf16[1024,512]{1,0:T(8,128)(2,1)}), bf16[1024,1024]{1,0:T(8,128)(2,1)}) %all-gather.8.cloned.1.call-update) | async-done | bytes 2097168 | tf_op jit(solution)/shard_map/all_gather | solution.py:211
  1789.4 2.9 convolution_convert_fusion.2
  1792.3 8.1 fusion.103
  1800.5 7.2 fusion.41
  1807.7 23.4 %fusion.39 = f32[512,4,2,64]{0,3,2,1:T(8,128)} fusion(f32[4,1024,512,2]{2,1,3,0:T(8,128)} %fusion.103, f32[4,2,512,1024]{2,3,1,0:T(8,128)} %get-tuple-element.61, f32[4,2,512]{2,1,0:T(2,128)S(1)} %bitcast.287, bf16[1024,4,32]{0,2,1:T(8,128)(2,1)} %copy-done.43, bf16[1024,4,32]{0,2,1:T(8,128)(2,1)S(1)} %copy-done.42), kind=kOutput, calls=%fused_computation.90 | convolution fusion | flops 567284736 | bytes 35143680 | tf_op jit(solution)/shard_map/hgqs,shd->qhgd/dot_general | solution.py:238
  1831.2 23.7 %fusion.40 = f32[4,64,1024]{2,1,0:T(8,128)} fusion(bf16[512,4,2,64]{0,3,2,1:T(8,128)(2,1)} %bitcast.273, f32[4,1024,512,2]{2,1,3,0:T(8,128)} %fusion.103, f32[4,2,512,1024]{2,3,1,0:T(8,128)} %get-tuple-element.61, f32[4,2,512]{2,1,0:T(2,128)S(1)} %bitcast.288), kind=kOutput, calls=%fused_computation.91 | convolution fusion | flops 566236160 | bytes 35143680 | tf_op jit(solution)/shard_map/hgqs,qhgd->shd/dot_general | solution.py:240
  1854.9 8.1 fusion.104
  1863.0 8.5 fusion.50
  1872.3 2.7 fusion.106
  1875.0 28.3 %fusion.35 = f32[512,4,2,64]{0,3,2,1:T(8,128)} fusion(f32[4,1024,512,2]{2,1,3,0:T(8,128)} %fusion.104, f32[4,2,512,1024]{2,3,1,0:T(8,128)} %get-tuple-element.59, f32[4,2,512]{2,1,0:T(2,128)S(1)} %bitcast.284, bf16[1024,4,32]{0,2,1:T(8,128)(2,1)S(1)} %copy-done.45, bf16[1024,4,32]{0,2,1:T(8,128)(2,1)S(1)} %copy-done.42), kind=kOutput, calls=%fused_computation.86 | convolution fusion | flops 567284736 | bytes 35143680 | tf_op jit(solution)/shard_map/hgqs,shd->qhgd/dot_general | solution.py:238
  1903.3 24.7 %fusion.38 = f32[1024,4,64]{0,2,1:T(8,128)S(1)} fusion(f32[4,64,1024]{2,1,0:T(8,128)} %fusion.40, bf16[512,4,2,64]{0,3,2,1:T(8,128)(2,1)} %bitcast.271, f32[4,1024,512,2]{2,1,3,0:T(8,128)} %fusion.104, f32[4,2,512,1024]{2,3,1,0:T(8,128)} %get-tuple-element.59, f32[4,2,512]{2,1,0:T(2,128)S(1)} %bitcast.285), kind=kOutput, calls=%fused_computation.89 | convolution fusion | flops 566498304 | bytes 36192256 | tf_op jit(solution)/shard_map/hgqs,qhgd->shd/dot_general | solution.py:240
  1931.9 2.7 add_convert_fusion
  1934.7 14.6 convolution_bitcast_fusion.1
  1958.0 14.8 convolution_bitcast_fusion.2
  1974.9 6.2 fusion.29
  1981.2 43.2 %all-reduce = (bf16[512]{0:T(512)(128)(2,1)S(1)}, bf16[512]{0:T(512)(128)(2,1)S(1)}) all-reduce(bf16[512]{0:T(512)(128)(2,1)S(1)} %dynamic_slice.41, bf16[512]{0:T(512)(128)(2,1)S(1)} %get-tuple-element.14), channel_id=1, replica_groups=mesh['expert'=16,'tensor'=2] {'expert'}, use_global_device_ids=true, to_apply=%region_31.32 | all-reduce | flops 1024 | bytes 4096 | tf_op jit(solution)/shard_map/psum | solution.py:281
  2025.6 4.6 fusion.32
  2030.2 87.1 %all-reduce.11.cloned.1.call-done = (bf16[1024,512]{1,0:T(8,128)(2,1)}, bf16[1024,256]{1,0:T(8,128)(2,1)}, bf16[1024,256]{1,0:T(8,128)(2,1)}, bf16[512,1024]{1,0:T(8,128)(2,1)}) async-done(((bf16[1024,512]{1,0:T(8,128)(2,1)}, bf16[1024,256]{1,0:T(8,128)(2,1)}, bf16[1024,256]{1,0:T(8,128)(2,1)}, bf16[512,1024]{1,0:T(8,128)(2,1)}), (bf16[1024,512]{1,0:T(8,128)(2,1)}, bf16[1024,256]{1,0:T(8,128)(2,1)}, ...) | async-done | bytes 3145744 | tf_op jit(solution)/shard_map/psum | solution.py:277
  2117.2 2.8 convert_element_type.206
  2124.2 2.8 convert_element_type.212
  (232 shorter events, 51.1 us)
Async XLA Ops:
  7.2 63.5 %copy-start = (bf16[512,1024]{1,0:T(8,128)(2,1)S(1)}, bf16[512,1024]{1,0:T(8,128)(2,1)}, u32[]{:S(2)}) copy-start(bf16[512,1024]{1,0:T(8,128)(2,1)} %param.22) | copy-start | bytes 3145732
  7.2 11.9 copy-start.6
  7.2 11.9 copy-start.66
  7.2 152.8 %all-reduce.7.cloned.1.call-start = ((), (), s32[]{:S(2)}) async-start(), calls=%async_computation.6 | async-start | bytes 8388608 | tf_op jit(solution)/shard_map/psum | solution.py:137
  11.3 7.9 copy-start.27
  13.7 6.9 copy-start.60
  16.3 45.6 %copy-start.17 = (bf16[1024,256]{0,1:T(8,128)(2,1)}, bf16[1024,256]{0,1:T(8,128)(2,1)S(1)}, u32[]{:S(2)}) copy-start(bf16[1024,256]{0,1:T(8,128)(2,1)S(1)} %convolution_convert_fusion.5) | copy-start | bytes 1572868
  21.9 9.1 copy-start.43
  21.9 24.6 %copy-start.41 = (bf16[1024,4,32]{0,2,1:T(8,128)(2,1)}, bf16[1024,4,32]{0,2,1:T(8,128)(2,1)S(1)}, u32[]{:S(2)}) copy-start(bf16[1024,4,32]{0,2,1:T(8,128)(2,1)S(1)} %get-tuple-element.43) | copy-start | bytes 786436
  22.9 8.1 copy-start.37
  22.9 23.7 %copy-start.38 = (bf16[512,8,64]{0,2,1:T(8,128)(2,1)}, bf16[512,8,64]{0,2,1:T(8,128)(2,1)S(1)}, u32[]{:S(2)}) copy-start(bf16[512,8,64]{0,2,1:T(8,128)(2,1)S(1)} %get-tuple-element.47) | copy-start | bytes 1572868
  31.0 8.1 copy-start.56
  39.1 7.5 copy-start.58
  39.1 7.5 copy-start.44
  53.8 8.1 copy-start.52
  61.9 7.6 copy-start.54
  69.5 4.4 copy-start.23
  74.9 89.9 %copy-start.64 = (f32[1024]{0:T(1024)S(1)}, f32[1024]{0:T(1024)}, u32[]{:S(2)}) copy-start(f32[1024]{0:T(1024)} %param.23) | copy-start | bytes 12292
  94.2 65.2 %copy-start.47 = (s32[8192,1]{0,1:T(1,128)}, s32[8192,1]{0,1:T(1,128)S(1)}, u32[]{:S(2)}) copy-start(s32[8192,1]{0,1:T(1,128)S(1)} %compare_select_fusion) | copy-start | bytes 98308
  128.9 91.0 %copy-start.49 = (pred[16,768]{1,0:T(8,128)(4,1)}, pred[16,768]{1,0:T(8,128)(4,1)S(1)}, u32[]{:S(2)}) copy-start(pred[16,768]{1,0:T(8,128)(4,1)S(1)} %broadcast_in_dim.80) | copy-start | bytes 36868
  160.1 7.3 copy-start.39
  162.9 57.0 %copy-start.62 = (f32[1024]{0:T(1024)}, f32[1024]{0:T(1024)S(1)}, u32[]{:S(2)}) copy-start(f32[1024]{0:T(1024)S(1)} %add_rsqrt_fusion) | copy-start | bytes 12292
  231.4 9.1 copy-start.1
  231.4 245.7 %all-to-all-start = ((bf16[16,768,512]{2,1,0:T(8,128)(2,1)}), bf16[16,768,512]{2,1,0:T(8,128)(2,1)}, u32[]{:S(2)}, u32[]{:S(2)}) async-start(bf16[16,768,512]{2,1,0:T(8,128)(2,1)} %dynamic-slice_select_fusion), calls=%async_computation | async-start | bytes 25165824 | tf_op jit(solution)/shard_map/all_to_all | solution.py:69
  240.0 690.9 %all-gather.4.cloned.1.call-start = ((), (), s32[]{:S(2)}) async-start(), calls=%async_computation.7 | async-start | bytes 37748736 | tf_op jit(solution)/shard_map/all_gather | solution.py:70
  240.5 66.5 %copy-start.24 = (s32[1024,8]{0,1:T(8,128)S(1)}, s32[1024,8]{0,1:T(8,128)}, u32[]{:S(2)}) copy-start(s32[1024,8]{0,1:T(8,128)} %param.17) | copy-start | bytes 98308
  306.5 171.8 %copy-start.46 = (s32[12288]{0:T(1024)S(1)}, s32[12288]{0:T(1024)}, u32[]{:S(2)}) copy-start(s32[12288]{0:T(1024)} %get-tuple-element.49) | copy-start | bytes 147460
  477.2 494.2 %all-gather.6.cloned.1.call-start = ((), (), s32[]{:S(2)}) async-start(), calls=%async_computation.9 | async-start | bytes 37748736 | tf_op jit(solution)/shard_map/all_gather | solution.py:70
  478.3 68.1 %copy-start.2 = (f32[1024,512]{1,0:T(8,128)S(1)}, f32[1024,512]{1,0:T(8,128)}, u32[]{:S(2)}) copy-start(f32[1024,512]{1,0:T(8,128)} %param.27) | copy-start | bytes 6291460
  478.3 68.1 %copy-start.40 = (s32[12288]{0:T(1024)S(1)}, s32[12288]{0:T(1024)}, u32[]{:S(2)}) copy-start(s32[12288]{0:T(1024)} %copy-done.39) | copy-start | bytes 147460
  546.4 48.4 %copy-start.50 = (pred[16,768]{1,0:T(8,128)(4,1)S(1)}, pred[16,768]{1,0:T(8,128)(4,1)}, u32[]{:S(2)}) copy-start(pred[16,768]{1,0:T(8,128)(4,1)} %copy-done.49) | copy-start | bytes 36868
  930.8 186.9 %reduce-scatter.5.cloned.1.call-start = ((), (), s32[]{:S(2)}) async-start(), calls=%async_computation.10 | async-start | bytes 75497472 | tf_op jit(solution)/shard_map/reduce_scatter | solution.py:73
  931.8 22.1 %copy-start.30 = (bf16[1,1024,256]{2,1,0:T(8,128)(2,1)S(1)}, bf16[1,1024,256]{2,1,0:T(8,128)(2,1)}, u32[]{:S(2)}) copy-start(bf16[1,1024,256]{2,1,0:T(8,128)(2,1)} %param.24) | copy-start | bytes 1572868
  953.8 17.6 copy-start.32
  1054.3 130.2 %reduce-scatter.3.cloned.1.call-start = ((), (), s32[]{:S(2)}) async-start(), calls=%async_computation.8 | async-start | bytes 75497472 | tf_op jit(solution)/shard_map/reduce_scatter | solution.py:73
  1132.0 244.7 %all-to-all-start.3 = ((bf16[16,768,512]{2,1,0:T(8,128)(2,1)}), bf16[16,768,512]{2,1,0:T(8,128)(2,1)}, u32[]{:S(2)}, u32[]{:S(2)}) async-start(bf16[16,768,512]{2,1,0:T(8,128)(2,1)} %convert_element_type.184), calls=%async_computation.5 | async-start | bytes 25165824 | tf_op jit(solution)/shard_map/all_to_all | solution.py:81
  1197.7 233.8 %copy-start.65 = (f32[1024]{0:T(1024)S(1)}, f32[1024]{0:T(1024)}, u32[]{:S(2)}) copy-start(f32[1024]{0:T(1024)} %param.23) | copy-start | bytes 12292
  1197.7 233.9 %copy-start.57 = (f32[4,2,512]{2,1,0:T(2,128)S(1)}, f32[4,2,512]{2,1,0:T(2,128)}, u32[]{:S(2)}) copy-start(f32[4,2,512]{2,1,0:T(2,128)} %copy-done.56) | copy-start | bytes 49156
  1197.7 233.9 %copy-start.59 = (f32[4,2,512]{2,1,0:T(2,128)S(1)}, f32[4,2,512]{2,1,0:T(2,128)}, u32[]{:S(2)}) copy-start(f32[4,2,512]{2,1,0:T(2,128)} %copy-done.58) | copy-start | bytes 49156
  1197.8 234.0 %copy-start.48 = (s32[8192,1]{0,1:T(1,128)S(1)}, s32[8192,1]{0,1:T(1,128)}, u32[]{:S(2)}) copy-start(s32[8192,1]{0,1:T(1,128)} %copy-done.47) | copy-start | bytes 98308
  1376.7 289.1 %all-to-all-start.1 = ((bf16[16,768,512]{2,1,0:T(8,128)(2,1)}), bf16[16,768,512]{2,1,0:T(8,128)(2,1)}, u32[]{:S(2)}, u32[]{:S(2)}) async-start(bf16[16,768,512]{2,1,0:T(8,128)(2,1)} %convert_element_type.177), calls=%async_computation.2 | async-start | bytes 25165824 | tf_op jit(solution)/shard_map/all_to_all | solution.py:81
  1431.5 357.8 %all-gather.8.cloned.1.call-start = ((), (), s32[]{:S(2)}) async-start(), calls=%async_computation.11 | async-start | bytes 3145728 | tf_op jit(solution)/shard_map/all_gather | solution.py:211
  1665.8 40.1 %copy-start.3 = (f32[1024,512]{1,0:T(8,128)S(1)}, f32[1024,512]{1,0:T(8,128)}, u32[]{:S(2)}) copy-start(f32[1024,512]{1,0:T(8,128)} %param.27) | copy-start | bytes 6291460
  1705.9 18.1 copy-start.63
  1717.4 11.1 copy-start.53
  1717.4 11.1 copy-start.55
  1728.5 246.5 %all-reduce.9.cloned.1.call-start = ((), (), s32[]{:S(2)}) async-start(), calls=%async_computation.12 | async-start | bytes 4194304 | tf_op jit(solution)/shard_map/psum | solution.py:268
  1742.8 49.6 %copy-start.18 = (bf16[1024,256]{0,1:T(8,128)(2,1)S(1)}, bf16[1024,256]{0,1:T(8,128)(2,1)}, u32[]{:S(2)}) copy-start(bf16[1024,256]{0,1:T(8,128)(2,1)} %copy-done.17) | copy-start | bytes 1572868
  1800.5 7.3 copy-start.42
  1863.0 9.3 copy-start.33
  1863.0 12.0 copy-start.45
  1903.3 24.7 %copy-start.16 = (f32[1024,32]{0,1:T(8,128)S(1)}, f32[1024,32]{0,1:T(8,128)}, u32[]{:S(2)}) copy-start(f32[1024,32]{0,1:T(8,128)} %copy-done.15) | copy-start | bytes 393220
  1903.3 24.7 %copy-start.26 = (f32[1024,32]{0,1:T(8,128)S(1)}, f32[1024,32]{0,1:T(8,128)}, u32[]{:S(2)}) copy-start(f32[1024,32]{0,1:T(8,128)} %get-tuple-element.51) | copy-start | bytes 393220
  1903.3 24.9 %copy-start.29 = (f32[512,4,2,64]{0,3,2,1:T(8,128)S(1)}, f32[512,4,2,64]{0,3,2,1:T(8,128)}, u32[]{:S(2)}) copy-start(f32[512,4,2,64]{0,3,2,1:T(8,128)} %fusion.39) | copy-start | bytes 3145732
  1934.6 14.7 copy-start.7
  1934.6 14.6 copy-start.61
  1934.7 14.6 copy-start.67
  1934.7 182.5 %all-reduce.11.cloned.1.call-start = ((), (), s32[]{:S(2)}) async-start(), calls=%async_computation.13 | async-start | bytes 6291456 | tf_op jit(solution)/shard_map/psum | solution.py:277
  1934.7 14.6 copy-start.20
  1951.3 4.1 copy-start.14
  1958.0 14.9 copy-start.36
  1958.0 14.9 copy-start.25
  1958.0 15.6 copy-start.5
  1958.0 15.6 copy-start.9
  (16 other events, 31.6 us)
Sparse Core Ops, SparseCore 0:
  74.1 31.1 all-reduce.6
  477.3 89.2 all-gather.3
  930.9 39.1 all-gather.5
  1054.4 63.1 reduce-scatter.4
  1119.9 64.5 reduce-scatter.2
  1728.6 60.7 all-gather.7
  1934.8 26.0 all-reduce.8
  1967.5 149.6 all-reduce.10
where the time goes:
time: 2140 us; the launch traced here: 2130 us
  waiting for transfers between devices  741 us (35%)
  local copies, waits for them, and re-layouts  398 us (19%)
  matrix products  390 us (18%)
  blocking collectives  374 us (17%)
  other arithmetic  144 us (7%)
  starting transfers between devices  70.8 us (3%)
    all_to_all x2, waiting for transfers between devices, home_back(): lax.all_to_all(cols, 'expert', split_axis=0, concat_axis=0, tiled=True)  363 us
    all_to_all x1, blocking collectives, to_expert(): lax.all_to_all(x_cols, 'expert', split_axis=0, concat_axis=0, tiled=True)  327 us
    all_to_all x1, waiting for transfers between devices, to_expert(): lax.all_to_all(x_cols, 'expert', split_axis=0, concat_axis=0, tiled=True)  170 us
    psum x1, waiting for transfers between devices, body(): lax.psum(query_grad.astype(jnp.bfloat16), 'expert').astype(jnp.float32)  87.1 us
    reduce_scatter x2, waiting for transfers between devices, part_sum(): lax.psum_scatter(terms.reshape(n_experts, capacity, model_width), 'tensor...  74.4 us
    gather x1, local copies, waits for them, and re-layouts, body(): slot_gate = gates.reshape(-1)[pair_of_slot]  68 us
    gather x5, local copies, waits for them, and re-layouts, body(): chosen = jnp.take_along_axis(router_logits, expert_ids, axis=1)  66.9 us
    all_to_all x2, starting transfers between devices, home_back(): lax.all_to_all(cols, 'expert', split_axis=0, concat_axis=0, tiled=True)  62 us
  transfers between devices with their start and end apart: 11, of which 7 were waited for; matrix products, arithmetic and copies ran while one was open for 23% of the time, Pallas kernels for 0%

commit v1 on v0

v1 whole, which is shorter than its diff:
```python
import functools

import jax
import jax.numpy as jnp
from jax import lax
from jax.experimental import pallas as pl
from jax.experimental.pallas import tpu as pltpu
from jax.sharding import PartitionSpec as P

HEAD_SIZE = 64
EPS = 1e-06
THETA = 10000.0
NEG = -1e30
PLANE = 4
F32 = jnp.float32
BF16 = jnp.bfloat16
NT = (((1,), (1,)), ((), ()))
TN = (((0,), (0,)), ((), ()))


def dot(a, b):
    return jnp.dot(a, b, preferred_element_type=F32)


def dot_nt(a, b):
    return lax.dot_general(a, b, NT, preferred_element_type=F32)


def dot_tn(a, b):
    return lax.dot_general(a, b, TN, preferred_element_type=F32)


def attn_mask(start, row_start, block, keys):
    first = start[:, row_start : row_start + block]
    first = jnp.concatenate([first, first], axis=1)
    key_at = lax.broadcasted_iota(jnp.int32, (keys, 2 * block), 0)
    lane = lax.broadcasted_iota(jnp.int32, (1, 2 * block), 1)
    row_at = row_start + jnp.where(lane >= block, lane - block, lane)
    return (key_at >= first) & (key_at <= row_at)


def rope(x, c, s):
    half = x.shape[0] // 2
    a, b = x[:half], x[half:]
    return jnp.concatenate([a * c - b * s, b * c + a * s], axis=0)


def attn_fwd_kernel(block, q_ref, k_ref, v_ref, cos_ref, sin_ref, start_ref, qo_ref, ko_ref, o_ref, lse_ref):
    hd = HEAD_SIZE
    n = k_ref.shape[1]
    c, s = cos_ref[...], sin_ref[...]
    k_rot = rope(k_ref[...], c, s)
    ko_ref[...] = k_rot.astype(BF16)
    keys = k_rot.T.astype(BF16)
    q0 = rope(q_ref[0:hd], c, s).astype(BF16)
    q1 = rope(q_ref[hd : 2 * hd], c, s).astype(BF16)
    qo_ref[0:hd] = q0
    qo_ref[hd : 2 * hd] = q1
    start = start_ref[...]
    for r0 in range(0, n, block):
        cn = r0 + block
        qb = jnp.concatenate([q0[:, r0:cn], q1[:, r0:cn]], axis=1) * jnp.asarray(hd**-0.5, BF16)
        scores = dot(keys[:cn], qb)
        scores = jnp.where(attn_mask(start, r0, block, cn), scores, NEG)
        peak = jnp.max(scores, axis=0, keepdims=True)
        p = jnp.exp(scores - peak)
        total = jnp.sum(p, axis=0, keepdims=True)
        o = dot(v_ref[:, :cn], p.astype(BF16)) / total
        o_ref[0:hd, r0:cn] = o[:, :block].astype(BF16)
        o_ref[hd : 2 * hd, r0:cn] = o[:, block:].astype(BF16)
        lse = peak + jnp.log(total)
        lse_ref[0, 0:1, r0:cn] = lse[:, :block]
        lse_ref[0, 1:2, r0:cn] = lse[:, block:]


def attn_bwd_kernel(
    block, q_ref, k_ref, v_ref, do_ref, lse_ref, cos_ref, sin_ref, start_ref, dq_ref, dk_ref, dv_ref, dk_acc, dv_acc
):
    hd = HEAD_SIZE
    n = k_ref.shape[1]
    c, s = cos_ref[...], sin_ref[...]
    keys = k_ref[...].astype(F32).T.astype(BF16)
    vals = v_ref[...].astype(F32).T.astype(BF16)
    start = start_ref[...]
    dk_acc[...] = jnp.zeros_like(dk_acc)
    dv_acc[...] = jnp.zeros_like(dv_acc)
    scale = hd**-0.5
    for r0 in range(0, n, block):
        cn = r0 + block
        qb = jnp.concatenate([q_ref[0:hd, r0:cn], q_ref[hd : 2 * hd, r0:cn]], axis=1)
        gb = jnp.concatenate([do_ref[0:hd, r0:cn], do_ref[hd : 2 * hd, r0:cn]], axis=1)
        lse = jnp.concatenate([lse_ref[0, 0:1, r0:cn], lse_ref[0, 1:2, r0:cn]], axis=1)
        scores = dot(keys[:cn], qb * jnp.asarray(scale, BF16))
        p = jnp.exp(jnp.where(attn_mask(start, r0, block, cn), scores, NEG) - lse)
        dv_acc[:, :cn] += dot_nt(gb, p.astype(BF16))
        dp = dot(vals[:cn], gb)
        delta = jnp.sum(p * dp, axis=0, keepdims=True)
        ds = (p * (dp - delta) * scale).astype(BF16)
        dq = dot(k_ref[:, :cn], ds)
        dk_acc[:, :cn] += dot_nt(qb, ds)
        cb, sb = c[:, r0:cn], -s[:, r0:cn]
        dq_ref[0:hd, r0:cn] = rope(dq[:, :block], cb, sb).astype(BF16)
        dq_ref[hd : 2 * hd, r0:cn] = rope(dq[:, block:], cb, sb).astype(BF16)
    dk_ref[...] = rope(dk_acc[...], c, -s).astype(BF16)
    dv_ref[...] = dv_acc[...].astype(BF16)


def attn_cost(heads, n, products):
    return pl.CostEstimate(
        flops=products * heads * n * n * HEAD_SIZE * 2, bytes_accessed=8 * heads * n * HEAD_SIZE, transcendentals=heads * n * n
    )


def attn_forward(q_t, k_t, v_t, cos_t, sin_t, start):
    n = q_t.shape[1]
    hd = HEAD_SIZE
    kv = k_t.shape[0] // hd
    block = min(256, n)
    pair = pl.BlockSpec((2 * hd, n), lambda h: (h, 0))
    one = pl.BlockSpec((hd, n), lambda h: (h, 0))
    table = pl.BlockSpec((hd // 2, n), lambda h: (0, 0))
    return pl.pallas_call(
        functools.partial(attn_fwd_kernel, block),
        grid=(kv,),
        in_specs=[pair, one, one, table, table, pl.BlockSpec((1, n), lambda h: (0, 0))],
        out_specs=[pair, one, pair, pl.BlockSpec((1, 2, n), lambda h: (h, 0, 0))],
        out_shape=[
            jax.ShapeDtypeStruct(q_t.shape, BF16),
            jax.ShapeDtypeStruct(k_t.shape, BF16),
            jax.ShapeDtypeStruct(q_t.shape, BF16),
            jax.ShapeDtypeStruct((kv, 2, n), F32),
        ],
        compiler_params=pltpu.CompilerParams(vmem_limit_bytes=48 * 2**20),
        cost_estimate=attn_cost(2 * kv, n, 4),
        name="attn_forward",
    )(q_t, k_t, v_t, cos_t, sin_t, start)


def attn_backward(q_t, k_t, v_t, do_t, lse, cos_t, sin_t, start):
    n = q_t.shape[1]
    hd = HEAD_SIZE
    kv = k_t.shape[0] // hd
    block = min(256, n)
    pair = pl.BlockSpec((2 * hd, n), lambda h: (h, 0))
    one = pl.BlockSpec((hd, n), lambda h: (h, 0))
    table = pl.BlockSpec((hd // 2, n), lambda h: (0, 0))
    return pl.pallas_call(
        functools.partial(attn_bwd_kernel, block),
        grid=(kv,),
        in_specs=[
            pair,
            one,
            one,
            pair,
            pl.BlockSpec((1, 2, n), lambda h: (h, 0, 0)),
            table,
            table,
            pl.BlockSpec((1, n), lambda h: (0, 0)),
        ],
        out_specs=[pair, one, one],
        out_shape=[
            jax.ShapeDtypeStruct(q_t.shape, BF16),
            jax.ShapeDtypeStruct(k_t.shape, BF16),
            jax.ShapeDtypeStruct(k_t.shape, BF16),
        ],
        scratch_shapes=[pltpu.VMEM((hd, n), F32), pltpu.VMEM((hd, n), F32)],
        compiler_params=pltpu.CompilerParams(vmem_limit_bytes=48 * 2**20),
        cost_estimate=attn_cost(2 * kv, n, 10),
        name="attn_backward",
    )(q_t, k_t, v_t, do_t, lse, cos_t, sin_t, start)


def moe_kernel(first, pieces, expert_ref, *refs):
    refs = list(refs)
    x_ref, g_ref, gates_ref = refs[:3]
    wg, wu, wd = refs[3 : 3 + pieces], refs[3 + pieces : 3 + 2 * pieces], refs[3 + 2 * pieces : 3 + 3 * pieces]
    refs = refs[3 + 3 * pieces :]
    if not first:
        out_in, dx_in, dgate_in = refs[:3]
        refs = refs[3:]
    out_ref, dx_ref, dgate_ref = refs[:3]
    refs = refs[3:]
    og, ou, od = refs[:pieces], refs[pieces : 2 * pieces], refs[2 * pieces : 3 * pieces]
    acc_g, acc_u, acc_d = refs[3 * pieces :]
    step, steps = pl.program_id(0), pl.num_programs(0)

    @pl.when(step == 0)
    def _():
        acc_g[...] = jnp.zeros_like(acc_g)
        acc_u[...] = jnp.zeros_like(acc_u)
        acc_d[...] = jnp.zeros_like(acc_d)

    x, g = x_ref[...], g_ref[...]
    here = lax.broadcasted_iota(jnp.int32, gates_ref.shape, 1) == expert_ref[0]
    gate = jnp.sum(jnp.where(here, gates_ref[...], 0.0), axis=1, keepdims=True)
    x_t = x.T
    row_sum = None
    for i in range(pieces):
        gate_pre = dot(x, wg[i][...])
        up_pre = dot(x, wu[i][...])
        d_hidden = dot_nt(g, wd[i][...])
        sig = jax.nn.sigmoid(gate_pre)
        silu = gate_pre * sig
        act = silu * up_pre
        part = jnp.sum(act * d_hidden, axis=1, keepdims=True)
        row_sum = part if row_sum is None else row_sum + part
        act_w = (act * gate).astype(BF16)
        d_hidden = d_hidden * gate
        d_up = (d_hidden * silu).astype(BF16)
        d_gate = (d_hidden * up_pre * sig * (1.0 + gate_pre * (1.0 - sig))).astype(BF16)
        out_term = dot(act_w, wd[i][...])
        dx_term = dot_nt(d_gate, wg[i][...]) + dot_nt(d_up, wu[i][...])
        if i == 0 and first:
            out_ref[...] = out_term
            dx_ref[...] = dx_term
        elif i == 0:
            out_ref[...] = out_in[...] + out_term
            dx_ref[...] = dx_in[...] + dx_term
        else:
            out_ref[...] += out_term
            dx_ref[...] += dx_term
        acc_g[i] += dot(x_t, d_gate)
        acc_u[i] += dot(x_t, d_up)
        acc_d[i] += dot_tn(act_w, g)
    dgate_term = jnp.where(here, row_sum, 0.0)
    dgate_ref[...] = dgate_term if first else dgate_in[...] + dgate_term

    @pl.when(step == steps - 1)
    def _():
        for i in range(pieces):
            og[i][...] = acc_g[i].astype(BF16)
            ou[i][...] = acc_u[i].astype(BF16)
            od[i][...] = acc_d[i].astype(BF16)


def moe_slot(expert, x, g, gates, wg, wu, wd, carry, tile):
    rows, width = x.shape
    experts = gates.shape[1]
    pieces = len(wg)
    hidden = wg[0].shape[1]
    first = carry is None
    wide = pl.BlockSpec((tile, width), lambda i: (i, 0))
    thin = pl.BlockSpec((tile, experts), lambda i: (i, 0))
    tall = pl.BlockSpec((width, hidden), lambda i: (0, 0))
    flat = pl.BlockSpec((hidden, width), lambda i: (0, 0))
    ins = [expert, x, g, gates, *wg, *wu, *wd]
    specs = [pl.BlockSpec(memory_space=pltpu.SMEM), wide, wide, thin] + [tall] * (2 * pieces) + [flat] * pieces
    if not first:
        ins += list(carry)
        specs += [wide, wide, thin]
    outs = pl.pallas_call(
        functools.partial(moe_kernel, first, pieces),
        grid=(rows // tile,),
        in_specs=specs,
        out_specs=[wide, wide, thin] + [tall] * (2 * pieces) + [flat] * pieces,
        out_shape=[
            jax.ShapeDtypeStruct((rows, width), F32),
            jax.ShapeDtypeStruct((rows, width), F32),
            jax.ShapeDtypeStruct((rows, experts), F32),
        ]
        + [jax.ShapeDtypeStruct((width, hidden), BF16)] * (2 * pieces)
        + [jax.ShapeDtypeStruct((hidden, width), BF16)] * pieces,
        scratch_shapes=[
            pltpu.VMEM((pieces, width, hidden), F32),
            pltpu.VMEM((pieces, width, hidden), F32),
            pltpu.VMEM((pieces, hidden, width), F32),
        ],
        compiler_params=pltpu.CompilerParams(vmem_limit_bytes=60 * 2**20),
        cost_estimate=pl.CostEstimate(
            flops=18 * rows * width * hidden * pieces,
            bytes_accessed=rows * width * 20 + width * hidden * pieces * 12,
            transcendentals=rows * hidden * pieces,
        ),
        name="moe_slot",
    )(*ins)
    grads = outs[3:]
    return (
        tuple(outs[:3]),
        [(grads[i], grads[pieces + i], grads[2 * pieces + i]) for i in range(pieces)],
    )


def body(
    tokens,
    segment_ids,
    router_logits,
    expert_ids,
    gain_attn,
    w_query,
    key_matrix,
    value_matrix,
    w_out,
    gain_mlp,
    w_gate,
    w_up,
    w_down,
    out_grad,
):
    n_tok, width = tokens.shape
    col_width = out_grad.shape[1]
    n_tensor = width // col_width
    n_expert = router_logits.shape[1]
    depth = n_expert // PLANE
    my_row = n_tok // n_tensor
    t_at = lax.axis_index("tensor")
    e_at = lax.axis_index("expert")

    def hop(x, step):
        pairs = [(i, (i + step) % n_tensor) for i in range(n_tensor)]
        return jax.tree.map(lambda a: lax.ppermute(a, "tensor", pairs), x)

    def plane(x, mask):
        pairs = [(i, i ^ mask) for i in range(n_expert)]
        return jax.tree.map(lambda a: lax.ppermute(a, "expert", pairs), x)

    def ring(x, step=1):
        pairs = [(i, (i + step * PLANE) % n_expert) for i in range(n_expert)]
        return jax.tree.map(lambda a: lax.ppermute(a, "expert", pairs), x)

    def peer(step):
        return lax.rem(t_at + step + n_tensor, n_tensor)

    def rows_of(x, who):
        return lax.dynamic_slice_in_dim(x, who * my_row, my_row, 0)

    def cols_of(x, who):
        return lax.dynamic_slice_in_dim(x, who * col_width, col_width, x.ndim - 1)

    def to_rows(x):
        out = jnp.zeros((my_row, width), x.dtype)
        out = lax.dynamic_update_slice(out, rows_of(x, t_at), (0, t_at * col_width))
        for s in range(1, n_tensor):
            got = hop(rows_of(x, peer(s)), s)
            out = lax.dynamic_update_slice(out, got, (0, peer(-s) * col_width))
        return out

    def to_cols(x):
        out = jnp.zeros((n_tok, col_width), x.dtype)
        out = lax.dynamic_update_slice(out, cols_of(x, t_at), (t_at * my_row, 0))
        for s in range(1, n_tensor):
            got = hop(cols_of(x, peer(s)), s)
            out = lax.dynamic_update_slice(out, got, (peer(-s) * my_row, 0))
        return out

    def gather_rows(x):
        out = jnp.zeros((n_tok,) + x.shape[1:], x.dtype)
        rest = (0,) * (x.ndim - 1)
        out = lax.dynamic_update_slice(out, x, (t_at * my_row,) + rest)
        for s in range(1, n_tensor):
            out = lax.dynamic_update_slice(out, hop(x, s), (peer(-s) * my_row,) + rest)
        return out

    slots = []
    held = (w_gate[0], w_up[0], w_down[0])
    for k in range(depth):
        if k:
            held = ring(held)
        slots.append([held] + [hop(held, s) for s in range(1, n_tensor)])

    ids_rows = rows_of(expert_ids, t_at)
    logit_rows = rows_of(router_logits, t_at)
    expert_range = jnp.arange(n_expert, dtype=jnp.int32)
    used = jnp.any(ids_rows[:, :, None] == expert_range[None, None, :], axis=1)
    masked = jnp.where(used, logit_rows, NEG)
    weights = jnp.where(used, jnp.exp(masked - jnp.max(masked, axis=1, keepdims=True)), 0.0)
    gates = weights / jnp.sum(weights, axis=1, keepdims=True)
    grad_rows = to_rows(out_grad.astype(BF16))
    masks = range(1, PLANE)
    gates_all = jnp.concatenate([gates] + [plane(gates, m) for m in masks], axis=0)
    grads_all = jnp.concatenate([grad_rows] + [plane(grad_rows, m) for m in masks], axis=0)
    out_pieces = [w_out] + [hop(w_out, s) for s in range(1, n_tensor)]

    start = jnp.sum((segment_ids[:, None] < segment_ids[None, :]).astype(jnp.int32), axis=0)
    places = jnp.arange(n_tok, dtype=jnp.int32) - start
    half = HEAD_SIZE // 2
    freq = jnp.power(THETA, -2.0 * jnp.arange(half, dtype=F32) / HEAD_SIZE)
    angles = freq[:, None] * places.astype(F32)[None, :]
    cos_t, sin_t = jnp.cos(angles), jnp.sin(angles)
    start = start[None, :]
    x_full = tokens.astype(F32)
    inv_one = lax.rsqrt(jnp.mean(x_full * x_full, axis=1, keepdims=True) + EPS)
    normed_one = x_full * inv_one
    attn_in = (normed_one * gain_attn).astype(BF16)

    def project(w):
        return jnp.einsum("td,dc->ct", attn_in, w, preferred_element_type=F32)

    q_t, k_t, o_t, lse = attn_forward(
        project(w_query), project(key_matrix), project(value_matrix).astype(BF16), cos_t, sin_t, start
    )
    v_t = project(value_matrix).astype(BF16)
    mixed = rows_of(tokens, t_at).astype(F32)
    for s in range(n_tensor):
        part = lax.dynamic_slice_in_dim(o_t, peer(s) * my_row, my_row, 1)
        if s:
            part = hop(part, s)
        mixed = mixed + jnp.einsum("ct,cd->td", part, out_pieces[s], preferred_element_type=F32)
    inv_two = lax.rsqrt(jnp.mean(mixed * mixed, axis=1, keepdims=True) + EPS)
    normed_two = mixed * inv_two
    mlp_in = (normed_two * gain_mlp).astype(BF16)
    mlp_all = jnp.concatenate([mlp_in] + [plane(mlp_in, m) for m in masks], axis=0)

    carry = None
    totals = []
    for k in range(depth):
        expert = lax.rem(e_at - k * PLANE + n_expert, n_expert).reshape(1)
        wg, wu, wd = zip(*slots[k])
        carry, grads = moe_slot(expert, mlp_all, grads_all, gates_all, wg, wu, wd, carry, my_row)
        total = [a.astype(F32) for a in grads[0]]
        for s in range(1, n_tensor):
            got = hop(grads[s], n_tensor - s)
            total = [a + b.astype(F32) for a, b in zip(total, got)]
        totals.append(total)
    moving = None
    for k in list(range(1, depth)) + [0]:
        total = totals[k]
        if moving is not None:
            total = [a + b.astype(F32) for a, b in zip(total, ring(moving))]
        moving = [a.astype(BF16) for a in total]
    grad_gate, grad_up, grad_down = (a[None] for a in total)

    out_all, dx_all, dgate_all = carry

    def home(x):
        total = x[:my_row].astype(F32)
        for m in masks:
            total = total + plane(x[m * my_row : (m + 1) * my_row], m).astype(F32)
        return total

    d_mlp_in = home(dx_all.astype(BF16))
    d_gates = home(dgate_all)
    block_out = to_cols((mixed + home(out_all.astype(BF16))).astype(BF16))
    grad_logits = gather_rows(gates * (d_gates - jnp.sum(gates * d_gates, axis=1, keepdims=True)))

    scaled_two = d_mlp_in * gain_mlp
    norm_dots = jnp.mean(scaled_two * normed_two, axis=1, keepdims=True)
    d_mixed = grad_rows.astype(F32) + inv_two * (scaled_two - normed_two * norm_dots)
    gain_two_all = jnp.sum(d_mlp_in * normed_two, axis=0)
    gain_two = cols_of(gain_two_all, t_at)
    for s in range(1, n_tensor):
        gain_two = gain_two + hop(cols_of(gain_two_all, peer(s)), s)
    dy_full = gather_rows(d_mixed.astype(BF16))

    out_grad_w = jnp.einsum("ct,td->cd", o_t, dy_full, preferred_element_type=F32)
    grad_out = lax.psum(out_grad_w.astype(BF16), "expert").astype(F32)
    do_t = jnp.einsum("td,cd->ct", dy_full, w_out, preferred_element_type=F32).astype(BF16)
    dq_t, dk_t, dv_t = attn_backward(q_t, k_t, v_t, do_t, lse, cos_t, sin_t, start)

    def weight_grad(d_t):
        return jnp.einsum("td,ct->dc", attn_in, d_t, preferred_element_type=F32).astype(BF16)

    def input_grad(d_t, w):
        return jnp.einsum("ct,dc->td", d_t, w, preferred_element_type=F32)

    grad_query, grad_key, grad_value = (
        a.astype(F32) for a in lax.psum((weight_grad(dq_t), weight_grad(dk_t), weight_grad(dv_t)), "expert")
    )
    in_terms = input_grad(dq_t, w_query) + input_grad(dk_t, key_matrix) + input_grad(dv_t, value_matrix)
    dots = jnp.sum(in_terms * gain_attn * normed_one, axis=1)
    d_attn_in = cols_of(in_terms, t_at)
    all_dots = dots
    for s in range(1, n_tensor):
        d_attn_in = d_attn_in + hop(cols_of(in_terms, peer(s)).astype(BF16), s).astype(F32)
        all_dots = all_dots + hop(dots, s)
    normed_cols = cols_of(normed_one, t_at)
    scaled_one = d_attn_in * cols_of(gain_attn, t_at)
    d_norm_one = inv_one * (scaled_one - normed_cols * (all_dots / width)[:, None])
    grad_tokens = cols_of(dy_full, t_at).astype(F32) + d_norm_one
    gain_one = jnp.sum(d_attn_in * normed_cols, axis=0)

    gains = jnp.stack([gain_one, gain_two])
    for m in (1, 2):
        gains = gains + plane(gains, m)
    gains = functools.reduce(jnp.add, [gains] + [ring(gains, s) for s in range(1, depth)])
    return (
        block_out,
        grad_tokens,
        grad_logits,
        gains[0],
        grad_query,
        grad_key,
        grad_value,
        grad_out,
        gains[1],
        grad_gate,
        grad_up,
        grad_down,
    )


def solution(mesh):
    return jax.shard_map(
        body,
        mesh=mesh,
        in_specs=(
            P("expert", None),
            P("expert"),
            P("expert", None),
            P("expert", None),
            P(),
            P(None, "tensor"),
            P(None, "tensor"),
            P(None, "tensor"),
            P("tensor", None),
            P(),
            P("expert", None, "tensor"),
            P("expert", None, "tensor"),
            P("expert", "tensor", None),
            P("expert", "tensor"),
        ),
        out_specs=(
            P("expert", "tensor"),
            P("expert", "tensor"),
            P("expert", None),
            P("tensor"),
            P(None, "tensor"),
            P(None, "tensor"),
            P(None, "tensor"),
            P("tensor", None),
            P("tensor"),
            P("expert", None, "tensor"),
            P("expert", None, "tensor"),
            P("expert", "tensor", None),
        ),
        check_vma=False,
    )
```

time: 2140 us -> 736 us (0.34)
  local copies, waits for them, and re-layouts: 398 us -> 21.1 us
  blocking collectives: 374 us -> 0 us
  waiting for transfers between devices: 741 us -> 370 us
  matrix products: 390 us -> 27.5 us
  Pallas kernels: 0 us -> 162 us
  other arithmetic: 144 us -> 58.4 us
    all_to_all x3 -> x0, waiting for transfers between devices: 533 us -> none  [the longest x2 363 us: home_back(): lax.all_to_all(cols, 'expert', split_axis=0, concat_axis=0, tiled=True)]
    dot_general x33 -> x13, matrix products: 390 us -> 27.5 us  [the longest x3 7.22 us: input_grad(): return jnp.einsum('ct,dc->td', d_t, w, preferred_element_type=F32)]
    all_to_all x1 -> x0, blocking collectives: 327 us -> none  [to_expert(): lax.all_to_all(x_cols, 'expert', split_axis=0, concat_axis=0, tiled=True)]
    gather x10 -> x0, local copies, waits for them, and re-layouts: 316 us -> none  [the longest x1 68 us: body(): slot_gate = gates.reshape(-1)[pair_of_slot]]
    ppermute x0 -> x74, waiting for transfers between devices: none -> 294 us  [the longest x20 214 us: plane(): return jax.tree.map(lambda a: lax.ppermute(a, 'expert', pairs), x)]
    pallas_call x0 -> x6, Pallas kernels: none -> 162 us  [the longest x4 131 us: moe_slot(): pl.pallas_call(functools.partial(moe_kernel, first, pieces), grid=(rows /...]
    reduce_scatter x2 -> x0, waiting for transfers between devices: 74.4 us -> none  [part_sum(): lax.psum_scatter(terms.reshape(n_experts, capacity, model_width), 'tensor...]
    ppermute x0 -> x74, starting transfers between devices: none -> 72.5 us  [the longest x21 40.8 us: ring(): return jax.tree.map(lambda a: lax.ppermute(a, 'expert', pairs), x)]
  transfers between devices with their start and end apart: 11 -> 75, of which waited for: 7 -> 21; matrix products, arithmetic and copies ran while one was open for 23% -> 12% of each run, Pallas kernels for 0% -> 16%
where the time goes in v1:
time: 736 us; the launch traced here: 727 us
  waiting for transfers between devices  370 us (50%)
  Pallas kernels  162 us (22%)
  starting transfers between devices  72.5 us (10%)
  other arithmetic  58.4 us (8%)
  matrix products  27.5 us (4%)
  local copies, waits for them, and re-layouts  21.1 us (3%)
  between operations  15.5 us (2%)
    ppermute x20, waiting for transfers between devices, plane(): return jax.tree.map(lambda a: lax.ppermute(a, 'expert', pairs), x)  214 us
    pallas_call x4, Pallas kernels, moe_slot(): pl.pallas_call(functools.partial(moe_kernel, first, pieces), grid=(rows /...  131 us
    ppermute x21, waiting for transfers between devices, ring(): return jax.tree.map(lambda a: lax.ppermute(a, 'expert', pairs), x)  79.6 us
    psum x1, waiting for transfers between devices, body(): lax.psum((weight_grad(dq_t), weight_grad(dk_t), weight_grad(dv_t)), 'expe...  76 us
    ppermute x21, starting transfers between devices, ring(): return jax.tree.map(lambda a: lax.ppermute(a, 'expert', pairs), x)  40.8 us
    ppermute x20, starting transfers between devices, plane(): return jax.tree.map(lambda a: lax.ppermute(a, 'expert', pairs), x)  25.6 us
    pallas_call x1, Pallas kernels, attn_backward(): pl.pallas_call(functools.partial(attn_bwd_kernel, block), grid=(kv,), in_...  19.8 us
  transfers between devices with their start and end apart: 75, of which 21 were waited for; matrix products, arithmetic and copies ran while one was open for 12% of the time, Pallas kernels for 16%

profile of v1, /device:TPU:0, one launch (start us, length us, event | category | flops | bytes accessed | tf_op | source)
XLA Modules:
  0.0 727.4 jit_solution(13523608387544242275)
XLA Ops:
  7.2 2.8 convert_element_type.242
  11.1 2.4 constant_dynamic-slice_fusion.3
  15.5 2.8 convolution_bitcast_fusion.q_ref
  20.3 11.6 %attn_forward.1 = (bf16[512,1024]{1,0:T(8,128)(2,1)S(1)}, bf16[256,1024]{1,0:T(8,128)(2,1)S(1)}, bf16[512,1024]{1,0:T(8,128)(2,1)S(1)}, f32[4,2,1024]{2,1,0:T(2,128)S(1)}) custom-call(f32[512,1024]{1,0:T(8,128)} %convolution_bitcast_fusion.q_ref, f32[256,1024]{1,0:T(8,128)S(1)} %convolution_bitcast_fusion.1.k_ref, bf16[256,1024]{1,0:T(8,128)(2,1)S(1)} %fusion.2.v_ref, ...), custom_call_target="tpu_custom_call" | custom-call | flops 4294967296 | bytes 4194304 | tf_op jit(solution)/shard_map/attn_forward/pallas_call | solution.py:122
  37.6 1.9 fusion.6
  39.5 2.5 collective-permute-start.10
  43.4 1.9 constant_dynamic-update-slice_fusion.5
  45.4 2.1 fusion.3
  47.5 1.9 collective-permute-start.9
  49.5 2.3 multiply_reduce_fusion.4
  51.8 3.1 collective-permute-done.10
  54.9 1.8 collective-permute-start.12
  56.7 21.9 %collective-permute-done.9 = f32[512,16]{1,0:T(8,128)} collective-permute-done((f32[512,16]{1,0:T(8,128)}, f32[512,16]{1,0:T(8,128)}, u32[]{:S(2)}, u32[]{:S(2)}) %collective-permute-start.9) | collective-permute-done | bytes 32800 | tf_op jit(solution)/shard_map/ppermute | solution.py:314
  78.6 1.7 collective-permute-start.7
  85.0 1.7 collective-permute-start.3
  88.1 2.3 pad_maximum_fusion.2.refs_2_
  90.4 37.4 %collective-permute-done.7 = bf16[512,1024]{1,0:T(8,128)(2,1)} collective-permute-done((bf16[512,1024]{1,0:T(8,128)(2,1)}, bf16[512,1024]{1,0:T(8,128)(2,1)}, u32[]{:S(2)}, u32[]{:S(2)}) %collective-permute-start.7) | collective-permute-done | bytes 1048608 | tf_op jit(solution)/shard_map/ppermute | solution.py:314
  127.8 2.0 collective-permute-start.16
  129.8 1.7 collective-permute-start.20
  131.5 39.6 %collective-permute-done.3 = bf16[512,1024]{1,0:T(8,128)(2,1)} collective-permute-done((bf16[512,1024]{1,0:T(8,128)(2,1)}, bf16[512,1024]{1,0:T(8,128)(2,1)}, u32[]{:S(2)}, u32[]{:S(2)}) %collective-permute-start.3) | collective-permute-done | bytes 1048608 | tf_op jit(solution)/shard_map/ppermute | solution.py:314
  172.7 3.7 pad_maximum_fusion.1.refs_1_
  176.3 3.7 pad_maximum_fusion.refs_0_
  180.2 1.9 collective-permute-start.17
  183.7 4.2 collective-permute-done.13.refs_3_
  187.9 28.1 %moe_slot.4 = (f32[2048,1024]{1,0:T(8,128)}, f32[2048,1024]{1,0:T(8,128)}, f32[2048,16]{1,0:T(8,128)}, bf16[1024,256]{1,0:T(8,128)(2,1)}, bf16[1024,256]{1,0:T(8...) custom-call(s32[1]{0:T(128)} %bitcast.10.expert_ref, ...), custom_call_target="tpu_custom_call" | custom-call | flops 19327352832 | bytes 48234496 | tf_op jit(solution)/shard_map/moe_slot/pallas_call | solution.py:251
  219.1 30.2 %moe_slot.5 = (f32[2048,1024]{1,0:T(8,128)}, f32[2048,1024]{1,0:T(8,128)}, f32[2048,16]{1,0:T(8,128)}, bf16[1024,256]{1,0:T(8,128)(2,1)}, bf16[1024,256]{1,0:T(8...) custom-call(s32[1]{0:T(128)} %bitcast.9.expert_ref, ...), custom_call_target="tpu_custom_call" | custom-call | flops 19327352832 | bytes 48234496 | tf_op jit(solution)/shard_map/moe_slot/pallas_call | solution.py:251
  249.9 5.0 collective-permute-done.22.refs_7_
  255.0 30.2 %moe_slot.6 = (f32[2048,1024]{1,0:T(8,128)}, f32[2048,1024]{1,0:T(8,128)}, f32[2048,16]{1,0:T(8,128)}, bf16[1024,256]{1,0:T(8,128)(2,1)}, bf16[1024,256]{1,0:T(8...) custom-call(s32[1]{0:T(128)} %bitcast.8.expert_ref, ...), custom_call_target="tpu_custom_call" | custom-call | flops 19327352832 | bytes 48234496 | tf_op jit(solution)/shard_map/moe_slot/pallas_call | solution.py:251
  285.3 42.0 %moe_slot.7 = (f32[2048,1024]{1,0:T(8,128)}, f32[2048,1024]{1,0:T(8,128)}, f32[2048,16]{1,0:T(8,128)}, bf16[1024,256]{1,0:T(8,128)(2,1)}, bf16[1024,256]{1,0:T(8...) custom-call(s32[1]{0:T(128)} %bitcast.4.expert_ref, ...), custom_call_target="tpu_custom_call" | custom-call | flops 19327352832 | bytes 48234496 | tf_op jit(solution)/shard_map/moe_slot/pallas_call | solution.py:251
  327.3 4.2 convert_element_type.243
  340.3 25.9 %collective-permute-done.43 = f32[512,16]{1,0:T(8,128)S(1)} collective-permute-done((f32[512,16]{1,0:T(8,128)S(1)}, f32[512,16]{1,0:T(8,128)S(1)}, u32[]{:S(2)}, u32[]{:S(2)}) %collective-permute-start.43) | collective-permute-done | bytes 32800 | tf_op jit(solution)/shard_map/ppermute | solution.py:314
  366.7 5.5 collective-permute-done.45
  374.5 1.7 fusion.11
  377.0 2.3 collective-permute-start.35
  380.5 2.3 collective-permute-start.39
  388.9 36.1 %collective-permute-done.34 = bf16[512,1024]{1,0:T(8,128)(2,1)} collective-permute-done((bf16[512,1024]{1,0:T(8,128)(2,1)}, bf16[512,1024]{1,0:T(8,128)(2,1)}, u32[]{:S(2)}, u32[]{:S(2)}) %collective-permute-start.34) | collective-permute-done | bytes 1048608 | tf_op jit(solution)/shard_map/ppermute | solution.py:314
  426.6 43.0 %collective-permute-done.38 = bf16[512,1024]{1,0:T(8,128)(2,1)} collective-permute-done((bf16[512,1024]{1,0:T(8,128)(2,1)}, bf16[512,1024]{1,0:T(8,128)(2,1)}, u32[]{:S(2)}, u32[]{:S(2)}) %collective-permute-start.38) | collective-permute-done | bytes 1048608 | tf_op jit(solution)/shard_map/ppermute | solution.py:314
  469.6 5.1 multiply_reduce_fusion.1
  474.9 3.5 constant_dynamic-update-slice_fusion.2
  479.9 6.3 collective-permute-done.71
  487.8 9.7 %collective-permute-done.64 = bf16[1024,256]{1,0:T(8,128)(2,1)S(1)} collective-permute-done((bf16[1024,256]{1,0:T(8,128)(2,1)S(1)}, bf16[1024,256]{1,0:T(8,128)(2,1)S(1)}, u32[]{:S(2)}, u32[]{:S(2)}) %collective-permute-start.64) | collective-permute-done | bytes 524320 | tf_op jit(solution)/shard_map/ppermute | solution.py:318
  499.0 8.4 %collective-permute-done.57 = bf16[1024,256]{1,0:T(8,128)(2,1)S(1)} collective-permute-done((bf16[1024,256]{1,0:T(8,128)(2,1)S(1)}, bf16[1024,256]{1,0:T(8,128)(2,1)S(1)}, u32[]{:S(2)}, u32[]{:S(2)}) %collective-permute-start.57) | collective-permute-done | bytes 524320 | tf_op jit(solution)/shard_map/ppermute | solution.py:318
  509.2 2.2 convolution_convert_fusion
  511.5 2.6 fusion.1.do_ref
  514.1 19.8 %attn_backward.1 = (bf16[512,1024]{1,0:T(8,128)(2,1)S(1)}, bf16[256,1024]{1,0:T(8,128)(2,1)S(1)}, bf16[256,1024]{1,0:T(8,128)(2,1)S(1)}) custom-call(bf16[512,1024]{1,0:T(8,128)(2,1)S(1)} %copy-done.2, bf16[256,1024]{1,0:T(8,128)(2,1)S(1)} %get-tuple-element.68.k_ref, bf16[256,1024]{1,0:T(8,128)(2,1)S(1)} %fusion.2.v_ref, ...), custom_call_target="tpu_custom_call" | custom-call | flops 10737418240 | bytes 4194304 | tf_op jit(solution)/shard_map/attn_backward/pallas_call | solution.py:147
  534.0 2.6 convolution_convert_fusion.1
  538.4 5.7 multiply_reduce_fusion
  544.1 1.9 convolution_convert_fusion.3
  546.0 1.9 convolution_convert_fusion.4
  547.9 1.9 dynamic-slice_convert_fusion
  550.8 1.6 add_convert_fusion.2
  553.1 1.7 add_convert_fusion.5
  555.4 19.2 %collective-permute-done.58 = bf16[1024,256]{1,0:T(8,128)(2,1)S(1)} collective-permute-done((bf16[1024,256]{1,0:T(8,128)(2,1)}, bf16[1024,256]{1,0:T(8,128)(2,1)S(1)}, u32[]{:S(2)}, u32[]{:S(2)}) %collective-permute-start.58) | collective-permute-done | bytes 524320 | tf_op jit(solution)/shard_map/ppermute | solution.py:318
  576.0 15.8 %collective-permute-start.73 = (bf16[256,1024]{1,0:T(8,128)(2,1)S(1)}, bf16[256,1024]{1,0:T(8,128)(2,1)S(1)}, u32[]{:S(2)}, u32[]{:S(2)}) collective-permute-start(bf16[256,1024]{1,0:T(8,128)(2,1)S(1)} %add_convert_fusion.2), channel_id=1, source_target_pairs={{0,8},{2,10},{4,12},{6,14},{8,16},{10,18},{12,20},{14,22},{16,24},... | collective-permute-start | bytes 1572872 | tf_op jit(solution)/shard_map/ppermute | solution.py:318
  591.8 2.4 collective-permute-start.66
  594.2 2.1 multiply_reduce_fusion.2
  596.4 9.7 %collective-permute-done.73 = bf16[256,1024]{1,0:T(8,128)(2,1)S(1)} collective-permute-done((bf16[256,1024]{1,0:T(8,128)(2,1)S(1)}, bf16[256,1024]{1,0:T(8,128)(2,1)S(1)}, u32[]{:S(2)}, u32[]{:S(2)}) %collective-permute-start.73) | collective-permute-done | bytes 524320 | tf_op jit(solution)/shard_map/ppermute | solution.py:318
  609.9 11.6 %collective-permute-done.66 = bf16[1024,256]{1,0:T(8,128)(2,1)S(1)} collective-permute-done((bf16[1024,256]{1,0:T(8,128)(2,1)S(1)}, bf16[1024,256]{1,0:T(8,128)(2,1)S(1)}, u32[]{:S(2)}, u32[]{:S(2)}) %collective-permute-start.66) | collective-permute-done | bytes 524320 | tf_op jit(solution)/shard_map/ppermute | solution.py:318
  622.8 2.5 collective-permute-start.50
  625.3 2.0 collective-permute-start.51
  627.3 2.8 collective-permute-start.52
  630.2 5.5 collective-permute-done.59
  637.5 76.0 %all-reduce.3.cloned.1.call-done = (bf16[1024,512]{1,0:T(8,128)(2,1)}, bf16[1024,256]{1,0:T(8,128)(2,1)}, bf16[1024,256]{1,0:T(8,128)(2,1)}, bf16[512,1024]{1,0:T(8,128)(2,1)}) async-done(((bf16[1024,512]{1,0:T(8,128)(2,1)}, bf16[1024,256]{1,0:T(8,128)(2,1)}, bf16[1024,256]{1,0:T(8,128)(2,1)}, bf16[512,1024]{1,0:T(8,128)(2,1)}), (bf16[1024,512]{1,0:T(8,128)(2,1)}, bf16[1024,256]{1,0:T(8,128)(2,1)}, ...) | async-done | bytes 3145744 | tf_op jit(solution)/shard_map/psum | solution.py:456
  713.5 2.9 convert_element_type.262
  (306 shorter events, 69.1 us)
Async XLA Ops:
  7.2 706.3 %all-reduce.3.cloned.1.call-start = ((), (), s32[]{:S(2)}) async-start(), calls=%async_computation | async-start | bytes 6291456 | tf_op jit(solution)/shard_map/psum | solution.py:456
  13.5 29.9 %collective-permute-start.5 = (bf16[512,512]{1,0:T(8,128)(2,1)}, bf16[512,512]{1,0:T(8,128)(2,1)}, u32[]{:S(2)}, u32[]{:S(2)}) collective-permute-start(bf16[512,512]{1,0:T(8,128)(2,1)} %get-tuple-element.124), channel_id=1, source_target_pairs={{0,1},{1,0},{2,3},{3,2},{4,5},{5,4},{6,7},{7,6},{8,9},{9,8},{10,11... | collective-permute-start | bytes 1572872 | tf_op jit(solution)/shard_map/ppermute | solution.py:310
  33.7 13.8 %collective-permute-start = (bf16[512,512]{1,0:T(8,128)(2,1)}, bf16[512,512]{1,0:T(8,128)(2,1)}, u32[]{:S(2)}, u32[]{:S(2)}) collective-permute-start(bf16[512,512]{1,0:T(8,128)(2,1)} %constant_dynamic-slice_fusion.4), channel_id=1, source_target_pairs={{0,1},{1,0},{2,3},{3,2},{4,5},{5,4},{6,7},{7,6},{8,9},{9,8},{10,11... | collective-permute-start | bytes 1572872 | tf_op jit(solution)/shard_map/ppermute | solution.py:310
  33.8 15.6 %collective-permute-start.1 = (bf16[512,1024]{1,0:T(8,128)(2,1)}, bf16[512,1024]{1,0:T(8,128)(2,1)}, u32[]{:S(2)}, u32[]{:S(2)}) collective-permute-start(bf16[512,1024]{1,0:T(8,128)(2,1)} %param.22), channel_id=1, source_target_pairs={{0,1},{1,0},{2,3},{3,2},{4,5},{5,4},{6,7},{7,6},{8,9},{9,8},{10,11... | collective-permute-start | bytes 3145736 | tf_op jit(solution)/shard_map/ppermute | solution.py:310
  39.5 15.4 %collective-permute-start.10 = (f32[512,16]{1,0:T(8,128)}, f32[512,16]{1,0:T(8,128)}, u32[]{:S(2)}, u32[]{:S(2)}) collective-permute-start(f32[512,16]{1,0:T(8,128)} %fusion.6), channel_id=1, source_target_pairs={{0,4},{2,6},{4,0},{6,2},{8,12},{10,14},{12,8},{14,10},{16,20},{18,... | collective-permute-start | bytes 98312 | tf_op jit(solution)/shard_map/ppermute | solution.py:314
  42.0 14.7 %collective-permute-start.11 = (f32[512,16]{1,0:T(8,128)}, f32[512,16]{1,0:T(8,128)}, u32[]{:S(2)}, u32[]{:S(2)}) collective-permute-start(f32[512,16]{1,0:T(8,128)} %fusion.6), channel_id=1, source_target_pairs={{0,6},{2,4},{4,2},{6,0},{8,14},{10,12},{12,10},{14,8},{16,22},{18,... | collective-permute-start | bytes 98312 | tf_op jit(solution)/shard_map/ppermute | solution.py:314
  45.3 41.4 %collective-permute-start.6 = (bf16[512,1024]{1,0:T(8,128)(2,1)}, bf16[512,1024]{1,0:T(8,128)(2,1)}, u32[]{:S(2)}, u32[]{:S(2)}) collective-permute-start(bf16[512,1024]{1,0:T(8,128)(2,1)} %constant_dynamic-update-slice_fusion.5), channel_id=1, source_target_pairs={{0,2},{2,0},{4,6},{6,4},{8,10},{10,8},{12,14},{14,12},{16,18},{18,... | collective-permute-start | bytes 3145736 | tf_op jit(solution)/shard_map/ppermute | solution.py:314
  47.5 31.2 %collective-permute-start.9 = (f32[512,16]{1,0:T(8,128)}, f32[512,16]{1,0:T(8,128)}, u32[]{:S(2)}, u32[]{:S(2)}) collective-permute-start(f32[512,16]{1,0:T(8,128)} %fusion.6), channel_id=1, source_target_pairs={{0,2},{2,0},{4,6},{6,4},{8,10},{10,8},{12,14},{14,12},{16,18},{18,... | collective-permute-start | bytes 98312 | tf_op jit(solution)/shard_map/ppermute | solution.py:314
  49.4 30.9 %collective-permute-start.30 = (bf16[1024,256]{1,0:T(8,128)(2,1)S(1)}, bf16[1024,256]{1,0:T(8,128)(2,1)S(1)}, u32[]{:S(2)}, u32[]{:S(2)}) collective-permute-start(bf16[1024,256]{1,0:T(8,128)(2,1)S(1)} %bitcast.58), channel_id=1, source_target_pairs={{0,1},{1,0},{2,3},{3,2},{4,5},{5,4},{6,7},{7,6},{8,9},{9,8},{10,11... | collective-permute-start | bytes 1572872 | tf_op jit(solution)/shard_map/ppermute | solution.py:310
  54.9 29.3 %collective-permute-start.12 = (bf16[1024,256]{1,0:T(8,128)(2,1)S(1)}, bf16[1024,256]{1,0:T(8,128)(2,1)S(1)}, u32[]{:S(2)}, u32[]{:S(2)}) collective-permute-start(bf16[1024,256]{1,0:T(8,128)(2,1)S(1)} %bitcast.59), channel_id=1, source_target_pairs={{0,8},{2,10},{4,12},{6,14},{8,16},{10,18},{12,20},{14,22},{16,24},... | collective-permute-start | bytes 1572872 | tf_op jit(solution)/shard_map/ppermute | solution.py:318
  56.7 27.1 %collective-permute-start.31 = (bf16[1024,256]{1,0:T(8,128)(2,1)S(1)}, bf16[1024,256]{1,0:T(8,128)(2,1)S(1)}, u32[]{:S(2)}, u32[]{:S(2)}) collective-permute-start(bf16[1024,256]{1,0:T(8,128)(2,1)S(1)} %bitcast.61), channel_id=1, source_target_pairs={{0,1},{1,0},{2,3},{3,2},{4,5},{5,4},{6,7},{7,6},{8,9},{9,8},{10,11... | collective-permute-start | bytes 1572872 | tf_op jit(solution)/shard_map/ppermute | solution.py:310
  78.6 49.2 %collective-permute-start.7 = (bf16[512,1024]{1,0:T(8,128)(2,1)}, bf16[512,1024]{1,0:T(8,128)(2,1)}, u32[]{:S(2)}, u32[]{:S(2)}) collective-permute-start(bf16[512,1024]{1,0:T(8,128)(2,1)} %constant_dynamic-update-slice_fusion.5), channel_id=1, source_target_pairs={{0,4},{2,6},{4,0},{6,2},{8,12},{10,14},{12,8},{14,10},{16,20},{18,... | collective-permute-start | bytes 3145736 | tf_op jit(solution)/shard_map/ppermute | solution.py:314
  81.1 48.7 %collective-permute-start.8 = (bf16[512,1024]{1,0:T(8,128)(2,1)}, bf16[512,1024]{1,0:T(8,128)(2,1)}, u32[]{:S(2)}, u32[]{:S(2)}) collective-permute-start(bf16[512,1024]{1,0:T(8,128)(2,1)} %constant_dynamic-update-slice_fusion.5), channel_id=1, source_target_pairs={{0,6},{2,4},{4,2},{6,0},{8,14},{10,12},{12,10},{14,8},{16,22},{18,... | collective-permute-start | bytes 3145736 | tf_op jit(solution)/shard_map/ppermute | solution.py:314
  83.8 46.0 %collective-permute-start.2 = (bf16[512,1024]{1,0:T(8,128)(2,1)}, bf16[512,1024]{1,0:T(8,128)(2,1)}, u32[]{:S(2)}, u32[]{:S(2)}) collective-permute-start(bf16[512,1024]{1,0:T(8,128)(2,1)} %multiply_convert_fusion.1), channel_id=1, source_target_pairs={{0,2},{2,0},{4,6},{6,4},{8,10},{10,8},{12,14},{14,12},{16,18},{18,... | collective-permute-start | bytes 3145736 | tf_op jit(solution)/shard_map/ppermute | solution.py:314
  85.0 86.2 %collective-permute-start.3 = (bf16[512,1024]{1,0:T(8,128)(2,1)}, bf16[512,1024]{1,0:T(8,128)(2,1)}, u32[]{:S(2)}, u32[]{:S(2)}) collective-permute-start(bf16[512,1024]{1,0:T(8,128)(2,1)} %multiply_convert_fusion.1), channel_id=1, source_target_pairs={{0,4},{2,6},{4,0},{6,2},{8,12},{10,14},{12,8},{14,10},{16,20},{18,... | collective-permute-start | bytes 3145736 | tf_op jit(solution)/shard_map/ppermute | solution.py:314
  86.6 84.5 %collective-permute-start.4 = (bf16[512,1024]{1,0:T(8,128)(2,1)}, bf16[512,1024]{1,0:T(8,128)(2,1)}, u32[]{:S(2)}, u32[]{:S(2)}) collective-permute-start(bf16[512,1024]{1,0:T(8,128)(2,1)} %multiply_convert_fusion.1), channel_id=1, source_target_pairs={{0,6},{2,4},{4,2},{6,0},{8,14},{10,12},{12,10},{14,8},{16,22},{18,... | collective-permute-start | bytes 3145736 | tf_op jit(solution)/shard_map/ppermute | solution.py:314
  127.8 52.2 %collective-permute-start.16 = (bf16[1024,256]{1,0:T(8,128)(2,1)S(1)}, bf16[1024,256]{1,0:T(8,128)(2,1)}, u32[]{:S(2)}, u32[]{:S(2)}) collective-permute-start(bf16[1024,256]{1,0:T(8,128)(2,1)S(1)} %bitcast.62), channel_id=1, source_target_pairs={{0,8},{2,10},{4,12},{6,14},{8,16},{10,18},{12,20},{14,22},{16,24},... | collective-permute-start | bytes 1572872 | tf_op jit(solution)/shard_map/ppermute | solution.py:318
  129.8 50.4 %collective-permute-start.32 = (bf16[256,1024]{1,0:T(8,128)(2,1)S(1)}, bf16[256,1024]{1,0:T(8,128)(2,1)S(1)}, u32[]{:S(2)}, u32[]{:S(2)}) collective-permute-start(bf16[256,1024]{1,0:T(8,128)(2,1)S(1)} %bitcast.64), channel_id=1, source_target_pairs={{0,1},{1,0},{2,3},{3,2},{4,5},{5,4},{6,7},{7,6},{8,9},{9,8},{10,11... | collective-permute-start | bytes 1572872 | tf_op jit(solution)/shard_map/ppermute | solution.py:310
  129.8 52.2 %collective-permute-start.20 = (bf16[256,1024]{1,0:T(8,128)(2,1)S(1)}, bf16[256,1024]{1,0:T(8,128)(2,1)}, u32[]{:S(2)}, u32[]{:S(2)}) collective-permute-start(bf16[256,1024]{1,0:T(8,128)(2,1)S(1)} %bitcast.65), channel_id=1, source_target_pairs={{0,8},{2,10},{4,12},{6,14},{8,16},{10,18},{12,20},{14,22},{16,24},... | collective-permute-start | bytes 1572872 | tf_op jit(solution)/shard_map/ppermute | solution.py:318
  171.2 16.7 %collective-permute-start.13 = (bf16[1024,256]{1,0:T(8,128)(2,1)S(1)}, bf16[1024,256]{1,0:T(8,128)(2,1)}, u32[]{:S(2)}, u32[]{:S(2)}) collective-permute-start(bf16[1024,256]{1,0:T(8,128)(2,1)S(1)} %copy-done.53), channel_id=1, source_target_pairs={{0,8},{2,10},{4,12},{6,14},{8,16},{10,18},{12,20},{14,22},{16,24},... | collective-permute-start | bytes 1572872 | tf_op jit(solution)/shard_map/ppermute | solution.py:318
  180.0 36.0 %collective-permute-start.28 = (bf16[1024,256]{1,0:T(8,128)(2,1)}, bf16[1024,256]{1,0:T(8,128)(2,1)}, u32[]{:S(2)}, u32[]{:S(2)}) collective-permute-start(bf16[1024,256]{1,0:T(8,128)(2,1)} %collective-permute-done.16.refs_5_), channel_id=1, source_target_pairs={{0,1},{1,0},{2,3},{3,2},{4,5},{5,4},{6,7},{7,6},{8,9},{9,8},{10,11... | collective-permute-start | bytes 1572872 | tf_op jit(solution)/shard_map/ppermute | solution.py:310
  180.2 35.9 %collective-permute-start.17 = (bf16[1024,256]{1,0:T(8,128)(2,1)}, bf16[1024,256]{1,0:T(8,128)(2,1)S(1)}, u32[]{:S(2)}, u32[]{:S(2)}) collective-permute-start(bf16[1024,256]{1,0:T(8,128)(2,1)} %collective-permute-done.16.refs_5_), channel_id=1, source_target_pairs={{0,8},{2,10},{4,12},{6,14},{8,16},{10,18},{12,20},{14,22},{16,24},... | collective-permute-start | bytes 1572872 | tf_op jit(solution)/shard_map/ppermute | solution.py:318
  182.0 34.6 %collective-permute-start.29 = (bf16[256,1024]{1,0:T(8,128)(2,1)}, bf16[256,1024]{1,0:T(8,128)(2,1)}, u32[]{:S(2)}, u32[]{:S(2)}) collective-permute-start(bf16[256,1024]{1,0:T(8,128)(2,1)} %collective-permute-done.20.refs_7_), channel_id=1, source_target_pairs={{0,1},{1,0},{2,3},{3,2},{4,5},{5,4},{6,7},{7,6},{8,9},{9,8},{10,11... | collective-permute-start | bytes 1572872 | tf_op jit(solution)/shard_map/ppermute | solution.py:310
  182.1 35.4 %collective-permute-start.21 = (bf16[256,1024]{1,0:T(8,128)(2,1)}, bf16[256,1024]{1,0:T(8,128)(2,1)}, u32[]{:S(2)}, u32[]{:S(2)}) collective-permute-start(bf16[256,1024]{1,0:T(8,128)(2,1)} %collective-permute-done.20.refs_7_), channel_id=1, source_target_pairs={{0,8},{2,10},{4,12},{6,14},{8,16},{10,18},{12,20},{14,22},{16,24},... | collective-permute-start | bytes 1572872 | tf_op jit(solution)/shard_map/ppermute | solution.py:318
  187.9 29.7 %collective-permute-start.24 = (bf16[1024,256]{1,0:T(8,128)(2,1)}, bf16[1024,256]{1,0:T(8,128)(2,1)}, u32[]{:S(2)}, u32[]{:S(2)}) collective-permute-start(bf16[1024,256]{1,0:T(8,128)(2,1)} %collective-permute-done.13.refs_3_), channel_id=1, source_target_pairs={{0,1},{1,0},{2,3},{3,2},{4,5},{5,4},{6,7},{7,6},{8,9},{9,8},{10,11... | collective-permute-start | bytes 1572872 | tf_op jit(solution)/shard_map/ppermute | solution.py:310
  216.0 33.3 %collective-permute-start.14 = (bf16[1024,256]{1,0:T(8,128)(2,1)}, bf16[1024,256]{1,0:T(8,128)(2,1)}, u32[]{:S(2)}, u32[]{:S(2)}) collective-permute-start(bf16[1024,256]{1,0:T(8,128)(2,1)} %collective-permute-done.13.refs_3_), channel_id=1, source_target_pairs={{0,8},{2,10},{4,12},{6,14},{8,16},{10,18},{12,20},{14,22},{16,24},... | collective-permute-start | bytes 1572872 | tf_op jit(solution)/shard_map/ppermute | solution.py:318
  216.1 38.9 %collective-permute-start.25 = (bf16[1024,256]{1,0:T(8,128)(2,1)S(1)}, bf16[1024,256]{1,0:T(8,128)(2,1)}, u32[]{:S(2)}, u32[]{:S(2)}) collective-permute-start(bf16[1024,256]{1,0:T(8,128)(2,1)S(1)} %collective-permute-done.17.refs_5_), channel_id=1, source_target_pairs={{0,1},{1,0},{2,3},{3,2},{4,5},{5,4},{6,7},{7,6},{8,9},{9,8},{10,11... | collective-permute-start | bytes 1572872 | tf_op jit(solution)/shard_map/ppermute | solution.py:310
  216.7 32.9 %collective-permute-start.18 = (bf16[1024,256]{1,0:T(8,128)(2,1)S(1)}, bf16[1024,256]{1,0:T(8,128)(2,1)}, u32[]{:S(2)}, u32[]{:S(2)}) collective-permute-start(bf16[1024,256]{1,0:T(8,128)(2,1)S(1)} %collective-permute-done.17.refs_5_), channel_id=1, source_target_pairs={{0,8},{2,10},{4,12},{6,14},{8,16},{10,18},{12,20},{14,22},{16,24},... | collective-permute-start | bytes 1572872 | tf_op jit(solution)/shard_map/ppermute | solution.py:318
  217.5 37.5 %collective-permute-start.26 = (bf16[256,1024]{1,0:T(8,128)(2,1)}, bf16[256,1024]{1,0:T(8,128)(2,1)}, u32[]{:S(2)}, u32[]{:S(2)}) collective-permute-start(bf16[256,1024]{1,0:T(8,128)(2,1)} %collective-permute-done.21.refs_7_), channel_id=1, source_target_pairs={{0,1},{1,0},{2,3},{3,2},{4,5},{5,4},{6,7},{7,6},{8,9},{9,8},{10,11... | collective-permute-start | bytes 1572872 | tf_op jit(solution)/shard_map/ppermute | solution.py:310
  217.5 37.4 %collective-permute-start.22 = (bf16[256,1024]{1,0:T(8,128)(2,1)}, bf16[256,1024]{1,0:T(8,128)(2,1)}, u32[]{:S(2)}, u32[]{:S(2)}) collective-permute-start(bf16[256,1024]{1,0:T(8,128)(2,1)} %collective-permute-done.21.refs_7_), channel_id=1, source_target_pairs={{0,8},{2,10},{4,12},{6,14},{8,16},{10,18},{12,20},{14,22},{16,24},... | collective-permute-start | bytes 1572872 | tf_op jit(solution)/shard_map/ppermute | solution.py:318
  249.4 35.9 %collective-permute-start.15 = (bf16[1024,256]{1,0:T(8,128)(2,1)}, bf16[1024,256]{1,0:T(8,128)(2,1)}, u32[]{:S(2)}, u32[]{:S(2)}) collective-permute-start(bf16[1024,256]{1,0:T(8,128)(2,1)} %collective-permute-done.14.refs_3_), channel_id=1, source_target_pairs={{0,1},{1,0},{2,3},{3,2},{4,5},{5,4},{6,7},{7,6},{8,9},{9,8},{10,11... | collective-permute-start | bytes 1572872 | tf_op jit(solution)/shard_map/ppermute | solution.py:310
  249.6 35.7 %collective-permute-start.19 = (bf16[1024,256]{1,0:T(8,128)(2,1)}, bf16[1024,256]{1,0:T(8,128)(2,1)}, u32[]{:S(2)}, u32[]{:S(2)}) collective-permute-start(bf16[1024,256]{1,0:T(8,128)(2,1)} %collective-permute-done.18.refs_5_), channel_id=1, source_target_pairs={{0,1},{1,0},{2,3},{3,2},{4,5},{5,4},{6,7},{7,6},{8,9},{9,8},{10,11... | collective-permute-start | bytes 1572872 | tf_op jit(solution)/shard_map/ppermute | solution.py:310
  255.0 30.3 %collective-permute-start.23 = (bf16[256,1024]{1,0:T(8,128)(2,1)}, bf16[256,1024]{1,0:T(8,128)(2,1)}, u32[]{:S(2)}, u32[]{:S(2)}) collective-permute-start(bf16[256,1024]{1,0:T(8,128)(2,1)} %collective-permute-done.22.refs_7_), channel_id=1, source_target_pairs={{0,1},{1,0},{2,3},{3,2},{4,5},{5,4},{6,7},{7,6},{8,9},{9,8},{10,11... | collective-permute-start | bytes 1572872 | tf_op jit(solution)/shard_map/ppermute | solution.py:310
  334.6 45.9 %collective-permute-start.33 = (bf16[512,1024]{1,0:T(8,128)(2,1)S(1)}, bf16[512,1024]{1,0:T(8,128)(2,1)}, u32[]{:S(2)}, u32[]{:S(2)}) collective-permute-start(bf16[512,1024]{1,0:T(8,128)(2,1)S(1)} %get-tuple-element.113), channel_id=1, source_target_pairs={{0,2},{2,0},{4,6},{6,4},{8,10},{10,8},{12,14},{14,12},{16,18},{18,... | collective-permute-start | bytes 3145736 | tf_op jit(solution)/shard_map/ppermute | solution.py:314
  336.0 30.2 %collective-permute-start.43 = (f32[512,16]{1,0:T(8,128)S(1)}, f32[512,16]{1,0:T(8,128)S(1)}, u32[]{:S(2)}, u32[]{:S(2)}) collective-permute-start(f32[512,16]{1,0:T(8,128)S(1)} %get-tuple-element.119), channel_id=1, source_target_pairs={{0,2},{2,0},{4,6},{6,4},{8,10},{10,8},{12,14},{14,12},{16,18},{18,... | collective-permute-start | bytes 98312 | tf_op jit(solution)/shard_map/ppermute | solution.py:314
  337.0 29.2 %collective-permute-start.44 = (f32[512,16]{1,0:T(8,128)S(1)}, f32[512,16]{1,0:T(8,128)S(1)}, u32[]{:S(2)}, u32[]{:S(2)}) collective-permute-start(f32[512,16]{1,0:T(8,128)S(1)} %get-tuple-element.121), channel_id=1, source_target_pairs={{0,4},{2,6},{4,0},{6,2},{8,12},{10,14},{12,8},{14,10},{16,20},{18,... | collective-permute-start | bytes 98312 | tf_op jit(solution)/shard_map/ppermute | solution.py:314
  338.5 33.7 %collective-permute-start.45 = (f32[512,16]{1,0:T(8,128)S(1)}, f32[512,16]{1,0:T(8,128)S(1)}, u32[]{:S(2)}, u32[]{:S(2)}) collective-permute-start(f32[512,16]{1,0:T(8,128)S(1)} %get-tuple-element.120), channel_id=1, source_target_pairs={{0,6},{2,4},{4,2},{6,0},{8,14},{10,12},{12,10},{14,8},{16,22},{18,... | collective-permute-start | bytes 98312 | tf_op jit(solution)/shard_map/ppermute | solution.py:314
  339.5 37.4 %collective-permute-start.70 = (bf16[256,1024]{1,0:T(8,128)(2,1)S(1)}, bf16[256,1024]{1,0:T(8,128)(2,1)S(1)}, u32[]{:S(2)}, u32[]{:S(2)}) collective-permute-start(bf16[256,1024]{1,0:T(8,128)(2,1)S(1)} %copy-done.58), channel_id=1, source_target_pairs={{0,1},{1,0},{2,3},{3,2},{4,5},{5,4},{6,7},{7,6},{8,9},{9,8},{10,11... | collective-permute-start | bytes 1572872 | tf_op jit(solution)/shard_map/ppermute | solution.py:310
  376.2 48.8 %collective-permute-start.34 = (bf16[512,1024]{1,0:T(8,128)(2,1)}, bf16[512,1024]{1,0:T(8,128)(2,1)}, u32[]{:S(2)}, u32[]{:S(2)}) collective-permute-start(bf16[512,1024]{1,0:T(8,128)(2,1)} %get-tuple-element.115), channel_id=1, source_target_pairs={{0,4},{2,6},{4,0},{6,2},{8,12},{10,14},{12,8},{14,10},{16,20},{18,... | collective-permute-start | bytes 3145736 | tf_op jit(solution)/shard_map/ppermute | solution.py:314
  377.0 48.1 %collective-permute-start.35 = (bf16[512,1024]{1,0:T(8,128)(2,1)}, bf16[512,1024]{1,0:T(8,128)(2,1)}, u32[]{:S(2)}, u32[]{:S(2)}) collective-permute-start(bf16[512,1024]{1,0:T(8,128)(2,1)} %get-tuple-element.114), channel_id=1, source_target_pairs={{0,6},{2,4},{4,2},{6,0},{8,14},{10,12},{12,10},{14,8},{16,22},{18,... | collective-permute-start | bytes 3145736 | tf_op jit(solution)/shard_map/ppermute | solution.py:314
  379.3 47.3 %collective-permute-start.37 = (bf16[512,1024]{1,0:T(8,128)(2,1)}, bf16[512,1024]{1,0:T(8,128)(2,1)}, u32[]{:S(2)}, u32[]{:S(2)}) collective-permute-start(bf16[512,1024]{1,0:T(8,128)(2,1)} %get-tuple-element.110), channel_id=1, source_target_pairs={{0,2},{2,0},{4,6},{6,4},{8,10},{10,8},{12,14},{14,12},{16,18},{18,... | collective-permute-start | bytes 3145736 | tf_op jit(solution)/shard_map/ppermute | solution.py:314
  379.8 89.8 %collective-permute-start.38 = (bf16[512,1024]{1,0:T(8,128)(2,1)}, bf16[512,1024]{1,0:T(8,128)(2,1)}, u32[]{:S(2)}, u32[]{:S(2)}) collective-permute-start(bf16[512,1024]{1,0:T(8,128)(2,1)} %get-tuple-element.112), channel_id=1, source_target_pairs={{0,4},{2,6},{4,0},{6,2},{8,12},{10,14},{12,8},{14,10},{16,20},{18,... | collective-permute-start | bytes 3145736 | tf_op jit(solution)/shard_map/ppermute | solution.py:314
  380.5 89.1 %collective-permute-start.39 = (bf16[512,1024]{1,0:T(8,128)(2,1)}, bf16[512,1024]{1,0:T(8,128)(2,1)}, u32[]{:S(2)}, u32[]{:S(2)}) collective-permute-start(bf16[512,1024]{1,0:T(8,128)(2,1)} %get-tuple-element.111), channel_id=1, source_target_pairs={{0,6},{2,4},{4,2},{6,0},{8,14},{10,12},{12,10},{14,8},{16,22},{18,... | collective-permute-start | bytes 3145736 | tf_op jit(solution)/shard_map/ppermute | solution.py:314
  425.0 53.7 %collective-permute-start.69 = (bf16[256,1024]{1,0:T(8,128)(2,1)S(1)}, bf16[256,1024]{1,0:T(8,128)(2,1)S(1)}, u32[]{:S(2)}, u32[]{:S(2)}) collective-permute-start(bf16[256,1024]{1,0:T(8,128)(2,1)S(1)} %copy-done.51), channel_id=1, source_target_pairs={{0,1},{1,0},{2,3},{3,2},{4,5},{5,4},{6,7},{7,6},{8,9},{9,8},{10,11... | collective-permute-start | bytes 1572872 | tf_op jit(solution)/shard_map/ppermute | solution.py:310
  425.1 62.2 %collective-permute-start.62 = (bf16[1024,256]{1,0:T(8,128)(2,1)S(1)}, bf16[1024,256]{1,0:T(8,128)(2,1)S(1)}, u32[]{:S(2)}, u32[]{:S(2)}) collective-permute-start(bf16[1024,256]{1,0:T(8,128)(2,1)S(1)} %copy-done.50), channel_id=1, source_target_pairs={{0,1},{1,0},{2,3},{3,2},{4,5},{5,4},{6,7},{7,6},{8,9},{9,8},{10,11... | collective-permute-start | bytes 1572872 | tf_op jit(solution)/shard_map/ppermute | solution.py:310
  426.6 71.9 %collective-permute-start.55 = (bf16[1024,256]{1,0:T(8,128)(2,1)S(1)}, bf16[1024,256]{1,0:T(8,128)(2,1)S(1)}, u32[]{:S(2)}, u32[]{:S(2)}) collective-permute-start(bf16[1024,256]{1,0:T(8,128)(2,1)S(1)} %copy-done.49), channel_id=1, source_target_pairs={{0,1},{1,0},{2,3},{3,2},{4,5},{5,4},{6,7},{7,6},{8,9},{9,8},{10,11... | collective-permute-start | bytes 1572872 | tf_op jit(solution)/shard_map/ppermute | solution.py:310
  469.6 16.6 %collective-permute-start.71 = (bf16[256,1024]{1,0:T(8,128)(2,1)S(1)}, bf16[256,1024]{1,0:T(8,128)(2,1)S(1)}, u32[]{:S(2)}, u32[]{:S(2)}) collective-permute-start(bf16[256,1024]{1,0:T(8,128)(2,1)S(1)} %add_convert_fusion.4), channel_id=1, source_target_pairs={{0,8},{2,10},{4,12},{6,14},{8,16},{10,18},{12,20},{14,22},{16,24},... | collective-permute-start | bytes 1572872 | tf_op jit(solution)/shard_map/ppermute | solution.py:318
  469.6 27.9 %collective-permute-start.64 = (bf16[1024,256]{1,0:T(8,128)(2,1)S(1)}, bf16[1024,256]{1,0:T(8,128)(2,1)S(1)}, u32[]{:S(2)}, u32[]{:S(2)}) collective-permute-start(bf16[1024,256]{1,0:T(8,128)(2,1)S(1)} %add_convert_fusion.7), channel_id=1, source_target_pairs={{0,8},{2,10},{4,12},{6,14},{8,16},{10,18},{12,20},{14,22},{16,24},... | collective-permute-start | bytes 1572872 | tf_op jit(solution)/shard_map/ppermute | solution.py:318
  478.8 28.6 %collective-permute-start.57 = (bf16[1024,256]{1,0:T(8,128)(2,1)S(1)}, bf16[1024,256]{1,0:T(8,128)(2,1)S(1)}, u32[]{:S(2)}, u32[]{:S(2)}) collective-permute-start(bf16[1024,256]{1,0:T(8,128)(2,1)S(1)} %add_convert_fusion.10), channel_id=1, source_target_pairs={{0,8},{2,10},{4,12},{6,14},{8,16},{10,18},{12,20},{14,22},{16,24},... | collective-permute-start | bytes 1572872 | tf_op jit(solution)/shard_map/ppermute | solution.py:318
  486.2 22.8 %collective-permute-start.40 = (bf16[512,1024]{1,0:T(8,128)(2,1)S(1)}, bf16[512,1024]{1,0:T(8,128)(2,1)S(1)}, u32[]{:S(2)}, u32[]{:S(2)}) collective-permute-start(bf16[512,1024]{1,0:T(8,128)(2,1)S(1)} %get-tuple-element.107), channel_id=1, source_target_pairs={{0,1},{1,0},{2,3},{3,2},{4,5},{5,4},{6,7},{7,6},{8,9},{9,8},{10,11... | collective-permute-start | bytes 3145736 | tf_op jit(solution)/shard_map/ppermute | solution.py:310
  487.3 62.5 %collective-permute-start.68 = (bf16[256,1024]{1,0:T(8,128)(2,1)}, bf16[256,1024]{1,0:T(8,128)(2,1)}, u32[]{:S(2)}, u32[]{:S(2)}) collective-permute-start(bf16[256,1024]{1,0:T(8,128)(2,1)} %get-tuple-element.93), channel_id=1, source_target_pairs={{0,1},{1,0},{2,3},{3,2},{4,5},{5,4},{6,7},{7,6},{8,9},{9,8},{10,11... | collective-permute-start | bytes 1572872 | tf_op jit(solution)/shard_map/ppermute | solution.py:310
  498.5 53.9 %collective-permute-start.61 = (bf16[1024,256]{1,0:T(8,128)(2,1)}, bf16[1024,256]{1,0:T(8,128)(2,1)}, u32[]{:S(2)}, u32[]{:S(2)}) collective-permute-start(bf16[1024,256]{1,0:T(8,128)(2,1)} %get-tuple-element.85), channel_id=1, source_target_pairs={{0,1},{1,0},{2,3},{3,2},{4,5},{5,4},{6,7},{7,6},{8,9},{9,8},{10,11... | collective-permute-start | bytes 1572872 | tf_op jit(solution)/shard_map/ppermute | solution.py:310
  508.5 46.3 %collective-permute-start.54 = (bf16[1024,256]{1,0:T(8,128)(2,1)}, bf16[1024,256]{1,0:T(8,128)(2,1)}, u32[]{:S(2)}, u32[]{:S(2)}) collective-permute-start(bf16[1024,256]{1,0:T(8,128)(2,1)} %get-tuple-element.77), channel_id=1, source_target_pairs={{0,1},{1,0},{2,3},{3,2},{4,5},{5,4},{6,7},{7,6},{8,9},{9,8},{10,11... | collective-permute-start | bytes 1572872 | tf_op jit(solution)/shard_map/ppermute | solution.py:310
  509.0 41.8 %collective-permute-start.72 = (bf16[256,1024]{1,0:T(8,128)(2,1)}, bf16[256,1024]{1,0:T(8,128)(2,1)}, u32[]{:S(2)}, u32[]{:S(2)}) collective-permute-start(bf16[256,1024]{1,0:T(8,128)(2,1)} %add_convert_fusion.3), channel_id=1, source_target_pairs={{0,8},{2,10},{4,12},{6,14},{8,16},{10,18},{12,20},{14,22},{16,24},... | collective-permute-start | bytes 1572872 | tf_op jit(solution)/shard_map/ppermute | solution.py:318
  509.0 43.9 %collective-permute-start.65 = (bf16[1024,256]{1,0:T(8,128)(2,1)}, bf16[1024,256]{1,0:T(8,128)(2,1)}, u32[]{:S(2)}, u32[]{:S(2)}) collective-permute-start(bf16[1024,256]{1,0:T(8,128)(2,1)} %add_convert_fusion.6), channel_id=1, source_target_pairs={{0,8},{2,10},{4,12},{6,14},{8,16},{10,18},{12,20},{14,22},{16,24},... | collective-permute-start | bytes 1572872 | tf_op jit(solution)/shard_map/ppermute | solution.py:318
  549.8 24.8 %collective-permute-start.58 = (bf16[1024,256]{1,0:T(8,128)(2,1)}, bf16[1024,256]{1,0:T(8,128)(2,1)S(1)}, u32[]{:S(2)}, u32[]{:S(2)}) collective-permute-start(bf16[1024,256]{1,0:T(8,128)(2,1)} %add_convert_fusion.9), channel_id=1, source_target_pairs={{0,8},{2,10},{4,12},{6,14},{8,16},{10,18},{12,20},{14,22},{16,24},... | collective-permute-start | bytes 1572872 | tf_op jit(solution)/shard_map/ppermute | solution.py:318
  550.8 41.0 %collective-permute-start.41 = (bf16[1024,512]{1,0:T(8,128)(2,1)S(1)}, bf16[1024,512]{1,0:T(8,128)(2,1)S(1)}, u32[]{:S(2)}, u32[]{:S(2)}) collective-permute-start(bf16[1024,512]{1,0:T(8,128)(2,1)S(1)} %dynamic-slice_convert_fusion), channel_id=1, source_target_pairs={{0,1},{1,0},{2,3},{3,2},{4,5},{5,4},{6,7},{7,6},{8,9},{9,8},{10,11... | collective-permute-start | bytes 3145736 | tf_op jit(solution)/shard_map/ppermute | solution.py:310
  552.4 43.9 %collective-permute-start.67 = (bf16[256,1024]{1,0:T(8,128)(2,1)}, bf16[256,1024]{1,0:T(8,128)(2,1)S(1)}, u32[]{:S(2)}, u32[]{:S(2)}) collective-permute-start(bf16[256,1024]{1,0:T(8,128)(2,1)} %get-tuple-element.91), channel_id=1, source_target_pairs={{0,1},{1,0},{2,3},{3,2},{4,5},{5,4},{6,7},{7,6},{8,9},{9,8},{10,11... | collective-permute-start | bytes 1572872 | tf_op jit(solution)/shard_map/ppermute | solution.py:310
  553.0 57.0 %collective-permute-start.60 = (bf16[1024,256]{1,0:T(8,128)(2,1)}, bf16[1024,256]{1,0:T(8,128)(2,1)S(1)}, u32[]{:S(2)}, u32[]{:S(2)}) collective-permute-start(bf16[1024,256]{1,0:T(8,128)(2,1)} %get-tuple-element.83), channel_id=1, source_target_pairs={{0,1},{1,0},{2,3},{3,2},{4,5},{5,4},{6,7},{7,6},{8,9},{9,8},{10,11... | collective-permute-start | bytes 1572872 | tf_op jit(solution)/shard_map/ppermute | solution.py:310
  554.8 75.4 %collective-permute-start.53 = (bf16[1024,256]{1,0:T(8,128)(2,1)}, bf16[1024,256]{1,0:T(8,128)(2,1)S(1)}, u32[]{:S(2)}, u32[]{:S(2)}) collective-permute-start(bf16[1024,256]{1,0:T(8,128)(2,1)} %get-tuple-element.75), channel_id=1, source_target_pairs={{0,1},{1,0},{2,3},{3,2},{4,5},{5,4},{6,7},{7,6},{8,9},{9,8},{10,11... | collective-permute-start | bytes 1572872 | tf_op jit(solution)/shard_map/ppermute | solution.py:310
  576.0 30.1 %collective-permute-start.73 = (bf16[256,1024]{1,0:T(8,128)(2,1)S(1)}, bf16[256,1024]{1,0:T(8,128)(2,1)S(1)}, u32[]{:S(2)}, u32[]{:S(2)}) collective-permute-start(bf16[256,1024]{1,0:T(8,128)(2,1)S(1)} %add_convert_fusion.2), channel_id=1, source_target_pairs={{0,8},{2,10},{4,12},{6,14},{8,16},{10,18},{12,20},{14,22},{16,24},... | collective-permute-start | bytes 1572872 | tf_op jit(solution)/shard_map/ppermute | solution.py:318
  591.8 29.8 %collective-permute-start.66 = (bf16[1024,256]{1,0:T(8,128)(2,1)S(1)}, bf16[1024,256]{1,0:T(8,128)(2,1)S(1)}, u32[]{:S(2)}, u32[]{:S(2)}) collective-permute-start(bf16[1024,256]{1,0:T(8,128)(2,1)S(1)} %add_convert_fusion.5), channel_id=1, source_target_pairs={{0,8},{2,10},{4,12},{6,14},{8,16},{10,18},{12,20},{14,22},{16,24},... | collective-permute-start | bytes 1572872 | tf_op jit(solution)/shard_map/ppermute | solution.py:318
  596.3 39.4 %collective-permute-start.59 = (bf16[1024,256]{1,0:T(8,128)(2,1)S(1)}, bf16[1024,256]{1,0:T(8,128)(2,1)S(1)}, u32[]{:S(2)}, u32[]{:S(2)}) collective-permute-start(bf16[1024,256]{1,0:T(8,128)(2,1)S(1)} %add_convert_fusion.8), channel_id=1, source_target_pairs={{0,8},{2,10},{4,12},{6,14},{8,16},{10,18},{12,20},{14,22},{16,24},... | collective-permute-start | bytes 1572872 | tf_op jit(solution)/shard_map/ppermute | solution.py:318
  622.8 14.0 %collective-permute-start.50 = (f32[2,512]{1,0:T(2,128)S(1)}, f32[2,512]{1,0:T(2,128)S(1)}, u32[]{:S(2)}, u32[]{:S(2)}) collective-permute-start(f32[2,512]{1,0:T(2,128)S(1)} %fusion.36), channel_id=1, source_target_pairs={{0,8},{2,10},{4,12},{6,14},{8,16},{10,18},{12,20},{14,22},{16,24},... | collective-permute-start | bytes 12296 | tf_op jit(solution)/shard_map/ppermute | solution.py:318
  (75 other events, 1147.3 us)
Sparse Core Ops, SparseCore 0:
  548.0 165.4 all-reduce.2

commit v2 on v1

--- a/solution.py
+++ b/solution.py
@@ -12,6 +12,7 @@
 THETA = 10000.0
 NEG = -1e30
 PLANE = 4
+LANES = 128
 F32 = jnp.float32
 BF16 = jnp.bfloat16
 NT = (((1,), (1,)), ((), ()))
@@ -170,114 +171,210 @@
     )(q_t, k_t, v_t, do_t, lse, cos_t, sin_t, start)
 
 
-def moe_kernel(first, pieces, expert_ref, *refs):
+def data_kernel(first, last, blocks, slots, pieces, expert_ref, *refs):
     refs = list(refs)
-    x_ref, g_ref, gates_ref = refs[:3]
-    wg, wu, wd = refs[3 : 3 + pieces], refs[3 + pieces : 3 + 2 * pieces], refs[3 + 2 * pieces : 3 + 3 * pieces]
-    refs = refs[3 + 3 * pieces :]
+    x, g_all = refs[0][...], refs[blocks][...]
+    for i in range(1, blocks):
+        here = pl.program_id(0) == i
+        x = jnp.where(here, refs[i][...], x)
+        g_all = jnp.where(here, refs[blocks + i][...], g_all)
+    ws = refs[2 * blocks : 2 * blocks + slots * pieces]
+    refs = refs[2 * blocks + slots * pieces :]
     if not first:
         out_in, dx_in, dgate_in = refs[:3]
         refs = refs[3:]
-    out_ref, dx_ref, dgate_ref = refs[:3]
-    refs = refs[3:]
-    og, ou, od = refs[:pieces], refs[pieces : 2 * pieces], refs[2 * pieces : 3 * pieces]
-    acc_g, acc_u, acc_d = refs[3 * pieces :]
-    step, steps = pl.program_id(0), pl.num_programs(0)
-
-    @pl.when(step == 0)
-    def _():
-        acc_g[...] = jnp.zeros_like(acc_g)
-        acc_u[...] = jnp.zeros_like(acc_u)
-        acc_d[...] = jnp.zeros_like(acc_d)
-
-    x, g = x_ref[...], g_ref[...]
-    here = lax.broadcasted_iota(jnp.int32, gates_ref.shape, 1) == expert_ref[0]
-    gate = jnp.sum(jnp.where(here, gates_ref[...], 0.0), axis=1, keepdims=True)
-    x_t = x.T
-    row_sum = None
-    for i in range(pieces):
-        gate_pre = dot(x, wg[i][...])
-        up_pre = dot(x, wu[i][...])
-        d_hidden = dot_nt(g, wd[i][...])
-        sig = jax.nn.sigmoid(gate_pre)
-        silu = gate_pre * sig
-        act = silu * up_pre
-        part = jnp.sum(act * d_hidden, axis=1, keepdims=True)
-        row_sum = part if row_sum is None else row_sum + part
-        act_w = (act * gate).astype(BF16)
-        d_hidden = d_hidden * gate
-        d_up = (d_hidden * silu).astype(BF16)
-        d_gate = (d_hidden * up_pre * sig * (1.0 + gate_pre * (1.0 - sig))).astype(BF16)
-        out_term = dot(act_w, wd[i][...])
-        dx_term = dot_nt(d_gate, wg[i][...]) + dot_nt(d_up, wu[i][...])
-        if i == 0 and first:
-            out_ref[...] = out_term
-            dx_ref[...] = dx_term
-        elif i == 0:
-            out_ref[...] = out_in[...] + out_term
-            dx_ref[...] = dx_in[...] + dx_term
-        else:
-            out_ref[...] += out_term
-            dx_ref[...] += dx_term
-        acc_g[i] += dot(x_t, d_gate)
-        acc_u[i] += dot(x_t, d_up)
-        acc_d[i] += dot_tn(act_w, g)
-    dgate_term = jnp.where(here, row_sum, 0.0)
-    dgate_ref[...] = dgate_term if first else dgate_in[...] + dgate_term
-
-    @pl.when(step == steps - 1)
-    def _():
+    if last:
+        out_ref, dx_ref = refs[:2]
+        refs = refs[2:]
+    else:
+        out_ref, dx_ref, dgate_ref = refs[:3]
+        refs = refs[3:]
+    hs, acts = refs[:slots], refs[slots : 2 * slots]
+    acc_o, acc_x = refs[2 * slots :]
+    width = x.shape[1]
+    g = g_all[:, :width]
+    gates = g_all[:, width:].astype(F32)
+    lane = lax.broadcasted_iota(jnp.int32, gates.shape, 1)
+    dgate = None if first else dgate_in[...]
+    for j in range(slots):
+        here = lane == expert_ref[j]
+        both = here | (lane == expert_ref[j] + LANES // 2)
+        gate = jnp.sum(jnp.where(both, gates, 0.0), axis=1, keepdims=True)
+        row_sum = None
         for i in range(pieces):
-            og[i][...] = acc_g[i].astype(BF16)
-            ou[i][...] = acc_u[i].astype(BF16)
-            od[i][...] = acc_d[i].astype(BF16)
-
-
-def moe_slot(expert, x, g, gates, wg, wu, wd, carry, tile):
-    rows, width = x.shape
-    experts = gates.shape[1]
-    pieces = len(wg)
-    hidden = wg[0].shape[1]
+            w = ws[j * pieces + i]
+            hid = w.shape[2]
+            gate_pre = dot(x, w[0])
+            up_pre = dot(x, w[1])
+            d_hidden = dot(g, w[2])
+            sig = jax.nn.sigmoid(gate_pre)
+            silu = gate_pre * sig
+            act = silu * up_pre
+            part = jnp.sum(act * d_hidden, axis=1, keepdims=True)
+            row_sum = part if row_sum is None else row_sum + part
+            act_w = (act * gate).astype(BF16)
+            d_hidden = d_hidden * gate
+            d_up = (d_hidden * silu).astype(BF16)
+            d_gate = (d_hidden * up_pre * (sig + silu * (1.0 - sig))).astype(BF16)
+            hs[j][:, 2 * i * hid : (2 * i + 1) * hid] = d_gate
+            hs[j][:, (2 * i + 1) * hid : (2 * i + 2) * hid] = d_up
+            acts[j][:, i * hid : (i + 1) * hid] = act_w
+            out_term = dot_nt(act_w, w[2])
+            dx_term = dot_nt(d_gate, w[0]) + dot_nt(d_up, w[1])
+            if i == 0 and j == 0 and first:
+                acc_o[...] = out_term
+                acc_x[...] = dx_term
+            elif i == 0 and j == 0:
+                acc_o[...] = out_in[...] + out_term
+                acc_x[...] = dx_in[...] + dx_term
+            else:
+                acc_o[...] += out_term
+                acc_x[...] += dx_term
+        term = jnp.where(here, row_sum, 0.0)
+        dgate = term if dgate is None else dgate + term
+    out_ref[...] = acc_o[...].astype(out_ref.dtype)
+    if last:
+        dx_ref[:, :width] = acc_x[...].astype(BF16)
+        high = dgate.astype(BF16).astype(F32)
+        low = pltpu.roll(dgate - high, LANES // 2, 1)
+        dx_ref[:, width:] = jnp.where(lane < LANES // 2, high, low).astype(BF16)
+    else:
+        dx_ref[...] = acc_x[...]
+        dgate_ref[...] = dgate
+
+
+def expert_data(experts, xs, gs, ws, carry, last):
+    blocks = len(xs)
+    rows, width = xs[0].shape
+    tile = min(256, rows)
+    tiles = rows // tile
+    full = gs[0].shape[1]
+    slots = experts.shape[0]
+    pieces = len(ws) // slots
+    hidden = ws[0].shape[2]
     first = carry is None
-    wide = pl.BlockSpec((tile, width), lambda i: (i, 0))
-    thin = pl.BlockSpec((tile, experts), lambda i: (i, 0))
-    tall = pl.BlockSpec((width, hidden), lambda i: (0, 0))
-    flat = pl.BlockSpec((hidden, width), lambda i: (0, 0))
-    ins = [expert, x, g, gates, *wg, *wu, *wd]
-    specs = [pl.BlockSpec(memory_space=pltpu.SMEM), wide, wide, thin] + [tall] * (2 * pieces) + [flat] * pieces
+    total = blocks * rows
+
+    def out_spec(columns):
+        return pl.BlockSpec((tile, columns), lambda b, i: (b * tiles + i, 0))
+
+    def in_spec(columns):
+        return pl.BlockSpec((tile, columns), lambda b, i: (i, 0))
+
+    weight = pl.BlockSpec((3, width, hidden), lambda b, i: (0, 0, 0), pipeline_mode=pl.Buffered(1))
+    ins = [experts, *xs, *gs, *ws]
+    specs = [pl.BlockSpec(memory_space=pltpu.SMEM)] + [in_spec(width)] * blocks + [in_spec(full)] * blocks + [weight] * len(ws)
     if not first:
         ins += list(carry)
-        specs += [wide, wide, thin]
+        specs += [out_spec(width), out_spec(width), out_spec(LANES)]
+    if last:
+        out_columns, out_types = [width, full], [BF16, BF16]
+    else:
+        out_columns, out_types = [width, width, LANES], [F32] * 3
+    n = len(out_columns)
+    out_columns += [2 * pieces * hidden] * slots + [pieces * hidden] * slots
+    out_types += [BF16] * (2 * slots)
+    single = pieces * hidden
     outs = pl.pallas_call(
-        functools.partial(moe_kernel, first, pieces),
-        grid=(rows // tile,),
+        functools.partial(data_kernel, first, last, blocks, slots, pieces),
+        grid=(blocks, tiles),
         in_specs=specs,
-        out_specs=[wide, wide, thin] + [tall] * (2 * pieces) + [flat] * pieces,
-        out_shape=[
-            jax.ShapeDtypeStruct((rows, width), F32),
-            jax.ShapeDtypeStruct((rows, width), F32),
-            jax.ShapeDtypeStruct((rows, experts), F32),
-        ]
-        + [jax.ShapeDtypeStruct((width, hidden), BF16)] * (2 * pieces)
-        + [jax.ShapeDtypeStruct((hidden, width), BF16)] * pieces,
-        scratch_shapes=[
-            pltpu.VMEM((pieces, width, hidden), F32),
-            pltpu.VMEM((pieces, width, hidden), F32),
-            pltpu.VMEM((pieces, hidden, width), F32),
-        ],
+        out_specs=[out_spec(c) for c in out_columns],
+        out_shape=[jax.ShapeDtypeStruct((total, c), t) for c, t in zip(out_columns, out_types)],
+        scratch_shapes=[pltpu.VMEM((tile, width), F32), pltpu.VMEM((tile, width), F32)],
         compiler_params=pltpu.CompilerParams(vmem_limit_bytes=60 * 2**20),
         cost_estimate=pl.CostEstimate(
-            flops=18 * rows * width * hidden * pieces,
-            bytes_accessed=rows * width * 20 + width * hidden * pieces * 12,
-            transcendentals=rows * hidden * pieces,
+            flops=3 * slots * total * width * single,
+            bytes_accessed=total * width * 12 + slots * pieces * width * hidden * 6,
+            transcendentals=slots * total * single,
         ),
-        name="moe_slot",
+        name="expert_data",
     )(*ins)
-    grads = outs[3:]
-    return (
-        tuple(outs[:3]),
-        [(grads[i], grads[pieces + i], grads[2 * pieces + i]) for i in range(pieces)],
-    )
+    return outs[:n], outs[n : n + slots], outs[n + slots :]
+
+
+def weight_kernel(shape, pieces, *refs):
+    xt = gt = None
+    refs = list(refs)
+    for blocks in shape:
+        xs, gs, h, a = refs[:blocks], refs[blocks : 2 * blocks], refs[2 * blocks], refs[2 * blocks + 1]
+        refs = refs[2 * blocks + 2 :]
+        rows = xs[0].shape[0]
+        for i in range(blocks):
+            span = slice(i * rows, (i + 1) * rows)
+            xp, gp = dot_tn(xs[i][...], h[span]), dot_tn(gs[i][...], a[span])
+            xt, gt = (xp, gp) if xt is None else (xt + xp, gt + gp)
+    outs = refs
+    hid = outs[0].shape[2]
+    for i in range(pieces):
+        outs[i][0] = xt[:, 2 * i * hid : (2 * i + 1) * hid].astype(BF16)
+        outs[i][1] = xt[:, (2 * i + 1) * hid : (2 * i + 2) * hid].astype(BF16)
+        outs[i][2] = gt[:, i * hid : (i + 1) * hid].astype(BF16)
+
+
+def expert_weight(parts, pieces, width):
+    hidden = parts[0][3].shape[1] // pieces
+    block = 256
+    ins, specs, shape, total = [], [], [], 0
+    for xs, gs, h, a in parts:
+        rows = xs[0].shape[0]
+        col = pl.BlockSpec((rows, block), lambda i: (0, i))
+        ins += [*xs, *gs, h, a]
+        specs += [col] * (2 * len(xs))
+        for v in (h, a):
+            specs.append(pl.BlockSpec(v.shape, lambda i: (0, 0), pipeline_mode=pl.Buffered(1)))
+        shape.append(len(xs))
+        total += h.shape[0]
+    return pl.pallas_call(
+        functools.partial(weight_kernel, tuple(shape), pieces),
+        grid=(width // block,),
+        in_specs=specs,
+        out_specs=[pl.BlockSpec((3, block, hidden), lambda i: (0, i, 0))] * pieces,
+        out_shape=[jax.ShapeDtypeStruct((3, width, hidden), BF16)] * pieces,
+        compiler_params=pltpu.CompilerParams(vmem_limit_bytes=60 * 2**20),
+        cost_estimate=pl.CostEstimate(
+            flops=total * width * hidden * pieces,
+            bytes_accessed=total * (width * 4 + hidden * pieces * 6) + width * hidden * pieces * 6,
+            transcendentals=0,
+        ),
+        name="expert_weight",
+    )(*ins)
+
+
+def lay_out_kernel(quarters, cuts, at_ref, *refs):
+    pieces, outs = refs[:PLANE], refs[PLANE:]
+    first, second = quarters
+    for m in range(PLANE):
+        who = at_ref[0] ^ m
+        left = 0
+        rows = pl.ds(pl.multiple_of(who * first, first), first)
+        for out, cut in zip(outs, cuts):
+            out[rows, :] = pieces[m][:first, left : left + cut].astype(F32)
+            left += cut
+        rows = pl.ds(pl.multiple_of(who * second, second), second)
+        outs[-1][rows, :] = pieces[m][first : first + second].astype(F32)
+
+
+def lay_out(at, pieces, quarters, cuts):
+    first, second = (PLANE * q for q in quarters)
+    whole = pl.BlockSpec(memory_space=pltpu.VMEM)
+    return pl.pallas_call(
+        functools.partial(lay_out_kernel, quarters, cuts),
+        in_specs=[pl.BlockSpec(memory_space=pltpu.SMEM)] + [whole] * PLANE,
+        out_specs=[whole] * (len(cuts) + 1),
+        out_shape=[jax.ShapeDtypeStruct((first, c), F32) for c in cuts]
+        + [jax.ShapeDtypeStruct((second, pieces[0].shape[1]), F32)],
+        compiler_params=pltpu.CompilerParams(vmem_limit_bytes=48 * 2**20),
+        cost_estimate=pl.CostEstimate(flops=0, bytes_accessed=6 * first * sum(cuts), transcendentals=0),
+        name="lay_out",
+    )(at, *pieces)
+
+
+def after(x, *others):
+    leaves, tree = jax.tree.flatten(x)
+    extra = jax.tree.leaves(others)
+    held = lax.optimization_barrier(tuple(leaves) + tuple(extra))
+    return jax.tree.unflatten(tree, held[: len(leaves)])
 
 
 def body(
@@ -326,36 +423,25 @@
     def cols_of(x, who):
         return lax.dynamic_slice_in_dim(x, who * col_width, col_width, x.ndim - 1)
 
+    def place(parts, axis):
+        if n_tensor == 2:
+            return jnp.where(t_at == 0, jnp.concatenate(parts, axis), jnp.concatenate(parts[::-1], axis))
+        size = parts[0].shape[axis]
+        shape = list(parts[0].shape)
+        shape[axis] *= n_tensor
+        out = jnp.zeros(shape, parts[0].dtype)
+        for s, v in enumerate(parts):
+            out = lax.dynamic_update_slice_in_dim(out, v, peer(-s) * size, axis)
+        return out
+
     def to_rows(x):
-        out = jnp.zeros((my_row, width), x.dtype)
-        out = lax.dynamic_update_slice(out, rows_of(x, t_at), (0, t_at * col_width))
-        for s in range(1, n_tensor):
-            got = hop(rows_of(x, peer(s)), s)
-            out = lax.dynamic_update_slice(out, got, (0, peer(-s) * col_width))
-        return out
+        return place([rows_of(x, t_at)] + [hop(rows_of(x, peer(s)), s) for s in range(1, n_tensor)], 1)
 
     def to_cols(x):
-        out = jnp.zeros((n_tok, col_width), x.dtype)
-        out = lax.dynamic_update_slice(out, cols_of(x, t_at), (t_at * my_row, 0))
-        for s in range(1, n_tensor):
-            got = hop(cols_of(x, peer(s)), s)
-            out = lax.dynamic_update_slice(out, got, (peer(-s) * my_row, 0))
-        return out
+        return place([cols_of(x, t_at)] + [hop(cols_of(x, peer(s)), s) for s in range(1, n_tensor)], 0)
 
     def gather_rows(x):
-        out = jnp.zeros((n_tok,) + x.shape[1:], x.dtype)
-        rest = (0,) * (x.ndim - 1)
-        out = lax.dynamic_update_slice(out, x, (t_at * my_row,) + rest)
-        for s in range(1, n_tensor):
-            out = lax.dynamic_update_slice(out, hop(x, s), (peer(-s) * my_row,) + rest)
-        return out
-
-    slots = []
-    held = (w_gate[0], w_up[0], w_down[0])
-    for k in range(depth):
-        if k:
-            held = ring(held)
-        slots.append([held] + [hop(held, s) for s in range(1, n_tensor)])
+        return place([x] + [hop(x, s) for s in range(1, n_tensor)], 0)
 
     ids_rows = rows_of(expert_ids, t_at)
     logit_rows = rows_of(router_logits, t_at)
@@ -364,11 +450,13 @@
     masked = jnp.where(used, logit_rows, NEG)
     weights = jnp.where(used, jnp.exp(masked - jnp.max(masked, axis=1, keepdims=True)), 0.0)
     gates = weights / jnp.sum(weights, axis=1, keepdims=True)
+    pad = ((0, 0), (0, LANES // 2 - n_expert))
+    high = lax.optimization_barrier(gates.astype(BF16))
+    low = (gates - high.astype(F32)).astype(BF16)
     grad_rows = to_rows(out_grad.astype(BF16))
-    masks = range(1, PLANE)
-    gates_all = jnp.concatenate([gates] + [plane(gates, m) for m in masks], axis=0)
-    grads_all = jnp.concatenate([grad_rows] + [plane(grad_rows, m) for m in masks], axis=0)
-    out_pieces = [w_out] + [hop(w_out, s) for s in range(1, n_tensor)]
+    grad_wide = jnp.concatenate([grad_rows, jnp.pad(high, pad), jnp.pad(low, pad)], axis=1)
+    held = [jnp.stack([w_gate[0], w_up[0], w_down[0].T])]
+    half_row = my_row // 2
 
     start = jnp.sum((segment_ids[:, None] < segment_ids[None, :]).astype(jnp.int32), axis=0)
     places = jnp.arange(n_tok, dtype=jnp.int32) - start
@@ -377,6 +465,11 @@
     angles = freq[:, None] * places.astype(F32)[None, :]
     cos_t, sin_t = jnp.cos(angles), jnp.sin(angles)
     start = start[None, :]
+    held.append(ring(held[0]))
+    tokens, grad_wide = after((tokens, grad_wide))
+    grad_x, grad_y = plane(grad_wide, 1), plane(grad_wide, 2)
+    out_pieces = [w_out] + [hop(w_out, s) for s in range(1, n_tensor)]
+    slots = [[held[0]] + [hop(held[0], s) for s in range(1, n_tensor)]]
     x_full = tokens.astype(F32)
     inv_one = lax.rsqrt(jnp.mean(x_full * x_full, axis=1, keepdims=True) + EPS)
     normed_one = x_full * inv_one
@@ -385,10 +478,11 @@
     def project(w):
         return jnp.einsum("td,dc->ct", attn_in, w, preferred_element_type=F32)
 
-    q_t, k_t, o_t, lse = attn_forward(
-        project(w_query), project(key_matrix), project(value_matrix).astype(BF16), cos_t, sin_t, start
-    )
     v_t = project(value_matrix).astype(BF16)
+    q_t, k_t, o_t, lse = attn_forward(project(w_query), project(key_matrix), v_t, cos_t, sin_t, start)
+    o_t, grad_x, grad_y, slots[0], out_pieces, held[1] = after((o_t, grad_x, grad_y, slots[0], out_pieces, held[1]))
+    held.append(ring(held[1]))
+    grad_diag = [plane(grad_x[:half_row], 2), plane(grad_y[half_row:], 1)]
     mixed = rows_of(tokens, t_at).astype(F32)
     for s in range(n_tensor):
         part = lax.dynamic_slice_in_dim(o_t, peer(s) * my_row, my_row, 1)
@@ -398,53 +492,133 @@
     inv_two = lax.rsqrt(jnp.mean(mixed * mixed, axis=1, keepdims=True) + EPS)
     normed_two = mixed * inv_two
     mlp_in = (normed_two * gain_mlp).astype(BF16)
-    mlp_all = jnp.concatenate([mlp_in] + [plane(mlp_in, m) for m in masks], axis=0)
-
-    carry = None
-    totals = []
-    for k in range(depth):
-        expert = lax.rem(e_at - k * PLANE + n_expert, n_expert).reshape(1)
-        wg, wu, wd = zip(*slots[k])
-        carry, grads = moe_slot(expert, mlp_all, grads_all, gates_all, wg, wu, wd, carry, my_row)
-        total = [a.astype(F32) for a in grads[0]]
+    mlp_in, grad_diag = after((mlp_in, grad_diag))
+
+    near = ([mlp_in], [grad_wide])
+    sides, diag = None, None
+    group = 2 if depth % 2 == 0 else 1
+    carry = {"near": None, "sides": None, "diag": None}
+    saved = [{} for _ in range(depth)]
+
+    def run(name, blocks, k, ws):
+        ks = range(k, k + group)
+        experts = jnp.stack([lax.rem(e_at - i * PLANE + n_expert, n_expert) for i in ks])
+        flat = [w for i in ks for w in ws[i]]
+        carry[name], hs, acts = expert_data(experts, *blocks, flat, carry[name], k + group == depth)
+        for i, h, a in zip(ks, hs, acts):
+            saved[i][name] = (*blocks, h, a)
+
+    def add_slot():
+        k = len(slots)
+        slots.append([held[k]] + [hop(held[k], s) for s in range(1, n_tensor)])
+
+    mlp_x, mlp_y = plane(mlp_in, 1), plane(mlp_in, 2)
+    for _ in range(1, group):
+        add_slot()
+    run("near", near, 0, slots)
+    mlp_x, mlp_y, carry["near"], held[2] = after((mlp_x, mlp_y, carry["near"], held[2]))
+    for _ in range(3, depth):
+        held.append(ring(held[-1]))
+    mlp_diag = [plane(mlp_x[:half_row], 2), plane(mlp_y[half_row:], 1)]
+    sides = ([mlp_x, mlp_y], [grad_x, grad_y])
+    run("sides", sides, 0, slots)
+    carry["sides"], mlp_diag = after((carry["sides"], mlp_diag))
+    diag = (mlp_diag, grad_diag)
+    add_slot()
+    run("diag", diag, 0, slots)
+
+    def weight_total(k):
+        grads = expert_weight(list(saved[k].values()), n_tensor, width)
+        total = grads[0].astype(F32)
         for s in range(1, n_tensor):
-            got = hop(grads[s], n_tensor - s)
-            total = [a + b.astype(F32) for a, b in zip(total, got)]
-        totals.append(total)
+            total = total + hop(grads[s], n_tensor - s).astype(F32)
+        return total
+
+    for k in range(group, depth - group, group):
+        while len(slots) < k + group:
+            add_slot()
+        for name, blocks in (("near", near), ("sides", sides), ("diag", diag)):
+            run(name, blocks, k, slots)
+    carry["diag"] = after(carry["diag"], slots[-1])
+    totals = {}
+    order = list(range(1, depth)) + [0]
+    early = order[: depth - group - 1]
+    for k in early:
+        totals[k] = weight_total(k)
+    while len(slots) < depth:
+        add_slot()
+    slots[-1], totals = after((slots[-1], totals))
     moving = None
-    for k in list(range(1, depth)) + [0]:
+
+    def send_on(k, moving):
         total = totals[k]
         if moving is not None:
-            total = [a + b.astype(F32) for a, b in zip(total, ring(moving))]
-        moving = [a.astype(BF16) for a in total]
-    grad_gate, grad_up, grad_down = (a[None] for a in total)
-
-    out_all, dx_all, dgate_all = carry
-
-    def home(x):
-        total = x[:my_row].astype(F32)
-        for m in masks:
-            total = total + plane(x[m * my_row : (m + 1) * my_row], m).astype(F32)
-        return total
-
-    d_mlp_in = home(dx_all.astype(BF16))
-    d_gates = home(dgate_all)
-    block_out = to_cols((mixed + home(out_all.astype(BF16))).astype(BF16))
-    grad_logits = gather_rows(gates * (d_gates - jnp.sum(gates * d_gates, axis=1, keepdims=True)))
-
+            total = total + moving.astype(F32)
+        return ring(total.astype(BF16)) if k else total
+
+    for k in early:
+        moving = send_on(k, moving)
+    rest = order[len(early) :]
+    last = depth - group
+    run("diag", diag, last, slots)
+    top, low = slice(0, half_row), slice(half_row, my_row)
+
+    def first_half(rows):
+        return plane(rows[top], 1), plane(rows[low], 2)
+
+    def second_half(rows):
+        return plane(rows[:my_row][top], 1), plane(rows[my_row:][low], 2)
+
+    def third_half(rows, part_y, part_x):
+        low_x = rows[:my_row][low].astype(F32) + part_x.astype(F32)
+        top_y = rows[my_row:][top].astype(F32) + part_y.astype(F32)
+        return plane(low_x.astype(BF16), 1), plane(top_y.astype(BF16), 2)
+
+    def home(own, top_x, low_y, low_x, top_y):
+        first = own[top].astype(F32) + top_x.astype(F32) + top_y.astype(F32)
+        return jnp.concatenate([first, own[low].astype(F32) + low_x.astype(F32) + low_y.astype(F32)], axis=0)
+
+    parts = first_half(carry["diag"][1])
+    run("sides", sides, last, slots)
+    carry["sides"], near[0][0] = after((carry["sides"], near[0][0]))
+    halves = second_half(carry["sides"][1])
+    run("near", near, last, slots)
+    parts, halves, carry["near"] = after((parts, halves, carry["near"]))
+    others = third_half(carry["sides"][1], *parts)
+    totals[rest[0]] = weight_total(rest[0])
+    others, totals, moving = after((others, totals, moving))
+
+    moving = send_on(rest[0], moving)
+    out_parts = first_half(carry["diag"][0])
+    back = home(carry["near"][1], *halves, *others)
+    d_mlp_in = back[:, :width]
+    d_gates = back[:, width : width + n_expert] + back[:, width + LANES // 2 : width + LANES // 2 + n_expert]
     scaled_two = d_mlp_in * gain_mlp
     norm_dots = jnp.mean(scaled_two * normed_two, axis=1, keepdims=True)
     d_mixed = grad_rows.astype(F32) + inv_two * (scaled_two - normed_two * norm_dots)
+    dy_full = gather_rows(d_mixed.astype(BF16))
+    for k in rest[1:]:
+        if k:
+            totals[k] = weight_total(k)
+    dy_full, totals, out_parts = after((dy_full, totals, out_parts))
+    halves = second_half(carry["sides"][0])
+    others = third_half(carry["sides"][0], *out_parts)
+
+    do_t = jnp.einsum("td,cd->ct", dy_full, w_out, preferred_element_type=F32).astype(BF16)
+    out_grad_w = jnp.einsum("ct,td->cd", o_t, dy_full, preferred_element_type=F32)
+    out_grad_w = out_grad_w.astype(BF16)
+    dq_t, dk_t, dv_t = attn_backward(q_t, k_t, v_t, do_t, lse, cos_t, sin_t, start)
     gain_two_all = jnp.sum(d_mlp_in * normed_two, axis=0)
     gain_two = cols_of(gain_two_all, t_at)
     for s in range(1, n_tensor):
         gain_two = gain_two + hop(cols_of(gain_two_all, peer(s)), s)
-    dy_full = gather_rows(d_mixed.astype(BF16))
-
-    out_grad_w = jnp.einsum("ct,td->cd", o_t, dy_full, preferred_element_type=F32)
-    grad_out = lax.psum(out_grad_w.astype(BF16), "expert").astype(F32)
-    do_t = jnp.einsum("td,cd->ct", dy_full, w_out, preferred_element_type=F32).astype(BF16)
-    dq_t, dk_t, dv_t = attn_backward(q_t, k_t, v_t, do_t, lse, cos_t, sin_t, start)
+    grad_logits = gather_rows(gates * (d_gates - jnp.sum(gates * d_gates, axis=1, keepdims=True)))
+    dq_t, halves, others, moving, gain_two = after((dq_t, halves, others, moving, gain_two))
+    for k in rest[1:-1]:
+        moving = send_on(k, moving)
+    saved[0], dq_t = after((saved[0], dq_t))
+    totals[0] = weight_total(0)
+    block_out = to_cols((mixed + home(carry["near"][0], *halves, *others)).astype(BF16))
 
     def weight_grad(d_t):
         return jnp.einsum("td,ct->dc", attn_in, d_t, preferred_element_type=F32).astype(BF16)
@@ -452,9 +626,24 @@
     def input_grad(d_t, w):
         return jnp.einsum("ct,dc->td", d_t, w, preferred_element_type=F32)
 
-    grad_query, grad_key, grad_value = (
-        a.astype(F32) for a in lax.psum((weight_grad(dq_t), weight_grad(dk_t), weight_grad(dv_t)), "expert")
-    )
+    def part(a, who, rows):
+        return lax.dynamic_slice_in_dim(a, who * rows, rows, 0)
+
+    local = jnp.concatenate([weight_grad(dq_t), weight_grad(dk_t), weight_grad(dv_t)], axis=1)
+    quarters = (local.shape[0] // PLANE, out_grad_w.shape[0] // PLANE)
+    wide = local.shape[1]
+    out_rows = out_grad_w.shape[0] * width // wide
+    out_grad_w = out_grad_w.reshape(out_rows, wide)
+    quarters = (local.shape[0] // PLANE, out_rows // PLANE)
+    p_at, z_at = lax.rem(e_at, PLANE), e_at // PLANE
+
+    def quarter_of(who):
+        return jnp.concatenate([part(v, who, q) for v, q in zip((local, out_grad_w), quarters)], axis=0)
+
+    sent = [plane(quarter_of(p_at ^ m), m) for m in range(1, PLANE)]
+    quarter = sum(quarters)
+    small = quarter // depth
+
     in_terms = input_grad(dq_t, w_query) + input_grad(dk_t, key_matrix) + input_grad(dv_t, value_matrix)
     dots = jnp.sum(in_terms * gain_attn * normed_one, axis=1)
     d_attn_in = cols_of(in_terms, t_at)
@@ -468,23 +657,42 @@
     grad_tokens = cols_of(dy_full, t_at).astype(F32) + d_norm_one
     gain_one = jnp.sum(d_attn_in * normed_cols, axis=0)
 
-    gains = jnp.stack([gain_one, gain_two])
-    for m in (1, 2):
-        gains = gains + plane(gains, m)
-    gains = functools.reduce(jnp.add, [gains] + [ring(gains, s) for s in range(1, depth)])
+    gains = jnp.concatenate([gain_one, gain_two]).astype(BF16)
+    gains = jnp.broadcast_to(gains[None, :], (16, gains.shape[0]))
+    mine = quarter_of(p_at).astype(F32)
+    for v in sent:
+        mine = mine + v.astype(F32)
+    mine, gains = after((mine.astype(BF16), gains))
+    rows = [jnp.concatenate([part(mine, lax.rem(z_at + s, depth), small), gains], axis=0) for s in range(depth)]
+    total = rows[0].astype(F32)
+    for v in [ring(rows[s], s) for s in range(1, depth)]:
+        total = total + v.astype(F32)
+    total = total.astype(BF16)
+    gains, total = total[small:], total[:small]
+    got = [ring(total, s) for s in range(1, depth)]
+    out = jnp.zeros((quarter, total.shape[1]), BF16)
+    out = lax.dynamic_update_slice(out, total, (z_at * small, 0))
+    for s in range(1, depth):
+        out = lax.dynamic_update_slice(out, got[s - 1], (lax.rem(z_at - s + depth, depth) * small, 0))
+    out = jnp.concatenate([out, gains], axis=0)
+    got = [out] + [plane(out, m) for m in range(1, PLANE)]
+    gains = functools.reduce(jnp.add, [v[quarter].astype(F32) for v in got])
+    cuts = [w_query.shape[1], key_matrix.shape[1], value_matrix.shape[1]]
+    grad_query, grad_key, grad_value, grad_out = lay_out(p_at.reshape(1), got, quarters, cuts)
+    moving = send_on(rest[-1], moving)
     return (
         block_out,
         grad_tokens,
         grad_logits,
-        gains[0],
+        gains[:col_width],
         grad_query,
         grad_key,
         grad_value,
-        grad_out,
-        gains[1],
-        grad_gate,
-        grad_up,
-        grad_down,
+        grad_out.reshape(w_out.shape),
+        gains[col_width:],
+        moving[0][None],
+        moving[1][None],
+        moving[2].T[None],
     )
 
 

time: 736 us -> 485 us (0.66)
  waiting for transfers between devices: 370 us -> 139 us
  starting transfers between devices: 72.5 us -> 47.4 us
  Pallas kernels: 162 us -> 178 us
  local copies, waits for them, and re-layouts: 21.1 us -> 35.4 us
  between operations: 15.5 us -> 2.05 us
  matrix products: 27.5 us -> 19.9 us
    ppermute x20 -> x26, waiting for transfers between devices: 214 us -> 82.5 us  [plane(): return jax.tree.map(lambda a: lax.ppermute(a, 'expert', pairs), x)]
    psum x1 -> x0, waiting for transfers between devices: 76 us -> none  [body(): lax.psum((weight_grad(dq_t), weight_grad(dk_t), weight_grad(dv_t)), 'expe...]
    ppermute x21 -> x12, waiting for transfers between devices: 79.6 us -> 52.2 us  [ring(): return jax.tree.map(lambda a: lax.ppermute(a, 'expert', pairs), x)]
    ppermute x21 -> x12, starting transfers between devices: 40.8 us -> 16.8 us  [ring(): return jax.tree.map(lambda a: lax.ppermute(a, 'expert', pairs), x)]
    pallas_call x4 -> x11, Pallas kernels: 131 us -> 147 us  [the longest x6 95.1 us: expert_data(): pl.pallas_call(functools.partial(data_kernel, first, last, blocks, slots,...]
    add x3 -> x7, other arithmetic: 0.03 us -> 12.6 us  [the longest x3 7.29 us: weight_total(): total = total + hop(grads[s], n_tensor - s).astype(F32)]
    slice x4 -> x11, local copies, waits for them, and re-layouts: 3.99 us -> 13.5 us  [the longest x2 3.73 us: body(): mlp_diag = [plane(mlp_x[:half_row], 2), plane(mlp_y[half_row:], 1)]]
    convert_element_type x15 -> x10, other arithmetic: 22.5 us -> 16.1 us  [the longest x2 6.05 us: send_on(): return ring(total.astype(BF16)) if k else total]
  transfers between devices with their start and end apart: 75 -> 55, of which waited for: 21 -> 23; matrix products, arithmetic and copies ran while one was open for 12% -> 19% of each run, Pallas kernels for 16% -> 24%
where the time goes in v2:
time: 485 us; the launch traced here: 476 us
  Pallas kernels  178 us (37%)
  waiting for transfers between devices  139 us (29%)
  other arithmetic  54.2 us (11%)
  starting transfers between devices  47.4 us (10%)
  local copies, waits for them, and re-layouts  35.4 us (7%)
  matrix products  19.9 us (4%)
    pallas_call x6, Pallas kernels, expert_data(): pl.pallas_call(functools.partial(data_kernel, first, last, blocks, slots,...  95.1 us
    ppermute x26, waiting for transfers between devices, plane(): return jax.tree.map(lambda a: lax.ppermute(a, 'expert', pairs), x)  82.5 us
    ppermute x12, waiting for transfers between devices, ring(): return jax.tree.map(lambda a: lax.ppermute(a, 'expert', pairs), x)  52.2 us
    pallas_call x4, Pallas kernels, expert_weight(): pl.pallas_call(functools.partial(weight_kernel, tuple(shape), pieces), gr...  47.9 us
    ppermute x26, starting transfers between devices, plane(): return jax.tree.map(lambda a: lax.ppermute(a, 'expert', pairs), x)  26.9 us
    pallas_call x1, Pallas kernels, attn_backward(): pl.pallas_call(functools.partial(attn_bwd_kernel, block), grid=(kv,), in_...  19.8 us
    ppermute x12, starting transfers between devices, ring(): return jax.tree.map(lambda a: lax.ppermute(a, 'expert', pairs), x)  16.8 us
    pallas_call x1, Pallas kernels, attn_forward(): pl.pallas_call(functools.partial(attn_fwd_kernel, block), grid=(kv,), in_...  11.5 us
  transfers between devices with their start and end apart: 55, of which 23 were waited for; matrix products, arithmetic and copies ran while one was open for 19% of the time, Pallas kernels for 24%

profile of v2, /device:TPU:0, one launch (start us, length us, event | category | flops | bytes accessed | tf_op | source)
XLA Modules:
  0.0 476.3 jit_solution(398100920386500707)
XLA Ops:
  2.0 2.5 pad_maximum_fusion.1.refs_2_.refs_4_
  5.0 2.6 collective-permute-start.5
  7.5 1.8 convert_element_type.242
  14.5 3.2 concatenate.73.refs_1_.refs_13_.refs_7_
  20.7 2.1 fusion
  24.8 2.7 convolution_bitcast_fusion.q_ref
  27.6 11.5 %attn_forward.1 = (bf16[512,1024]{1,0:T(8,128)(2,1)S(1)}, bf16[256,1024]{1,0:T(8,128)(2,1)S(1)}, bf16[512,1024]{1,0:T(8,128)(2,1)S(1)}, f32[4,2,1024]{2,1,0:T(2,128)S(1)}) custom-call(f32[512,1024]{1,0:T(8,128)} %convolution_bitcast_fusion.q_ref, f32[256,1024]{1,0:T(8,128)S(1)} %convolution_bitcast_fusion.1.k_ref, bf16[256,1024]{1,0:T(8,128)(2,1)S(1)} %fusion.4.v_ref, ...), custom_call_target="tpu_custom_call" | custom-call | flops 4294967296 | bytes 4194304 | tf_op jit(solution)/shard_map/attn_forward/pallas_call | solution.py:123
  40.0 4.9 %collective-permute-done.5.refs_4_.refs_6_ = bf16[3,1024,256]{2,1,0:T(8,128)(2,1)} collective-permute-done((bf16[3,1024,256]{2,1,0:T(8,128)(2,1)}, bf16[3,1024,256]{2,1,0:T(8,128)(2,1)}, u32[]{:S(2)}, u32[]{:S(2)}) %collective-permute-start.5) | collective-permute-done | bytes 1572896 | tf_op jit(solution)/shard_map/ppermute | solution.py:415
  48.7 1.8 collective-permute-start.12
  51.6 1.6 collective-permute-start.7
  55.8 2.3 multiply_reduce_fusion.4
  60.7 6.0 %collective-permute-done.7.refs_2_.refs_12_ = bf16[256,1152]{1,0:T(8,128)(2,1)} collective-permute-done((bf16[256,1152]{1,0:T(8,128)(2,1)S(1)}, bf16[256,1152]{1,0:T(8,128)(2,1)}, u32[]{:S(2)}, u32[]{:S(2)}) %collective-permute-start.7) | collective-permute-done | bytes 589856 | tf_op jit(solution)/shard_map/ppermute | solution.py:411
  66.7 2.4 collective-permute-done.8.refs_3_.refs_13_
  70.7 12.2 %expert_data.6 = (f32[512,1024]{1,0:T(8,128)}, f32[512,1024]{1,0:T(8,128)}, f32[512,128]{1,0:T(8,128)}, bf16[512,1024]{1,0:T(8,128)(2,1)}, bf16[512,1024]{1,0:T(...) custom-call(s32[2]{0:T(128)} %pad_add_fusion.1.expert_ref, ...), custom_call_target="tpu_custom_call" | custom-call | flops 1610612736 | bytes 12582912 | tf_op jit(solution)/shard_map/expert_data/pallas_call | solution.py:278
  83.0 4.3 collective-permute-done.12.refs_4_.refs_2_
  87.3 5.7 %collective-permute-done.10.refs_1_.refs_5_.refs_7_.refs_11_ = bf16[512,1024]{1,0:T(8,128)(2,1)} collective-permute-done((bf16[512,1024]{1,0:T(8,128)(2,1)}, bf16[512,1024]{1,0:T(8,128)(2,1)}, u32[]{:S(2)}, u32[]{:S(2)}) %collective-permute-start.10) | collective-permute-done | bytes 1048608 | tf_op jit(solution)/shard_map/ppermute | solution.py:411
  93.2 1.6 collective-permute-start.16
  94.8 1.9 slice.127
  98.2 1.9 slice.128
  100.6 20.8 %expert_data.7 = (f32[1024,1024]{1,0:T(8,128)}, f32[1024,1024]{1,0:T(8,128)}, f32[1024,128]{1,0:T(8,128)}, bf16[1024,1024]{1,0:T(8,128)(2,1)}, bf16[1024,1024]{1...) custom-call(s32[2]{0:T(128)} %pad_add_fusion.1.expert_ref, ...), custom_call_target="tpu_custom_call" | custom-call | flops 3221225472 | bytes 18874368 | tf_op jit(solution)/shard_map/expert_data/pallas_call | solution.py:278
  122.2 12.6 %expert_data.8 = (f32[512,1024]{1,0:T(8,128)}, f32[512,1024]{1,0:T(8,128)}, f32[512,128]{1,0:T(8,128)}, bf16[512,1024]{1,0:T(8,128)(2,1)}, bf16[512,1024]{1,0:T(...) custom-call(s32[2]{0:T(128)} %pad_add_fusion.1.expert_ref, bf16[256,1024]{1,0:T(8,128)(2,1)} %copy-done.6, ...), custom_call_target="tpu_custom_call" | custom-call | flops 1610612736 | bytes 12582912 | tf_op jit(solution)/shard_map/expert_data/pallas_call | solution.py:278
  134.8 11.9 %expert_weight.4 = (bf16[3,1024,256]{2,1,0:T(8,128)(2,1)}, bf16[3,1024,256]{2,1,0:T(8,128)(2,1)}) custom-call(bf16[512,1024]{1,0:T(8,128)(2,1)} %multiply_convert_fusion.1.refs_0_.refs_12_.refs_6_, bf16[512,1152]{1,0:T(8,128)(2,1)} %concatenate.73.refs_1_.refs_13_.refs_7_, bf16[512,1024]{1,0:T(8,128)(2,1)} %get-tuple-element.168.refs_2_, ...), custom_call_target="tpu_custom_call" | custom-call | flops 1073741824 | bytes 17825792 | tf_op jit(solution)/shard_map/expert_weight/pallas_call | solution.py:328
  147.9 2.7 collective-permute-done.18
  150.6 3.4 convert_add_fusion.3
  154.0 22.4 %expert_data.10 = (bf16[1024,1024]{1,0:T(8,128)(2,1)}, bf16[1024,1152]{1,0:T(8,128)(2,1)}, bf16[1024,1024]{1,0:T(8,128)(2,1)}, bf16[1024,1024]{1,0:T(8,128)(2,1)...) custom-call(s32[2]{0:T(128)} %pad_add_fusion.expert_ref, ...), custom_call_target="tpu_custom_call" | custom-call | flops 3221225472 | bytes 18874368 | tf_op jit(solution)/shard_map/expert_data/pallas_call | solution.py:278
  176.5 13.6 %expert_data.9 = (bf16[512,1024]{1,0:T(8,128)(2,1)}, bf16[512,1152]{1,0:T(8,128)(2,1)}, bf16[512,1024]{1,0:T(8,128)(2,1)}, bf16[512,1024]{1,0:T(8,128)(2,1)}, bf...) custom-call(s32[2]{0:T(128)} %pad_add_fusion.expert_ref, bf16[256,1024]{1,0:T(8,128)(2,1)} %copy-done.6, ...), custom_call_target="tpu_custom_call" | custom-call | flops 1610612736 | bytes 12582912 | tf_op jit(solution)/shard_map/expert_data/pallas_call | solution.py:278
  190.1 13.5 %expert_data.11 = (bf16[512,1024]{1,0:T(8,128)(2,1)}, bf16[512,1152]{1,0:T(8,128)(2,1)}, bf16[512,1024]{1,0:T(8,128)(2,1)}, bf16[512,1024]{1,0:T(8,128)(2,1)}, b...) custom-call(s32[2]{0:T(128)} %pad_add_fusion.expert_ref, ...), custom_call_target="tpu_custom_call" | custom-call | flops 1610612736 | bytes 12582912 | tf_op jit(solution)/shard_map/expert_data/pallas_call | solution.py:278
  203.6 12.1 %expert_weight.5 = (bf16[3,1024,256]{2,1,0:T(8,128)(2,1)}, bf16[3,1024,256]{2,1,0:T(8,128)(2,1)}) custom-call(bf16[256,1024]{1,0:T(8,128)(2,1)} %copy-done.6, bf16[256,1024]{1,0:T(8,128)(2,1)} %collective-permute-done.14.refs_1_.refs_11_, bf16[256,1152]{1,0:T(8,128)(2,1)} %collective-permute-done.7.refs_2_.refs_12_, ...), custom_call_target="tpu_custom_call" | custom-call | flops 1073741824 | bytes 17825792 | tf_op jit(solution)/shard_map/expert_weight/pallas_call | solution.py:328
  216.1 2.3 fusion.20
  223.7 11.2 %collective-permute-done.21 = bf16[256,1152]{1,0:T(8,128)(2,1)} collective-permute-done((bf16[256,1152]{1,0:T(8,128)(2,1)}, bf16[256,1152]{1,0:T(8,128)(2,1)}, u32[]{:S(2)}, u32[]{:S(2)}) %collective-permute-start.21) | collective-permute-done | bytes 589856 | tf_op jit(solution)/shard_map/ppermute | solution.py:411
  235.5 11.9 %expert_weight.6 = (bf16[3,1024,256]{2,1,0:T(8,128)(2,1)}, bf16[3,1024,256]{2,1,0:T(8,128)(2,1)}) custom-call(bf16[256,1024]{1,0:T(8,128)(2,1)} %copy-done.6, bf16[256,1024]{1,0:T(8,128)(2,1)} %collective-permute-done.14.refs_1_.refs_11_, bf16[256,1152]{1,0:T(8,128)(2,1)} %collective-permute-done.7.refs_2_.refs_12_, ...), custom_call_target="tpu_custom_call" | custom-call | flops 1073741824 | bytes 17825792 | tf_op jit(solution)/shard_map/expert_weight/pallas_call | solution.py:328
  247.4 2.4 fusion.23
  249.9 2.0 add_convert_fusion.4
  251.9 1.6 collective-permute-start.23
  255.6 1.8 convert_add_fusion.2
  257.5 10.7 %collective-permute-done.23 = bf16[256,1152]{1,0:T(8,128)(2,1)S(1)} collective-permute-done((bf16[256,1152]{1,0:T(8,128)(2,1)S(1)}, bf16[256,1152]{1,0:T(8,128)(2,1)S(1)}, u32[]{:S(2)}, u32[]{:S(2)}) %collective-permute-start.23) | collective-permute-done | bytes 589856 | tf_op jit(solution)/shard_map/ppermute | solution.py:411
  270.1 1.9 collective-permute-done.26
  272.1 1.6 convert_add_fusion.6
  275.0 1.6 add_convert_fusion.2
  276.6 2.0 convert_add_fusion.1
  278.8 3.0 add_convert_fusion.1
  287.8 3.4 maximum_select_fusion
  291.3 3.3 add_convert_fusion.6
  298.6 19.8 %attn_backward.1 = (bf16[512,1024]{1,0:T(8,128)(2,1)S(1)}, bf16[256,1024]{1,0:T(8,128)(2,1)S(1)}, bf16[256,1024]{1,0:T(8,128)(2,1)S(1)}) custom-call(bf16[512,1024]{1,0:T(8,128)(2,1)S(1)} %copy-done.2, bf16[256,1024]{1,0:T(8,128)(2,1)S(1)} %get-tuple-element.199.k_ref, bf16[256,1024]{1,0:T(8,128)(2,1)S(1)} %fusion.4.v_ref, ...), custom_call_target="tpu_custom_call" | custom-call | flops 10737418240 | bytes 4194304 | tf_op jit(solution)/shard_map/attn_backward/pallas_call | solution.py:148
  325.9 1.6 convolution_convert_fusion.1
  327.6 4.4 multiply_reduce_fusion
  340.4 2.3 convert_add_fusion.8
  342.7 3.0 add_convert_fusion
  345.7 12.0 %expert_weight.7 = (bf16[3,1024,256]{2,1,0:T(8,128)(2,1)}, bf16[3,1024,256]{2,1,0:T(8,128)(2,1)}) custom-call(bf16[256,1024]{1,0:T(8,128)(2,1)} %copy-done.6, bf16[256,1024]{1,0:T(8,128)(2,1)} %collective-permute-done.14.refs_1_.refs_11_, bf16[256,1152]{1,0:T(8,128)(2,1)} %collective-permute-done.7.refs_2_.refs_12_, ...), custom_call_target="tpu_custom_call" | custom-call | flops 1073741824 | bytes 17825792 | tf_op jit(solution)/shard_map/expert_weight/pallas_call | solution.py:328
  358.2 15.7 %collective-permute-done.42 = bf16[384,1024]{1,0:T(8,128)(2,1)} collective-permute-done((bf16[384,1024]{1,0:T(8,128)(2,1)}, bf16[384,1024]{1,0:T(8,128)(2,1)}, u32[]{:S(2)}, u32[]{:S(2)}) %collective-permute-start.42) | collective-permute-done | bytes 786464 | tf_op jit(solution)/shard_map/ppermute | solution.py:411
  373.9 2.2 add_convert_fusion.3
  376.1 4.6 multiply_reduce_fusion.1
  380.9 2.8 collective-permute-start.45
  385.3 17.1 %collective-permute-done.44 = bf16[112,1024]{1,0:T(8,128)(2,1)S(1)} collective-permute-done((bf16[112,1024]{1,0:T(8,128)(2,1)S(1)}, bf16[112,1024]{1,0:T(8,128)(2,1)S(1)}, u32[]{:S(2)}, u32[]{:S(2)}) %collective-permute-start.44) | collective-permute-done | bytes 229408 | tf_op jit(solution)/shard_map/ppermute | solution.py:415
  402.4 9.4 %collective-permute-done.45 = bf16[112,1024]{1,0:T(8,128)(2,1)S(1)} collective-permute-done((bf16[112,1024]{1,0:T(8,128)(2,1)S(1)}, bf16[112,1024]{1,0:T(8,128)(2,1)S(1)}, u32[]{:S(2)}, u32[]{:S(2)}) %collective-permute-start.45) | collective-permute-done | bytes 229408 | tf_op jit(solution)/shard_map/ppermute | solution.py:415
  412.1 5.4 %collective-permute-start.47 = (bf16[96,1024]{1,0:T(8,128)(2,1)S(1)}, bf16[96,1024]{1,0:T(8,128)(2,1)S(1)}, u32[]{:S(2)}, u32[]{:S(2)}) collective-permute-start(bf16[96,1024]{1,0:T(8,128)(2,1)S(1)} %get-tuple-element.369), channel_id=1, source_target_pairs={{0,8},{2,10},{4,12},{6,14},{8,16},{10,18},{12,20},{14,22},{16,24},... | collective-permute-start | bytes 589832 | tf_op jit(solution)/shard_map/ppermute | solution.py:415
  418.4 4.4 collective-permute-done.47
  423.1 6.8 %collective-permute-done.48 = bf16[96,1024]{1,0:T(8,128)(2,1)S(1)} collective-permute-done((bf16[96,1024]{1,0:T(8,128)(2,1)S(1)}, bf16[96,1024]{1,0:T(8,128)(2,1)S(1)}, u32[]{:S(2)}, u32[]{:S(2)}) %collective-permute-start.48) | collective-permute-done | bytes 196640 | tf_op jit(solution)/shard_map/ppermute | solution.py:415
  429.9 2.8 collective-permute-done.49
  438.3 1.7 slice_bitcast_fusion
  440.0 2.5 copy.85
  442.6 11.4 %collective-permute-done.50.refs_1_ = bf16[400,1024]{1,0:T(8,128)(2,1)S(1)} collective-permute-done((bf16[400,1024]{1,0:T(8,128)(2,1)S(1)}, bf16[400,1024]{1,0:T(8,128)(2,1)S(1)}, u32[]{:S(2)}, u32[]{:S(2)}) %collective-permute-start.50) | collective-permute-done | bytes 819232 | tf_op jit(solution)/shard_map/ppermute | solution.py:411
  454.0 16.3 %collective-permute-done.51.refs_2_ = bf16[400,1024]{1,0:T(8,128)(2,1)S(1)} collective-permute-done((bf16[400,1024]{1,0:T(8,128)(2,1)S(1)}, bf16[400,1024]{1,0:T(8,128)(2,1)S(1)}, u32[]{:S(2)}, u32[]{:S(2)}) %collective-permute-start.51) | collective-permute-done | bytes 819232 | tf_op jit(solution)/shard_map/ppermute | solution.py:411
  471.7 4.2 lay_out.1
  (239 shorter events, 76.8 us)
Async XLA Ops:
  0.6 24.2 %copy-start = (bf16[1024,512]{1,0:T(8,128)(2,1)S(1)}, bf16[1024,512]{1,0:T(8,128)(2,1)}, u32[]{:S(2)}) copy-start(bf16[1024,512]{1,0:T(8,128)(2,1)} %param.19) | copy-start | bytes 3145732
  4.5 35.5 %collective-permute-start.3 = (bf16[3,1024,256]{2,1,0:T(8,128)(2,1)}, bf16[3,1024,256]{2,1,0:T(8,128)(2,1)}, u32[]{:S(2)}, u32[]{:S(2)}) collective-permute-start(bf16[3,1024,256]{2,1,0:T(8,128)(2,1)} %pad_maximum_fusion.1.refs_2_.refs_4_), channel_id=1, source_target_pairs={{0,1},{1,0},{2,3},{3,2},{4,5},{5,4},{6,7},{7,6},{8,9},{9,8},{10,11... | collective-permute-start | bytes 4718600 | tf_op jit(solution)/shard_map/ppermute | solution.py:407
  5.0 40.0 %collective-permute-start.5 = (bf16[3,1024,256]{2,1,0:T(8,128)(2,1)}, bf16[3,1024,256]{2,1,0:T(8,128)(2,1)}, u32[]{:S(2)}, u32[]{:S(2)}) collective-permute-start(bf16[3,1024,256]{2,1,0:T(8,128)(2,1)} %pad_maximum_fusion.1.refs_2_.refs_4_), channel_id=1, source_target_pairs={{0,8},{2,10},{4,12},{6,14},{8,16},{10,18},{12,20},{14,22},{16,24},... | collective-permute-start | bytes 4718600 | tf_op jit(solution)/shard_map/ppermute | solution.py:415
  10.2 4.0 collective-permute-start
  10.4 29.6 %collective-permute-start.4 = (bf16[512,1024]{1,0:T(8,128)(2,1)}, bf16[512,1024]{1,0:T(8,128)(2,1)}, u32[]{:S(2)}, u32[]{:S(2)}) collective-permute-start(bf16[512,1024]{1,0:T(8,128)(2,1)} %param.22), channel_id=1, source_target_pairs={{0,1},{1,0},{2,3},{3,2},{4,5},{5,4},{6,7},{7,6},{8,9},{9,8},{10,11... | collective-permute-start | bytes 3145736 | tf_op jit(solution)/shard_map/ppermute | solution.py:407
  14.5 8.3 %copy-start.12 = (bf16[512,1024]{1,0:T(8,128)(2,1)}, bf16[512,1024]{1,0:T(8,128)(2,1)S(1)}, u32[]{:S(2)}) copy-start(bf16[512,1024]{1,0:T(8,128)(2,1)S(1)} %maximum_select_fusion.1) | copy-start | bytes 3145732
  14.5 8.3 %copy-start.30 = (bf16[1024,256]{1,0:T(8,128)(2,1)S(1)}, bf16[1024,256]{1,0:T(8,128)(2,1)}, u32[]{:S(2)}) copy-start(bf16[1024,256]{1,0:T(8,128)(2,1)} %param.20) | copy-start | bytes 1572868
  14.5 8.3 %copy-start.37 = (f32[1024]{0:T(1024)S(1)}, f32[1024]{0:T(1024)}, u32[]{:S(2)}) copy-start(f32[1024]{0:T(1024)} %param.18) | copy-start | bytes 12292
  17.7 28.4 %collective-permute-start.1 = (bf16[512,1152]{1,0:T(8,128)(2,1)}, bf16[512,1152]{1,0:T(8,128)(2,1)}, u32[]{:S(2)}, u32[]{:S(2)}) collective-permute-start(bf16[512,1152]{1,0:T(8,128)(2,1)} %concatenate.73.refs_1_.refs_13_.refs_7_), channel_id=1, source_target_pairs={{0,2},{2,0},{4,6},{6,4},{8,10},{10,8},{12,14},{14,12},{16,18},{18,... | collective-permute-start | bytes 3538952 | tf_op jit(solution)/shard_map/ppermute | solution.py:411
  19.2 28.1 %collective-permute-start.2 = (bf16[512,1152]{1,0:T(8,128)(2,1)}, bf16[512,1152]{1,0:T(8,128)(2,1)}, u32[]{:S(2)}, u32[]{:S(2)}) collective-permute-start(bf16[512,1152]{1,0:T(8,128)(2,1)} %concatenate.73.refs_1_.refs_13_.refs_7_), channel_id=1, source_target_pairs={{0,4},{2,6},{4,0},{6,2},{8,12},{10,14},{12,8},{14,10},{16,20},{18,... | collective-permute-start | bytes 3538952 | tf_op jit(solution)/shard_map/ppermute | solution.py:411
  48.2 7.5 %collective-permute-start.6 = (bf16[512,512]{1,0:T(8,128)(2,1)}, bf16[512,512]{1,0:T(8,128)(2,1)}, u32[]{:S(2)}, u32[]{:S(2)}) collective-permute-start(bf16[512,512]{1,0:T(8,128)(2,1)} %constant_dynamic-slice_fusion.14), channel_id=1, source_target_pairs={{0,1},{1,0},{2,3},{3,2},{4,5},{5,4},{6,7},{7,6},{8,9},{9,8},{10,11... | collective-permute-start | bytes 1572872 | tf_op jit(solution)/shard_map/ppermute | solution.py:407
  48.2 22.6 %collective-permute-start.11 = (bf16[3,1024,256]{2,1,0:T(8,128)(2,1)}, bf16[3,1024,256]{2,1,0:T(8,128)(2,1)}, u32[]{:S(2)}, u32[]{:S(2)}) collective-permute-start(bf16[3,1024,256]{2,1,0:T(8,128)(2,1)} %collective-permute-done.5.refs_4_.refs_6_), channel_id=1, source_target_pairs={{0,1},{1,0},{2,3},{3,2},{4,5},{5,4},{6,7},{7,6},{8,9},{9,8},{10,11... | collective-permute-start | bytes 4718600 | tf_op jit(solution)/shard_map/ppermute | solution.py:407
  48.7 38.6 %collective-permute-start.12 = (bf16[3,1024,256]{2,1,0:T(8,128)(2,1)}, bf16[3,1024,256]{2,1,0:T(8,128)(2,1)}, u32[]{:S(2)}, u32[]{:S(2)}) collective-permute-start(bf16[3,1024,256]{2,1,0:T(8,128)(2,1)} %collective-permute-done.5.refs_4_.refs_6_), channel_id=1, source_target_pairs={{0,8},{2,10},{4,12},{6,14},{8,16},{10,18},{12,20},{14,22},{16,24},... | collective-permute-start | bytes 4718600 | tf_op jit(solution)/shard_map/ppermute | solution.py:415
  51.6 15.1 %collective-permute-start.7 = (bf16[256,1152]{1,0:T(8,128)(2,1)S(1)}, bf16[256,1152]{1,0:T(8,128)(2,1)}, u32[]{:S(2)}, u32[]{:S(2)}) collective-permute-start(bf16[256,1152]{1,0:T(8,128)(2,1)S(1)} %slice.125), channel_id=1, source_target_pairs={{0,4},{2,6},{4,0},{6,2},{8,12},{10,14},{12,8},{14,10},{16,20},{18,... | collective-permute-start | bytes 1769480 | tf_op jit(solution)/shard_map/ppermute | solution.py:411
  54.3 14.8 %collective-permute-start.8 = (bf16[256,1152]{1,0:T(8,128)(2,1)S(1)}, bf16[256,1152]{1,0:T(8,128)(2,1)}, u32[]{:S(2)}, u32[]{:S(2)}) collective-permute-start(bf16[256,1152]{1,0:T(8,128)(2,1)S(1)} %slice.126), channel_id=1, source_target_pairs={{0,2},{2,0},{4,6},{6,4},{8,10},{10,8},{12,14},{14,12},{16,18},{18,... | collective-permute-start | bytes 1769480 | tf_op jit(solution)/shard_map/ppermute | solution.py:411
  69.1 23.9 %collective-permute-start.10 = (bf16[512,1024]{1,0:T(8,128)(2,1)}, bf16[512,1024]{1,0:T(8,128)(2,1)}, u32[]{:S(2)}, u32[]{:S(2)}) collective-permute-start(bf16[512,1024]{1,0:T(8,128)(2,1)} %multiply_convert_fusion.1.refs_0_.refs_12_.refs_6_), channel_id=1, source_target_pairs={{0,4},{2,6},{4,0},{6,2},{8,12},{10,14},{12,8},{14,10},{16,20},{18,... | collective-permute-start | bytes 3145736 | tf_op jit(solution)/shard_map/ppermute | solution.py:411
  69.6 23.6 %collective-permute-start.9 = (bf16[512,1024]{1,0:T(8,128)(2,1)}, bf16[512,1024]{1,0:T(8,128)(2,1)}, u32[]{:S(2)}, u32[]{:S(2)}) collective-permute-start(bf16[512,1024]{1,0:T(8,128)(2,1)} %multiply_convert_fusion.1.refs_0_.refs_12_.refs_6_), channel_id=1, source_target_pairs={{0,2},{2,0},{4,6},{6,4},{8,10},{10,8},{12,14},{14,12},{16,18},{18,... | collective-permute-start | bytes 3145736 | tf_op jit(solution)/shard_map/ppermute | solution.py:411
  93.2 54.0 %collective-permute-start.16 = (bf16[3,1024,256]{2,1,0:T(8,128)(2,1)}, bf16[3,1024,256]{2,1,0:T(8,128)(2,1)}, u32[]{:S(2)}, u32[]{:S(2)}) collective-permute-start(bf16[3,1024,256]{2,1,0:T(8,128)(2,1)} %collective-permute-done.12.refs_4_.refs_2_), channel_id=1, source_target_pairs={{0,8},{2,10},{4,12},{6,14},{8,16},{10,18},{12,20},{14,22},{16,24},... | collective-permute-start | bytes 4718600 | tf_op jit(solution)/shard_map/ppermute | solution.py:415
  96.7 24.7 %collective-permute-start.13 = (bf16[256,1024]{1,0:T(8,128)(2,1)}, bf16[256,1024]{1,0:T(8,128)(2,1)S(1)}, u32[]{:S(2)}, u32[]{:S(2)}) collective-permute-start(bf16[256,1024]{1,0:T(8,128)(2,1)} %slice.127), channel_id=1, source_target_pairs={{0,4},{2,6},{4,0},{6,2},{8,12},{10,14},{12,8},{14,10},{16,20},{18,... | collective-permute-start | bytes 1572872 | tf_op jit(solution)/shard_map/ppermute | solution.py:411
  100.1 21.4 %collective-permute-start.14 = (bf16[256,1024]{1,0:T(8,128)(2,1)}, bf16[256,1024]{1,0:T(8,128)(2,1)}, u32[]{:S(2)}, u32[]{:S(2)}) collective-permute-start(bf16[256,1024]{1,0:T(8,128)(2,1)} %slice.128), channel_id=1, source_target_pairs={{0,2},{2,0},{4,6},{6,4},{8,10},{10,8},{12,14},{14,12},{16,18},{18,... | collective-permute-start | bytes 1572872 | tf_op jit(solution)/shard_map/ppermute | solution.py:411
  100.6 47.3 %collective-permute-start.15 = (bf16[3,1024,256]{2,1,0:T(8,128)(2,1)}, bf16[3,1024,256]{2,1,0:T(8,128)(2,1)}, u32[]{:S(2)}, u32[]{:S(2)}) collective-permute-start(bf16[3,1024,256]{2,1,0:T(8,128)(2,1)} %collective-permute-done.12.refs_4_.refs_2_), channel_id=1, source_target_pairs={{0,1},{1,0},{2,3},{3,2},{4,5},{5,4},{6,7},{7,6},{8,9},{9,8},{10,11... | collective-permute-start | bytes 4718600 | tf_op jit(solution)/shard_map/ppermute | solution.py:407
  146.7 4.0 collective-permute-start.18
  147.2 6.8 %collective-permute-start.17 = (bf16[3,1024,256]{2,1,0:T(8,128)(2,1)}, bf16[3,1024,256]{2,1,0:T(8,128)(2,1)}, u32[]{:S(2)}, u32[]{:S(2)}) collective-permute-start(bf16[3,1024,256]{2,1,0:T(8,128)(2,1)} %collective-permute-done.16.refs_6_.refs_4_), channel_id=1, source_target_pairs={{0,1},{1,0},{2,3},{3,2},{4,5},{5,4},{6,7},{7,6},{8,9},{9,8},{10,11... | collective-permute-start | bytes 4718600 | tf_op jit(solution)/shard_map/ppermute | solution.py:407
  215.7 39.4 %collective-permute-start.25 = (bf16[3,1024,256]{2,1,0:T(8,128)(2,1)}, bf16[3,1024,256]{2,1,0:T(8,128)(2,1)}, u32[]{:S(2)}, u32[]{:S(2)}) collective-permute-start(bf16[3,1024,256]{2,1,0:T(8,128)(2,1)} %get-tuple-element.212), channel_id=1, source_target_pairs={{0,1},{1,0},{2,3},{3,2},{4,5},{5,4},{6,7},{7,6},{8,9},{9,8},{10,11... | collective-permute-start | bytes 4718600 | tf_op jit(solution)/shard_map/ppermute | solution.py:407
  218.5 16.5 %collective-permute-start.21 = (bf16[256,1152]{1,0:T(8,128)(2,1)}, bf16[256,1152]{1,0:T(8,128)(2,1)}, u32[]{:S(2)}, u32[]{:S(2)}) collective-permute-start(bf16[256,1152]{1,0:T(8,128)(2,1)} %get-tuple-element.338), channel_id=1, source_target_pairs={{0,2},{2,0},{4,6},{6,4},{8,10},{10,8},{12,14},{14,12},{16,18},{18,... | collective-permute-start | bytes 1769480 | tf_op jit(solution)/shard_map/ppermute | solution.py:411
  219.9 29.9 %collective-permute-start.22 = (bf16[256,1152]{1,0:T(8,128)(2,1)}, bf16[256,1152]{1,0:T(8,128)(2,1)}, u32[]{:S(2)}, u32[]{:S(2)}) collective-permute-start(bf16[256,1152]{1,0:T(8,128)(2,1)} %get-tuple-element.337), channel_id=1, source_target_pairs={{0,4},{2,6},{4,0},{6,2},{8,12},{10,14},{12,8},{14,10},{16,20},{18,... | collective-permute-start | bytes 1769480 | tf_op jit(solution)/shard_map/ppermute | solution.py:411
  221.6 28.3 %collective-permute-start.19 = (bf16[256,1152]{1,0:T(8,128)(2,1)}, bf16[256,1152]{1,0:T(8,128)(2,1)}, u32[]{:S(2)}, u32[]{:S(2)}) collective-permute-start(bf16[256,1152]{1,0:T(8,128)(2,1)} %get-tuple-element.352), channel_id=1, source_target_pairs={{0,2},{2,0},{4,6},{6,4},{8,10},{10,8},{12,14},{14,12},{16,18},{18,... | collective-permute-start | bytes 1769480 | tf_op jit(solution)/shard_map/ppermute | solution.py:411
  222.1 27.8 %collective-permute-start.20 = (bf16[256,1152]{1,0:T(8,128)(2,1)}, bf16[256,1152]{1,0:T(8,128)(2,1)}, u32[]{:S(2)}, u32[]{:S(2)}) collective-permute-start(bf16[256,1152]{1,0:T(8,128)(2,1)} %get-tuple-element.351), channel_id=1, source_target_pairs={{0,4},{2,6},{4,0},{6,2},{8,12},{10,14},{12,8},{14,10},{16,20},{18,... | collective-permute-start | bytes 1769480 | tf_op jit(solution)/shard_map/ppermute | solution.py:411
  234.9 37.2 %collective-permute-start.26 = (bf16[3,1024,256]{2,1,0:T(8,128)(2,1)}, bf16[3,1024,256]{2,1,0:T(8,128)(2,1)}, u32[]{:S(2)}, u32[]{:S(2)}) collective-permute-start(bf16[3,1024,256]{2,1,0:T(8,128)(2,1)} %convert_add_fusion.3), channel_id=1, source_target_pairs={{0,8},{2,10},{4,12},{6,14},{8,16},{10,18},{12,20},{14,22},{16,24},... | collective-permute-start | bytes 4718600 | tf_op jit(solution)/shard_map/ppermute | solution.py:415
  249.8 26.7 %collective-permute-start.28 = (bf16[3,1024,256]{2,1,0:T(8,128)(2,1)S(1)}, bf16[3,1024,256]{2,1,0:T(8,128)(2,1)S(1)}, u32[]{:S(2)}, u32[]{:S(2)}) collective-permute-start(bf16[3,1024,256]{2,1,0:T(8,128)(2,1)S(1)} %copy-done.39), channel_id=1, source_target_pairs={{0,1},{1,0},{2,3},{3,2},{4,5},{5,4},{6,7},{7,6},{8,9},{9,8},{10,11... | collective-permute-start | bytes 4718600 | tf_op jit(solution)/shard_map/ppermute | solution.py:407
  251.9 16.2 %collective-permute-start.23 = (bf16[256,1152]{1,0:T(8,128)(2,1)S(1)}, bf16[256,1152]{1,0:T(8,128)(2,1)S(1)}, u32[]{:S(2)}, u32[]{:S(2)}) collective-permute-start(bf16[256,1152]{1,0:T(8,128)(2,1)S(1)} %get-tuple-element.336), channel_id=1, source_target_pairs={{0,2},{2,0},{4,6},{6,4},{8,10},{10,8},{12,14},{14,12},{16,18},{18,... | collective-permute-start | bytes 1769480 | tf_op jit(solution)/shard_map/ppermute | solution.py:411
  253.5 15.4 %collective-permute-start.24 = (bf16[256,1152]{1,0:T(8,128)(2,1)S(1)}, bf16[256,1152]{1,0:T(8,128)(2,1)S(1)}, u32[]{:S(2)}, u32[]{:S(2)}) collective-permute-start(bf16[256,1152]{1,0:T(8,128)(2,1)S(1)} %get-tuple-element.335), channel_id=1, source_target_pairs={{0,4},{2,6},{4,0},{6,2},{8,12},{10,14},{12,8},{14,10},{16,20},{18,... | collective-permute-start | bytes 1769480 | tf_op jit(solution)/shard_map/ppermute | solution.py:411
  255.1 36.2 %collective-permute-start.29 = (bf16[256,1024]{1,0:T(8,128)(2,1)}, bf16[256,1024]{1,0:T(8,128)(2,1)}, u32[]{:S(2)}, u32[]{:S(2)}) collective-permute-start(bf16[256,1024]{1,0:T(8,128)(2,1)} %get-tuple-element.362), channel_id=1, source_target_pairs={{0,2},{2,0},{4,6},{6,4},{8,10},{10,8},{12,14},{14,12},{16,18},{18,... | collective-permute-start | bytes 1572872 | tf_op jit(solution)/shard_map/ppermute | solution.py:411
  255.6 16.5 %copy-start.25 = (bf16[512,1152]{1,0:T(8,128)(2,1)S(1)}, bf16[512,1152]{1,0:T(8,128)(2,1)}, u32[]{:S(2)}) copy-start(bf16[512,1152]{1,0:T(8,128)(2,1)} %get-tuple-element.200) | copy-start | bytes 3538948
  268.1 23.1 %collective-permute-start.30 = (bf16[256,1024]{1,0:T(8,128)(2,1)}, bf16[256,1024]{1,0:T(8,128)(2,1)}, u32[]{:S(2)}, u32[]{:S(2)}) collective-permute-start(bf16[256,1024]{1,0:T(8,128)(2,1)} %get-tuple-element.361), channel_id=1, source_target_pairs={{0,4},{2,6},{4,0},{6,2},{8,12},{10,14},{12,8},{14,10},{16,20},{18,... | collective-permute-start | bytes 1572872 | tf_op jit(solution)/shard_map/ppermute | solution.py:411
  268.9 56.4 %collective-permute-start.31 = (bf16[256,1024]{1,0:T(8,128)(2,1)}, bf16[256,1024]{1,0:T(8,128)(2,1)}, u32[]{:S(2)}, u32[]{:S(2)}) collective-permute-start(bf16[256,1024]{1,0:T(8,128)(2,1)} %get-tuple-element.348), channel_id=1, source_target_pairs={{0,2},{2,0},{4,6},{6,4},{8,10},{10,8},{12,14},{14,12},{16,18},{18,... | collective-permute-start | bytes 1572872 | tf_op jit(solution)/shard_map/ppermute | solution.py:411
  274.5 9.3 %collective-permute-start.36 = (f32[512]{0:T(512)S(1)}, f32[512]{0:T(512)S(1)}, u32[]{:S(2)}, u32[]{:S(2)}) collective-permute-start(f32[512]{0:T(512)S(1)} %dynamic_slice.92), channel_id=1, source_target_pairs={{0,1},{1,0},{2,3},{3,2},{4,5},{5,4},{6,7},{7,6},{8,9},{9,8},{10,11... | collective-permute-start | bytes 6152 | tf_op jit(solution)/shard_map/ppermute | solution.py:407
  276.5 10.9 %collective-permute-start.27 = (bf16[512,1024]{1,0:T(8,128)(2,1)}, bf16[512,1024]{1,0:T(8,128)(2,1)}, u32[]{:S(2)}, u32[]{:S(2)}) collective-permute-start(bf16[512,1024]{1,0:T(8,128)(2,1)} %add_convert_fusion.2), channel_id=1, source_target_pairs={{0,1},{1,0},{2,3},{3,2},{4,5},{5,4},{6,7},{7,6},{8,9},{9,8},{10,11... | collective-permute-start | bytes 3145736 | tf_op jit(solution)/shard_map/ppermute | solution.py:407
  283.8 2.1 collective-permute-start.40
  285.8 39.5 %collective-permute-start.32 = (bf16[256,1024]{1,0:T(8,128)(2,1)}, bf16[256,1024]{1,0:T(8,128)(2,1)}, u32[]{:S(2)}, u32[]{:S(2)}) collective-permute-start(bf16[256,1024]{1,0:T(8,128)(2,1)} %get-tuple-element.347), channel_id=1, source_target_pairs={{0,4},{2,6},{4,0},{6,2},{8,12},{10,14},{12,8},{14,10},{16,20},{18,... | collective-permute-start | bytes 1572872 | tf_op jit(solution)/shard_map/ppermute | solution.py:411
  287.4 38.5 %collective-permute-start.35 = (bf16[3,1024,256]{2,1,0:T(8,128)(2,1)}, bf16[3,1024,256]{2,1,0:T(8,128)(2,1)}, u32[]{:S(2)}, u32[]{:S(2)}) collective-permute-start(bf16[3,1024,256]{2,1,0:T(8,128)(2,1)} %add_convert_fusion.1), channel_id=1, source_target_pairs={{0,8},{2,10},{4,12},{6,14},{8,16},{10,18},{12,20},{14,22},{16,24},... | collective-permute-start | bytes 4718600 | tf_op jit(solution)/shard_map/ppermute | solution.py:415
  294.6 31.3 %collective-permute-start.33 = (bf16[256,1024]{1,0:T(8,128)(2,1)}, bf16[256,1024]{1,0:T(8,128)(2,1)}, u32[]{:S(2)}, u32[]{:S(2)}) collective-permute-start(bf16[256,1024]{1,0:T(8,128)(2,1)} %get-tuple-element.346), channel_id=1, source_target_pairs={{0,2},{2,0},{4,6},{6,4},{8,10},{10,8},{12,14},{14,12},{16,18},{18,... | collective-permute-start | bytes 1572872 | tf_op jit(solution)/shard_map/ppermute | solution.py:411
  295.7 30.2 %collective-permute-start.34 = (bf16[256,1024]{1,0:T(8,128)(2,1)}, bf16[256,1024]{1,0:T(8,128)(2,1)}, u32[]{:S(2)}, u32[]{:S(2)}) collective-permute-start(bf16[256,1024]{1,0:T(8,128)(2,1)} %get-tuple-element.345), channel_id=1, source_target_pairs={{0,4},{2,6},{4,0},{6,2},{8,12},{10,14},{12,8},{14,10},{16,20},{18,... | collective-permute-start | bytes 1572872 | tf_op jit(solution)/shard_map/ppermute | solution.py:411
  298.6 19.8 %copy-start.9 = (bf16[1024,1024]{1,0:T(8,128)(2,1)S(1)}, bf16[1024,1024]{1,0:T(8,128)(2,1)}, u32[]{:S(2)}) copy-start(bf16[1024,1024]{1,0:T(8,128)(2,1)} %param.14) | copy-start | bytes 6291460
  332.0 25.8 %collective-permute-start.39 = (f32[1024]{0:T(1024)S(1)}, f32[1024]{0:T(1024)S(1)}, u32[]{:S(2)}, u32[]{:S(2)}) collective-permute-start(f32[1024]{0:T(1024)S(1)} %get-tuple-element.339), channel_id=1, source_target_pairs={{0,1},{1,0},{2,3},{3,2},{4,5},{5,4},{6,7},{7,6},{8,9},{9,8},{10,11... | collective-permute-start | bytes 12296 | tf_op jit(solution)/shard_map/ppermute | solution.py:407
  333.2 42.9 %collective-permute-start.38 = (bf16[1024,512]{1,0:T(8,128)(2,1)}, bf16[1024,512]{1,0:T(8,128)(2,1)}, u32[]{:S(2)}, u32[]{:S(2)}) collective-permute-start(bf16[1024,512]{1,0:T(8,128)(2,1)} %dynamic-slice_convert_fusion), channel_id=1, source_target_pairs={{0,1},{1,0},{2,3},{3,2},{4,5},{5,4},{6,7},{7,6},{8,9},{9,8},{10,11... | collective-permute-start | bytes 3145736 | tf_op jit(solution)/shard_map/ppermute | solution.py:407
  335.0 22.8 %collective-permute-start.41 = (bf16[384,1024]{1,0:T(8,128)(2,1)}, bf16[384,1024]{1,0:T(8,128)(2,1)}, u32[]{:S(2)}, u32[]{:S(2)}) collective-permute-start(bf16[384,1024]{1,0:T(8,128)(2,1)} %pad_maximum_fusion.3), channel_id=1, source_target_pairs={{0,2},{2,0},{4,6},{6,4},{8,10},{10,8},{12,14},{14,12},{16,18},{18,... | collective-permute-start | bytes 2359304 | tf_op jit(solution)/shard_map/ppermute | solution.py:411
  337.4 36.5 %collective-permute-start.42 = (bf16[384,1024]{1,0:T(8,128)(2,1)}, bf16[384,1024]{1,0:T(8,128)(2,1)}, u32[]{:S(2)}, u32[]{:S(2)}) collective-permute-start(bf16[384,1024]{1,0:T(8,128)(2,1)} %pad_maximum_fusion.4), channel_id=1, source_target_pairs={{0,4},{2,6},{4,0},{6,2},{8,12},{10,14},{12,8},{14,10},{16,20},{18,... | collective-permute-start | bytes 2359304 | tf_op jit(solution)/shard_map/ppermute | solution.py:411
  339.9 34.0 %collective-permute-start.43 = (bf16[384,1024]{1,0:T(8,128)(2,1)}, bf16[384,1024]{1,0:T(8,128)(2,1)}, u32[]{:S(2)}, u32[]{:S(2)}) collective-permute-start(bf16[384,1024]{1,0:T(8,128)(2,1)} %pad_maximum_fusion.5), channel_id=1, source_target_pairs={{0,6},{2,4},{4,2},{6,0},{8,14},{10,12},{12,10},{14,8},{16,22},{18,... | collective-permute-start | bytes 2359304 | tf_op jit(solution)/shard_map/ppermute | solution.py:411
  357.7 18.4 %copy-start.16 = (bf16[1024,1024]{1,0:T(8,128)(2,1)S(1)}, bf16[1024,1024]{1,0:T(8,128)(2,1)}, u32[]{:S(2)}) copy-start(bf16[1024,1024]{1,0:T(8,128)(2,1)} %copy-done.14) | copy-start | bytes 6291460
  357.7 80.0 %collective-permute-start.53 = (bf16[3,1024,256]{2,1,0:T(8,128)(2,1)}, bf16[3,1024,256]{2,1,0:T(8,128)(2,1)S(1)}, u32[]{:S(2)}, u32[]{:S(2)}) collective-permute-start(bf16[3,1024,256]{2,1,0:T(8,128)(2,1)} %get-tuple-element.271), channel_id=1, source_target_pairs={{0,1},{1,0},{2,3},{3,2},{4,5},{5,4},{6,7},{7,6},{8,9},{9,8},{10,11... | collective-permute-start | bytes 4718600 | tf_op jit(solution)/shard_map/ppermute | solution.py:407
  357.8 79.9 %collective-permute-start.54 = (bf16[3,1024,256]{2,1,0:T(8,128)(2,1)}, bf16[3,1024,256]{2,1,0:T(8,128)(2,1)S(1)}, u32[]{:S(2)}, u32[]{:S(2)}) collective-permute-start(bf16[3,1024,256]{2,1,0:T(8,128)(2,1)} %add_convert_fusion), channel_id=1, source_target_pairs={{0,8},{2,10},{4,12},{6,14},{8,16},{10,18},{12,20},{14,22},{16,24},... | collective-permute-start | bytes 4718600 | tf_op jit(solution)/shard_map/ppermute | solution.py:415
  380.9 21.5 %collective-permute-start.44 = (bf16[112,1024]{1,0:T(8,128)(2,1)S(1)}, bf16[112,1024]{1,0:T(8,128)(2,1)S(1)}, u32[]{:S(2)}, u32[]{:S(2)}) collective-permute-start(bf16[112,1024]{1,0:T(8,128)(2,1)S(1)} %get-tuple-element.371), channel_id=1, source_target_pairs={{0,8},{2,10},{4,12},{6,14},{8,16},{10,18},{12,20},{14,22},{16,24},... | collective-permute-start | bytes 688136 | tf_op jit(solution)/shard_map/ppermute | solution.py:415
  380.9 30.8 %collective-permute-start.45 = (bf16[112,1024]{1,0:T(8,128)(2,1)S(1)}, bf16[112,1024]{1,0:T(8,128)(2,1)S(1)}, u32[]{:S(2)}, u32[]{:S(2)}) collective-permute-start(bf16[112,1024]{1,0:T(8,128)(2,1)S(1)} %get-tuple-element.372), channel_id=1, source_target_pairs={{0,16},{2,18},{4,20},{6,22},{8,24},{10,26},{12,28},{14,30},{16,0},... | collective-permute-start | bytes 688136 | tf_op jit(solution)/shard_map/ppermute | solution.py:415
  383.8 28.0 %collective-permute-start.46 = (bf16[112,1024]{1,0:T(8,128)(2,1)S(1)}, bf16[112,1024]{1,0:T(8,128)(2,1)S(1)}, u32[]{:S(2)}, u32[]{:S(2)}) collective-permute-start(bf16[112,1024]{1,0:T(8,128)(2,1)S(1)} %get-tuple-element.373), channel_id=1, source_target_pairs={{0,24},{2,26},{4,28},{6,30},{8,0},{10,2},{12,4},{14,6},{16,8},{18,... | collective-permute-start | bytes 688136 | tf_op jit(solution)/shard_map/ppermute | solution.py:415
  411.9 17.9 %copy-start.29 = (bf16[112,1024]{1,0:T(8,128)(2,1)}, bf16[112,1024]{1,0:T(8,128)(2,1)S(1)}, u32[]{:S(2)}) copy-start(bf16[112,1024]{1,0:T(8,128)(2,1)S(1)} %add_convert_fusion.8) | copy-start | bytes 688132
  412.1 10.7 %collective-permute-start.47 = (bf16[96,1024]{1,0:T(8,128)(2,1)S(1)}, bf16[96,1024]{1,0:T(8,128)(2,1)S(1)}, u32[]{:S(2)}, u32[]{:S(2)}) collective-permute-start(bf16[96,1024]{1,0:T(8,128)(2,1)S(1)} %get-tuple-element.369), channel_id=1, source_target_pairs={{0,8},{2,10},{4,12},{6,14},{8,16},{10,18},{12,20},{14,22},{16,24},... | collective-permute-start | bytes 589832 | tf_op jit(solution)/shard_map/ppermute | solution.py:415
  417.6 18.0 %collective-permute-start.37 = (bf16[512,512]{1,0:T(8,128)(2,1)S(1)}, bf16[512,512]{1,0:T(8,128)(2,1)S(1)}, u32[]{:S(2)}, u32[]{:S(2)}) collective-permute-start(bf16[512,512]{1,0:T(8,128)(2,1)S(1)} %get-tuple-element.358), channel_id=1, source_target_pairs={{0,1},{1,0},{2,3},{3,2},{4,5},{5,4},{6,7},{7,6},{8,9},{9,8},{10,11... | collective-permute-start | bytes 1572872 | tf_op jit(solution)/shard_map/ppermute | solution.py:407
  417.7 12.1 %collective-permute-start.48 = (bf16[96,1024]{1,0:T(8,128)(2,1)S(1)}, bf16[96,1024]{1,0:T(8,128)(2,1)S(1)}, u32[]{:S(2)}, u32[]{:S(2)}) collective-permute-start(bf16[96,1024]{1,0:T(8,128)(2,1)S(1)} %get-tuple-element.369), channel_id=1, source_target_pairs={{0,16},{2,18},{4,20},{6,22},{8,24},{10,26},{12,28},{14,30},{16,0},... | collective-permute-start | bytes 589832 | tf_op jit(solution)/shard_map/ppermute | solution.py:415
  422.8 9.9 %collective-permute-start.49 = (bf16[96,1024]{1,0:T(8,128)(2,1)S(1)}, bf16[96,1024]{1,0:T(8,128)(2,1)S(1)}, u32[]{:S(2)}, u32[]{:S(2)}) collective-permute-start(bf16[96,1024]{1,0:T(8,128)(2,1)S(1)} %get-tuple-element.369), channel_id=1, source_target_pairs={{0,24},{2,26},{4,28},{6,30},{8,0},{10,2},{12,4},{14,6},{16,8},{18,... | collective-permute-start | bytes 589832 | tf_op jit(solution)/shard_map/ppermute | solution.py:415
  429.8 7.9 %copy-start.23 = (bf16[3,1024,256]{2,1,0:T(8,128)(2,1)S(1)}, bf16[3,1024,256]{2,1,0:T(8,128)(2,1)}, u32[]{:S(2)}) copy-start(bf16[3,1024,256]{2,1,0:T(8,128)(2,1)} %get-tuple-element.270) | copy-start | bytes 4718596
  432.8 21.2 %collective-permute-start.50 = (bf16[400,1024]{1,0:T(8,128)(2,1)S(1)}, bf16[400,1024]{1,0:T(8,128)(2,1)S(1)}, u32[]{:S(2)}, u32[]{:S(2)}) collective-permute-start(bf16[400,1024]{1,0:T(8,128)(2,1)S(1)} %pad_maximum_fusion.2.refs_0_), channel_id=1, source_target_pairs={{0,2},{2,0},{4,6},{6,4},{8,10},{10,8},{12,14},{14,12},{16,18},{18,... | collective-permute-start | bytes 2457608 | tf_op jit(solution)/shard_map/ppermute | solution.py:411
  434.1 36.3 %collective-permute-start.51 = (bf16[400,1024]{1,0:T(8,128)(2,1)S(1)}, bf16[400,1024]{1,0:T(8,128)(2,1)S(1)}, u32[]{:S(2)}, u32[]{:S(2)}) collective-permute-start(bf16[400,1024]{1,0:T(8,128)(2,1)S(1)} %pad_maximum_fusion.2.refs_0_), channel_id=1, source_target_pairs={{0,4},{2,6},{4,0},{6,2},{8,12},{10,14},{12,8},{14,10},{16,20},{18,... | collective-permute-start | bytes 2457608 | tf_op jit(solution)/shard_map/ppermute | solution.py:411
  435.6 34.7 %collective-permute-start.52 = (bf16[400,1024]{1,0:T(8,128)(2,1)S(1)}, bf16[400,1024]{1,0:T(8,128)(2,1)}, u32[]{:S(2)}, u32[]{:S(2)}) collective-permute-start(bf16[400,1024]{1,0:T(8,128)(2,1)S(1)} %pad_maximum_fusion.2.refs_0_), channel_id=1, source_target_pairs={{0,6},{2,4},{4,2},{6,0},{8,14},{10,12},{12,10},{14,8},{16,22},{18,... | collective-permute-start | bytes 2457608 | tf_op jit(solution)/shard_map/ppermute | solution.py:411
  (31 other events, 101.7 us)

commit v3 on v2

v3 whole, which is shorter than its diff:
```python
import functools

import jax
import jax.numpy as jnp
from jax import lax
from jax.experimental import pallas as pl
from jax.experimental.pallas import tpu as pltpu
from jax.sharding import PartitionSpec as P

HEAD_SIZE = 64
EPS = 1e-06
THETA = 10000.0
NEG = -1e30
PLANE = 4
LANES = 128
F32 = jnp.float32
BF16 = jnp.bfloat16
NT = (((1,), (1,)), ((), ()))
TN = (((0,), (0,)), ((), ()))


def dot(a, b):
    return jnp.dot(a, b, preferred_element_type=F32)


def dot_nt(a, b):
    return lax.dot_general(a, b, NT, preferred_element_type=F32)


def dot_tn(a, b):
    return lax.dot_general(a, b, TN, preferred_element_type=F32)


def attn_mask(start, row_start, block, keys):
    first = start[:, row_start : row_start + block]
    first = jnp.concatenate([first, first], axis=1)
    key_at = lax.broadcasted_iota(jnp.int32, (keys, 2 * block), 0)
    lane = lax.broadcasted_iota(jnp.int32, (1, 2 * block), 1)
    row_at = row_start + jnp.where(lane >= block, lane - block, lane)
    return (key_at >= first) & (key_at <= row_at)


def rope(x, c, s):
    half = x.shape[0] // 2
    a, b = x[:half], x[half:]
    return jnp.concatenate([a * c - b * s, b * c + a * s], axis=0)


def attn_fwd_kernel(block, q_ref, k_ref, v_ref, cos_ref, sin_ref, start_ref, qo_ref, ko_ref, o_ref, lse_ref):
    hd = HEAD_SIZE
    n = k_ref.shape[1]
    c, s = cos_ref[...], sin_ref[...]
    k_rot = rope(k_ref[...], c, s)
    ko_ref[...] = k_rot.astype(BF16)
    keys = k_rot.T.astype(BF16)
    q0 = rope(q_ref[0:hd], c, s).astype(BF16)
    q1 = rope(q_ref[hd : 2 * hd], c, s).astype(BF16)
    qo_ref[0:hd] = q0
    qo_ref[hd : 2 * hd] = q1
    start = start_ref[...]
    for r0 in range(0, n, block):
        cn = r0 + block
        qb = jnp.concatenate([q0[:, r0:cn], q1[:, r0:cn]], axis=1) * jnp.asarray(hd**-0.5, BF16)
        scores = dot(keys[:cn], qb)
        scores = jnp.where(attn_mask(start, r0, block, cn), scores, NEG)
        peak = jnp.max(scores, axis=0, keepdims=True)
        p = jnp.exp(scores - peak)
        total = jnp.sum(p, axis=0, keepdims=True)
        o = dot(v_ref[:, :cn], p.astype(BF16)) / total
        o_ref[0:hd, r0:cn] = o[:, :block].astype(BF16)
        o_ref[hd : 2 * hd, r0:cn] = o[:, block:].astype(BF16)
        lse = peak + jnp.log(total)
        lse_ref[0, 0:1, r0:cn] = lse[:, :block]
        lse_ref[0, 1:2, r0:cn] = lse[:, block:]


def attn_bwd_kernel(
    block, q_ref, k_ref, v_ref, do_ref, lse_ref, cos_ref, sin_ref, start_ref, dq_ref, dk_ref, dv_ref, dk_acc, dv_acc
):
    hd = HEAD_SIZE
    n = k_ref.shape[1]
    c, s = cos_ref[...], sin_ref[...]
    keys = k_ref[...].astype(F32).T.astype(BF16)
    vals = v_ref[...].astype(F32).T.astype(BF16)
    start = start_ref[...]
    dk_acc[...] = jnp.zeros_like(dk_acc)
    dv_acc[...] = jnp.zeros_like(dv_acc)
    scale = hd**-0.5
    for r0 in range(0, n, block):
        cn = r0 + block
        qb = jnp.concatenate([q_ref[0:hd, r0:cn], q_ref[hd : 2 * hd, r0:cn]], axis=1)
        gb = jnp.concatenate([do_ref[0:hd, r0:cn], do_ref[hd : 2 * hd, r0:cn]], axis=1)
        lse = jnp.concatenate([lse_ref[0, 0:1, r0:cn], lse_ref[0, 1:2, r0:cn]], axis=1)
        scores = dot(keys[:cn], qb * jnp.asarray(scale, BF16))
        p = jnp.exp(jnp.where(attn_mask(start, r0, block, cn), scores, NEG) - lse)
        dv_acc[:, :cn] += dot_nt(gb, p.astype(BF16))
        dp = dot(vals[:cn], gb)
        delta = jnp.sum(p * dp, axis=0, keepdims=True)
        ds = (p * (dp - delta) * scale).astype(BF16)
        dq = dot(k_ref[:, :cn], ds)
        dk_acc[:, :cn] += dot_nt(qb, ds)
        cb, sb = c[:, r0:cn], -s[:, r0:cn]
        dq_ref[0:hd, r0:cn] = rope(dq[:, :block], cb, sb).astype(BF16)
        dq_ref[hd : 2 * hd, r0:cn] = rope(dq[:, block:], cb, sb).astype(BF16)
    dk_ref[...] = rope(dk_acc[...], c, -s).astype(BF16)
    dv_ref[...] = dv_acc[...].astype(BF16)


def attn_cost(heads, n, products):
    return pl.CostEstimate(
        flops=products * heads * n * n * HEAD_SIZE * 2, bytes_accessed=8 * heads * n * HEAD_SIZE, transcendentals=heads * n * n
    )


def attn_forward(q_t, k_t, v_t, cos_t, sin_t, start):
    n = q_t.shape[1]
    hd = HEAD_SIZE
    kv = k_t.shape[0] // hd
    block = min(256, n)
    pair = pl.BlockSpec((2 * hd, n), lambda h: (h, 0))
    one = pl.BlockSpec((hd, n), lambda h: (h, 0))
    table = pl.BlockSpec((hd // 2, n), lambda h: (0, 0))
    return pl.pallas_call(
        functools.partial(attn_fwd_kernel, block),
        grid=(kv,),
        in_specs=[pair, one, one, table, table, pl.BlockSpec((1, n), lambda h: (0, 0))],
        out_specs=[pair, one, pair, pl.BlockSpec((1, 2, n), lambda h: (h, 0, 0))],
        out_shape=[
            jax.ShapeDtypeStruct(q_t.shape, BF16),
            jax.ShapeDtypeStruct(k_t.shape, BF16),
            jax.ShapeDtypeStruct(q_t.shape, BF16),
            jax.ShapeDtypeStruct((kv, 2, n), F32),
        ],
        compiler_params=pltpu.CompilerParams(vmem_limit_bytes=48 * 2**20),
        cost_estimate=attn_cost(2 * kv, n, 4),
        name="attn_forward",
    )(q_t, k_t, v_t, cos_t, sin_t, start)


def attn_backward(q_t, k_t, v_t, do_t, lse, cos_t, sin_t, start, first, count):
    n = q_t.shape[1]
    hd = HEAD_SIZE
    block = min(256, n)
    pair = pl.BlockSpec((2 * hd, n), lambda h: (h + first, 0))
    one = pl.BlockSpec((hd, n), lambda h: (h + first, 0))
    table = pl.BlockSpec((hd // 2, n), lambda h: (0, 0))
    return pl.pallas_call(
        functools.partial(attn_bwd_kernel, block),
        grid=(count,),
        in_specs=[
            pair,
            one,
            one,
            pair,
            pl.BlockSpec((1, 2, n), lambda h: (h + first, 0, 0)),
            table,
            table,
            pl.BlockSpec((1, n), lambda h: (0, 0)),
        ],
        out_specs=[pl.BlockSpec((r * hd, n), lambda h: (h, 0)) for r in (2, 1, 1)],
        out_shape=[jax.ShapeDtypeStruct((r * count * hd, n), BF16) for r in (2, 1, 1)],
        scratch_shapes=[pltpu.VMEM((hd, n), F32), pltpu.VMEM((hd, n), F32)],
        compiler_params=pltpu.CompilerParams(vmem_limit_bytes=48 * 2**20),
        cost_estimate=attn_cost(2 * count, n, 4),
        name="attn_backward",
    )(q_t, k_t, v_t, do_t, lse, cos_t, sin_t, start)


def data_kernel(first, last, blocks, tiles, slots, pieces, expert_ref, *refs):
    refs = list(refs)
    at, tile_at = pl.program_id(0), pl.program_id(1)
    x, g_all = refs[0][...], refs[blocks][...]
    for i in range(1, blocks):
        x = jnp.where(at == i, refs[i][...], x)
        g_all = jnp.where(at == i, refs[blocks + i][...], g_all)
    weights = refs[2 * blocks : 2 * blocks + slots * pieces]
    refs = refs[2 * blocks + slots * pieces :]
    if not first:
        out_in, dx_in, dgate_in = refs[:3]
        refs = refs[3:]
    if last:
        out_refs, dx_refs = refs[:blocks], refs[blocks : 2 * blocks]
        refs = refs[2 * blocks :]
    else:
        out_ref, dx_ref, dgate_ref = refs[:3]
        refs = refs[3:]
    hs, acts = refs[:slots], refs[slots : 2 * slots]
    acc_o, acc_x, held, sems = refs[2 * slots :]
    opening = (at == 0) & (tile_at == 0)

    def copies(n):
        return [pltpu.make_async_copy(weights[n].at[c], held.at[n, c], sems.at[n, c]) for c in range(3)]

    @pl.when(opening)
    def _():
        for n in range(slots * pieces):
            for copy in copies(n):
                copy.start()

    width = x.shape[1]
    g = g_all[:, :width]
    gates = g_all[:, width:].astype(F32)
    lane = lax.broadcasted_iota(jnp.int32, gates.shape, 1)
    dgate = None if first else dgate_in[...]
    for j in range(slots):
        here = lane == expert_ref[j]
        both = here | (lane == expert_ref[j] + LANES // 2)
        gate = jnp.sum(jnp.where(both, gates, 0.0), axis=1, keepdims=True)
        row_sum = None
        for i in range(pieces):
            n = j * pieces + i

            @pl.when(opening)
            def _():
                for copy in copies(n):
                    copy.wait()

            hid = held.shape[3]
            gate_pre = dot(x, held[n, 0])
            up_pre = dot(x, held[n, 1])
            d_hidden = dot(g, held[n, 2])
            sig = jax.nn.sigmoid(gate_pre)
            silu = gate_pre * sig
            act = silu * up_pre
            part = jnp.sum(act * d_hidden, axis=1, keepdims=True)
            row_sum = part if row_sum is None else row_sum + part
            act_w = (act * gate).astype(BF16)
            d_hidden = d_hidden * gate
            d_up = (d_hidden * silu).astype(BF16)
            d_gate = (d_hidden * up_pre * (sig + silu * (1.0 - sig))).astype(BF16)
            hs[j][:, 2 * i * hid : (2 * i + 1) * hid] = d_gate
            hs[j][:, (2 * i + 1) * hid : (2 * i + 2) * hid] = d_up
            acts[j][:, i * hid : (i + 1) * hid] = act_w
            out_term = dot_nt(act_w, held[n, 2])
            dx_term = dot_nt(d_gate, held[n, 0]) + dot_nt(d_up, held[n, 1])
            if n == 0 and first:
                acc_o[...] = out_term
                acc_x[...] = dx_term
            elif n == 0:
                acc_o[...] = out_in[...].astype(F32) + out_term
                acc_x[...] = dx_in[...].astype(F32) + dx_term
            else:
                acc_o[...] += out_term
                acc_x[...] += dx_term
        term = jnp.where(here, row_sum, 0.0)
        dgate = term if dgate is None else dgate + term
    if last:
        high = dgate.astype(BF16).astype(F32)
        low = pltpu.roll(dgate - high, LANES // 2, 1)
        tail = jnp.where(lane < LANES // 2, high, low).astype(BF16)
        for i in range(blocks):

            @pl.when(at == i)
            def _():
                out_refs[i][...] = acc_o[...].astype(BF16)
                dx_refs[i][:, :width] = acc_x[...].astype(BF16)
                dx_refs[i][:, width:] = tail
    else:
        out_ref[...] = acc_o[...].astype(BF16)
        dx_ref[...] = acc_x[...].astype(BF16)
        dgate_ref[...] = dgate


def expert_data(experts, xs, gs, rows, ws, carry, last):
    blocks = len(xs)
    width = xs[0][0].shape[1]
    tile = min(256, rows)
    tiles = rows // tile
    full = gs[0][0].shape[1]
    slots = experts.shape[0]
    pieces = len(ws) // slots
    hidden = ws[0].shape[2]
    first = carry is None
    total = blocks * rows

    def out_spec(columns):
        return pl.BlockSpec((tile, columns), lambda b, i: (b * tiles + i, 0))

    def in_spec(columns, offset):
        return pl.BlockSpec((tile, columns), lambda b, i: (offset * tiles + i, 0))

    def own_spec(columns, j):
        return pl.BlockSpec((tile, columns), lambda b, i: (jnp.clip((b - j) * tiles + i, 0, tiles - 1), 0))

    ins = [experts, *[x for x, _ in xs], *[g for g, _ in gs], *ws]
    specs = [pl.BlockSpec(memory_space=pltpu.SMEM)]
    specs += [in_spec(width, o) for _, o in xs] + [in_spec(full, o) for _, o in gs]
    specs += [pl.BlockSpec(memory_space=pl.ANY)] * len(ws)
    if not first:
        ins += list(carry)
        specs += [out_spec(width), out_spec(width), out_spec(LANES)]
    if last:
        out_specs = [own_spec(c, j) for c in (width, full) for j in range(blocks)]
        out_shape = [jax.ShapeDtypeStruct((rows, c), BF16) for c in (width, full) for _ in range(blocks)]
    else:
        out_specs = [out_spec(c) for c in (width, width, LANES)]
        out_shape = [jax.ShapeDtypeStruct((total, c), t) for c, t in ((width, BF16), (width, BF16), (LANES, F32))]
    n = len(out_specs)
    kept = [2 * pieces * hidden] * slots + [pieces * hidden] * slots
    single = pieces * hidden
    outs = pl.pallas_call(
        functools.partial(data_kernel, first, last, blocks, tiles, slots, pieces),
        grid=(blocks, tiles),
        in_specs=specs,
        out_specs=out_specs + [out_spec(c) for c in kept],
        out_shape=out_shape + [jax.ShapeDtypeStruct((total, c), BF16) for c in kept],
        scratch_shapes=[
            pltpu.VMEM((tile, width), F32),
            pltpu.VMEM((tile, width), F32),
            pltpu.VMEM((len(ws), 3, width, hidden), BF16),
            pltpu.SemaphoreType.DMA((len(ws), 3)),
        ],
        compiler_params=pltpu.CompilerParams(vmem_limit_bytes=60 * 2**20),
        cost_estimate=pl.CostEstimate(
            flops=3 * slots * total * width * single,
            bytes_accessed=total * width * 12 + slots * pieces * width * hidden * 6,
            transcendentals=slots * total * single,
        ),
        name="expert_data",
    )(*ins)
    result = (outs[:blocks], outs[blocks:n]) if last else outs[:n]
    return result, outs[n : n + slots], outs[n + slots :]


def weight_kernel(shape, pieces, *refs):
    xt = gt = None
    refs = list(refs)
    for blocks in shape:
        xs, gs, h, a = refs[:blocks], refs[blocks : 2 * blocks], refs[2 * blocks], refs[2 * blocks + 1]
        refs = refs[2 * blocks + 2 :]
        rows = xs[0].shape[0]
        for i in range(blocks):
            span = slice(i * rows, (i + 1) * rows)
            xp, gp = dot_tn(xs[i][...], h[span]), dot_tn(gs[i][...], a[span])
            xt, gt = (xp, gp) if xt is None else (xt + xp, gt + gp)
    outs = refs
    hid = outs[0].shape[2]
    for i in range(pieces):
        outs[i][0] = xt[:, 2 * i * hid : (2 * i + 1) * hid].astype(BF16)
        outs[i][1] = xt[:, (2 * i + 1) * hid : (2 * i + 2) * hid].astype(BF16)
        outs[i][2] = gt[:, i * hid : (i + 1) * hid].astype(BF16)


def expert_weight(parts, pieces, width):
    hidden = parts[0][4].shape[1] // pieces
    block = 256
    ins, specs, shape, total = [], [], [], 0
    for xs, gs, rows, h, a in parts:
        for v, o in [*xs, *gs]:
            ins.append(v)
            specs.append(pl.BlockSpec((rows, block), lambda i, o=o: (o, i)))
        for v in (h, a):
            ins.append(v)
            specs.append(pl.BlockSpec(v.shape, lambda i: (0, 0), pipeline_mode=pl.Buffered(1)))
        shape.append(len(xs))
        total += h.shape[0]
    return pl.pallas_call(
        functools.partial(weight_kernel, tuple(shape), pieces),
        grid=(width // block,),
        in_specs=specs,
        out_specs=[pl.BlockSpec((3, block, hidden), lambda i: (0, i, 0))] * pieces,
        out_shape=[jax.ShapeDtypeStruct((3, width, hidden), BF16)] * pieces,
        compiler_params=pltpu.CompilerParams(vmem_limit_bytes=60 * 2**20),
        cost_estimate=pl.CostEstimate(
            flops=total * width * hidden * pieces,
            bytes_accessed=total * (width * 4 + hidden * pieces * 6) + width * hidden * pieces * 6,
            transcendentals=0,
        ),
        name="expert_weight",
    )(*ins)


def rms_parts(v):
    inv = lax.rsqrt(jnp.mean(v * v, axis=1, keepdims=True) + EPS)
    return inv, v * inv


def join_kernel(pieces, at_ref, x_ref, gain_ref, *refs):
    os, ws = refs[:pieces], refs[pieces : 2 * pieces]
    mixed_ref, top_ref, low_ref = refs[2 * pieces :]
    mixed = x_ref[...].astype(F32)
    for o, w in zip(os, ws):
        mixed = mixed + dot_tn(o[...], w[...])
    mixed_ref[...] = mixed
    rows = (rms_parts(mixed)[1] * gain_ref[...]).astype(BF16)
    for i, ref in enumerate((top_ref, low_ref)):

        @pl.when(pl.program_id(0) == i)
        def _():
            ref[...] = rows


def join_heads(at, tokens, gain, os, ws, rows):
    width = tokens.shape[1]
    half = rows // 2
    heads = os[0].shape[0]
    own = pl.BlockSpec((heads, half), lambda i, at: (0, at[0] * 2 + i))
    o_specs = [own] + [pl.BlockSpec((heads, half), lambda i, at: (0, i))] * (len(os) - 1)
    if half % LANES:
        os = [lax.dynamic_slice_in_dim(os[0], at[0] * rows, rows, 1)] + os[1:]
        os = [jnp.stack([o[:, :half], o[:, half:]]) for o in os]
        o_specs = [pl.BlockSpec((None, heads, half), lambda i, at: (i, 0, 0))] * len(os)
    once = pl.BlockSpec((half, width), lambda i, at: (0, 0))
    return pl.pallas_call(
        functools.partial(join_kernel, len(os)),
        grid_spec=pltpu.PrefetchScalarGridSpec(
            num_scalar_prefetch=1,
            grid=(2,),
            in_specs=[
                pl.BlockSpec((half, width), lambda i, at: (at[0] * 2 + i, 0)),
                pl.BlockSpec((1, width), lambda i, at: (0, 0)),
            ]
            + o_specs
            + [pl.BlockSpec((heads, width), lambda i, at: (0, 0))] * len(ws),
            out_specs=[pl.BlockSpec((half, width), lambda i, at: (i, 0)), once, once],
        ),
        out_shape=[
            jax.ShapeDtypeStruct((rows, width), F32),
            jax.ShapeDtypeStruct((half, width), BF16),
            jax.ShapeDtypeStruct((half, width), BF16),
        ],
        compiler_params=pltpu.CompilerParams(vmem_limit_bytes=48 * 2**20),
        cost_estimate=pl.CostEstimate(
            flops=2 * rows * heads * len(os) * width, bytes_accessed=rows * width * 8, transcendentals=0
        ),
        name="join_heads",
    )(at, tokens, gain[None, :], *os, *ws)


def turn_kernel(near_ref, xt_ref, yl_ref, xl_ref, yt_ref, mixed_ref, grad_ref, gain_ref, dy_ref, gates_ref, sum_ref):
    step = pl.program_id(0)
    width = mixed_ref.shape[1]
    upper = step == 0
    back = near_ref[...].astype(F32)
    back = back + jnp.where(upper, xt_ref[...], xl_ref[...]).astype(F32)
    back = back + jnp.where(upper, yt_ref[...], yl_ref[...]).astype(F32)
    gates_ref[...] = back[:, width:]
    d_in = back[:, :width]
    inv, normed = rms_parts(mixed_ref[...])
    scaled = d_in * gain_ref[...]
    dots = jnp.mean(scaled * normed, axis=1, keepdims=True)
    dy_ref[...] = (grad_ref[...].astype(F32) + inv * (scaled - normed * dots)).astype(BF16)
    part = jnp.sum(d_in * normed, axis=0, keepdims=True)

    @pl.when(upper)
    def _():
        sum_ref[...] = part

    @pl.when(jnp.logical_not(upper))
    def _():
        sum_ref[...] += part


def turn_back(near, halves, others, mixed, grad_wide, gain):
    rows, width = mixed.shape
    half, full = rows // 2, near.shape[1]

    def spec(c):
        return pl.BlockSpec((half, c), lambda i: (i, 0))

    const = pl.BlockSpec((half, full), lambda i: (0, 0))
    line = pl.BlockSpec((1, width), lambda i: (0, 0))
    return pl.pallas_call(
        turn_kernel,
        grid=(2,),
        in_specs=[spec(full)] + [const] * 4 + [spec(width), spec(width), line],
        out_specs=[spec(width), spec(LANES), line],
        out_shape=[
            jax.ShapeDtypeStruct((rows, width), BF16),
            jax.ShapeDtypeStruct((rows, LANES), F32),
            jax.ShapeDtypeStruct((1, width), F32),
        ],
        compiler_params=pltpu.CompilerParams(vmem_limit_bytes=48 * 2**20),
        cost_estimate=pl.CostEstimate(flops=0, bytes_accessed=rows * width * 16, transcendentals=0),
        name="turn_back",
    )(near, *halves, *others, mixed, grad_wide, gain[None, :])


def lay_out_kernel(halves, cuts, at_ref, *refs):
    q_out, k_out, v_out, o_out = refs[2 * PLANE :]
    rows = q_out.shape[0]
    for m in range(PLANE):

        @pl.when(pl.program_id(0) == m)
        def _():
            first, second = refs[m], refs[PLANE + m]
            parts = [second] if halves == 1 else [first, second]
            for out, cut, left in zip((q_out, k_out, v_out), cuts, (0, cuts[0], cuts[0] + cuts[1])):
                for i, part in enumerate(parts):
                    out[:, i * cut : (i + 1) * cut] = part[:rows, left : left + cut].astype(F32)
            wide = 0 if halves == 1 else sum(cuts)
            o_out[...] = first[:, wide:].astype(F32).T


def lay_out(at, first, second, halves, cuts):
    rows = first[0].shape[0]
    out_width = first[0].shape[1] - (0 if halves == 1 else sum(cuts))
    shapes = [(PLANE * rows, halves * c) for c in cuts] + [(out_width, PLANE * rows)]
    specs = [pl.BlockSpec((rows, halves * c), lambda m, at: (at[0] ^ m, 0)) for c in cuts]
    return pl.pallas_call(
        functools.partial(lay_out_kernel, halves, cuts),
        grid_spec=pltpu.PrefetchScalarGridSpec(
            num_scalar_prefetch=1,
            grid=(PLANE,),
            in_specs=[pl.BlockSpec(v.shape, lambda m, at: (0, 0)) for v in [*first, *second]],
            out_specs=specs + [pl.BlockSpec((out_width, rows), lambda m, at: (0, at[0] ^ m))],
        ),
        out_shape=[jax.ShapeDtypeStruct(v, F32) for v in shapes],
        compiler_params=pltpu.CompilerParams(vmem_limit_bytes=48 * 2**20),
        cost_estimate=pl.CostEstimate(flops=0, bytes_accessed=24 * rows * out_width, transcendentals=0),
        name="lay_out",
    )(at, *first, *second)


def after(x, *others):
    leaves, tree = jax.tree.flatten(x)
    extra = jax.tree.leaves(others)
    held = lax.optimization_barrier(tuple(leaves) + tuple(extra))
    return jax.tree.unflatten(tree, held[: len(leaves)])


def body(
    tokens,
    segment_ids,
    router_logits,
    expert_ids,
    gain_attn,
    w_query,
    key_matrix,
    value_matrix,
    w_out,
    gain_mlp,
    w_gate,
    w_up,
    w_down,
    out_grad,
):
    n_tok, width = tokens.shape
    col_width = out_grad.shape[1]
    n_tensor = width // col_width
    n_expert = router_logits.shape[1]
    depth = n_expert // PLANE
    my_row = n_tok // n_tensor
    t_at = lax.axis_index("tensor")
    e_at = lax.axis_index("expert")

    def hop(x, step):
        pairs = [(i, (i + step) % n_tensor) for i in range(n_tensor)]
        return jax.tree.map(lambda a: lax.ppermute(a, "tensor", pairs), x)

    def plane(x, mask):
        pairs = [(i, i ^ mask) for i in range(n_expert)]
        return jax.tree.map(lambda a: lax.ppermute(a, "expert", pairs), x)

    def ring(x, step=1):
        pairs = [(i, (i + step * PLANE) % n_expert) for i in range(n_expert)]
        return jax.tree.map(lambda a: lax.ppermute(a, "expert", pairs), x)

    def peer(step):
        return lax.rem(t_at + step + n_tensor, n_tensor)

    def rows_of(x, who):
        return lax.dynamic_slice_in_dim(x, who * my_row, my_row, 0)

    def cols_of(x, who):
        return lax.dynamic_slice_in_dim(x, who * col_width, col_width, x.ndim - 1)

    def place(parts, axis):
        if n_tensor == 2:
            return jnp.where(t_at == 0, jnp.concatenate(parts, axis), jnp.concatenate(parts[::-1], axis))
        size = parts[0].shape[axis]
        shape = list(parts[0].shape)
        shape[axis] *= n_tensor
        out = jnp.zeros(shape, parts[0].dtype)
        for s, v in enumerate(parts):
            out = lax.dynamic_update_slice_in_dim(out, v, peer(-s) * size, axis)
        return out

    def to_rows(x):
        return place([rows_of(x, t_at)] + [hop(rows_of(x, peer(s)), s) for s in range(1, n_tensor)], 1)

    def to_cols(x):
        return place([cols_of(x, t_at)] + [hop(cols_of(x, peer(s)), s) for s in range(1, n_tensor)], 0)

    def gather_rows(x):
        return place([x] + [hop(x, s) for s in range(1, n_tensor)], 0)

    ids_rows = rows_of(expert_ids, t_at)
    logit_rows = rows_of(router_logits, t_at)
    expert_range = jnp.arange(n_expert, dtype=jnp.int32)
    used = jnp.any(ids_rows[:, :, None] == expert_range[None, None, :], axis=1)
    masked = jnp.where(used, logit_rows, NEG)
    weights = jnp.where(used, jnp.exp(masked - jnp.max(masked, axis=1, keepdims=True)), 0.0)
    gates = weights / jnp.sum(weights, axis=1, keepdims=True)
    pad = ((0, 0), (0, LANES // 2 - n_expert))
    high = lax.optimization_barrier(gates.astype(BF16))
    low = (gates - high.astype(F32)).astype(BF16)
    grad_rows = to_rows(out_grad.astype(BF16))
    grad_wide = jnp.concatenate([grad_rows, jnp.pad(high, pad), jnp.pad(low, pad)], axis=1)
    held = [jnp.stack([w_gate[0], w_up[0], w_down[0].T])]
    half_row = my_row // 2

    start = jnp.sum((segment_ids[:, None] < segment_ids[None, :]).astype(jnp.int32), axis=0)
    places = jnp.arange(n_tok, dtype=jnp.int32) - start
    half = HEAD_SIZE // 2
    freq = jnp.power(THETA, -2.0 * jnp.arange(half, dtype=F32) / HEAD_SIZE)
    angles = freq[:, None] * places.astype(F32)[None, :]
    cos_t, sin_t = jnp.cos(angles), jnp.sin(angles)
    start = start[None, :]
    held.append(ring(held[0]))
    tokens, grad_wide = after((tokens, grad_wide))
    grad_x, grad_y = plane(grad_wide, 1), plane(grad_wide, 2)
    out_pieces = [w_out] + [hop(w_out, s) for s in range(1, n_tensor)]
    slots = [[held[0]] + [hop(held[0], s) for s in range(1, n_tensor)]]
    x_full = tokens.astype(F32)
    inv_one = lax.rsqrt(jnp.mean(x_full * x_full, axis=1, keepdims=True) + EPS)
    normed_one = x_full * inv_one
    attn_in = (normed_one * gain_attn).astype(BF16)

    def project(w):
        return jnp.einsum("td,dc->ct", attn_in, w, preferred_element_type=F32)

    v_t = project(value_matrix).astype(BF16)
    q_t, k_t, o_t, lse = attn_forward(project(w_query), project(key_matrix), v_t, cos_t, sin_t, start)
    o_t, grad_x, grad_y, slots[0], out_pieces, held[1] = after((o_t, grad_x, grad_y, slots[0], out_pieces, held[1]))
    held.append(ring(held[1]))
    grad_diag = [plane(grad_x[:half_row], 2), plane(grad_y[half_row:], 1)]
    sent = [lax.dynamic_slice_in_dim(o_t, peer(s) * my_row, my_row, 1) for s in range(1, n_tensor)]
    os = [o_t] + [hop(v, s) for s, v in enumerate(sent, 1)]
    mixed, mlp_top, mlp_low = join_heads(t_at.reshape(1), tokens, gain_mlp, os, out_pieces, my_row)
    mlp_top, mlp_low, grad_diag = after((mlp_top, mlp_low, grad_diag))

    group = 2 if depth % 2 == 0 else 1
    last = depth - group
    carry = dict.fromkeys(("near", "one", "two", "diag"))
    saved = [{} for _ in range(depth)]
    where = {
        "near": ([(mlp_top, 0), (mlp_low, 0)], [(grad_wide, 0), (grad_wide, 1)]),
    }

    def run(name, k, fence=()):
        ks = range(k, k + group)
        experts = jnp.stack([lax.rem(e_at - i * PLANE + n_expert, n_expert) for i in ks])
        experts = after(experts, *fence) if fence else experts
        flat = [w for i in ks for w in slots[i]]
        xs, gs = where[name]
        carry[name], hs, acts = expert_data(experts, xs, gs, half_row, flat, carry[name], k == last)
        for i, h, a in zip(ks, hs, acts):
            saved[i][name] = (xs, gs, half_row, h, a)

    def add_slot():
        k = len(slots)
        slots.append([held[k]] + [hop(held[k], s) for s in range(1, n_tensor)])

    def weight_pieces(k, fence=()):
        parts = list(saved[k].values())
        if fence:
            xs, gs, rows, h, a = parts[0]
            parts[0] = (xs, gs, rows, after(h, *fence), a)
        return expert_weight(parts, n_tensor, width)

    def hop_back(grads):
        return [hop(grads[s], n_tensor - s) for s in range(1, n_tensor)]

    def total_of(grads, got):
        return functools.reduce(jnp.add, [v.astype(F32) for v in [grads[0], *got]])

    def weight_total(k):
        grads = weight_pieces(k)
        return total_of(grads, hop_back(grads))

    def send_on(k, moving):
        total = totals[k]
        if moving is not None:
            total = total + moving.astype(F32)
        return ring(total.astype(BF16)) if k else total

    for _ in range(1, group):
        add_slot()
    slots, mlp_top, mlp_low = after((slots, mlp_top, mlp_low))
    x_top, y_low = plane(mlp_top, 1), plane(mlp_low, 2)
    run("near", 0)
    x_top, y_low, carry["near"], held[2] = after((x_top, y_low, carry["near"], held[2]))
    for _ in range(3, depth):
        held.append(ring(held[-1]))
    x_low, y_top = plane(mlp_low, 1), plane(mlp_top, 2)
    where["one"] = ([(x_top, 0), (y_low, 0)], [(grad_x, 0), (grad_y, 1)])
    run("one", 0)
    x_low, y_top, carry["one"] = after((x_low, y_top, carry["one"]))
    mlp_diag = [plane(x_top, 2), plane(y_low, 1)]
    where["two"] = ([(x_low, 0), (y_top, 0)], [(grad_x, 1), (grad_y, 0)])
    run("two", 0)
    mlp_diag, carry["two"] = after((mlp_diag, carry["two"]))
    add_slot()
    where["diag"] = ([(v, 0) for v in mlp_diag], [(v, 0) for v in grad_diag])
    run("diag", 0)
    slots, carry["diag"] = after((slots, carry["diag"]))
    for k in range(group, last, group):
        while len(slots) < k + group:
            add_slot()
        for name in ("near", "one", "two", "diag"):
            run(name, k)
    totals = {}
    order = list(range(1, depth)) + [0]
    early = order[: depth - group - 1]
    for k in early:
        totals[k] = weight_total(k)
    while len(slots) < depth:
        add_slot()
    slots[-1], totals = after((slots[-1], totals))
    moving = None
    for k in early:
        moving = send_on(k, moving)
    rest = order[len(early) :]

    run("diag", last)
    parts = [plane(v, m) for v, m in zip(carry["diag"][1], (1, 2))]
    run("one", last, [carry["diag"]])
    parts, carry["one"] = after((parts, carry["one"]))
    halves = [plane(v, m) for v, m in zip(carry["one"][1], (1, 2))]
    run("two", last, [carry["one"]])
    low_x, top_y = ((v.astype(F32) + p.astype(F32)).astype(BF16) for v, p in zip(carry["two"][1], parts[::-1]))
    halves, low_x, top_y = after((halves, low_x, top_y))
    others = [plane(low_x, 1), plane(top_y, 2)]
    run("near", last, [low_x, top_y])
    others, carry["near"], moving = after((others, carry["near"], moving))

    near_dx = jnp.concatenate(carry["near"][1], axis=0)
    dy, d_gates, gain_two_all = turn_back(near_dx, halves, others, mixed, grad_wide, gain_mlp)
    out_diag, dy = after((carry["diag"][0], dy))
    out_parts = [plane(v, m) for v, m in zip(out_diag, (1, 2))]
    dy_full = gather_rows(dy)
    late = {rest[0]: weight_pieces(rest[0], [dy])}
    dy_full, late, out_parts = after((dy_full, late, out_parts))
    d_gates = d_gates[:, :n_expert] + d_gates[:, LANES // 2 : LANES // 2 + n_expert]

    arrived = moving
    late_got = hop_back(late[rest[0]])
    out_halves = [plane(v, m) for v, m in zip(carry["one"][0], (1, 2))]
    do_t = jnp.einsum("td,cd->ct", dy_full, w_out, preferred_element_type=F32).astype(BF16)
    out_w_grad = jnp.einsum("td,ct->dc", dy_full, o_t, preferred_element_type=F32).astype(BF16)
    kv = k_t.shape[0] // HEAD_SIZE
    parts = 2 if kv % 2 == 0 else 1
    count = kv // parts

    def backward(i, do_t):
        return attn_backward(q_t, k_t, v_t, do_t, lse, cos_t, sin_t, start, i * count, count)

    def columns(w, i):
        size = w.shape[1] // parts
        return w[:, i * size : (i + 1) * size]

    def weight_grads(ds):
        return [jnp.einsum("td,ct->dc", attn_in, d, preferred_element_type=F32).astype(BF16) for d in ds]

    def input_grads(ds, i):
        ws = (w_query, key_matrix, value_matrix)
        terms = [jnp.einsum("ct,dc->td", d, columns(w, i), preferred_element_type=F32) for d, w in zip(ds, ws)]
        return functools.reduce(jnp.add, terms)

    def part(a, who, rows):
        return lax.dynamic_slice_in_dim(a, who * rows, rows, 0)

    p_at, z_at = lax.rem(e_at, PLANE), e_at // PLANE

    def plane_shares(a):
        quarter = a.shape[0] // PLANE
        return [plane(part(a, p_at ^ m, quarter), m) for m in range(1, PLANE)]

    def plane_sum(a, shares):
        total = part(a, p_at, a.shape[0] // PLANE).astype(F32)
        for v in shares:
            total = total + v.astype(F32)
        return total.astype(BF16)

    def swap(a, bit):
        pairs = [(i, i ^ (bit * PLANE)) for i in range(n_expert)]
        return lax.ppermute(a, "expert", pairs)

    bits = [1 << i for i in range(depth.bit_length() - 1)]

    def upper(bit):
        return (z_at // bit) % 2

    def z_cut(a, bit, tail=None):
        rows = a.shape[0] // 2
        stay, go = part(a, upper(bit), rows), part(a, 1 - upper(bit), rows)
        return stay, go if tail is None else jnp.concatenate([go, tail], axis=0)

    def add(a, b):
        return (a.astype(F32) + b.astype(F32)).astype(BF16)

    def z_join(a, got, bit):
        return jnp.where(upper(bit) == 0, jnp.concatenate([a, got], 0), jnp.concatenate([got, a], 0))

    first = out_w_grad
    ds = []
    do_t, out_w_grad = after((do_t, out_w_grad))
    if parts == 2:
        ds.append(backward(0, do_t))
        ds[0], out_halves, do_t, late_got = after((ds[0], out_halves, do_t, late_got))
        first = jnp.concatenate(weight_grads(ds[0]) + [out_w_grad], axis=1)

    def next_moving(k, got, arrived):
        total = total_of(late[k], got)
        if arrived is not None:
            total = total + arrived.astype(F32)
        return total.astype(BF16)

    moving = next_moving(rest[0], late_got, arrived)
    first, out_halves, moving, do_t = after((first, out_halves, moving, do_t))
    ring_on = [ring(moving[c]) for c in range(2)]
    first_sent = plane_shares(first)
    ds.append(backward(parts - 1, do_t))
    first_sent, ring_on, ds = after((first_sent, ring_on, ds))

    second = jnp.concatenate(weight_grads(ds[-1]), axis=1)
    first = plane_sum(first, first_sent)
    stay, go = z_cut(first, bits[0])
    second, stay, go, ds = after((second, stay, go, ds))
    second_sent = plane_shares(second)
    got = swap(go, bits[0])
    ring_on.append(ring(moving[2]))
    in_terms = functools.reduce(jnp.add, [input_grads(d, i) for i, d in enumerate(ds)])
    dots = jnp.sum(in_terms * gain_attn * normed_one, axis=1)
    own_terms = cols_of(in_terms, t_at)
    far_terms = [cols_of(in_terms, peer(s)).astype(BF16) for s in range(1, n_tensor)]
    second_sent, got, ring_on, far_terms, dots = after((second_sent, got, ring_on, far_terms, dots))

    first = add(stay, got)
    out_two = [add(v, p) for v, p in zip(carry["two"][0], out_parts[::-1])]
    gain_two = cols_of(gain_two_all[0], t_at)
    far_gains = [cols_of(gain_two_all[0], peer(s)) for s in range(1, n_tensor)]
    cuts = [z_cut(first, bits[1])] if len(bits) > 1 else []
    cuts, out_two, far_terms, dots = after((cuts, out_two, far_terms, dots))
    out_others = [plane(v, m) for v, m in zip(out_two, (1, 2))]
    far_terms = [hop(v, s) for s, v in enumerate(far_terms, 1)]
    far_dots = [hop(jnp.concatenate([dots, v]), s) for s, v in enumerate(far_gains, 1)]
    gots = [swap(go, bits[1]) for _, go in cuts]
    for k in rest[1:-1]:
        late[k] = weight_pieces(k, [dots])
    gots, out_others, far_terms, far_dots, late = after((gots, out_others, far_terms, far_dots, late))
    second = plane_sum(second, second_sent)
    for (stay, _), got in zip(cuts, gots):
        first = add(stay, got)
    for bit in bits[2:]:
        stay, go = z_cut(first, bit)
        first = add(stay, swap(go, bit))
    gain_two = functools.reduce(jnp.add, [gain_two] + [v[n_tok:] for v in far_dots])
    far_dots = [v[:n_tok] for v in far_dots]

    d_attn_in = functools.reduce(jnp.add, [own_terms] + [v.astype(F32) for v in far_terms])
    all_dots = functools.reduce(jnp.add, [dots] + far_dots)
    normed_cols = cols_of(normed_one, t_at)
    scaled_one = d_attn_in * cols_of(gain_attn, t_at)
    d_norm_one = inv_one * (scaled_one - normed_cols * (all_dots / width)[:, None])
    grad_tokens = cols_of(dy_full, t_at).astype(F32) + d_norm_one
    gain_one = jnp.sum(d_attn_in * normed_cols, axis=0)
    wide = second.shape[1]
    gains = jnp.concatenate([gain_one, gain_two]).astype(BF16).reshape(-1, wide)
    gain_rows = gains.shape[0]
    gains = jnp.pad(gains, ((0, 16 - gain_rows), (0, 0)))
    grad_logits = gather_rows(gates * (d_gates - jnp.sum(gates * d_gates, axis=1, keepdims=True)))
    late_got = {k: hop_back(late[k]) for k in rest[1:-1]}
    for i, bit in enumerate(bits):
        rows = second.shape[0] // 2
        stay, go = z_cut(second, bit, gains)
        back = bits[-1 - i]
        first, go, late_got = after((first, go, late_got))
        got, first_got = swap(go, bit), swap(first, back)
        got, first_got = after((got, first_got))
        second, gains = add(stay, got[:rows]), add(gains, got[rows:])
        first = z_join(first, first_got, back)
    moving = jnp.stack(ring_on)
    for k in rest[1:-1]:
        moving = next_moving(k, late_got[k], moving)
        first, second, moving = after((first, second, moving))
        ring_on = [ring(moving[c]) for c in range(3)]
        moving = jnp.stack(ring_on[:2] + [ring_on[2]])
    first_all = [first] + [plane(first, m) for m in range(1, PLANE)]
    late[0] = weight_pieces(0, [first])
    for bit in bits[::-1]:
        second = z_join(second, swap(second, bit), bit)
    rows = second.shape[0]
    second = jnp.concatenate([second, gains], axis=0)
    out_top, out_low = carry["near"][0]
    top_rows = out_top.astype(F32) + out_halves[0].astype(F32) + out_others[1].astype(F32)
    low_rows = out_low.astype(F32) + out_others[0].astype(F32) + out_halves[1].astype(F32)
    block_out = to_cols((mixed + jnp.concatenate([top_rows, low_rows], axis=0)).astype(BF16))
    second, block_out, first_all, ring_on[:2], late[0] = after((second, block_out, first_all, ring_on[:2], late[0]))
    late_got[0] = hop_back(late[0])
    second_all = [second] + [plane(second, m) for m in range(1, PLANE)]
    gains = functools.reduce(jnp.add, [v[rows : rows + gain_rows].astype(F32) for v in second_all]).reshape(-1)
    final = [a + b.astype(F32) for a, b in zip(total_of(late[0], late_got[0]), ring_on)]
    cuts = [w.shape[1] // parts for w in (w_query, key_matrix, value_matrix)]
    grad_query, grad_key, grad_value, grad_out = lay_out(p_at.reshape(1), first_all, second_all, parts, cuts)
    return (
        block_out,
        grad_tokens,
        grad_logits,
        gains[:col_width],
        grad_query,
        grad_key,
        grad_value,
        grad_out,
        gains[col_width:],
        final[0][None],
        final[1][None],
        final[2].T[None],
    )


def solution(mesh):
    return jax.shard_map(
        body,
        mesh=mesh,
        in_specs=(
            P("expert", None),
            P("expert"),
            P("expert", None),
            P("expert", None),
            P(),
            P(None, "tensor"),
            P(None, "tensor"),
            P(None, "tensor"),
            P("tensor", None),
            P(),
            P("expert", None, "tensor"),
            P("expert", None, "tensor"),
            P("expert", "tensor", None),
            P("expert", "tensor"),
        ),
        out_specs=(
            P("expert", "tensor"),
            P("expert", "tensor"),
            P("expert", None),
            P("tensor"),
            P(None, "tensor"),
            P(None, "tensor"),
            P(None, "tensor"),
            P("tensor", None),
            P("tensor"),
            P("expert", None, "tensor"),
            P("expert", None, "tensor"),
            P("expert", "tensor", None),
        ),
        check_vma=False,
    )
```

time: 485 us -> 449 us (0.926); the launches traced: 476 us -> 447 us
  waiting for transfers between devices: 139 us -> 68.8 us
  Pallas kernels: 178 us -> 203 us
  starting transfers between devices: 47.4 us -> 71.2 us
  local copies, waits for them, and re-layouts: 35.4 us -> 23.7 us
  matrix products: 19.9 us -> 31.2 us
  other arithmetic: 54.2 us -> 46.7 us
    ppermute x26 -> x34, waiting for transfers between devices: 82.5 us -> 25.8 us  [plane(): return jax.tree.map(lambda a: lax.ppermute(a, 'expert', pairs), x)]
    ppermute x12 -> x10, waiting for transfers between devices: 52.2 us -> 21.3 us  [ring(): return jax.tree.map(lambda a: lax.ppermute(a, 'expert', pairs), x)]
    pallas_call x8 -> x13, Pallas kernels: 119 us -> 143 us  [the longest x8 110 us: expert_data(): pl.pallas_call(functools.partial(data_kernel, first, last, blocks, tiles,...]
    ppermute x0 -> x8, waiting for transfers between devices: none -> 16.1 us  [swap(): return lax.ppermute(a, 'expert', pairs)]
    slice x8 -> x0, local copies, waits for them, and re-layouts: 10.7 us -> none  [the longest x2 3.73 us: body(): mlp_diag = [plane(mlp_x[:half_row], 2), plane(mlp_y[half_row:], 1)]]
    dot_general x9 -> x13, matrix products: 14 us -> 24.1 us  [the longest x6 14.7 us: input_grads(): jnp.einsum('ct,dc->td', d, columns(w, i), preferred_element_type=F32)]
    ppermute x26 -> x34, starting transfers between devices: 26.9 us -> 36.9 us  [plane(): return jax.tree.map(lambda a: lax.ppermute(a, 'expert', pairs), x)]
    ppermute x0 -> x8, starting transfers between devices: none -> 9.74 us  [swap(): return lax.ppermute(a, 'expert', pairs)]
  transfers between devices with their start and end apart: 55 -> 68, of which waited for: 23 -> 19; matrix products, arithmetic and copies ran while one was open for 19% -> 17% of each run, Pallas kernels for 24% -> 41%
where the time goes in v3:
time: 449 us; the launch traced here: 447 us
  Pallas kernels  203 us (45%)
  starting transfers between devices  71.2 us (16%)
  waiting for transfers between devices  68.8 us (15%)
  other arithmetic  46.7 us (10%)
  matrix products  31.2 us (7%)
  local copies, waits for them, and re-layouts  23.7 us (5%)
    pallas_call x8, Pallas kernels, expert_data(): pl.pallas_call(functools.partial(data_kernel, first, last, blocks, tiles,...  110 us
    pallas_call x4, Pallas kernels, expert_weight(): pl.pallas_call(functools.partial(weight_kernel, tuple(shape), pieces), gr...  48.8 us
    ppermute x34, starting transfers between devices, plane(): return jax.tree.map(lambda a: lax.ppermute(a, 'expert', pairs), x)  36.9 us
    ppermute x34, waiting for transfers between devices, plane(): return jax.tree.map(lambda a: lax.ppermute(a, 'expert', pairs), x)  25.8 us
    ppermute x10, starting transfers between devices, ring(): return jax.tree.map(lambda a: lax.ppermute(a, 'expert', pairs), x)  22.5 us
    ppermute x10, waiting for transfers between devices, ring(): return jax.tree.map(lambda a: lax.ppermute(a, 'expert', pairs), x)  21.3 us
    pallas_call x2, Pallas kernels, attn_backward(): pl.pallas_call(functools.partial(attn_bwd_kernel, block), grid=(count,),...  20.1 us
    ppermute x8, waiting for transfers between devices, swap(): return lax.ppermute(a, 'expert', pairs)  16.1 us
  transfers between devices with their start and end apart: 68, of which 19 were waited for; matrix products, arithmetic and copies ran while one was open for 17% of the time, Pallas kernels for 41%

profile of v3, /device:TPU:0, one launch (start us, length us, event | category | flops | bytes accessed | tf_op | source)
XLA Modules:
  0.0 446.8 jit_solution(14148950144223009247)
XLA Ops:
  1.9 2.5 pad_maximum_fusion.1.refs_4_
  4.5 3.0 collective-permute-start.5
  7.5 1.8 convert_element_type.280
  16.8 2.2 concatenate.81.refs_2_.refs_3_.grad_ref.refs_20_.refs_21_
  19.0 1.6 collective-permute-start.2
  22.1 2.1 fusion
  24.2 2.1 convolution_bitcast_fusion.1.k_ref
  27.5 2.8 convolution_bitcast_fusion.q_ref
  30.3 11.5 %attn_forward.1 = (bf16[512,1024]{1,0:T(8,128)(2,1)S(1)}, bf16[256,1024]{1,0:T(8,128)(2,1)S(1)}, bf16[512,1024]{1,0:T(8,128)(2,1)S(1)}, f32[4,2,1024]{2,1,0:T(2,128)S(1)}) custom-call(f32[512,1024]{1,0:T(8,128)} %convolution_bitcast_fusion.q_ref, f32[256,1024]{1,0:T(8,128)S(1)} %convolution_bitcast_fusion.1.k_ref, bf16[256,1024]{1,0:T(8,128)(2,1)S(1)} %fusion.3.v_ref, ...), custom_call_target="tpu_custom_call" | custom-call | flops 4294967296 | bytes 4194304 | tf_op jit(solution)/shard_map/attn_forward/pallas_call | solution.py:123
  44.2 3.2 collective-permute-done.2.refs_3_.refs_9_.refs_15_
  48.6 13.1 %collective-permute-start.12 = (bf16[3,1024,256]{2,1,0:T(8,128)(2,1)}, bf16[3,1024,256]{2,1,0:T(8,128)(2,1)}, u32[]{:S(2)}, u32[]{:S(2)}) collective-permute-start(bf16[3,1024,256]{2,1,0:T(8,128)(2,1)} %collective-permute-done.5.refs_6_), channel_id=1, source_target_pairs={{0,8},{2,10},{4,12},{6,14},{8,16},{10,18},{12,20},{14,22},{16,24},... | collective-permute-start | bytes 4718600 | tf_op jit(solution)/shard_map/ppermute | solution.py:557
  62.1 1.6 collective-permute-start.9
  64.2 4.3 join_heads.1
  68.5 9.2 %collective-permute-done.9.refs_3_.refs_21_ = bf16[256,1152]{1,0:T(8,128)(2,1)S(1)} collective-permute-done((bf16[256,1152]{1,0:T(8,128)(2,1)S(1)}, bf16[256,1152]{1,0:T(8,128)(2,1)S(1)}, u32[]{:S(2)}, u32[]{:S(2)}) %collective-permute-start.9) | collective-permute-done | bytes 589856 | tf_op jit(solution)/shard_map/ppermute | solution.py:553
  82.0 12.9 %expert_data.8 = (bf16[512,1024]{1,0:T(8,128)(2,1)}, bf16[512,1024]{1,0:T(8,128)(2,1)}, f32[512,128]{1,0:T(8,128)}, bf16[512,1024]{1,0:T(8,128)(2,1)}, bf16[512,...) custom-call(s32[2]{0:T(128)} %get-tuple-element.581.expert_ref, bf16[256,1024]{1,0:T(8,128)(2,1)} %copy-done.4, ...), custom_call_target="tpu_custom_call" | custom-call | flops 1610612736 | bytes 12582912 | tf_op jit(solution)/shard_map/expert_data/pallas_call | solution.py:301
  94.9 4.2 collective-permute-done.12.refs_4_
  103.2 12.7 %expert_data.9 = (bf16[512,1024]{1,0:T(8,128)(2,1)}, bf16[512,1024]{1,0:T(8,128)(2,1)}, f32[512,128]{1,0:T(8,128)}, bf16[512,1024]{1,0:T(8,128)(2,1)}, bf16[512,...) custom-call(s32[2]{0:T(128)} %get-tuple-element.581.expert_ref, ...), custom_call_target="tpu_custom_call" | custom-call | flops 1610612736 | bytes 12582912 | tf_op jit(solution)/shard_map/expert_data/pallas_call | solution.py:301
  117.0 12.9 %expert_data.10 = (bf16[512,1024]{1,0:T(8,128)(2,1)}, bf16[512,1024]{1,0:T(8,128)(2,1)}, f32[512,128]{1,0:T(8,128)}, bf16[512,1024]{1,0:T(8,128)(2,1)}, bf16[512...) custom-call(s32[2]{0:T(128)} %get-tuple-element.581.expert_ref, ...), custom_call_target="tpu_custom_call" | custom-call | flops 1610612736 | bytes 12582912 | tf_op jit(solution)/shard_map/expert_data/pallas_call | solution.py:301
  129.9 12.8 %expert_data.11 = (bf16[512,1024]{1,0:T(8,128)(2,1)}, bf16[512,1024]{1,0:T(8,128)(2,1)}, f32[512,128]{1,0:T(8,128)}, bf16[512,1024]{1,0:T(8,128)(2,1)}, bf16[512...) custom-call(s32[2]{0:T(128)} %get-tuple-element.581.expert_ref, ...), custom_call_target="tpu_custom_call" | custom-call | flops 1610612736 | bytes 12582912 | tf_op jit(solution)/shard_map/expert_data/pallas_call | solution.py:301
  142.7 12.3 %expert_weight.4 = (bf16[3,1024,256]{2,1,0:T(8,128)(2,1)}, bf16[3,1024,256]{2,1,0:T(8,128)(2,1)}) custom-call(bf16[256,1024]{1,0:T(8,128)(2,1)} %copy-done.4, bf16[256,1024]{1,0:T(8,128)(2,1)} %copy-done.5, bf16[512,1152]{1,0:T(8,128)(2,1)} %copy-done.2, bf16[512,1152]{1,0:T(8,128)(2,1)} %copy-done.2, bf16[512,1024]{1,0:T(8,128)(2,1)} %get-tuple-element.300.refs_4_, ...), custom_call_target="tpu_custom_call" | custom-call | flops 1073741824 | bytes 17825792 | tf_op jit(solution)/shard_map/expert_weight/pallas_call | solution.py:357
  155.6 4.1 collective-permute-done.20
  159.7 3.0 convert_add_fusion.1
  163.9 14.6 %expert_data.12 = (bf16[256,1024]{1,0:T(8,128)(2,1)}, bf16[256,1024]{1,0:T(8,128)(2,1)}, bf16[256,1152]{1,0:T(8,128)(2,1)}, bf16[256,1152]{1,0:T(8,128)(2,1)}, b...) custom-call(s32[2]{0:T(128)} %get-tuple-element.341.expert_ref, ...), custom_call_target="tpu_custom_call" | custom-call | flops 1610612736 | bytes 12582912 | tf_op jit(solution)/shard_map/expert_data/pallas_call | solution.py:301
  178.5 1.6 collective-permute-start.21
  181.9 15.0 %expert_data.13 = (bf16[256,1024]{1,0:T(8,128)(2,1)}, bf16[256,1024]{1,0:T(8,128)(2,1)}, bf16[256,1152]{1,0:T(8,128)(2,1)}, bf16[256,1152]{1,0:T(8,128)(2,1)}, b...) custom-call(s32[2]{0:T(128)} %get-tuple-element.341.expert_ref, ...), custom_call_target="tpu_custom_call" | custom-call | flops 1610612736 | bytes 12582912 | tf_op jit(solution)/shard_map/expert_data/pallas_call | solution.py:301
  197.5 1.6 collective-permute-start.24
  199.1 14.6 %expert_data.14 = (bf16[256,1024]{1,0:T(8,128)(2,1)}, bf16[256,1024]{1,0:T(8,128)(2,1)}, bf16[256,1152]{1,0:T(8,128)(2,1)}, bf16[256,1152]{1,0:T(8,128)(2,1)}, b...) custom-call(s32[2]{0:T(128)} %get-tuple-element.341.expert_ref, ...), custom_call_target="tpu_custom_call" | custom-call | flops 1610612736 | bytes 12582912 | tf_op jit(solution)/shard_map/expert_data/pallas_call | solution.py:301
  213.7 2.1 add_convert_fusion.3
  219.6 14.8 %expert_data.15 = (bf16[256,1024]{1,0:T(8,128)(2,1)}, bf16[256,1024]{1,0:T(8,128)(2,1)}, bf16[256,1152]{1,0:T(8,128)(2,1)}, bf16[256,1152]{1,0:T(8,128)(2,1)}, b...) custom-call(s32[2]{0:T(128)} %get-tuple-element.341.expert_ref, ...), custom_call_target="tpu_custom_call" | custom-call | flops 1610612736 | bytes 12582912 | tf_op jit(solution)/shard_map/expert_data/pallas_call | solution.py:301
  236.1 4.0 turn_back.1
  240.6 1.6 collective-permute-start.30
  242.2 12.1 %expert_weight.5 = (bf16[3,1024,256]{2,1,0:T(8,128)(2,1)}, bf16[3,1024,256]{2,1,0:T(8,128)(2,1)}) custom-call(bf16[256,1024]{1,0:T(8,128)(2,1)} %collective-permute-done.13.refs_0_.refs_18_, bf16[256,1024]{1,0:T(8,128)(2,1)} %collective-permute-done.14.refs_1_.refs_19_, bf16[256,1152]{1,0:T(8,128)(2,1)} %copy-done.26, bf16[256,1152]{1,0:T(8,128)(2,1)} %copy-done.25, ...), custom_call_target="tpu_custom_call" | custom-call | flops 1073741824 | bytes 17825792 | tf_op jit(solution)/shard_map/expert_weight/pallas_call | solution.py:357
  254.3 3.9 maximum_select_fusion
  258.5 1.5 collective-permute-start.31
  260.5 2.9 convolution_convert_fusion
  265.0 10.0 %attn_backward.2 = (bf16[256,1024]{1,0:T(8,128)(2,1)S(1)}, bf16[128,1024]{1,0:T(8,128)(2,1)S(1)}, bf16[128,1024]{1,0:T(8,128)(2,1)S(1)}) custom-call(bf16[512,1024]{1,0:T(8,128)(2,1)S(1)} %copy-done.15, bf16[256,1024]{1,0:T(8,128)(2,1)S(1)} %copy-done.17, bf16[256,1024]{1,0:T(8,128)(2,1)S(1)} %copy-done.13, bf16[512,1024]{1,0:T(8,128)(2,1)S(1)} %fusion.2.do_ref, ...), custom_call_target="tpu_custom_call" | custom-call | flops 2147483648 | bytes 2097152 | tf_op jit(solution)/shard_map/attn_backward/pallas_call | solution.py:147
  278.6 2.5 add_convert_fusion.1
  282.8 3.3 collective-permute-start.37
  286.2 1.5 collective-permute-start.36
  291.8 10.2 %attn_backward.3 = (bf16[256,1024]{1,0:T(8,128)(2,1)S(1)}, bf16[128,1024]{1,0:T(8,128)(2,1)S(1)}, bf16[128,1024]{1,0:T(8,128)(2,1)S(1)}) custom-call(bf16[512,1024]{1,0:T(8,128)(2,1)S(1)} %copy-done.15, bf16[256,1024]{1,0:T(8,128)(2,1)S(1)} %copy-done.17, bf16[256,1024]{1,0:T(8,128)(2,1)S(1)} %copy-done.13, bf16[512,1024]{1,0:T(8,128)(2,1)S(1)} %fusion.2.do_ref, ...), custom_call_target="tpu_custom_call" | custom-call | flops 2147483648 | bytes 2097152 | tf_op jit(solution)/shard_map/attn_backward/pallas_call | solution.py:147
  302.1 8.5 %collective-permute-done.37 = bf16[1024,256]{1,0:T(8,128)(2,1)S(1)} collective-permute-done((bf16[1024,256]{1,0:T(8,128)(2,1)S(1)}, bf16[1024,256]{1,0:T(8,128)(2,1)S(1)}, u32[]{:S(2)}, u32[]{:S(2)}) %collective-permute-start.37) | collective-permute-done | bytes 524320 | tf_op jit(solution)/shard_map/ppermute | solution.py:557
  322.7 2.8 fusion.15
  325.4 2.7 fusion.17
  328.1 7.0 %convert_multiply_fusion = (f32[1024,1024]{1,0:T(8,128)}, f32[1024]{0:T(1024)S(1)}, f32[1024,1024]{1,0:T(8,128)}) fusion(bf16[1024,1024]{1,0:T(8,128)(2,1)S(1)} %copy-done.30, f32[1024]{0:T(1024)S(1)} %add_rsqrt_fusion, f32[1024]{0:T(1024)S(1)} %copy-done.66, bf16[128,1024]{1,0:T(8,128)(2,1)S(1)} %get-tuple-element.414, bf16[1024,256]{1,0:T(8,128)(2,1)S(1)} %copy-done.46, ...), kind=kOutput, calls=%fused_computation | convolution fusion | flops 278920192 | bytes 31993856 | tf_op jit(solution)/shard_map/ct,dc->td/dot_general | solution.py:758
  335.1 2.7 dynamic-slice_convert_fusion
  342.5 12.2 %expert_weight.6 = (bf16[3,1024,256]{2,1,0:T(8,128)(2,1)}, bf16[3,1024,256]{2,1,0:T(8,128)(2,1)}) custom-call(bf16[256,1024]{1,0:T(8,128)(2,1)} %collective-permute-done.13.refs_0_.refs_18_, bf16[256,1024]{1,0:T(8,128)(2,1)} %collective-permute-done.14.refs_1_.refs_19_, bf16[256,1152]{1,0:T(8,128)(2,1)} %copy-done.26, bf16[256,1152]{1,0:T(8,128)(2,1)} %copy-done.25, ...), custom_call_target="tpu_custom_call" | custom-call | flops 1073741824 | bytes 17825792 | tf_op jit(solution)/shard_map/expert_weight/pallas_call | solution.py:357
  355.1 4.6 %multiply_add_fusion = (f32[1024,512]{1,0:T(8,128)}, bf16[512]{0:T(512)(128)(2,1)S(1)}) fusion(f32[1024,1024]{1,0:T(8,128)} %get-tuple-element.551, s32[]{:T(128)S(6)} %select_n.179, bf16[1024,512]{1,0:T(8,128)(2,1)} %collective-permute-done.47, f32[1024,1024]{1,0:T(8,128)} %get-tuple-element.579, f32[1024]{0:T(1024)S(1)} %add_multiply_fusion, ...), kind=kLoop, calls=%fused_computation.15 | loop fusion | flops 5242368 | bytes 8399876 | tf_op jit(solution)/shard_map/add | solution.py:857
  360.9 1.6 convert_add_fusion.3
  363.8 1.7 collective-permute-start.50
  366.1 2.2 collective-permute-start.51
  368.4 6.9 %collective-permute-done.51 = bf16[64,1024]{1,0:T(8,128)(2,1)S(1)} collective-permute-done((bf16[64,1024]{1,0:T(8,128)(2,1)S(1)}, bf16[64,1024]{1,0:T(8,128)(2,1)S(1)}, u32[]{:S(2)}, u32[]{:S(2)}) %collective-permute-start.51) | collective-permute-done | bytes 131104 | tf_op jit(solution)/shard_map/ppermute | solution.py:778
  375.7 2.4 collective-permute-start.53
  378.0 2.0 add_convert_fusion
  381.2 3.6 collective-permute-done.53
  389.7 1.6 collective-permute-start.57
  394.5 4.4 collective-permute-done.55
  398.8 12.2 %expert_weight.7 = (bf16[3,1024,256]{2,1,0:T(8,128)(2,1)}, bf16[3,1024,256]{2,1,0:T(8,128)(2,1)}) custom-call(bf16[256,1024]{1,0:T(8,128)(2,1)} %copy-done.4, bf16[256,1024]{1,0:T(8,128)(2,1)} %copy-done.5, bf16[512,1152]{1,0:T(8,128)(2,1)} %copy-done.2, bf16[512,1152]{1,0:T(8,128)(2,1)} %copy-done.2, bf16[512,1024]{1,0:T(8,128)(2,1)} %get-tuple-element.471.refs_4_, ...), custom_call_target="tpu_custom_call" | custom-call | flops 1073741824 | bytes 17825792 | tf_op jit(solution)/shard_map/expert_weight/pallas_call | solution.py:357
  411.1 7.7 %collective-permute-done.60 = bf16[1024,256]{1,0:T(8,128)(2,1)} collective-permute-done((bf16[1024,256]{1,0:T(8,128)(2,1)S(1)}, bf16[1024,256]{1,0:T(8,128)(2,1)}, u32[]{:S(2)}, u32[]{:S(2)}) %collective-permute-start.60) | collective-permute-done | bytes 524320 | tf_op jit(solution)/shard_map/ppermute | solution.py:557
  420.6 1.7 collective-permute-start.64
  425.2 4.3 collective-permute-done.65.refs_7_
  429.6 5.5 %collective-permute-done.64.refs_6_ = bf16[272,512]{1,0:T(8,128)(2,1)S(1)} collective-permute-done((bf16[272,512]{1,0:T(8,128)(2,1)S(1)}, bf16[272,512]{1,0:T(8,128)(2,1)S(1)}, u32[]{:S(2)}, u32[]{:S(2)}) %collective-permute-start.64) | collective-permute-done | bytes 278560 | tf_op jit(solution)/shard_map/ppermute | solution.py:553
  435.2 4.1 lay_out.1
  440.6 1.8 convert_add_fusion
  442.4 2.9 fusion.5
  (329 shorter events, 84.0 us)
Async XLA Ops:
  4.5 39.8 %collective-permute-start.5 = (bf16[3,1024,256]{2,1,0:T(8,128)(2,1)}, bf16[3,1024,256]{2,1,0:T(8,128)(2,1)}, u32[]{:S(2)}, u32[]{:S(2)}) collective-permute-start(bf16[3,1024,256]{2,1,0:T(8,128)(2,1)} %pad_maximum_fusion.1.refs_4_), channel_id=1, source_target_pairs={{0,8},{2,10},{4,12},{6,14},{8,16},{10,18},{12,20},{14,22},{16,24},... | collective-permute-start | bytes 4718600 | tf_op jit(solution)/shard_map/ppermute | solution.py:557
  7.5 36.7 %collective-permute-start.3 = (bf16[3,1024,256]{2,1,0:T(8,128)(2,1)}, bf16[3,1024,256]{2,1,0:T(8,128)(2,1)}, u32[]{:S(2)}, u32[]{:S(2)}) collective-permute-start(bf16[3,1024,256]{2,1,0:T(8,128)(2,1)} %pad_maximum_fusion.1.refs_4_), channel_id=1, source_target_pairs={{0,1},{1,0},{2,3},{3,2},{4,5},{5,4},{6,7},{7,6},{8,9},{9,8},{10,11... | collective-permute-start | bytes 4718600 | tf_op jit(solution)/shard_map/ppermute | solution.py:549
  10.9 32.3 %collective-permute-start.4 = (bf16[512,1024]{1,0:T(8,128)(2,1)S(1)}, bf16[512,1024]{1,0:T(8,128)(2,1)}, u32[]{:S(2)}, u32[]{:S(2)}) collective-permute-start(bf16[512,1024]{1,0:T(8,128)(2,1)S(1)} %copy-done.6), channel_id=1, source_target_pairs={{0,1},{1,0},{2,3},{3,2},{4,5},{5,4},{6,7},{7,6},{8,9},{9,8},{10,11... | collective-permute-start | bytes 3145736 | tf_op jit(solution)/shard_map/ppermute | solution.py:549
  19.0 28.4 %collective-permute-start.2 = (bf16[512,1152]{1,0:T(8,128)(2,1)S(1)}, bf16[512,1152]{1,0:T(8,128)(2,1)S(1)}, u32[]{:S(2)}, u32[]{:S(2)}) collective-permute-start(bf16[512,1152]{1,0:T(8,128)(2,1)S(1)} %concatenate.81.refs_2_.refs_3_.grad_ref.refs_20_.refs_21_), channel_id=1, source_target_pairs={{0,4},{2,6},{4,0},{6,2},{8,12},{10,14},{12,8},{14,10},{16,20},{18,... | collective-permute-start | bytes 3538952 | tf_op jit(solution)/shard_map/ppermute | solution.py:553
  20.6 28.0 %collective-permute-start.1 = (bf16[512,1152]{1,0:T(8,128)(2,1)S(1)}, bf16[512,1152]{1,0:T(8,128)(2,1)S(1)}, u32[]{:S(2)}, u32[]{:S(2)}) collective-permute-start(bf16[512,1152]{1,0:T(8,128)(2,1)S(1)} %concatenate.81.refs_2_.refs_3_.grad_ref.refs_20_.refs_21_), channel_id=1, source_target_pairs={{0,2},{2,0},{4,6},{6,4},{8,10},{10,8},{12,14},{14,12},{16,18},{18,... | collective-permute-start | bytes 3538952 | tf_op jit(solution)/shard_map/ppermute | solution.py:553
  48.6 30.3 %collective-permute-start.6 = (bf16[3,1024,256]{2,1,0:T(8,128)(2,1)}, bf16[3,1024,256]{2,1,0:T(8,128)(2,1)S(1)}, u32[]{:S(2)}, u32[]{:S(2)}) collective-permute-start(bf16[3,1024,256]{2,1,0:T(8,128)(2,1)} %collective-permute-done.5.refs_6_), channel_id=1, source_target_pairs={{0,1},{1,0},{2,3},{3,2},{4,5},{5,4},{6,7},{7,6},{8,9},{9,8},{10,11... | collective-permute-start | bytes 4718600 | tf_op jit(solution)/shard_map/ppermute | solution.py:549
  48.6 50.4 %collective-permute-start.12 = (bf16[3,1024,256]{2,1,0:T(8,128)(2,1)}, bf16[3,1024,256]{2,1,0:T(8,128)(2,1)}, u32[]{:S(2)}, u32[]{:S(2)}) collective-permute-start(bf16[3,1024,256]{2,1,0:T(8,128)(2,1)} %collective-permute-done.5.refs_6_), channel_id=1, source_target_pairs={{0,8},{2,10},{4,12},{6,14},{8,16},{10,18},{12,20},{14,22},{16,24},... | collective-permute-start | bytes 4718600 | tf_op jit(solution)/shard_map/ppermute | solution.py:557
  62.1 15.6 %collective-permute-start.9 = (bf16[256,1152]{1,0:T(8,128)(2,1)S(1)}, bf16[256,1152]{1,0:T(8,128)(2,1)S(1)}, u32[]{:S(2)}, u32[]{:S(2)}) collective-permute-start(bf16[256,1152]{1,0:T(8,128)(2,1)S(1)} %slice.91), channel_id=1, source_target_pairs={{0,2},{2,0},{4,6},{6,4},{8,10},{10,8},{12,14},{14,12},{16,18},{18,... | collective-permute-start | bytes 1769480 | tf_op jit(solution)/shard_map/ppermute | solution.py:553
  63.7 15.2 %collective-permute-start.8 = (bf16[256,1152]{1,0:T(8,128)(2,1)S(1)}, bf16[256,1152]{1,0:T(8,128)(2,1)S(1)}, u32[]{:S(2)}, u32[]{:S(2)}) collective-permute-start(bf16[256,1152]{1,0:T(8,128)(2,1)S(1)} %slice.90), channel_id=1, source_target_pairs={{0,4},{2,6},{4,0},{6,2},{8,12},{10,14},{12,8},{14,10},{16,20},{18,... | collective-permute-start | bytes 1769480 | tf_op jit(solution)/shard_map/ppermute | solution.py:553
  80.1 18.9 %collective-permute-start.10 = (bf16[256,1024]{1,0:T(8,128)(2,1)S(1)}, bf16[256,1024]{1,0:T(8,128)(2,1)}, u32[]{:S(2)}, u32[]{:S(2)}) collective-permute-start(bf16[256,1024]{1,0:T(8,128)(2,1)S(1)} %get-tuple-element.271.refs_0_.refs_18_), channel_id=1, source_target_pairs={{0,2},{2,0},{4,6},{6,4},{8,10},{10,8},{12,14},{14,12},{16,18},{18,... | collective-permute-start | bytes 1572872 | tf_op jit(solution)/shard_map/ppermute | solution.py:553
  80.7 18.4 %collective-permute-start.11 = (bf16[256,1024]{1,0:T(8,128)(2,1)S(1)}, bf16[256,1024]{1,0:T(8,128)(2,1)}, u32[]{:S(2)}, u32[]{:S(2)}) collective-permute-start(bf16[256,1024]{1,0:T(8,128)(2,1)S(1)} %get-tuple-element.272.refs_1_.refs_19_), channel_id=1, source_target_pairs={{0,4},{2,6},{4,0},{6,2},{8,12},{10,14},{12,8},{14,10},{16,20},{18,... | collective-permute-start | bytes 1572872 | tf_op jit(solution)/shard_map/ppermute | solution.py:553
  99.1 56.4 %collective-permute-start.18 = (bf16[3,1024,256]{2,1,0:T(8,128)(2,1)}, bf16[3,1024,256]{2,1,0:T(8,128)(2,1)S(1)}, u32[]{:S(2)}, u32[]{:S(2)}) collective-permute-start(bf16[3,1024,256]{2,1,0:T(8,128)(2,1)} %collective-permute-done.12.refs_4_), channel_id=1, source_target_pairs={{0,8},{2,10},{4,12},{6,14},{8,16},{10,18},{12,20},{14,22},{16,24},... | collective-permute-start | bytes 4718600 | tf_op jit(solution)/shard_map/ppermute | solution.py:557
  99.1 16.9 %collective-permute-start.16 = (bf16[256,1024]{1,0:T(8,128)(2,1)}, bf16[256,1024]{1,0:T(8,128)(2,1)S(1)}, u32[]{:S(2)}, u32[]{:S(2)}) collective-permute-start(bf16[256,1024]{1,0:T(8,128)(2,1)} %copy-done.4), channel_id=1, source_target_pairs={{0,4},{2,6},{4,0},{6,2},{8,12},{10,14},{12,8},{14,10},{16,20},{18,... | collective-permute-start | bytes 1572872 | tf_op jit(solution)/shard_map/ppermute | solution.py:553
  99.6 16.4 %collective-permute-start.15 = (bf16[256,1024]{1,0:T(8,128)(2,1)}, bf16[256,1024]{1,0:T(8,128)(2,1)S(1)}, u32[]{:S(2)}, u32[]{:S(2)}) collective-permute-start(bf16[256,1024]{1,0:T(8,128)(2,1)} %copy-done.5), channel_id=1, source_target_pairs={{0,2},{2,0},{4,6},{6,4},{8,10},{10,8},{12,14},{14,12},{16,18},{18,... | collective-permute-start | bytes 1572872 | tf_op jit(solution)/shard_map/ppermute | solution.py:553
  101.1 28.7 %collective-permute-start.13 = (bf16[256,1024]{1,0:T(8,128)(2,1)}, bf16[256,1024]{1,0:T(8,128)(2,1)}, u32[]{:S(2)}, u32[]{:S(2)}) collective-permute-start(bf16[256,1024]{1,0:T(8,128)(2,1)} %collective-permute-done.10.refs_0_.refs_6_), channel_id=1, source_target_pairs={{0,4},{2,6},{4,0},{6,2},{8,12},{10,14},{12,8},{14,10},{16,20},{18,... | collective-permute-start | bytes 1572872 | tf_op jit(solution)/shard_map/ppermute | solution.py:553
  102.7 27.2 %collective-permute-start.14 = (bf16[256,1024]{1,0:T(8,128)(2,1)}, bf16[256,1024]{1,0:T(8,128)(2,1)}, u32[]{:S(2)}, u32[]{:S(2)}) collective-permute-start(bf16[256,1024]{1,0:T(8,128)(2,1)} %collective-permute-done.11.refs_1_.refs_7_), channel_id=1, source_target_pairs={{0,2},{2,0},{4,6},{6,4},{8,10},{10,8},{12,14},{14,12},{16,18},{18,... | collective-permute-start | bytes 1572872 | tf_op jit(solution)/shard_map/ppermute | solution.py:553
  116.0 39.7 %collective-permute-start.17 = (bf16[3,1024,256]{2,1,0:T(8,128)(2,1)}, bf16[3,1024,256]{2,1,0:T(8,128)(2,1)}, u32[]{:S(2)}, u32[]{:S(2)}) collective-permute-start(bf16[3,1024,256]{2,1,0:T(8,128)(2,1)} %collective-permute-done.12.refs_4_), channel_id=1, source_target_pairs={{0,1},{1,0},{2,3},{3,2},{4,5},{5,4},{6,7},{7,6},{8,9},{9,8},{10,11... | collective-permute-start | bytes 4718600 | tf_op jit(solution)/shard_map/ppermute | solution.py:549
  155.5 7.3 %collective-permute-start.19 = (bf16[3,1024,256]{2,1,0:T(8,128)(2,1)S(1)}, bf16[3,1024,256]{2,1,0:T(8,128)(2,1)S(1)}, u32[]{:S(2)}, u32[]{:S(2)}) collective-permute-start(bf16[3,1024,256]{2,1,0:T(8,128)(2,1)S(1)} %collective-permute-done.18.refs_6_), channel_id=1, source_target_pairs={{0,1},{1,0},{2,3},{3,2},{4,5},{5,4},{6,7},{7,6},{8,9},{9,8},{10,11... | collective-permute-start | bytes 4718600 | tf_op jit(solution)/shard_map/ppermute | solution.py:549
  178.5 18.4 %collective-permute-start.21 = (bf16[256,1152]{1,0:T(8,128)(2,1)}, bf16[256,1152]{1,0:T(8,128)(2,1)S(1)}, u32[]{:S(2)}, u32[]{:S(2)}) collective-permute-start(bf16[256,1152]{1,0:T(8,128)(2,1)} %get-tuple-element.317), channel_id=1, source_target_pairs={{0,2},{2,0},{4,6},{6,4},{8,10},{10,8},{12,14},{14,12},{16,18},{18,... | collective-permute-start | bytes 1769480 | tf_op jit(solution)/shard_map/ppermute | solution.py:553
  180.1 16.8 %collective-permute-start.22 = (bf16[256,1152]{1,0:T(8,128)(2,1)}, bf16[256,1152]{1,0:T(8,128)(2,1)S(1)}, u32[]{:S(2)}, u32[]{:S(2)}) collective-permute-start(bf16[256,1152]{1,0:T(8,128)(2,1)} %get-tuple-element.318), channel_id=1, source_target_pairs={{0,4},{2,6},{4,0},{6,2},{8,12},{10,14},{12,8},{14,10},{16,20},{18,... | collective-permute-start | bytes 1769480 | tf_op jit(solution)/shard_map/ppermute | solution.py:553
  180.6 53.8 %collective-permute-start.27 = (bf16[3,1024,256]{2,1,0:T(8,128)(2,1)}, bf16[3,1024,256]{2,1,0:T(8,128)(2,1)}, u32[]{:S(2)}, u32[]{:S(2)}) collective-permute-start(bf16[3,1024,256]{2,1,0:T(8,128)(2,1)} %convert_add_fusion.1), channel_id=1, source_target_pairs={{0,8},{2,10},{4,12},{6,14},{8,16},{10,18},{12,20},{14,22},{16,24},... | collective-permute-start | bytes 4718600 | tf_op jit(solution)/shard_map/ppermute | solution.py:557
  196.9 19.8 %collective-permute-start.23 = (bf16[256,1152]{1,0:T(8,128)(2,1)}, bf16[256,1152]{1,0:T(8,128)(2,1)S(1)}, u32[]{:S(2)}, u32[]{:S(2)}) collective-permute-start(bf16[256,1152]{1,0:T(8,128)(2,1)} %get-tuple-element.327), channel_id=1, source_target_pairs={{0,2},{2,0},{4,6},{6,4},{8,10},{10,8},{12,14},{14,12},{16,18},{18,... | collective-permute-start | bytes 1769480 | tf_op jit(solution)/shard_map/ppermute | solution.py:553
  197.5 19.3 %collective-permute-start.24 = (bf16[256,1152]{1,0:T(8,128)(2,1)}, bf16[256,1152]{1,0:T(8,128)(2,1)S(1)}, u32[]{:S(2)}, u32[]{:S(2)}) collective-permute-start(bf16[256,1152]{1,0:T(8,128)(2,1)} %get-tuple-element.328), channel_id=1, source_target_pairs={{0,4},{2,6},{4,0},{6,2},{8,12},{10,14},{12,8},{14,10},{16,20},{18,... | collective-permute-start | bytes 1769480 | tf_op jit(solution)/shard_map/ppermute | solution.py:553
  217.6 16.8 %collective-permute-start.25 = (bf16[256,1152]{1,0:T(8,128)(2,1)}, bf16[256,1152]{1,0:T(8,128)(2,1)}, u32[]{:S(2)}, u32[]{:S(2)}) collective-permute-start(bf16[256,1152]{1,0:T(8,128)(2,1)} %add_convert_fusion.3), channel_id=1, source_target_pairs={{0,2},{2,0},{4,6},{6,4},{8,10},{10,8},{12,14},{14,12},{16,18},{18,... | collective-permute-start | bytes 1769480 | tf_op jit(solution)/shard_map/ppermute | solution.py:553
  219.1 15.3 %collective-permute-start.26 = (bf16[256,1152]{1,0:T(8,128)(2,1)}, bf16[256,1152]{1,0:T(8,128)(2,1)}, u32[]{:S(2)}, u32[]{:S(2)}) collective-permute-start(bf16[256,1152]{1,0:T(8,128)(2,1)} %add_convert_fusion.2), channel_id=1, source_target_pairs={{0,4},{2,6},{4,0},{6,2},{8,12},{10,14},{12,8},{14,10},{16,20},{18,... | collective-permute-start | bytes 1769480 | tf_op jit(solution)/shard_map/ppermute | solution.py:553
  240.1 14.2 %collective-permute-start.28 = (bf16[512,1024]{1,0:T(8,128)(2,1)}, bf16[512,1024]{1,0:T(8,128)(2,1)S(1)}, u32[]{:S(2)}, u32[]{:S(2)}) collective-permute-start(bf16[512,1024]{1,0:T(8,128)(2,1)} %get-tuple-element.358), channel_id=1, source_target_pairs={{0,1},{1,0},{2,3},{3,2},{4,5},{5,4},{6,7},{7,6},{8,9},{9,8},{10,11... | collective-permute-start | bytes 3145736 | tf_op jit(solution)/shard_map/ppermute | solution.py:549
  240.1 18.1 %collective-permute-start.29 = (bf16[256,1024]{1,0:T(8,128)(2,1)}, bf16[256,1024]{1,0:T(8,128)(2,1)S(1)}, u32[]{:S(2)}, u32[]{:S(2)}) collective-permute-start(bf16[256,1024]{1,0:T(8,128)(2,1)} %get-tuple-element.370), channel_id=1, source_target_pairs={{0,2},{2,0},{4,6},{6,4},{8,10},{10,8},{12,14},{14,12},{16,18},{18,... | collective-permute-start | bytes 1572872 | tf_op jit(solution)/shard_map/ppermute | solution.py:553
  240.6 17.6 %collective-permute-start.30 = (bf16[256,1024]{1,0:T(8,128)(2,1)}, bf16[256,1024]{1,0:T(8,128)(2,1)S(1)}, u32[]{:S(2)}, u32[]{:S(2)}) collective-permute-start(bf16[256,1024]{1,0:T(8,128)(2,1)} %get-tuple-element.371), channel_id=1, source_target_pairs={{0,4},{2,6},{4,0},{6,2},{8,12},{10,14},{12,8},{14,10},{16,20},{18,... | collective-permute-start | bytes 1572872 | tf_op jit(solution)/shard_map/ppermute | solution.py:553
  258.3 16.7 %collective-permute-start.33 = (bf16[3,1024,256]{2,1,0:T(8,128)(2,1)}, bf16[3,1024,256]{2,1,0:T(8,128)(2,1)}, u32[]{:S(2)}, u32[]{:S(2)}) collective-permute-start(bf16[3,1024,256]{2,1,0:T(8,128)(2,1)} %get-tuple-element.378), channel_id=1, source_target_pairs={{0,1},{1,0},{2,3},{3,2},{4,5},{5,4},{6,7},{7,6},{8,9},{9,8},{10,11... | collective-permute-start | bytes 4718600 | tf_op jit(solution)/shard_map/ppermute | solution.py:549
  258.5 16.5 %collective-permute-start.31 = (bf16[256,1024]{1,0:T(8,128)(2,1)}, bf16[256,1024]{1,0:T(8,128)(2,1)S(1)}, u32[]{:S(2)}, u32[]{:S(2)}) collective-permute-start(bf16[256,1024]{1,0:T(8,128)(2,1)} %get-tuple-element.329), channel_id=1, source_target_pairs={{0,2},{2,0},{4,6},{6,4},{8,10},{10,8},{12,14},{14,12},{16,18},{18,... | collective-permute-start | bytes 1572872 | tf_op jit(solution)/shard_map/ppermute | solution.py:553
  260.0 15.0 %collective-permute-start.32 = (bf16[256,1024]{1,0:T(8,128)(2,1)}, bf16[256,1024]{1,0:T(8,128)(2,1)S(1)}, u32[]{:S(2)}, u32[]{:S(2)}) collective-permute-start(bf16[256,1024]{1,0:T(8,128)(2,1)} %get-tuple-element.330), channel_id=1, source_target_pairs={{0,4},{2,6},{4,0},{6,2},{8,12},{10,14},{12,8},{14,10},{16,20},{18,... | collective-permute-start | bytes 1572872 | tf_op jit(solution)/shard_map/ppermute | solution.py:553
  282.5 19.4 %collective-permute-start.38 = (bf16[1024,256]{1,0:T(8,128)(2,1)}, bf16[1024,256]{1,0:T(8,128)(2,1)S(1)}, u32[]{:S(2)}, u32[]{:S(2)}) collective-permute-start(bf16[1024,256]{1,0:T(8,128)(2,1)} %get-tuple-element.560), channel_id=1, source_target_pairs={{0,8},{2,10},{4,12},{6,14},{8,16},{10,18},{12,20},{14,22},{16,24},... | collective-permute-start | bytes 1572872 | tf_op jit(solution)/shard_map/ppermute | solution.py:557
  282.8 27.8 %collective-permute-start.37 = (bf16[1024,256]{1,0:T(8,128)(2,1)S(1)}, bf16[1024,256]{1,0:T(8,128)(2,1)S(1)}, u32[]{:S(2)}, u32[]{:S(2)}) collective-permute-start(bf16[1024,256]{1,0:T(8,128)(2,1)S(1)} %get-tuple-element.561), channel_id=1, source_target_pairs={{0,8},{2,10},{4,12},{6,14},{8,16},{10,18},{12,20},{14,22},{16,24},... | collective-permute-start | bytes 1572872 | tf_op jit(solution)/shard_map/ppermute | solution.py:557
  286.2 24.3 %collective-permute-start.36 = (bf16[256,1024]{1,0:T(8,128)(2,1)S(1)}, bf16[256,1024]{1,0:T(8,128)(2,1)S(1)}, u32[]{:S(2)}, u32[]{:S(2)}) collective-permute-start(bf16[256,1024]{1,0:T(8,128)(2,1)S(1)} %get-tuple-element.553), channel_id=1, source_target_pairs={{0,6},{2,4},{4,2},{6,0},{8,14},{10,12},{12,10},{14,8},{16,22},{18,... | collective-permute-start | bytes 1572872 | tf_op jit(solution)/shard_map/ppermute | solution.py:553
  287.8 23.7 %collective-permute-start.35 = (bf16[256,1024]{1,0:T(8,128)(2,1)S(1)}, bf16[256,1024]{1,0:T(8,128)(2,1)S(1)}, u32[]{:S(2)}, u32[]{:S(2)}) collective-permute-start(bf16[256,1024]{1,0:T(8,128)(2,1)S(1)} %get-tuple-element.554), channel_id=1, source_target_pairs={{0,4},{2,6},{4,0},{6,2},{8,12},{10,14},{12,8},{14,10},{16,20},{18,... | collective-permute-start | bytes 1572872 | tf_op jit(solution)/shard_map/ppermute | solution.py:553
  288.3 23.2 %collective-permute-start.34 = (bf16[256,1024]{1,0:T(8,128)(2,1)S(1)}, bf16[256,1024]{1,0:T(8,128)(2,1)S(1)}, u32[]{:S(2)}, u32[]{:S(2)}) collective-permute-start(bf16[256,1024]{1,0:T(8,128)(2,1)S(1)} %get-tuple-element.555), channel_id=1, source_target_pairs={{0,2},{2,0},{4,6},{6,4},{8,10},{10,8},{12,14},{14,12},{16,18},{18,... | collective-permute-start | bytes 1572872 | tf_op jit(solution)/shard_map/ppermute | solution.py:553
  302.0 35.8 %collective-permute-start.43 = (bf16[1024,256]{1,0:T(8,128)(2,1)}, bf16[1024,256]{1,0:T(8,128)(2,1)S(1)}, u32[]{:S(2)}, u32[]{:S(2)}) collective-permute-start(bf16[1024,256]{1,0:T(8,128)(2,1)} %get-tuple-element.559), channel_id=1, source_target_pairs={{0,8},{2,10},{4,12},{6,14},{8,16},{10,18},{12,20},{14,22},{16,24},... | collective-permute-start | bytes 1572872 | tf_op jit(solution)/shard_map/ppermute | solution.py:557
  315.4 22.5 %collective-permute-start.42 = (bf16[128,1024]{1,0:T(8,128)(2,1)S(1)}, bf16[128,1024]{1,0:T(8,128)(2,1)S(1)}, u32[]{:S(2)}, u32[]{:S(2)}) collective-permute-start(bf16[128,1024]{1,0:T(8,128)(2,1)S(1)} %get-tuple-element.406), channel_id=1, source_target_pairs={{0,8},{2,10},{4,12},{6,14},{8,0},{10,2},{12,4},{14,6},{16,24},{18,... | collective-permute-start | bytes 786440 | tf_op jit(solution)/shard_map/ppermute | solution.py:778
  316.6 21.2 %collective-permute-start.41 = (bf16[256,512]{1,0:T(8,128)(2,1)}, bf16[256,512]{1,0:T(8,128)(2,1)S(1)}, u32[]{:S(2)}, u32[]{:S(2)}) collective-permute-start(bf16[256,512]{1,0:T(8,128)(2,1)} %get-tuple-element.564), channel_id=1, source_target_pairs={{0,6},{2,4},{4,2},{6,0},{8,14},{10,12},{12,10},{14,8},{16,22},{18,... | collective-permute-start | bytes 786440 | tf_op jit(solution)/shard_map/ppermute | solution.py:553
  318.0 19.8 %collective-permute-start.40 = (bf16[256,512]{1,0:T(8,128)(2,1)}, bf16[256,512]{1,0:T(8,128)(2,1)S(1)}, u32[]{:S(2)}, u32[]{:S(2)}) collective-permute-start(bf16[256,512]{1,0:T(8,128)(2,1)} %get-tuple-element.565), channel_id=1, source_target_pairs={{0,4},{2,6},{4,0},{6,2},{8,12},{10,14},{12,8},{14,10},{16,20},{18,... | collective-permute-start | bytes 786440 | tf_op jit(solution)/shard_map/ppermute | solution.py:553
  318.8 19.0 %collective-permute-start.39 = (bf16[256,512]{1,0:T(8,128)(2,1)S(1)}, bf16[256,512]{1,0:T(8,128)(2,1)S(1)}, u32[]{:S(2)}, u32[]{:S(2)}) collective-permute-start(bf16[256,512]{1,0:T(8,128)(2,1)S(1)} %get-tuple-element.566), channel_id=1, source_target_pairs={{0,2},{2,0},{4,6},{6,4},{8,10},{10,8},{12,14},{14,12},{16,18},{18,... | collective-permute-start | bytes 786440 | tf_op jit(solution)/shard_map/ppermute | solution.py:553
  338.7 16.0 %collective-permute-start.47 = (bf16[1024,512]{1,0:T(8,128)(2,1)}, bf16[1024,512]{1,0:T(8,128)(2,1)}, u32[]{:S(2)}, u32[]{:S(2)}) collective-permute-start(bf16[1024,512]{1,0:T(8,128)(2,1)} %dynamic-slice_convert_fusion), channel_id=1, source_target_pairs={{0,1},{1,0},{2,3},{3,2},{4,5},{5,4},{6,7},{7,6},{8,9},{9,8},{10,11... | collective-permute-start | bytes 3145736 | tf_op jit(solution)/shard_map/ppermute | solution.py:549
  338.8 15.9 %collective-permute-start.45 = (bf16[256,1024]{1,0:T(8,128)(2,1)}, bf16[256,1024]{1,0:T(8,128)(2,1)S(1)}, u32[]{:S(2)}, u32[]{:S(2)}) collective-permute-start(bf16[256,1024]{1,0:T(8,128)(2,1)} %add_convert_fusion.5), channel_id=1, source_target_pairs={{0,2},{2,0},{4,6},{6,4},{8,10},{10,8},{12,14},{14,12},{16,18},{18,... | collective-permute-start | bytes 1572872 | tf_op jit(solution)/shard_map/ppermute | solution.py:553
  339.6 15.2 %collective-permute-start.46 = (bf16[256,1024]{1,0:T(8,128)(2,1)}, bf16[256,1024]{1,0:T(8,128)(2,1)}, u32[]{:S(2)}, u32[]{:S(2)}) collective-permute-start(bf16[256,1024]{1,0:T(8,128)(2,1)} %add_convert_fusion.4), channel_id=1, source_target_pairs={{0,4},{2,6},{4,0},{6,2},{8,12},{10,14},{12,8},{14,10},{16,20},{18,... | collective-permute-start | bytes 1572872 | tf_op jit(solution)/shard_map/ppermute | solution.py:553
  340.8 13.9 %collective-permute-start.48 = (f32[1536]{0:T(1024)S(1)}, f32[1536]{0:T(1024)S(1)}, u32[]{:S(2)}, u32[]{:S(2)}) collective-permute-start(f32[1536]{0:T(1024)S(1)} %pad_maximum_fusion.7), channel_id=1, source_target_pairs={{0,1},{1,0},{2,3},{3,2},{4,5},{5,4},{6,7},{7,6},{8,9},{9,8},{10,11... | collective-permute-start | bytes 18440 | tf_op jit(solution)/shard_map/ppermute | solution.py:549
  340.8 13.9 %collective-permute-start.44 = (bf16[64,1024]{1,0:T(8,128)(2,1)}, bf16[64,1024]{1,0:T(8,128)(2,1)}, u32[]{:S(2)}, u32[]{:S(2)}) collective-permute-start(bf16[64,1024]{1,0:T(8,128)(2,1)} %get-tuple-element.423), channel_id=1, source_target_pairs={{0,16},{2,18},{4,20},{6,22},{8,24},{10,26},{12,28},{14,30},{16,0},... | collective-permute-start | bytes 393224 | tf_op jit(solution)/shard_map/ppermute | solution.py:778
  354.7 9.1 %collective-permute-start.49 = (bf16[3,1024,256]{2,1,0:T(8,128)(2,1)}, bf16[3,1024,256]{2,1,0:T(8,128)(2,1)}, u32[]{:S(2)}, u32[]{:S(2)}) collective-permute-start(bf16[3,1024,256]{2,1,0:T(8,128)(2,1)} %get-tuple-element.446), channel_id=1, source_target_pairs={{0,1},{1,0},{2,3},{3,2},{4,5},{5,4},{6,7},{7,6},{8,9},{9,8},{10,11... | collective-permute-start | bytes 4718600 | tf_op jit(solution)/shard_map/ppermute | solution.py:549
  363.8 11.6 %collective-permute-start.50 = (bf16[144,512]{1,0:T(8,128)(2,1)S(1)}, bf16[144,512]{1,0:T(8,128)(2,1)S(1)}, u32[]{:S(2)}, u32[]{:S(2)}) collective-permute-start(bf16[144,512]{1,0:T(8,128)(2,1)S(1)} %pad_maximum_fusion.5), channel_id=1, source_target_pairs={{0,8},{2,10},{4,12},{6,14},{8,0},{10,2},{12,4},{14,6},{16,24},{18,... | collective-permute-start | bytes 442376 | tf_op jit(solution)/shard_map/ppermute | solution.py:778
  366.1 9.3 %collective-permute-start.51 = (bf16[64,1024]{1,0:T(8,128)(2,1)S(1)}, bf16[64,1024]{1,0:T(8,128)(2,1)S(1)}, u32[]{:S(2)}, u32[]{:S(2)}) collective-permute-start(bf16[64,1024]{1,0:T(8,128)(2,1)S(1)} %add_convert_fusion.10), channel_id=1, source_target_pairs={{0,16},{2,18},{4,20},{6,22},{8,24},{10,26},{12,28},{14,30},{16,0},... | collective-permute-start | bytes 393224 | tf_op jit(solution)/shard_map/ppermute | solution.py:778
  368.4 18.0 %collective-permute-start.56 = (bf16[512,512]{1,0:T(8,128)(2,1)S(1)}, bf16[512,512]{1,0:T(8,128)(2,1)S(1)}, u32[]{:S(2)}, u32[]{:S(2)}) collective-permute-start(bf16[512,512]{1,0:T(8,128)(2,1)S(1)} %get-tuple-element.563), channel_id=1, source_target_pairs={{0,1},{1,0},{2,3},{3,2},{4,5},{5,4},{6,7},{7,6},{8,9},{9,8},{10,11... | collective-permute-start | bytes 1572872 | tf_op jit(solution)/shard_map/ppermute | solution.py:549
  375.5 5.7 %collective-permute-start.52 = (bf16[80,512]{1,0:T(8,128)(2,1)S(1)}, bf16[80,512]{1,0:T(8,128)(2,1)S(1)}, u32[]{:S(2)}, u32[]{:S(2)}) collective-permute-start(bf16[80,512]{1,0:T(8,128)(2,1)S(1)} %pad_maximum_fusion.6), channel_id=1, source_target_pairs={{0,16},{2,18},{4,20},{6,22},{8,24},{10,26},{12,28},{14,30},{16,0},... | collective-permute-start | bytes 245768 | tf_op jit(solution)/shard_map/ppermute | solution.py:778
  375.7 9.2 %collective-permute-start.53 = (bf16[128,1024]{1,0:T(8,128)(2,1)S(1)}, bf16[128,1024]{1,0:T(8,128)(2,1)S(1)}, u32[]{:S(2)}, u32[]{:S(2)}) collective-permute-start(bf16[128,1024]{1,0:T(8,128)(2,1)S(1)} %maximum_select_fusion.4), channel_id=1, source_target_pairs={{0,8},{2,10},{4,12},{6,14},{8,0},{10,2},{12,4},{14,6},{16,24},{18,... | collective-permute-start | bytes 786440 | tf_op jit(solution)/shard_map/ppermute | solution.py:778
  385.0 6.3 %collective-permute-start.54 = (bf16[64,512]{1,0:T(8,128)(2,1)S(1)}, bf16[64,512]{1,0:T(8,128)(2,1)S(1)}, u32[]{:S(2)}, u32[]{:S(2)}) collective-permute-start(bf16[64,512]{1,0:T(8,128)(2,1)S(1)} %add_convert_fusion.11), channel_id=1, source_target_pairs={{0,16},{2,18},{4,20},{6,22},{8,24},{10,26},{12,28},{14,30},{16,0},... | collective-permute-start | bytes 196616 | tf_op jit(solution)/shard_map/ppermute | solution.py:778
  387.8 31.0 %collective-permute-start.59 = (bf16[256,1024]{1,0:T(8,128)(2,1)S(1)}, bf16[256,1024]{1,0:T(8,128)(2,1)S(1)}, u32[]{:S(2)}, u32[]{:S(2)}) collective-permute-start(bf16[256,1024]{1,0:T(8,128)(2,1)S(1)} %maximum_select_fusion.3.refs_0_), channel_id=1, source_target_pairs={{0,6},{2,4},{4,2},{6,0},{8,14},{10,12},{12,10},{14,8},{16,22},{18,... | collective-permute-start | bytes 1572872 | tf_op jit(solution)/shard_map/ppermute | solution.py:553
  389.3 29.5 %collective-permute-start.58 = (bf16[256,1024]{1,0:T(8,128)(2,1)S(1)}, bf16[256,1024]{1,0:T(8,128)(2,1)S(1)}, u32[]{:S(2)}, u32[]{:S(2)}) collective-permute-start(bf16[256,1024]{1,0:T(8,128)(2,1)S(1)} %maximum_select_fusion.3.refs_0_), channel_id=1, source_target_pairs={{0,4},{2,6},{4,0},{6,2},{8,12},{10,14},{12,8},{14,10},{16,20},{18,... | collective-permute-start | bytes 1572872 | tf_op jit(solution)/shard_map/ppermute | solution.py:553
  389.7 29.1 %collective-permute-start.57 = (bf16[256,1024]{1,0:T(8,128)(2,1)S(1)}, bf16[256,1024]{1,0:T(8,128)(2,1)S(1)}, u32[]{:S(2)}, u32[]{:S(2)}) collective-permute-start(bf16[256,1024]{1,0:T(8,128)(2,1)S(1)} %maximum_select_fusion.3.refs_0_), channel_id=1, source_target_pairs={{0,2},{2,0},{4,6},{6,4},{8,10},{10,8},{12,14},{14,12},{16,18},{18,... | collective-permute-start | bytes 1572872 | tf_op jit(solution)/shard_map/ppermute | solution.py:553
  391.3 7.5 %collective-permute-start.55 = (bf16[128,512]{1,0:T(8,128)(2,1)S(1)}, bf16[128,512]{1,0:T(8,128)(2,1)S(1)}, u32[]{:S(2)}, u32[]{:S(2)}) collective-permute-start(bf16[128,512]{1,0:T(8,128)(2,1)S(1)} %maximum_select_fusion.6), channel_id=1, source_target_pairs={{0,8},{2,10},{4,12},{6,14},{8,0},{10,2},{12,4},{14,6},{16,24},{18,... | collective-permute-start | bytes 393224 | tf_op jit(solution)/shard_map/ppermute | solution.py:778
  393.1 18.0 %collective-permute-start.61 = (bf16[1024,256]{1,0:T(8,128)(2,1)}, bf16[1024,256]{1,0:T(8,128)(2,1)}, u32[]{:S(2)}, u32[]{:S(2)}) collective-permute-start(bf16[1024,256]{1,0:T(8,128)(2,1)} %get-tuple-element.557), channel_id=1, source_target_pairs={{0,8},{2,10},{4,12},{6,14},{8,16},{10,18},{12,20},{14,22},{16,24},... | collective-permute-start | bytes 1572872 | tf_op jit(solution)/shard_map/ppermute | solution.py:557
  398.8 20.0 %collective-permute-start.60 = (bf16[1024,256]{1,0:T(8,128)(2,1)S(1)}, bf16[1024,256]{1,0:T(8,128)(2,1)}, u32[]{:S(2)}, u32[]{:S(2)}) collective-permute-start(bf16[1024,256]{1,0:T(8,128)(2,1)S(1)} %get-tuple-element.558), channel_id=1, source_target_pairs={{0,8},{2,10},{4,12},{6,14},{8,16},{10,18},{12,20},{14,22},{16,24},... | collective-permute-start | bytes 1572872 | tf_op jit(solution)/shard_map/ppermute | solution.py:557
  418.8 21.8 %collective-permute-start.66 = (bf16[3,1024,256]{2,1,0:T(8,128)(2,1)}, bf16[3,1024,256]{2,1,0:T(8,128)(2,1)}, u32[]{:S(2)}, u32[]{:S(2)}) collective-permute-start(bf16[3,1024,256]{2,1,0:T(8,128)(2,1)} %get-tuple-element.493), channel_id=1, source_target_pairs={{0,1},{1,0},{2,3},{3,2},{4,5},{5,4},{6,7},{7,6},{8,9},{9,8},{10,11... | collective-permute-start | bytes 4718600 | tf_op jit(solution)/shard_map/ppermute | solution.py:549
  419.1 10.5 %collective-permute-start.65 = (bf16[272,512]{1,0:T(8,128)(2,1)S(1)}, bf16[272,512]{1,0:T(8,128)(2,1)S(1)}, u32[]{:S(2)}, u32[]{:S(2)}) collective-permute-start(bf16[272,512]{1,0:T(8,128)(2,1)S(1)} %pad_maximum_fusion.4.refs_4_), channel_id=1, source_target_pairs={{0,6},{2,4},{4,2},{6,0},{8,14},{10,12},{12,10},{14,8},{16,22},{18,... | collective-permute-start | bytes 835592 | tf_op jit(solution)/shard_map/ppermute | solution.py:553
  420.6 14.5 %collective-permute-start.64 = (bf16[272,512]{1,0:T(8,128)(2,1)S(1)}, bf16[272,512]{1,0:T(8,128)(2,1)S(1)}, u32[]{:S(2)}, u32[]{:S(2)}) collective-permute-start(bf16[272,512]{1,0:T(8,128)(2,1)S(1)} %pad_maximum_fusion.4.refs_4_), channel_id=1, source_target_pairs={{0,4},{2,6},{4,0},{6,2},{8,12},{10,14},{12,8},{14,10},{16,20},{18,... | collective-permute-start | bytes 835592 | tf_op jit(solution)/shard_map/ppermute | solution.py:553
  422.4 12.8 %collective-permute-start.63 = (bf16[272,512]{1,0:T(8,128)(2,1)S(1)}, bf16[272,512]{1,0:T(8,128)(2,1)}, u32[]{:S(2)}, u32[]{:S(2)}) collective-permute-start(bf16[272,512]{1,0:T(8,128)(2,1)S(1)} %pad_maximum_fusion.4.refs_4_), channel_id=1, source_target_pairs={{0,2},{2,0},{4,6},{6,4},{8,10},{10,8},{12,14},{14,12},{16,18},{18,... | collective-permute-start | bytes 835592 | tf_op jit(solution)/shard_map/ppermute | solution.py:553
  425.2 17.1 %collective-permute-start.67 = (bf16[1024,256]{1,0:T(8,128)(2,1)}, bf16[1024,256]{1,0:T(8,128)(2,1)S(1)}, u32[]{:S(2)}, u32[]{:S(2)}) collective-permute-start(bf16[1024,256]{1,0:T(8,128)(2,1)} %get-tuple-element.556), channel_id=1, source_target_pairs={{0,8},{2,10},{4,12},{6,14},{8,16},{10,18},{12,20},{14,22},{16,24},... | collective-permute-start | bytes 1572872 | tf_op jit(solution)/shard_map/ppermute | solution.py:557
  (72 other events, 428.2 us)

commit v4 on v3

--- a/solution.py
+++ b/solution.py
@@ -112,32 +112,7 @@
     )
 
 
-def attn_forward(q_t, k_t, v_t, cos_t, sin_t, start):
-    n = q_t.shape[1]
-    hd = HEAD_SIZE
-    kv = k_t.shape[0] // hd
-    block = min(256, n)
-    pair = pl.BlockSpec((2 * hd, n), lambda h: (h, 0))
-    one = pl.BlockSpec((hd, n), lambda h: (h, 0))
-    table = pl.BlockSpec((hd // 2, n), lambda h: (0, 0))
-    return pl.pallas_call(
-        functools.partial(attn_fwd_kernel, block),
-        grid=(kv,),
-        in_specs=[pair, one, one, table, table, pl.BlockSpec((1, n), lambda h: (0, 0))],
-        out_specs=[pair, one, pair, pl.BlockSpec((1, 2, n), lambda h: (h, 0, 0))],
-        out_shape=[
-            jax.ShapeDtypeStruct(q_t.shape, BF16),
-            jax.ShapeDtypeStruct(k_t.shape, BF16),
-            jax.ShapeDtypeStruct(q_t.shape, BF16),
-            jax.ShapeDtypeStruct((kv, 2, n), F32),
-        ],
-        compiler_params=pltpu.CompilerParams(vmem_limit_bytes=48 * 2**20),
-        cost_estimate=attn_cost(2 * kv, n, 4),
-        name="attn_forward",
-    )(q_t, k_t, v_t, cos_t, sin_t, start)
-
-
-def attn_backward(q_t, k_t, v_t, do_t, lse, cos_t, sin_t, start, first, count):
+def attn_forward(q_t, k_t, v_t, cos_t, sin_t, start, first, count):
     n = q_t.shape[1]
     hd = HEAD_SIZE
     block = min(256, n)
@@ -145,14 +120,33 @@
     one = pl.BlockSpec((hd, n), lambda h: (h + first, 0))
     table = pl.BlockSpec((hd // 2, n), lambda h: (0, 0))
     return pl.pallas_call(
+        functools.partial(attn_fwd_kernel, block),
+        grid=(count,),
+        in_specs=[pair, one, one, table, table, pl.BlockSpec((1, n), lambda h: (0, 0))],
+        out_specs=[pl.BlockSpec((r * hd, n), lambda h: (h, 0)) for r in (2, 1, 2)]
+        + [pl.BlockSpec((1, 2, n), lambda h: (h, 0, 0))],
+        out_shape=[jax.ShapeDtypeStruct((r * count * hd, n), BF16) for r in (2, 1, 2)]
+        + [jax.ShapeDtypeStruct((count, 2, n), F32)],
+        compiler_params=pltpu.CompilerParams(vmem_limit_bytes=48 * 2**20),
+        cost_estimate=attn_cost(2 * count, n, 4),
+        name="attn_forward",
+    )(q_t, k_t, v_t, cos_t, sin_t, start)
+
+
+def attn_backward(q_t, k_t, v_t, do_t, lse, cos_t, sin_t, start, first, count):
+    n = q_t.shape[1]
+    hd = HEAD_SIZE
+    block = min(256, n)
+    table = pl.BlockSpec((hd // 2, n), lambda h: (0, 0))
+    return pl.pallas_call(
         functools.partial(attn_bwd_kernel, block),
         grid=(count,),
         in_specs=[
-            pair,
-            one,
-            one,
-            pair,
-            pl.BlockSpec((1, 2, n), lambda h: (h + first, 0, 0)),
+            pl.BlockSpec((2 * hd, n), lambda h: (h, 0)),
+            pl.BlockSpec((hd, n), lambda h: (h, 0)),
+            pl.BlockSpec((hd, n), lambda h: (h + first, 0)),
+            pl.BlockSpec((2 * hd, n), lambda h: (h + first, 0)),
+            pl.BlockSpec((1, 2, n), lambda h: (h, 0, 0)),
             table,
             table,
             pl.BlockSpec((1, n), lambda h: (0, 0)),
@@ -390,19 +384,21 @@
             ref[...] = rows
 
 
-def join_heads(at, tokens, gain, os, ws, rows):
+def join_heads(at, tokens, gain, own, far, ws, rows):
     width = tokens.shape[1]
     half = rows // 2
-    heads = os[0].shape[0]
-    own = pl.BlockSpec((heads, half), lambda i, at: (0, at[0] * 2 + i))
-    o_specs = [own] + [pl.BlockSpec((heads, half), lambda i, at: (0, i))] * (len(os) - 1)
+    heads = own[0].shape[0]
+    n = len(ws)
+    o_specs = [pl.BlockSpec((heads, half), lambda i, at: (0, at[0] * 2 + i))] * len(own)
+    o_specs += [pl.BlockSpec((heads, half), lambda i, at: (0, i))] * len(far)
+    os = [*own, *far]
     if half % LANES:
-        os = [lax.dynamic_slice_in_dim(os[0], at[0] * rows, rows, 1)] + os[1:]
+        os = [lax.dynamic_slice_in_dim(o, at[0] * rows, rows, 1) for o in own] + far
         os = [jnp.stack([o[:, :half], o[:, half:]]) for o in os]
-        o_specs = [pl.BlockSpec((None, heads, half), lambda i, at: (i, 0, 0))] * len(os)
+        o_specs = [pl.BlockSpec((None, heads, half), lambda i, at: (i, 0, 0))] * n
     once = pl.BlockSpec((half, width), lambda i, at: (0, 0))
     return pl.pallas_call(
-        functools.partial(join_kernel, len(os)),
+        functools.partial(join_kernel, n),
         grid_spec=pltpu.PrefetchScalarGridSpec(
             num_scalar_prefetch=1,
             grid=(2,),
@@ -411,7 +407,7 @@
                 pl.BlockSpec((1, width), lambda i, at: (0, 0)),
             ]
             + o_specs
-            + [pl.BlockSpec((heads, width), lambda i, at: (0, 0))] * len(ws),
+            + [pl.BlockSpec((heads, width), lambda i, at, b=b: (b, 0)) for _, b in ws],
             out_specs=[pl.BlockSpec((half, width), lambda i, at: (i, 0)), once, once],
         ),
         out_shape=[
@@ -421,17 +417,62 @@
         ],
         compiler_params=pltpu.CompilerParams(vmem_limit_bytes=48 * 2**20),
         cost_estimate=pl.CostEstimate(
-            flops=2 * rows * heads * len(os) * width, bytes_accessed=rows * width * 8, transcendentals=0
+            flops=2 * rows * heads * n * width, bytes_accessed=rows * width * 8, transcendentals=0
         ),
         name="join_heads",
-    )(at, tokens, gain[None, :], *os, *ws)
-
-
-def turn_kernel(near_ref, xt_ref, yl_ref, xl_ref, yt_ref, mixed_ref, grad_ref, gain_ref, dy_ref, gates_ref, sum_ref):
+    )(at, tokens, gain[None, :], *os, *[w for w, _ in ws])
+
+
+def input_kernel(groups, n_tensor, at_ref, x_ref, gain_ref, *refs):
+    ds, ws = refs[: 3 * groups], refs[3 * groups : 3 * groups + 3]
+    own_ref, *fars, dots_ref, acc = refs[3 * groups + 3 :]
+    total = None
+    for j in range(3):
+        d = jnp.concatenate([ds[3 * i + j][...] for i in range(groups)], axis=0)
+        term = lax.dot_general(d, ws[j][...], (((0,), (1,)), ((), ())), preferred_element_type=F32)
+        total = term if total is None else total + term
+    acc[...] = total
+    normed = rms_parts(x_ref[...].astype(F32))[1]
+    dots_ref[...] = jnp.sum(total * gain_ref[...] * normed, axis=1, keepdims=True)
+    cols = own_ref.shape[1]
+    for s, ref in enumerate([own_ref, *fars]):
+        who = lax.rem(at_ref[0] + s, n_tensor)
+        ref[...] = acc[:, pl.ds(pl.multiple_of(who * cols, cols), cols)].astype(ref.dtype)
+
+
+def input_terms(at, tokens, gain, ds, ws, n_tensor):
+    n, width = tokens.shape
+    cols = width // n_tensor
+    tile = min(256, n)
+    flat = [d for group in ds for d in group]
+    return pl.pallas_call(
+        functools.partial(input_kernel, len(ds), n_tensor),
+        grid_spec=pltpu.PrefetchScalarGridSpec(
+            num_scalar_prefetch=1,
+            grid=(n // tile,),
+            in_specs=[pl.BlockSpec((tile, width), lambda i, at: (i, 0)), pl.BlockSpec((1, width), lambda i, at: (0, 0))]
+            + [pl.BlockSpec((d.shape[0], tile), lambda i, at: (0, i)) for d in flat]
+            + [pl.BlockSpec(w.shape, lambda i, at: (0, 0)) for w in ws],
+            out_specs=[pl.BlockSpec((tile, cols), lambda i, at: (i, 0))] * n_tensor
+            + [pl.BlockSpec((tile, 1), lambda i, at: (i, 0))],
+            scratch_shapes=[pltpu.VMEM((tile, width), F32)],
+        ),
+        out_shape=[jax.ShapeDtypeStruct((n, cols), F32)]
+        + [jax.ShapeDtypeStruct((n, cols), BF16)] * (n_tensor - 1)
+        + [jax.ShapeDtypeStruct((n, 1), F32)],
+        compiler_params=pltpu.CompilerParams(vmem_limit_bytes=48 * 2**20),
+        cost_estimate=pl.CostEstimate(
+            flops=2 * n * width * sum(w.shape[1] for w in ws), bytes_accessed=n * width * 8, transcendentals=0
+        ),
+        name="input_terms",
+    )(at, tokens, gain[None, :], *flat, *ws)
+
+
+def turn_kernel(top_ref, low_ref, xt_ref, yl_ref, xl_ref, yt_ref, mixed_ref, grad_ref, gain_ref, dy_ref, gates_ref, sum_ref):
     step = pl.program_id(0)
     width = mixed_ref.shape[1]
     upper = step == 0
-    back = near_ref[...].astype(F32)
+    back = jnp.where(upper, top_ref[...], low_ref[...]).astype(F32)
     back = back + jnp.where(upper, xt_ref[...], xl_ref[...]).astype(F32)
     back = back + jnp.where(upper, yt_ref[...], yl_ref[...]).astype(F32)
     gates_ref[...] = back[:, width:]
@@ -453,7 +494,7 @@
 
 def turn_back(near, halves, others, mixed, grad_wide, gain):
     rows, width = mixed.shape
-    half, full = rows // 2, near.shape[1]
+    half, full = rows // 2, near[0].shape[1]
 
     def spec(c):
         return pl.BlockSpec((half, c), lambda i: (i, 0))
@@ -463,7 +504,7 @@
     return pl.pallas_call(
         turn_kernel,
         grid=(2,),
-        in_specs=[spec(full)] + [const] * 4 + [spec(width), spec(width), line],
+        in_specs=[const] * 6 + [spec(width), spec(width), line],
         out_specs=[spec(width), spec(LANES), line],
         out_shape=[
             jax.ShapeDtypeStruct((rows, width), BF16),
@@ -473,7 +514,7 @@
         compiler_params=pltpu.CompilerParams(vmem_limit_bytes=48 * 2**20),
         cost_estimate=pl.CostEstimate(flops=0, bytes_accessed=rows * width * 16, transcendentals=0),
         name="turn_back",
-    )(near, *halves, *others, mixed, grad_wide, gain[None, :])
+    )(*near, *halves, *others, mixed, grad_wide, gain[None, :])
 
 
 def lay_out_kernel(halves, cuts, at_ref, *refs):
@@ -595,9 +636,14 @@
     pad = ((0, 0), (0, LANES // 2 - n_expert))
     high = lax.optimization_barrier(gates.astype(BF16))
     low = (gates - high.astype(F32)).astype(BF16)
-    grad_rows = to_rows(out_grad.astype(BF16))
-    grad_wide = jnp.concatenate([grad_rows, jnp.pad(high, pad), jnp.pad(low, pad)], axis=1)
+    gate_pair = jnp.concatenate([jnp.pad(high, pad), jnp.pad(low, pad)], axis=1)
+    grad_low = out_grad.astype(BF16)
+    grad_cols = [rows_of(grad_low, peer(s)) for s in range(n_tensor)]
+    grad_cols, w_up, gate_pair = after((grad_cols, w_up, gate_pair))
+    grad_cols = [grad_cols[0]] + [hop(grad_cols[s], s) for s in range(1, n_tensor)]
     held = [jnp.stack([w_gate[0], w_up[0], w_down[0].T])]
+    grad_cols, held[0] = after((grad_cols, held[0]))
+    grad_wide = jnp.concatenate([place(grad_cols, 1), gate_pair], axis=1)
     half_row = my_row // 2
 
     start = jnp.sum((segment_ids[:, None] < segment_ids[None, :]).astype(jnp.int32), axis=0)
@@ -621,14 +667,30 @@
         return jnp.einsum("td,dc->ct", attn_in, w, preferred_element_type=F32)
 
     v_t = project(value_matrix).astype(BF16)
-    q_t, k_t, o_t, lse = attn_forward(project(w_query), project(key_matrix), v_t, cos_t, sin_t, start)
-    o_t, grad_x, grad_y, slots[0], out_pieces, held[1] = after((o_t, grad_x, grad_y, slots[0], out_pieces, held[1]))
+    q_pre, k_pre = project(w_query), project(key_matrix)
+    kv = k_pre.shape[0] // HEAD_SIZE
+    parts = 2 if kv % 2 == 0 else 1
+    count = kv // parts
+    q_t, k_t, o_t, lse = ([None] * parts for _ in range(4))
+    far_os = []
+
+    def head_group(i):
+        q_t[i], k_t[i], o_t[i], lse[i] = attn_forward(q_pre, k_pre, v_t, cos_t, sin_t, start, i * count, count)
+
+    def far_heads(i):
+        sent = [lax.dynamic_slice_in_dim(o_t[i], peer(s) * my_row, my_row, 1) for s in range(1, n_tensor)]
+        return [hop(v, s) for s, v in enumerate(sent, 1)]
+
+    for i in range(parts):
+        head_group(i)
+    o_t, grad_x, grad_y = after((o_t, grad_x, grad_y))
+    grad_diag = [plane(grad_x[:half_row], 2), plane(grad_y[half_row:], 1)]
+    far_os = [far_heads(i) for i in range(parts)]
+    far = [far_os[i][s] for s in range(n_tensor - 1) for i in range(parts)]
+    out_ws = [(w, i) for w in out_pieces for i in range(parts)]
+    mixed, mlp_top, mlp_low = join_heads(t_at.reshape(1), tokens, gain_mlp, o_t, far, out_ws, my_row)
+    mlp_top, mlp_low, grad_diag, held[1] = after((mlp_top, mlp_low, grad_diag, held[1]))
     held.append(ring(held[1]))
-    grad_diag = [plane(grad_x[:half_row], 2), plane(grad_y[half_row:], 1)]
-    sent = [lax.dynamic_slice_in_dim(o_t, peer(s) * my_row, my_row, 1) for s in range(1, n_tensor)]
-    os = [o_t] + [hop(v, s) for s, v in enumerate(sent, 1)]
-    mixed, mlp_top, mlp_low = join_heads(t_at.reshape(1), tokens, gain_mlp, os, out_pieces, my_row)
-    mlp_top, mlp_low, grad_diag = after((mlp_top, mlp_low, grad_diag))
 
     group = 2 if depth % 2 == 0 else 1
     last = depth - group
@@ -680,13 +742,13 @@
     slots, mlp_top, mlp_low = after((slots, mlp_top, mlp_low))
     x_top, y_low = plane(mlp_top, 1), plane(mlp_low, 2)
     run("near", 0)
-    x_top, y_low, carry["near"], held[2] = after((x_top, y_low, carry["near"], held[2]))
-    for _ in range(3, depth):
-        held.append(ring(held[-1]))
+    x_top, y_low, carry["near"] = after((x_top, y_low, carry["near"]))
     x_low, y_top = plane(mlp_low, 1), plane(mlp_top, 2)
     where["one"] = ([(x_top, 0), (y_low, 0)], [(grad_x, 0), (grad_y, 1)])
     run("one", 0)
-    x_low, y_top, carry["one"] = after((x_low, y_top, carry["one"]))
+    x_low, y_top, carry["one"], held[2] = after((x_low, y_top, carry["one"], held[2]))
+    for _ in range(3, depth):
+        held.append(ring(held[-1]))
     mlp_diag = [plane(x_top, 2), plane(y_low, 1)]
     where["two"] = ([(x_low, 0), (y_top, 0)], [(grad_x, 1), (grad_y, 0)])
     run("two", 0)
@@ -714,19 +776,18 @@
     rest = order[len(early) :]
 
     run("diag", last)
-    parts = [plane(v, m) for v, m in zip(carry["diag"][1], (1, 2))]
+    back_parts = [plane(v, m) for v, m in zip(carry["diag"][1], (1, 2))]
     run("one", last, [carry["diag"]])
-    parts, carry["one"] = after((parts, carry["one"]))
+    back_parts, carry["one"] = after((back_parts, carry["one"]))
     halves = [plane(v, m) for v, m in zip(carry["one"][1], (1, 2))]
     run("two", last, [carry["one"]])
-    low_x, top_y = ((v.astype(F32) + p.astype(F32)).astype(BF16) for v, p in zip(carry["two"][1], parts[::-1]))
+    low_x, top_y = ((v.astype(F32) + p.astype(F32)).astype(BF16) for v, p in zip(carry["two"][1], back_parts[::-1]))
     halves, low_x, top_y = after((halves, low_x, top_y))
     others = [plane(low_x, 1), plane(top_y, 2)]
     run("near", last, [low_x, top_y])
     others, carry["near"], moving = after((others, carry["near"], moving))
 
-    near_dx = jnp.concatenate(carry["near"][1], axis=0)
-    dy, d_gates, gain_two_all = turn_back(near_dx, halves, others, mixed, grad_wide, gain_mlp)
+    dy, d_gates, gain_two_all = turn_back(carry["near"][1], halves, others, mixed, grad_wide, gain_mlp)
     out_diag, dy = after((carry["diag"][0], dy))
     out_parts = [plane(v, m) for v, m in zip(out_diag, (1, 2))]
     dy_full = gather_rows(dy)
@@ -738,25 +799,13 @@
     late_got = hop_back(late[rest[0]])
     out_halves = [plane(v, m) for v, m in zip(carry["one"][0], (1, 2))]
     do_t = jnp.einsum("td,cd->ct", dy_full, w_out, preferred_element_type=F32).astype(BF16)
-    out_w_grad = jnp.einsum("td,ct->dc", dy_full, o_t, preferred_element_type=F32).astype(BF16)
-    kv = k_t.shape[0] // HEAD_SIZE
-    parts = 2 if kv % 2 == 0 else 1
-    count = kv // parts
+    out_w_grad = [jnp.einsum("td,ct->dc", dy_full, o, preferred_element_type=F32).astype(BF16) for o in o_t]
 
     def backward(i, do_t):
-        return attn_backward(q_t, k_t, v_t, do_t, lse, cos_t, sin_t, start, i * count, count)
-
-    def columns(w, i):
-        size = w.shape[1] // parts
-        return w[:, i * size : (i + 1) * size]
+        return attn_backward(q_t[i], k_t[i], v_t, do_t, lse[i], cos_t, sin_t, start, i * count, count)
 
     def weight_grads(ds):
         return [jnp.einsum("td,ct->dc", attn_in, d, preferred_element_type=F32).astype(BF16) for d in ds]
-
-    def input_grads(ds, i):
-        ws = (w_query, key_matrix, value_matrix)
-        terms = [jnp.einsum("ct,dc->td", d, columns(w, i), preferred_element_type=F32) for d, w in zip(ds, ws)]
-        return functools.reduce(jnp.add, terms)
 
     def part(a, who, rows):
         return lax.dynamic_slice_in_dim(a, who * rows, rows, 0)
@@ -793,13 +842,13 @@
     def z_join(a, got, bit):
         return jnp.where(upper(bit) == 0, jnp.concatenate([a, got], 0), jnp.concatenate([got, a], 0))
 
-    first = out_w_grad
+    first = jnp.concatenate(out_w_grad, axis=1)
     ds = []
     do_t, out_w_grad = after((do_t, out_w_grad))
     if parts == 2:
         ds.append(backward(0, do_t))
         ds[0], out_halves, do_t, late_got = after((ds[0], out_halves, do_t, late_got))
-        first = jnp.concatenate(weight_grads(ds[0]) + [out_w_grad], axis=1)
+        first = jnp.concatenate(weight_grads(ds[0]) + out_w_grad, axis=1)
 
     def next_moving(k, got, arrived):
         total = total_of(late[k], got)
@@ -812,7 +861,9 @@
     ring_on = [ring(moving[c]) for c in range(2)]
     first_sent = plane_shares(first)
     ds.append(backward(parts - 1, do_t))
-    first_sent, ring_on, ds = after((first_sent, ring_on, ds))
+    third = rest[1]
+    late[third] = weight_pieces(third, [ds[-1]])
+    first_sent, ring_on, ds, late = after((first_sent, ring_on, ds, late))
 
     second = jnp.concatenate(weight_grads(ds[-1]), axis=1)
     first = plane_sum(first, first_sent)
@@ -821,25 +872,25 @@
     second_sent = plane_shares(second)
     got = swap(go, bits[0])
     ring_on.append(ring(moving[2]))
-    in_terms = functools.reduce(jnp.add, [input_grads(d, i) for i, d in enumerate(ds)])
-    dots = jnp.sum(in_terms * gain_attn * normed_one, axis=1)
-    own_terms = cols_of(in_terms, t_at)
-    far_terms = [cols_of(in_terms, peer(s)).astype(BF16) for s in range(1, n_tensor)]
-    second_sent, got, ring_on, far_terms, dots = after((second_sent, got, ring_on, far_terms, dots))
+    late_got = hop_back(late[third])
+    own_terms, *far_terms, dots = input_terms(
+        t_at.reshape(1), tokens, gain_attn, ds, (w_query, key_matrix, value_matrix), n_tensor
+    )
+    dots = dots[:, 0]
+    second_sent, got, ring_on, far_terms, dots, late_got = after((second_sent, got, ring_on, far_terms, dots, late_got))
+    moving = next_moving(third, late_got, jnp.stack(ring_on))
 
     first = add(stay, got)
     out_two = [add(v, p) for v, p in zip(carry["two"][0], out_parts[::-1])]
     gain_two = cols_of(gain_two_all[0], t_at)
     far_gains = [cols_of(gain_two_all[0], peer(s)) for s in range(1, n_tensor)]
     cuts = [z_cut(first, bits[1])] if len(bits) > 1 else []
-    cuts, out_two, far_terms, dots = after((cuts, out_two, far_terms, dots))
-    out_others = [plane(v, m) for v, m in zip(out_two, (1, 2))]
+    cuts, far_terms, dots = after((cuts, far_terms, dots))
     far_terms = [hop(v, s) for s, v in enumerate(far_terms, 1)]
     far_dots = [hop(jnp.concatenate([dots, v]), s) for s, v in enumerate(far_gains, 1)]
     gots = [swap(go, bits[1]) for _, go in cuts]
-    for k in rest[1:-1]:
-        late[k] = weight_pieces(k, [dots])
-    gots, out_others, far_terms, far_dots, late = after((gots, out_others, far_terms, far_dots, late))
+    gots, far_terms, far_dots, out_two = after((gots, far_terms, far_dots, out_two))
+    out_others = [plane(v, m) for v, m in zip(out_two, (1, 2))]
     second = plane_sum(second, second_sent)
     for (stay, _), got in zip(cuts, gots):
         first = add(stay, got)
@@ -851,7 +902,7 @@
 
     d_attn_in = functools.reduce(jnp.add, [own_terms] + [v.astype(F32) for v in far_terms])
     all_dots = functools.reduce(jnp.add, [dots] + far_dots)
-    normed_cols = cols_of(normed_one, t_at)
+    normed_cols = cols_of(tokens, t_at).astype(F32) * inv_one
     scaled_one = d_attn_in * cols_of(gain_attn, t_at)
     d_norm_one = inv_one * (scaled_one - normed_cols * (all_dots / width)[:, None])
     grad_tokens = cols_of(dy_full, t_at).astype(F32) + d_norm_one
@@ -861,37 +912,35 @@
     gain_rows = gains.shape[0]
     gains = jnp.pad(gains, ((0, 16 - gain_rows), (0, 0)))
     grad_logits = gather_rows(gates * (d_gates - jnp.sum(gates * d_gates, axis=1, keepdims=True)))
-    late_got = {k: hop_back(late[k]) for k in rest[1:-1]}
     for i, bit in enumerate(bits):
         rows = second.shape[0] // 2
         stay, go = z_cut(second, bit, gains)
         back = bits[-1 - i]
-        first, go, late_got = after((first, go, late_got))
+        first, go = after((first, go))
         got, first_got = swap(go, bit), swap(first, back)
-        got, first_got = after((got, first_got))
+        got, first_got, out_others = after((got, first_got, out_others))
         second, gains = add(stay, got[:rows]), add(gains, got[rows:])
         first = z_join(first, first_got, back)
-    moving = jnp.stack(ring_on)
-    for k in rest[1:-1]:
-        moving = next_moving(k, late_got[k], moving)
-        first, second, moving = after((first, second, moving))
-        ring_on = [ring(moving[c]) for c in range(3)]
-        moving = jnp.stack(ring_on[:2] + [ring_on[2]])
+    first, second, moving = after((first, second, moving))
     first_all = [first] + [plane(first, m) for m in range(1, PLANE)]
     late[0] = weight_pieces(0, [first])
     for bit in bits[::-1]:
         second = z_join(second, swap(second, bit), bit)
+    moving, second = after((moving, second))
+    ring_on = [ring(moving[c]) for c in range(3)]
     rows = second.shape[0]
     second = jnp.concatenate([second, gains], axis=0)
     out_top, out_low = carry["near"][0]
     top_rows = out_top.astype(F32) + out_halves[0].astype(F32) + out_others[1].astype(F32)
     low_rows = out_low.astype(F32) + out_others[0].astype(F32) + out_halves[1].astype(F32)
     block_out = to_cols((mixed + jnp.concatenate([top_rows, low_rows], axis=0)).astype(BF16))
-    second, block_out, first_all, ring_on[:2], late[0] = after((second, block_out, first_all, ring_on[:2], late[0]))
-    late_got[0] = hop_back(late[0])
+    second, block_out, first_all, ring_on[0], late[0] = after((second, block_out, first_all, ring_on[0], late[0]))
+    late_got = hop_back(late[0])
     second_all = [second] + [plane(second, m) for m in range(1, PLANE)]
+    final = [a + b.astype(F32) for a, b in zip(total_of(late[0], late_got), ring_on)]
+    final[2] = final[2].T
+    second_all, final = after((second_all, final))
     gains = functools.reduce(jnp.add, [v[rows : rows + gain_rows].astype(F32) for v in second_all]).reshape(-1)
-    final = [a + b.astype(F32) for a, b in zip(total_of(late[0], late_got[0]), ring_on)]
     cuts = [w.shape[1] // parts for w in (w_query, key_matrix, value_matrix)]
     grad_query, grad_key, grad_value, grad_out = lay_out(p_at.reshape(1), first_all, second_all, parts, cuts)
     return (
@@ -906,7 +955,7 @@
         gains[col_width:],
         final[0][None],
         final[1][None],
-        final[2].T[None],
+        final[2][None],
     )
 
 

time: 449 us -> 440 us (0.980)
  matrix products: 31.2 us -> 12 us
  local copies, waits for them, and re-layouts: 23.7 us -> 37.4 us
  starting transfers between devices: 71.2 us -> 59.5 us
    unnamed x139 -> x180, local copies, waits for them, and re-layouts: 11.1 us -> 28.3 us
    dot_general x7 -> x2, matrix products: 17.6 us -> 1.52 us  [body(): jnp.einsum('td,ct->dc', dy_full, o, preferred_element_type=F32).astype(BF16)]
    ppermute x34, waiting for transfers between devices: 25.8 us -> 10.3 us  [plane(): return jax.tree.map(lambda a: lax.ppermute(a, 'expert', pairs), x)]
    ppermute x10, starting transfers between devices: 22.5 us -> 12.1 us  [ring(): return jax.tree.map(lambda a: lax.ppermute(a, 'expert', pairs), x)]
    ppermute x10, waiting for transfers between devices: 21.3 us -> 28.8 us  [ring(): return jax.tree.map(lambda a: lax.ppermute(a, 'expert', pairs), x)]
    ppermute x8, waiting for transfers between devices: 16.1 us -> 23.2 us  [swap(): return lax.ppermute(a, 'expert', pairs)]
    pallas_call x3 -> x5, Pallas kernels: 19.7 us -> 25 us  [the longest x2 10.5 us: attn_forward(): pl.pallas_call(functools.partial(attn_fwd_kernel, block), grid=(count,),...]
  transfers between devices with their start and end apart: 68 -> 69, of which waited for: 19 -> 20; matrix products, arithmetic and copies ran while one was open for 17% -> 13% of each run, Pallas kernels for 41% -> 42%
where the time goes in v4:
time: 440 us; the launch traced here: 435 us
  Pallas kernels  207 us (47%)
  waiting for transfers between devices  70.1 us (16%)
  starting transfers between devices  59.5 us (14%)
  other arithmetic  47.3 us (11%)
  local copies, waits for them, and re-layouts  37.4 us (8%)
  matrix products  12 us (3%)
    pallas_call x8, Pallas kernels, expert_data(): pl.pallas_call(functools.partial(data_kernel, first, last, blocks, tiles,...  110 us
    pallas_call x4, Pallas kernels, expert_weight(): pl.pallas_call(functools.partial(weight_kernel, tuple(shape), pieces), gr...  48.6 us
    ppermute x34, starting transfers between devices, plane(): return jax.tree.map(lambda a: lax.ppermute(a, 'expert', pairs), x)  38.4 us
    ppermute x10, waiting for transfers between devices, ring(): return jax.tree.map(lambda a: lax.ppermute(a, 'expert', pairs), x)  28.8 us
    unnamed x180, local copies, waits for them, and re-layouts  28.3 us
    ppermute x8, waiting for transfers between devices, swap(): return lax.ppermute(a, 'expert', pairs)  23.2 us
    pallas_call x2, Pallas kernels, attn_backward(): pl.pallas_call(functools.partial(attn_bwd_kernel, block), grid=(count,),...  20 us
    ppermute x10, starting transfers between devices, ring(): return jax.tree.map(lambda a: lax.ppermute(a, 'expert', pairs), x)  12.1 us
  transfers between devices with their start and end apart: 69, of which 20 were waited for; matrix products, arithmetic and copies ran while one was open for 13% of the time, Pallas kernels for 42%

profile of v4, /device:TPU:0, one launch (start us, length us, event | category | flops | bytes accessed | tf_op | source)
XLA Modules:
  0.0 435.4 jit_solution(11909261730736568872)
XLA Ops:
  6.0 2.0 copy.97
  8.5 2.7 pad_maximum_fusion.refs_4_
  11.8 1.7 maximum_select_fusion.1
  13.6 2.7 collective-permute-start.2
  16.3 1.5 collective-permute-start.3
  18.3 1.9 collective-permute-start.9
  24.8 5.3 %attn_forward.3 = (bf16[256,1024]{1,0:T(8,128)(2,1)S(1)}, bf16[128,1024]{1,0:T(8,128)(2,1)S(1)}, bf16[256,1024]{1,0:T(8,128)(2,1)S(1)}, f32[2,2,1024]{2,1,0:T(2,128)S(1)}) custom-call(f32[512,1024]{1,0:T(8,128)S(1)} %convolution_bitcast_fusion.q_ref, f32[256,1024]{1,0:T(8,128)S(1)} %convolution_bitcast_fusion.1.k_ref, bf16[256,1024]{1,0:T(8,128)(2,1)S(1)} %fusion.6.v_ref, ...), custom_call_target="tpu_custom_call" | custom-call | flops 2147483648 | bytes 2097152 | tf_op jit(solution)/shard_map/attn_forward/pallas_call | solution.py:122
  32.2 5.2 %attn_forward.2 = (bf16[256,1024]{1,0:T(8,128)(2,1)S(1)}, bf16[128,1024]{1,0:T(8,128)(2,1)S(1)}, bf16[256,1024]{1,0:T(8,128)(2,1)S(1)}, f32[2,2,1024]{2,1,0:T(2,128)S(1)}) custom-call(f32[512,1024]{1,0:T(8,128)S(1)} %convolution_bitcast_fusion.q_ref, f32[256,1024]{1,0:T(8,128)S(1)} %convolution_bitcast_fusion.1.k_ref, bf16[256,1024]{1,0:T(8,128)(2,1)S(1)} %fusion.6.v_ref, ...), custom_call_target="tpu_custom_call" | custom-call | flops 2147483648 | bytes 2097152 | tf_op jit(solution)/shard_map/attn_forward/pallas_call | solution.py:122
  37.5 5.3 %collective-permute-done.2.refs_2_.refs_8_.refs_14_ = bf16[512,1152]{1,0:T(8,128)(2,1)S(1)} collective-permute-done((bf16[512,1152]{1,0:T(8,128)(2,1)S(1)}, bf16[512,1152]{1,0:T(8,128)(2,1)S(1)}, u32[]{:S(2)}, u32[]{:S(2)}) %collective-permute-start.2) | collective-permute-done | bytes 1179680 | tf_op jit(solution)/shard_map/ppermute | solution.py:594
  44.3 1.6 collective-permute-start.7
  50.5 3.9 join_heads.1
  54.4 2.5 collective-permute-done.9.refs_6_
  56.9 2.0 collective-permute-done.7.refs_2_.refs_20_
  60.2 2.1 collective-permute-start.17
  62.3 1.5 collective-permute-done.10.refs_7_
  66.4 1.6 collective-permute-start.16
  68.6 12.8 %expert_data.8 = (bf16[512,1024]{1,0:T(8,128)(2,1)}, bf16[512,1024]{1,0:T(8,128)(2,1)}, f32[512,128]{1,0:T(8,128)}, bf16[512,1024]{1,0:T(8,128)(2,1)}, bf16[512,...) custom-call(s32[2]{0:T(128)} %get-tuple-element.632.expert_ref, bf16[256,1024]{1,0:T(8,128)(2,1)} %copy-done.4, ...), custom_call_target="tpu_custom_call" | custom-call | flops 1610612736 | bytes 12582912 | tf_op jit(solution)/shard_map/expert_data/pallas_call | solution.py:295
  82.3 12.8 %expert_data.9 = (bf16[512,1024]{1,0:T(8,128)(2,1)}, bf16[512,1024]{1,0:T(8,128)(2,1)}, f32[512,128]{1,0:T(8,128)}, bf16[512,1024]{1,0:T(8,128)(2,1)}, bf16[512,...) custom-call(s32[2]{0:T(128)} %get-tuple-element.632.expert_ref, ...), custom_call_target="tpu_custom_call" | custom-call | flops 1610612736 | bytes 12582912 | tf_op jit(solution)/shard_map/expert_data/pallas_call | solution.py:295
  95.0 4.7 %collective-permute-done.17.refs_4_ = bf16[3,1024,256]{2,1,0:T(8,128)(2,1)} collective-permute-done((bf16[3,1024,256]{2,1,0:T(8,128)(2,1)}, bf16[3,1024,256]{2,1,0:T(8,128)(2,1)}, u32[]{:S(2)}, u32[]{:S(2)}) %collective-permute-start.17) | collective-permute-done | bytes 1572896 | tf_op jit(solution)/shard_map/ppermute | solution.py:598
  101.1 12.8 %expert_data.10 = (bf16[512,1024]{1,0:T(8,128)(2,1)}, bf16[512,1024]{1,0:T(8,128)(2,1)}, f32[512,128]{1,0:T(8,128)}, bf16[512,1024]{1,0:T(8,128)(2,1)}, bf16[512...) custom-call(s32[2]{0:T(128)} %get-tuple-element.632.expert_ref, ...), custom_call_target="tpu_custom_call" | custom-call | flops 1610612736 | bytes 12582912 | tf_op jit(solution)/shard_map/expert_data/pallas_call | solution.py:295
  114.8 12.7 %expert_data.11 = (bf16[512,1024]{1,0:T(8,128)(2,1)}, bf16[512,1024]{1,0:T(8,128)(2,1)}, f32[512,128]{1,0:T(8,128)}, bf16[512,1024]{1,0:T(8,128)(2,1)}, bf16[512...) custom-call(s32[2]{0:T(128)} %get-tuple-element.632.expert_ref, ...), custom_call_target="tpu_custom_call" | custom-call | flops 1610612736 | bytes 12582912 | tf_op jit(solution)/shard_map/expert_data/pallas_call | solution.py:295
  127.5 12.2 %expert_weight.4 = (bf16[3,1024,256]{2,1,0:T(8,128)(2,1)}, bf16[3,1024,256]{2,1,0:T(8,128)(2,1)}) custom-call(bf16[256,1024]{1,0:T(8,128)(2,1)} %copy-done.4, bf16[256,1024]{1,0:T(8,128)(2,1)} %copy-done.5, bf16[512,1152]{1,0:T(8,128)(2,1)} %copy-done.2, bf16[512,1152]{1,0:T(8,128)(2,1)} %copy-done.2, bf16[512,1024]{1,0:T(8,128)(2,1)} %get-tuple-element.326.refs_4_, ...), custom_call_target="tpu_custom_call" | custom-call | flops 1073741824 | bytes 17825792 | tf_op jit(solution)/shard_map/expert_weight/pallas_call | solution.py:351
  140.3 4.4 %collective-permute-done.21 = bf16[3,1024,256]{2,1,0:T(8,128)(2,1)S(1)} collective-permute-done((bf16[3,1024,256]{2,1,0:T(8,128)(2,1)}, bf16[3,1024,256]{2,1,0:T(8,128)(2,1)S(1)}, u32[]{:S(2)}, u32[]{:S(2)}) %collective-permute-start.21) | collective-permute-done | bytes 1572896 | tf_op jit(solution)/shard_map/ppermute | solution.py:590
  144.7 2.9 convert_add_fusion.1
  148.7 14.8 %expert_data.12 = (bf16[256,1024]{1,0:T(8,128)(2,1)}, bf16[256,1024]{1,0:T(8,128)(2,1)}, bf16[256,1152]{1,0:T(8,128)(2,1)}, bf16[256,1152]{1,0:T(8,128)(2,1)}, b...) custom-call(s32[2]{0:T(128)} %get-tuple-element.367.expert_ref, ...), custom_call_target="tpu_custom_call" | custom-call | flops 1610612736 | bytes 12582912 | tf_op jit(solution)/shard_map/expert_data/pallas_call | solution.py:295
  165.1 1.5 collective-permute-start.23
  167.8 14.6 %expert_data.13 = (bf16[256,1024]{1,0:T(8,128)(2,1)}, bf16[256,1024]{1,0:T(8,128)(2,1)}, bf16[256,1152]{1,0:T(8,128)(2,1)}, bf16[256,1152]{1,0:T(8,128)(2,1)}, b...) custom-call(s32[2]{0:T(128)} %get-tuple-element.367.expert_ref, ...), custom_call_target="tpu_custom_call" | custom-call | flops 1610612736 | bytes 12582912 | tf_op jit(solution)/shard_map/expert_data/pallas_call | solution.py:295
  183.6 14.6 %expert_data.14 = (bf16[256,1024]{1,0:T(8,128)(2,1)}, bf16[256,1024]{1,0:T(8,128)(2,1)}, bf16[256,1152]{1,0:T(8,128)(2,1)}, bf16[256,1152]{1,0:T(8,128)(2,1)}, b...) custom-call(s32[2]{0:T(128)} %get-tuple-element.367.expert_ref, ...), custom_call_target="tpu_custom_call" | custom-call | flops 1610612736 | bytes 12582912 | tf_op jit(solution)/shard_map/expert_data/pallas_call | solution.py:295
  198.2 2.1 add_convert_fusion.2
  202.7 1.5 collective-permute-start.27
  204.3 15.0 %expert_data.15 = (bf16[256,1024]{1,0:T(8,128)(2,1)}, bf16[256,1024]{1,0:T(8,128)(2,1)}, bf16[256,1152]{1,0:T(8,128)(2,1)}, bf16[256,1152]{1,0:T(8,128)(2,1)}, b...) custom-call(s32[2]{0:T(128)} %get-tuple-element.367.expert_ref, ...), custom_call_target="tpu_custom_call" | custom-call | flops 1610612736 | bytes 12582912 | tf_op jit(solution)/shard_map/expert_data/pallas_call | solution.py:295
  221.4 4.2 turn_back.1
  226.7 12.1 %expert_weight.5 = (bf16[3,1024,256]{2,1,0:T(8,128)(2,1)}, bf16[3,1024,256]{2,1,0:T(8,128)(2,1)}) custom-call(bf16[256,1024]{1,0:T(8,128)(2,1)} %copy-done.62, bf16[256,1024]{1,0:T(8,128)(2,1)} %collective-permute-done.14.refs_1_.refs_19_, bf16[256,1152]{1,0:T(8,128)(2,1)} %copy-done.59, bf16[256,1152]{1,0:T(8,128)(2,1)} %copy-done.60, ...), custom_call_target="tpu_custom_call" | custom-call | flops 1073741824 | bytes 17825792 | tf_op jit(solution)/shard_map/expert_weight/pallas_call | solution.py:351
  238.9 3.7 maximum_select_fusion
  245.0 1.5 collective-permute-start.33
  246.5 2.9 fusion.4.do_ref
  252.1 10.0 %attn_backward.2 = (bf16[256,1024]{1,0:T(8,128)(2,1)S(1)}, bf16[128,1024]{1,0:T(8,128)(2,1)S(1)}, bf16[128,1024]{1,0:T(8,128)(2,1)S(1)}) custom-call(bf16[256,1024]{1,0:T(8,128)(2,1)S(1)} %copy-done.39, bf16[128,1024]{1,0:T(8,128)(2,1)S(1)} %copy-done.43, bf16[256,1024]{1,0:T(8,128)(2,1)S(1)} %copy-done.29, bf16[512,1024]{1,0:T(8,128)(2,1)S(1)} %fusion.4.do_ref, ...), custom_call_target="tpu_custom_call" | custom-call | flops 2147483648 | bytes 2097152 | tf_op jit(solution)/shard_map/attn_backward/pallas_call | solution.py:141
  266.6 3.0 add_convert_fusion.1
  271.9 2.4 collective-permute-start.37
  275.6 1.6 collective-permute-start.38
  277.2 2.1 collective-permute-start.39
  280.2 10.0 %attn_backward.3 = (bf16[256,1024]{1,0:T(8,128)(2,1)S(1)}, bf16[128,1024]{1,0:T(8,128)(2,1)S(1)}, bf16[128,1024]{1,0:T(8,128)(2,1)S(1)}) custom-call(bf16[256,1024]{1,0:T(8,128)(2,1)S(1)} %copy-done.37, bf16[128,1024]{1,0:T(8,128)(2,1)S(1)} %copy-done.41, bf16[256,1024]{1,0:T(8,128)(2,1)S(1)} %copy-done.29, bf16[512,1024]{1,0:T(8,128)(2,1)S(1)} %copy-done.35, ...), custom_call_target="tpu_custom_call" | custom-call | flops 2147483648 | bytes 2097152 | tf_op jit(solution)/shard_map/attn_backward/pallas_call | solution.py:141
  290.2 12.2 %expert_weight.6 = (bf16[3,1024,256]{2,1,0:T(8,128)(2,1)}, bf16[3,1024,256]{2,1,0:T(8,128)(2,1)}) custom-call(bf16[256,1024]{1,0:T(8,128)(2,1)} %copy-done.62, bf16[256,1024]{1,0:T(8,128)(2,1)} %collective-permute-done.14.refs_1_.refs_19_, bf16[256,1152]{1,0:T(8,128)(2,1)} %copy-done.59, bf16[256,1152]{1,0:T(8,128)(2,1)} %copy-done.60, ...), custom_call_target="tpu_custom_call" | custom-call | flops 1073741824 | bytes 17825792 | tf_op jit(solution)/shard_map/expert_weight/pallas_call | solution.py:351
  302.7 2.0 add_convert_fusion.6
  311.2 2.2 collective-permute-start.42
  313.3 3.6 collective-permute-done.44
  321.9 6.3 %input_terms.1 = (f32[1024,512]{1,0:T(8,128)}, bf16[1024,512]{1,0:T(8,128)(2,1)S(1)}, f32[1024,1]{1,0:T(8,128)S(1)}) custom-call(s32[1]{0:T(128)} %bitcast.9.at_ref, bf16[1024,1024]{1,0:T(8,128)(2,1)} %x_ref.1, f32[1,1024]{1,0:T(1,128)S(1)} %bitcast.90, bf16[256,1024]{1,0:T(8,128)(2,1)S(1)} %copy-done.33, bf16[128,1024]{1,0:T(8,128)(2,1)S(1)} %copy-done.25, ...), custom_call_target="tpu_custom_call" | custom-call | flops 2147483648 | bytes 8388608 | tf_op jit(solution)/shard_map/input_terms/pallas_call | solution.py:448
  331.8 2.4 add_convert_fusion.5
  336.0 7.8 %collective-permute-done.46 = bf16[64,1024]{1,0:T(8,128)(2,1)S(1)} collective-permute-done((bf16[64,1024]{1,0:T(8,128)(2,1)S(1)}, bf16[64,1024]{1,0:T(8,128)(2,1)S(1)}, u32[]{:S(2)}, u32[]{:S(2)}) %collective-permute-start.46) | collective-permute-done | bytes 131104 | tf_op jit(solution)/shard_map/ppermute | solution.py:827
  345.2 3.9 multiply_add_fusion
  350.0 1.5 collective-permute-start.50
  351.5 6.8 %collective-permute-done.50 = bf16[64,1024]{1,0:T(8,128)(2,1)} collective-permute-done((bf16[64,1024]{1,0:T(8,128)(2,1)S(1)}, bf16[64,1024]{1,0:T(8,128)(2,1)}, u32[]{:S(2)}, u32[]{:S(2)}) %collective-permute-start.50) | collective-permute-done | bytes 131104 | tf_op jit(solution)/shard_map/ppermute | solution.py:827
  360.9 2.5 add_convert_fusion
  363.5 1.6 collective-permute-done.53
  365.1 2.0 collective-permute-done.54
  374.2 2.1 collective-permute-done.55
  378.5 2.9 collective-permute-done.56
  383.8 12.1 %expert_weight.7 = (bf16[3,1024,256]{2,1,0:T(8,128)(2,1)}, bf16[3,1024,256]{2,1,0:T(8,128)(2,1)}) custom-call(bf16[256,1024]{1,0:T(8,128)(2,1)} %copy-done.4, bf16[256,1024]{1,0:T(8,128)(2,1)} %copy-done.5, bf16[512,1152]{1,0:T(8,128)(2,1)} %copy-done.2, bf16[512,1152]{1,0:T(8,128)(2,1)} %copy-done.2, bf16[512,1024]{1,0:T(8,128)(2,1)} %get-tuple-element.507.refs_4_, ...), custom_call_target="tpu_custom_call" | custom-call | flops 1073741824 | bytes 17825792 | tf_op jit(solution)/shard_map/expert_weight/pallas_call | solution.py:351
  405.5 2.2 convert_add_fusion
  407.7 7.6 %collective-permute-done.67 = bf16[1024,256]{1,0:T(8,128)(2,1)} collective-permute-done((bf16[1024,256]{1,0:T(8,128)(2,1)}, bf16[1024,256]{1,0:T(8,128)(2,1)}, u32[]{:S(2)}, u32[]{:S(2)}) %collective-permute-start.67) | collective-permute-done | bytes 524320 | tf_op jit(solution)/shard_map/ppermute | solution.py:598
  415.4 10.4 %collective-permute-done.68 = bf16[1024,256]{1,0:T(8,128)(2,1)} collective-permute-done((bf16[1024,256]{1,0:T(8,128)(2,1)}, bf16[1024,256]{1,0:T(8,128)(2,1)}, u32[]{:S(2)}, u32[]{:S(2)}) %collective-permute-start.68) | collective-permute-done | bytes 524320 | tf_op jit(solution)/shard_map/ppermute | solution.py:598
  425.7 3.2 fusion.10
  428.9 2.6 copy.112
  432.0 3.1 lay_out.1
  (369 shorter events, 95.8 us)
Async XLA Ops:
  5.2 6.6 %collective-permute-start = (bf16[512,512]{1,0:T(8,128)(2,1)}, bf16[512,512]{1,0:T(8,128)(2,1)}, u32[]{:S(2)}, u32[]{:S(2)}) collective-permute-start(bf16[512,512]{1,0:T(8,128)(2,1)} %get-tuple-element.276), channel_id=1, source_target_pairs={{0,1},{1,0},{2,3},{3,2},{4,5},{5,4},{6,7},{7,6},{8,9},{9,8},{10,11... | collective-permute-start | bytes 1572872 | tf_op jit(solution)/shard_map/ppermute | solution.py:590
  5.6 41.0 %collective-permute-start.6 = (bf16[512,1024]{1,0:T(8,128)(2,1)S(1)}, bf16[512,1024]{1,0:T(8,128)(2,1)S(1)}, u32[]{:S(2)}, u32[]{:S(2)}) collective-permute-start(bf16[512,1024]{1,0:T(8,128)(2,1)S(1)} %copy-done.6), channel_id=1, source_target_pairs={{0,1},{1,0},{2,3},{3,2},{4,5},{5,4},{6,7},{7,6},{8,9},{9,8},{10,11... | collective-permute-start | bytes 3145736 | tf_op jit(solution)/shard_map/ppermute | solution.py:590
  13.6 29.2 %collective-permute-start.2 = (bf16[512,1152]{1,0:T(8,128)(2,1)S(1)}, bf16[512,1152]{1,0:T(8,128)(2,1)S(1)}, u32[]{:S(2)}, u32[]{:S(2)}) collective-permute-start(bf16[512,1152]{1,0:T(8,128)(2,1)S(1)} %pad_maximum_fusion.1.refs_2_.refs_3_.grad_ref.refs_20_.refs_21_), channel_id=1, source_target_pairs={{0,2},{2,0},{4,6},{6,4},{8,10},{10,8},{12,14},{14,12},{16,18},{18,... | collective-permute-start | bytes 3538952 | tf_op jit(solution)/shard_map/ppermute | solution.py:594
  16.3 27.9 %collective-permute-start.3 = (bf16[512,1152]{1,0:T(8,128)(2,1)S(1)}, bf16[512,1152]{1,0:T(8,128)(2,1)S(1)}, u32[]{:S(2)}, u32[]{:S(2)}) collective-permute-start(bf16[512,1152]{1,0:T(8,128)(2,1)S(1)} %pad_maximum_fusion.1.refs_2_.refs_3_.grad_ref.refs_20_.refs_21_), channel_id=1, source_target_pairs={{0,4},{2,6},{4,0},{6,2},{8,12},{10,14},{12,8},{14,10},{16,20},{18,... | collective-permute-start | bytes 3538952 | tf_op jit(solution)/shard_map/ppermute | solution.py:594
  18.3 38.6 %collective-permute-start.9 = (bf16[3,1024,256]{2,1,0:T(8,128)(2,1)}, bf16[3,1024,256]{2,1,0:T(8,128)(2,1)}, u32[]{:S(2)}, u32[]{:S(2)}) collective-permute-start(bf16[3,1024,256]{2,1,0:T(8,128)(2,1)} %pad_maximum_fusion.refs_4_), channel_id=1, source_target_pairs={{0,8},{2,10},{4,12},{6,14},{8,16},{10,18},{12,20},{14,22},{16,24},... | collective-permute-start | bytes 4718600 | tf_op jit(solution)/shard_map/ppermute | solution.py:598
  44.3 14.6 %collective-permute-start.7 = (bf16[256,1152]{1,0:T(8,128)(2,1)S(1)}, bf16[256,1152]{1,0:T(8,128)(2,1)S(1)}, u32[]{:S(2)}, u32[]{:S(2)}) collective-permute-start(bf16[256,1152]{1,0:T(8,128)(2,1)S(1)} %slice.72), channel_id=1, source_target_pairs={{0,4},{2,6},{4,0},{6,2},{8,12},{10,14},{12,8},{14,10},{16,20},{18,... | collective-permute-start | bytes 1769480 | tf_op jit(solution)/shard_map/ppermute | solution.py:594
  45.9 14.3 %collective-permute-start.8 = (bf16[256,1152]{1,0:T(8,128)(2,1)S(1)}, bf16[256,1152]{1,0:T(8,128)(2,1)S(1)}, u32[]{:S(2)}, u32[]{:S(2)}) collective-permute-start(bf16[256,1152]{1,0:T(8,128)(2,1)S(1)} %slice.73), channel_id=1, source_target_pairs={{0,2},{2,0},{4,6},{6,4},{8,10},{10,8},{12,14},{14,12},{16,18},{18,... | collective-permute-start | bytes 1769480 | tf_op jit(solution)/shard_map/ppermute | solution.py:594
  48.1 14.2 %collective-permute-start.1 = (bf16[3,1024,256]{2,1,0:T(8,128)(2,1)}, bf16[3,1024,256]{2,1,0:T(8,128)(2,1)S(1)}, u32[]{:S(2)}, u32[]{:S(2)}) collective-permute-start(bf16[3,1024,256]{2,1,0:T(8,128)(2,1)} %pad_maximum_fusion.refs_4_), channel_id=1, source_target_pairs={{0,1},{1,0},{2,3},{3,2},{4,5},{5,4},{6,7},{7,6},{8,9},{9,8},{10,11... | collective-permute-start | bytes 4718600 | tf_op jit(solution)/shard_map/ppermute | solution.py:590
  60.2 39.5 %collective-permute-start.17 = (bf16[3,1024,256]{2,1,0:T(8,128)(2,1)}, bf16[3,1024,256]{2,1,0:T(8,128)(2,1)}, u32[]{:S(2)}, u32[]{:S(2)}) collective-permute-start(bf16[3,1024,256]{2,1,0:T(8,128)(2,1)} %collective-permute-done.9.refs_6_), channel_id=1, source_target_pairs={{0,8},{2,10},{4,12},{6,14},{8,16},{10,18},{12,20},{14,22},{16,24},... | collective-permute-start | bytes 4718600 | tf_op jit(solution)/shard_map/ppermute | solution.py:598
  63.9 17.6 %collective-permute-start.11 = (bf16[256,1024]{1,0:T(8,128)(2,1)S(1)}, bf16[256,1024]{1,0:T(8,128)(2,1)S(1)}, u32[]{:S(2)}, u32[]{:S(2)}) collective-permute-start(bf16[256,1024]{1,0:T(8,128)(2,1)S(1)} %get-tuple-element.297.refs_0_.refs_18_), channel_id=1, source_target_pairs={{0,2},{2,0},{4,6},{6,4},{8,10},{10,8},{12,14},{14,12},{16,18},{18,... | collective-permute-start | bytes 1572872 | tf_op jit(solution)/shard_map/ppermute | solution.py:594
  64.5 17.0 %collective-permute-start.12 = (bf16[256,1024]{1,0:T(8,128)(2,1)S(1)}, bf16[256,1024]{1,0:T(8,128)(2,1)}, u32[]{:S(2)}, u32[]{:S(2)}) collective-permute-start(bf16[256,1024]{1,0:T(8,128)(2,1)S(1)} %get-tuple-element.298.refs_1_.refs_19_), channel_id=1, source_target_pairs={{0,4},{2,6},{4,0},{6,2},{8,12},{10,14},{12,8},{14,10},{16,20},{18,... | collective-permute-start | bytes 1572872 | tf_op jit(solution)/shard_map/ppermute | solution.py:594
  65.0 34.7 %collective-permute-start.15 = (bf16[256,1024]{1,0:T(8,128)(2,1)S(1)}, bf16[256,1024]{1,0:T(8,128)(2,1)}, u32[]{:S(2)}, u32[]{:S(2)}) collective-permute-start(bf16[256,1024]{1,0:T(8,128)(2,1)S(1)} %get-tuple-element.298.refs_1_.refs_19_), channel_id=1, source_target_pairs={{0,2},{2,0},{4,6},{6,4},{8,10},{10,8},{12,14},{14,12},{16,18},{18,... | collective-permute-start | bytes 1572872 | tf_op jit(solution)/shard_map/ppermute | solution.py:594
  66.4 33.3 %collective-permute-start.16 = (bf16[256,1024]{1,0:T(8,128)(2,1)S(1)}, bf16[256,1024]{1,0:T(8,128)(2,1)}, u32[]{:S(2)}, u32[]{:S(2)}) collective-permute-start(bf16[256,1024]{1,0:T(8,128)(2,1)S(1)} %get-tuple-element.297.refs_0_.refs_18_), channel_id=1, source_target_pairs={{0,4},{2,6},{4,0},{6,2},{8,12},{10,14},{12,8},{14,10},{16,20},{18,... | collective-permute-start | bytes 1572872 | tf_op jit(solution)/shard_map/ppermute | solution.py:594
  99.7 40.5 %collective-permute-start.19 = (bf16[3,1024,256]{2,1,0:T(8,128)(2,1)}, bf16[3,1024,256]{2,1,0:T(8,128)(2,1)S(1)}, u32[]{:S(2)}, u32[]{:S(2)}) collective-permute-start(bf16[3,1024,256]{2,1,0:T(8,128)(2,1)} %collective-permute-done.17.refs_4_), channel_id=1, source_target_pairs={{0,8},{2,10},{4,12},{6,14},{8,16},{10,18},{12,20},{14,22},{16,24},... | collective-permute-start | bytes 4718600 | tf_op jit(solution)/shard_map/ppermute | solution.py:598
  99.9 14.0 %collective-permute-start.13 = (bf16[256,1024]{1,0:T(8,128)(2,1)}, bf16[256,1024]{1,0:T(8,128)(2,1)S(1)}, u32[]{:S(2)}, u32[]{:S(2)}) collective-permute-start(bf16[256,1024]{1,0:T(8,128)(2,1)} %copy-done.61), channel_id=1, source_target_pairs={{0,4},{2,6},{4,0},{6,2},{8,12},{10,14},{12,8},{14,10},{16,20},{18,... | collective-permute-start | bytes 1572872 | tf_op jit(solution)/shard_map/ppermute | solution.py:594
  100.5 13.7 %collective-permute-start.14 = (bf16[256,1024]{1,0:T(8,128)(2,1)}, bf16[256,1024]{1,0:T(8,128)(2,1)}, u32[]{:S(2)}, u32[]{:S(2)}) collective-permute-start(bf16[256,1024]{1,0:T(8,128)(2,1)} %collective-permute-done.12.refs_1_.refs_7_), channel_id=1, source_target_pairs={{0,2},{2,0},{4,6},{6,4},{8,10},{10,8},{12,14},{14,12},{16,18},{18,... | collective-permute-start | bytes 1572872 | tf_op jit(solution)/shard_map/ppermute | solution.py:594
  101.1 39.2 %collective-permute-start.18 = (bf16[3,1024,256]{2,1,0:T(8,128)(2,1)}, bf16[3,1024,256]{2,1,0:T(8,128)(2,1)}, u32[]{:S(2)}, u32[]{:S(2)}) collective-permute-start(bf16[3,1024,256]{2,1,0:T(8,128)(2,1)} %collective-permute-done.17.refs_4_), channel_id=1, source_target_pairs={{0,1},{1,0},{2,3},{3,2},{4,5},{5,4},{6,7},{7,6},{8,9},{9,8},{10,11... | collective-permute-start | bytes 4718600 | tf_op jit(solution)/shard_map/ppermute | solution.py:590
  139.7 5.0 %collective-permute-start.21 = (bf16[3,1024,256]{2,1,0:T(8,128)(2,1)}, bf16[3,1024,256]{2,1,0:T(8,128)(2,1)S(1)}, u32[]{:S(2)}, u32[]{:S(2)}) collective-permute-start(bf16[3,1024,256]{2,1,0:T(8,128)(2,1)} %get-tuple-element.335), channel_id=1, source_target_pairs={{0,1},{1,0},{2,3},{3,2},{4,5},{5,4},{6,7},{7,6},{8,9},{9,8},{10,11... | collective-permute-start | bytes 4718600 | tf_op jit(solution)/shard_map/ppermute | solution.py:590
  140.2 7.4 %collective-permute-start.20 = (bf16[3,1024,256]{2,1,0:T(8,128)(2,1)S(1)}, bf16[3,1024,256]{2,1,0:T(8,128)(2,1)S(1)}, u32[]{:S(2)}, u32[]{:S(2)}) collective-permute-start(bf16[3,1024,256]{2,1,0:T(8,128)(2,1)S(1)} %collective-permute-done.19.refs_6_), channel_id=1, source_target_pairs={{0,1},{1,0},{2,3},{3,2},{4,5},{5,4},{6,7},{7,6},{8,9},{9,8},{10,11... | collective-permute-start | bytes 4718600 | tf_op jit(solution)/shard_map/ppermute | solution.py:590
  163.6 18.8 %collective-permute-start.22 = (bf16[256,1152]{1,0:T(8,128)(2,1)}, bf16[256,1152]{1,0:T(8,128)(2,1)S(1)}, u32[]{:S(2)}, u32[]{:S(2)}) collective-permute-start(bf16[256,1152]{1,0:T(8,128)(2,1)} %get-tuple-element.343), channel_id=1, source_target_pairs={{0,2},{2,0},{4,6},{6,4},{8,10},{10,8},{12,14},{14,12},{16,18},{18,... | collective-permute-start | bytes 1769480 | tf_op jit(solution)/shard_map/ppermute | solution.py:594
  165.1 17.3 %collective-permute-start.23 = (bf16[256,1152]{1,0:T(8,128)(2,1)}, bf16[256,1152]{1,0:T(8,128)(2,1)S(1)}, u32[]{:S(2)}, u32[]{:S(2)}) collective-permute-start(bf16[256,1152]{1,0:T(8,128)(2,1)} %get-tuple-element.344), channel_id=1, source_target_pairs={{0,4},{2,6},{4,0},{6,2},{8,12},{10,14},{12,8},{14,10},{16,20},{18,... | collective-permute-start | bytes 1769480 | tf_op jit(solution)/shard_map/ppermute | solution.py:594
  166.6 52.7 %collective-permute-start.28 = (bf16[3,1024,256]{2,1,0:T(8,128)(2,1)}, bf16[3,1024,256]{2,1,0:T(8,128)(2,1)}, u32[]{:S(2)}, u32[]{:S(2)}) collective-permute-start(bf16[3,1024,256]{2,1,0:T(8,128)(2,1)} %convert_add_fusion.1), channel_id=1, source_target_pairs={{0,8},{2,10},{4,12},{6,14},{8,16},{10,18},{12,20},{14,22},{16,24},... | collective-permute-start | bytes 4718600 | tf_op jit(solution)/shard_map/ppermute | solution.py:598
  182.4 18.8 %collective-permute-start.24 = (bf16[256,1152]{1,0:T(8,128)(2,1)}, bf16[256,1152]{1,0:T(8,128)(2,1)S(1)}, u32[]{:S(2)}, u32[]{:S(2)}) collective-permute-start(bf16[256,1152]{1,0:T(8,128)(2,1)} %get-tuple-element.353), channel_id=1, source_target_pairs={{0,2},{2,0},{4,6},{6,4},{8,10},{10,8},{12,14},{14,12},{16,18},{18,... | collective-permute-start | bytes 1769480 | tf_op jit(solution)/shard_map/ppermute | solution.py:594
  183.1 18.2 %collective-permute-start.25 = (bf16[256,1152]{1,0:T(8,128)(2,1)}, bf16[256,1152]{1,0:T(8,128)(2,1)}, u32[]{:S(2)}, u32[]{:S(2)}) collective-permute-start(bf16[256,1152]{1,0:T(8,128)(2,1)} %get-tuple-element.354), channel_id=1, source_target_pairs={{0,4},{2,6},{4,0},{6,2},{8,12},{10,14},{12,8},{14,10},{16,20},{18,... | collective-permute-start | bytes 1769480 | tf_op jit(solution)/shard_map/ppermute | solution.py:594
  201.2 18.0 %collective-permute-start.26 = (bf16[256,1152]{1,0:T(8,128)(2,1)}, bf16[256,1152]{1,0:T(8,128)(2,1)}, u32[]{:S(2)}, u32[]{:S(2)}) collective-permute-start(bf16[256,1152]{1,0:T(8,128)(2,1)} %add_convert_fusion.3), channel_id=1, source_target_pairs={{0,2},{2,0},{4,6},{6,4},{8,10},{10,8},{12,14},{14,12},{16,18},{18,... | collective-permute-start | bytes 1769480 | tf_op jit(solution)/shard_map/ppermute | solution.py:594
  202.7 16.5 %collective-permute-start.27 = (bf16[256,1152]{1,0:T(8,128)(2,1)}, bf16[256,1152]{1,0:T(8,128)(2,1)}, u32[]{:S(2)}, u32[]{:S(2)}) collective-permute-start(bf16[256,1152]{1,0:T(8,128)(2,1)} %add_convert_fusion.2), channel_id=1, source_target_pairs={{0,4},{2,6},{4,0},{6,2},{8,12},{10,14},{12,8},{14,10},{16,20},{18,... | collective-permute-start | bytes 1769480 | tf_op jit(solution)/shard_map/ppermute | solution.py:594
  225.6 13.2 %collective-permute-start.29 = (bf16[512,1024]{1,0:T(8,128)(2,1)}, bf16[512,1024]{1,0:T(8,128)(2,1)S(1)}, u32[]{:S(2)}, u32[]{:S(2)}) collective-permute-start(bf16[512,1024]{1,0:T(8,128)(2,1)} %get-tuple-element.384), channel_id=1, source_target_pairs={{0,1},{1,0},{2,3},{3,2},{4,5},{5,4},{6,7},{7,6},{8,9},{9,8},{10,11... | collective-permute-start | bytes 3145736 | tf_op jit(solution)/shard_map/ppermute | solution.py:590
  225.6 17.0 %collective-permute-start.30 = (bf16[256,1024]{1,0:T(8,128)(2,1)}, bf16[256,1024]{1,0:T(8,128)(2,1)S(1)}, u32[]{:S(2)}, u32[]{:S(2)}) collective-permute-start(bf16[256,1024]{1,0:T(8,128)(2,1)} %get-tuple-element.396), channel_id=1, source_target_pairs={{0,2},{2,0},{4,6},{6,4},{8,10},{10,8},{12,14},{14,12},{16,18},{18,... | collective-permute-start | bytes 1572872 | tf_op jit(solution)/shard_map/ppermute | solution.py:594
  226.2 16.4 %collective-permute-start.31 = (bf16[256,1024]{1,0:T(8,128)(2,1)}, bf16[256,1024]{1,0:T(8,128)(2,1)S(1)}, u32[]{:S(2)}, u32[]{:S(2)}) collective-permute-start(bf16[256,1024]{1,0:T(8,128)(2,1)} %get-tuple-element.397), channel_id=1, source_target_pairs={{0,4},{2,6},{4,0},{6,2},{8,12},{10,14},{12,8},{14,10},{16,20},{18,... | collective-permute-start | bytes 1572872 | tf_op jit(solution)/shard_map/ppermute | solution.py:594
  243.6 18.6 %collective-permute-start.34 = (bf16[3,1024,256]{2,1,0:T(8,128)(2,1)}, bf16[3,1024,256]{2,1,0:T(8,128)(2,1)S(1)}, u32[]{:S(2)}, u32[]{:S(2)}) collective-permute-start(bf16[3,1024,256]{2,1,0:T(8,128)(2,1)} %get-tuple-element.404), channel_id=1, source_target_pairs={{0,1},{1,0},{2,3},{3,2},{4,5},{5,4},{6,7},{7,6},{8,9},{9,8},{10,11... | collective-permute-start | bytes 4718600 | tf_op jit(solution)/shard_map/ppermute | solution.py:590
  243.6 18.6 %collective-permute-start.32 = (bf16[256,1024]{1,0:T(8,128)(2,1)}, bf16[256,1024]{1,0:T(8,128)(2,1)S(1)}, u32[]{:S(2)}, u32[]{:S(2)}) collective-permute-start(bf16[256,1024]{1,0:T(8,128)(2,1)} %get-tuple-element.355), channel_id=1, source_target_pairs={{0,2},{2,0},{4,6},{6,4},{8,10},{10,8},{12,14},{14,12},{16,18},{18,... | collective-permute-start | bytes 1572872 | tf_op jit(solution)/shard_map/ppermute | solution.py:594
  245.0 17.2 %collective-permute-start.33 = (bf16[256,1024]{1,0:T(8,128)(2,1)}, bf16[256,1024]{1,0:T(8,128)(2,1)S(1)}, u32[]{:S(2)}, u32[]{:S(2)}) collective-permute-start(bf16[256,1024]{1,0:T(8,128)(2,1)} %get-tuple-element.356), channel_id=1, source_target_pairs={{0,4},{2,6},{4,0},{6,2},{8,12},{10,14},{12,8},{14,10},{16,20},{18,... | collective-permute-start | bytes 1572872 | tf_op jit(solution)/shard_map/ppermute | solution.py:594
  270.8 31.7 %collective-permute-start.35 = (bf16[256,1024]{1,0:T(8,128)(2,1)}, bf16[256,1024]{1,0:T(8,128)(2,1)}, u32[]{:S(2)}, u32[]{:S(2)}) collective-permute-start(bf16[256,1024]{1,0:T(8,128)(2,1)} %get-tuple-element.607), channel_id=1, source_target_pairs={{0,2},{2,0},{4,6},{6,4},{8,10},{10,8},{12,14},{14,12},{16,18},{18,... | collective-permute-start | bytes 1572872 | tf_op jit(solution)/shard_map/ppermute | solution.py:594
  271.4 31.2 %collective-permute-start.36 = (bf16[256,1024]{1,0:T(8,128)(2,1)}, bf16[256,1024]{1,0:T(8,128)(2,1)}, u32[]{:S(2)}, u32[]{:S(2)}) collective-permute-start(bf16[256,1024]{1,0:T(8,128)(2,1)} %get-tuple-element.606), channel_id=1, source_target_pairs={{0,4},{2,6},{4,0},{6,2},{8,12},{10,14},{12,8},{14,10},{16,20},{18,... | collective-permute-start | bytes 1572872 | tf_op jit(solution)/shard_map/ppermute | solution.py:594
  271.9 30.7 %collective-permute-start.37 = (bf16[256,1024]{1,0:T(8,128)(2,1)}, bf16[256,1024]{1,0:T(8,128)(2,1)}, u32[]{:S(2)}, u32[]{:S(2)}) collective-permute-start(bf16[256,1024]{1,0:T(8,128)(2,1)} %get-tuple-element.605), channel_id=1, source_target_pairs={{0,6},{2,4},{4,2},{6,0},{8,14},{10,12},{12,10},{14,8},{16,22},{18,... | collective-permute-start | bytes 1572872 | tf_op jit(solution)/shard_map/ppermute | solution.py:594
  275.6 27.1 %collective-permute-start.38 = (bf16[1024,256]{1,0:T(8,128)(2,1)}, bf16[1024,256]{1,0:T(8,128)(2,1)}, u32[]{:S(2)}, u32[]{:S(2)}) collective-permute-start(bf16[1024,256]{1,0:T(8,128)(2,1)} %get-tuple-element.613), channel_id=1, source_target_pairs={{0,8},{2,10},{4,12},{6,14},{8,16},{10,18},{12,20},{14,22},{16,24},... | collective-permute-start | bytes 1572872 | tf_op jit(solution)/shard_map/ppermute | solution.py:598
  277.2 25.5 %collective-permute-start.39 = (bf16[1024,256]{1,0:T(8,128)(2,1)}, bf16[1024,256]{1,0:T(8,128)(2,1)}, u32[]{:S(2)}, u32[]{:S(2)}) collective-permute-start(bf16[1024,256]{1,0:T(8,128)(2,1)} %get-tuple-element.612), channel_id=1, source_target_pairs={{0,8},{2,10},{4,12},{6,14},{8,16},{10,18},{12,20},{14,22},{16,24},... | collective-permute-start | bytes 1572872 | tf_op jit(solution)/shard_map/ppermute | solution.py:598
  302.5 14.4 %collective-permute-start.44 = (bf16[1024,256]{1,0:T(8,128)(2,1)}, bf16[1024,256]{1,0:T(8,128)(2,1)S(1)}, u32[]{:S(2)}, u32[]{:S(2)}) collective-permute-start(bf16[1024,256]{1,0:T(8,128)(2,1)} %get-tuple-element.611), channel_id=1, source_target_pairs={{0,8},{2,10},{4,12},{6,14},{8,16},{10,18},{12,20},{14,22},{16,24},... | collective-permute-start | bytes 1572872 | tf_op jit(solution)/shard_map/ppermute | solution.py:598
  302.7 26.8 %collective-permute-start.45 = (bf16[3,1024,256]{2,1,0:T(8,128)(2,1)}, bf16[3,1024,256]{2,1,0:T(8,128)(2,1)}, u32[]{:S(2)}, u32[]{:S(2)}) collective-permute-start(bf16[3,1024,256]{2,1,0:T(8,128)(2,1)} %get-tuple-element.458), channel_id=1, source_target_pairs={{0,1},{1,0},{2,3},{3,2},{4,5},{5,4},{6,7},{7,6},{8,9},{9,8},{10,11... | collective-permute-start | bytes 4718600 | tf_op jit(solution)/shard_map/ppermute | solution.py:590
  309.8 19.6 %collective-permute-start.40 = (bf16[256,512]{1,0:T(8,128)(2,1)}, bf16[256,512]{1,0:T(8,128)(2,1)}, u32[]{:S(2)}, u32[]{:S(2)}) collective-permute-start(bf16[256,512]{1,0:T(8,128)(2,1)} %get-tuple-element.618), channel_id=1, source_target_pairs={{0,2},{2,0},{4,6},{6,4},{8,10},{10,8},{12,14},{14,12},{16,18},{18,... | collective-permute-start | bytes 786440 | tf_op jit(solution)/shard_map/ppermute | solution.py:594
  310.4 19.0 %collective-permute-start.41 = (bf16[256,512]{1,0:T(8,128)(2,1)}, bf16[256,512]{1,0:T(8,128)(2,1)}, u32[]{:S(2)}, u32[]{:S(2)}) collective-permute-start(bf16[256,512]{1,0:T(8,128)(2,1)} %get-tuple-element.617), channel_id=1, source_target_pairs={{0,4},{2,6},{4,0},{6,2},{8,12},{10,14},{12,8},{14,10},{16,20},{18,... | collective-permute-start | bytes 786440 | tf_op jit(solution)/shard_map/ppermute | solution.py:594
  311.2 18.2 %collective-permute-start.42 = (bf16[256,512]{1,0:T(8,128)(2,1)}, bf16[256,512]{1,0:T(8,128)(2,1)}, u32[]{:S(2)}, u32[]{:S(2)}) collective-permute-start(bf16[256,512]{1,0:T(8,128)(2,1)} %get-tuple-element.616), channel_id=1, source_target_pairs={{0,6},{2,4},{4,2},{6,0},{8,14},{10,12},{12,10},{14,8},{16,22},{18,... | collective-permute-start | bytes 786440 | tf_op jit(solution)/shard_map/ppermute | solution.py:594
  316.9 12.5 %collective-permute-start.43 = (bf16[128,1024]{1,0:T(8,128)(2,1)}, bf16[128,1024]{1,0:T(8,128)(2,1)}, u32[]{:S(2)}, u32[]{:S(2)}) collective-permute-start(bf16[128,1024]{1,0:T(8,128)(2,1)} %get-tuple-element.447), channel_id=1, source_target_pairs={{0,8},{2,10},{4,12},{6,14},{8,0},{10,2},{12,4},{14,6},{16,24},{18,... | collective-permute-start | bytes 786440 | tf_op jit(solution)/shard_map/ppermute | solution.py:827
  330.6 13.2 %collective-permute-start.47 = (bf16[1024,512]{1,0:T(8,128)(2,1)}, bf16[1024,512]{1,0:T(8,128)(2,1)S(1)}, u32[]{:S(2)}, u32[]{:S(2)}) collective-permute-start(bf16[1024,512]{1,0:T(8,128)(2,1)} %copy-done.21), channel_id=1, source_target_pairs={{0,1},{1,0},{2,3},{3,2},{4,5},{5,4},{6,7},{7,6},{8,9},{9,8},{10,11... | collective-permute-start | bytes 3145736 | tf_op jit(solution)/shard_map/ppermute | solution.py:590
  334.6 9.2 %collective-permute-start.46 = (bf16[64,1024]{1,0:T(8,128)(2,1)S(1)}, bf16[64,1024]{1,0:T(8,128)(2,1)S(1)}, u32[]{:S(2)}, u32[]{:S(2)}) collective-permute-start(bf16[64,1024]{1,0:T(8,128)(2,1)S(1)} %get-tuple-element.463), channel_id=1, source_target_pairs={{0,16},{2,18},{4,20},{6,22},{8,24},{10,26},{12,28},{14,30},{16,0},... | collective-permute-start | bytes 393224 | tf_op jit(solution)/shard_map/ppermute | solution.py:827
  343.8 14.4 %collective-permute-start.51 = (bf16[256,1024]{1,0:T(8,128)(2,1)}, bf16[256,1024]{1,0:T(8,128)(2,1)S(1)}, u32[]{:S(2)}, u32[]{:S(2)}) collective-permute-start(bf16[256,1024]{1,0:T(8,128)(2,1)} %add_convert_fusion.5), channel_id=1, source_target_pairs={{0,2},{2,0},{4,6},{6,4},{8,10},{10,8},{12,14},{14,12},{16,18},{18,... | collective-permute-start | bytes 1572872 | tf_op jit(solution)/shard_map/ppermute | solution.py:594
  344.5 13.8 %collective-permute-start.52 = (bf16[256,1024]{1,0:T(8,128)(2,1)}, bf16[256,1024]{1,0:T(8,128)(2,1)}, u32[]{:S(2)}, u32[]{:S(2)}) collective-permute-start(bf16[256,1024]{1,0:T(8,128)(2,1)} %add_convert_fusion.4), channel_id=1, source_target_pairs={{0,4},{2,6},{4,0},{6,2},{8,12},{10,14},{12,8},{14,10},{16,20},{18,... | collective-permute-start | bytes 1572872 | tf_op jit(solution)/shard_map/ppermute | solution.py:594
  349.9 8.4 %collective-permute-start.49 = (bf16[144,512]{1,0:T(8,128)(2,1)}, bf16[144,512]{1,0:T(8,128)(2,1)S(1)}, u32[]{:S(2)}, u32[]{:S(2)}) collective-permute-start(bf16[144,512]{1,0:T(8,128)(2,1)} %pad_maximum_fusion.4), channel_id=1, source_target_pairs={{0,8},{2,10},{4,12},{6,14},{8,0},{10,2},{12,4},{14,6},{16,24},{18,... | collective-permute-start | bytes 442376 | tf_op jit(solution)/shard_map/ppermute | solution.py:827
  350.0 8.3 %collective-permute-start.50 = (bf16[64,1024]{1,0:T(8,128)(2,1)S(1)}, bf16[64,1024]{1,0:T(8,128)(2,1)}, u32[]{:S(2)}, u32[]{:S(2)}) collective-permute-start(bf16[64,1024]{1,0:T(8,128)(2,1)S(1)} %add_convert_fusion.10), channel_id=1, source_target_pairs={{0,16},{2,18},{4,20},{6,22},{8,24},{10,26},{12,28},{14,30},{16,0},... | collective-permute-start | bytes 393224 | tf_op jit(solution)/shard_map/ppermute | solution.py:827
  359.4 7.6 %collective-permute-start.54 = (bf16[128,1024]{1,0:T(8,128)(2,1)S(1)}, bf16[128,1024]{1,0:T(8,128)(2,1)S(1)}, u32[]{:S(2)}, u32[]{:S(2)}) collective-permute-start(bf16[128,1024]{1,0:T(8,128)(2,1)S(1)} %maximum_select_fusion.4), channel_id=1, source_target_pairs={{0,8},{2,10},{4,12},{6,14},{8,0},{10,2},{12,4},{14,6},{16,24},{18,... | collective-permute-start | bytes 786440 | tf_op jit(solution)/shard_map/ppermute | solution.py:827
  359.5 5.6 %collective-permute-start.53 = (bf16[80,512]{1,0:T(8,128)(2,1)S(1)}, bf16[80,512]{1,0:T(8,128)(2,1)S(1)}, u32[]{:S(2)}, u32[]{:S(2)}) collective-permute-start(bf16[80,512]{1,0:T(8,128)(2,1)S(1)} %pad_maximum_fusion.5), channel_id=1, source_target_pairs={{0,16},{2,18},{4,20},{6,22},{8,24},{10,26},{12,28},{14,30},{16,0},... | collective-permute-start | bytes 245768 | tf_op jit(solution)/shard_map/ppermute | solution.py:827
  367.2 30.2 %collective-permute-start.58 = (bf16[256,1024]{1,0:T(8,128)(2,1)S(1)}, bf16[256,1024]{1,0:T(8,128)(2,1)S(1)}, u32[]{:S(2)}, u32[]{:S(2)}) collective-permute-start(bf16[256,1024]{1,0:T(8,128)(2,1)S(1)} %maximum_select_fusion.3.refs_0_), channel_id=1, source_target_pairs={{0,2},{2,0},{4,6},{6,4},{8,10},{10,8},{12,14},{14,12},{16,18},{18,... | collective-permute-start | bytes 1572872 | tf_op jit(solution)/shard_map/ppermute | solution.py:594
  368.7 28.7 %collective-permute-start.59 = (bf16[256,1024]{1,0:T(8,128)(2,1)S(1)}, bf16[256,1024]{1,0:T(8,128)(2,1)S(1)}, u32[]{:S(2)}, u32[]{:S(2)}) collective-permute-start(bf16[256,1024]{1,0:T(8,128)(2,1)S(1)} %maximum_select_fusion.3.refs_0_), channel_id=1, source_target_pairs={{0,4},{2,6},{4,0},{6,2},{8,12},{10,14},{12,8},{14,10},{16,20},{18,... | collective-permute-start | bytes 1572872 | tf_op jit(solution)/shard_map/ppermute | solution.py:594
  369.9 27.5 %collective-permute-start.60 = (bf16[256,1024]{1,0:T(8,128)(2,1)S(1)}, bf16[256,1024]{1,0:T(8,128)(2,1)S(1)}, u32[]{:S(2)}, u32[]{:S(2)}) collective-permute-start(bf16[256,1024]{1,0:T(8,128)(2,1)S(1)} %maximum_select_fusion.3.refs_0_), channel_id=1, source_target_pairs={{0,6},{2,4},{4,2},{6,0},{8,14},{10,12},{12,10},{14,8},{16,22},{18,... | collective-permute-start | bytes 1572872 | tf_op jit(solution)/shard_map/ppermute | solution.py:594
  370.7 5.6 %collective-permute-start.55 = (bf16[64,512]{1,0:T(8,128)(2,1)S(1)}, bf16[64,512]{1,0:T(8,128)(2,1)S(1)}, u32[]{:S(2)}, u32[]{:S(2)}) collective-permute-start(bf16[64,512]{1,0:T(8,128)(2,1)S(1)} %add_convert_fusion.11), channel_id=1, source_target_pairs={{0,16},{2,18},{4,20},{6,22},{8,24},{10,26},{12,28},{14,30},{16,0},... | collective-permute-start | bytes 196616 | tf_op jit(solution)/shard_map/ppermute | solution.py:827
  376.3 5.0 %collective-permute-start.56 = (bf16[128,512]{1,0:T(8,128)(2,1)S(1)}, bf16[128,512]{1,0:T(8,128)(2,1)S(1)}, u32[]{:S(2)}, u32[]{:S(2)}) collective-permute-start(bf16[128,512]{1,0:T(8,128)(2,1)S(1)} %maximum_select_fusion.6), channel_id=1, source_target_pairs={{0,8},{2,10},{4,12},{6,14},{8,0},{10,2},{12,4},{14,6},{16,24},{18,... | collective-permute-start | bytes 393224 | tf_op jit(solution)/shard_map/ppermute | solution.py:827
  378.5 17.5 %collective-permute-start.57 = (bf16[512,512]{1,0:T(8,128)(2,1)}, bf16[512,512]{1,0:T(8,128)(2,1)S(1)}, u32[]{:S(2)}, u32[]{:S(2)}) collective-permute-start(bf16[512,512]{1,0:T(8,128)(2,1)} %get-tuple-element.615), channel_id=1, source_target_pairs={{0,1},{1,0},{2,3},{3,2},{4,5},{5,4},{6,7},{7,6},{8,9},{9,8},{10,11... | collective-permute-start | bytes 1572872 | tf_op jit(solution)/shard_map/ppermute | solution.py:590
  382.6 14.7 %collective-permute-start.61 = (bf16[1024,256]{1,0:T(8,128)(2,1)}, bf16[1024,256]{1,0:T(8,128)(2,1)}, u32[]{:S(2)}, u32[]{:S(2)}) collective-permute-start(bf16[1024,256]{1,0:T(8,128)(2,1)} %get-tuple-element.610), channel_id=1, source_target_pairs={{0,8},{2,10},{4,12},{6,14},{8,16},{10,18},{12,20},{14,22},{16,24},... | collective-permute-start | bytes 1572872 | tf_op jit(solution)/shard_map/ppermute | solution.py:598
  397.4 7.3 %collective-permute-start.66 = (bf16[3,1024,256]{2,1,0:T(8,128)(2,1)}, bf16[3,1024,256]{2,1,0:T(8,128)(2,1)}, u32[]{:S(2)}, u32[]{:S(2)}) collective-permute-start(bf16[3,1024,256]{2,1,0:T(8,128)(2,1)} %get-tuple-element.521), channel_id=1, source_target_pairs={{0,1},{1,0},{2,3},{3,2},{4,5},{5,4},{6,7},{7,6},{8,9},{9,8},{10,11... | collective-permute-start | bytes 4718600 | tf_op jit(solution)/shard_map/ppermute | solution.py:590
  398.5 16.9 %collective-permute-start.67 = (bf16[1024,256]{1,0:T(8,128)(2,1)}, bf16[1024,256]{1,0:T(8,128)(2,1)}, u32[]{:S(2)}, u32[]{:S(2)}) collective-permute-start(bf16[1024,256]{1,0:T(8,128)(2,1)} %get-tuple-element.609), channel_id=1, source_target_pairs={{0,8},{2,10},{4,12},{6,14},{8,16},{10,18},{12,20},{14,22},{16,24},... | collective-permute-start | bytes 1572872 | tf_op jit(solution)/shard_map/ppermute | solution.py:598
  399.6 26.2 %collective-permute-start.68 = (bf16[1024,256]{1,0:T(8,128)(2,1)}, bf16[1024,256]{1,0:T(8,128)(2,1)}, u32[]{:S(2)}, u32[]{:S(2)}) collective-permute-start(bf16[1024,256]{1,0:T(8,128)(2,1)} %get-tuple-element.608), channel_id=1, source_target_pairs={{0,8},{2,10},{4,12},{6,14},{8,16},{10,18},{12,20},{14,22},{16,24},... | collective-permute-start | bytes 1572872 | tf_op jit(solution)/shard_map/ppermute | solution.py:598
  402.0 26.9 %collective-permute-start.63 = (bf16[272,512]{1,0:T(8,128)(2,1)S(1)}, bf16[272,512]{1,0:T(8,128)(2,1)S(1)}, u32[]{:S(2)}, u32[]{:S(2)}) collective-permute-start(bf16[272,512]{1,0:T(8,128)(2,1)S(1)} %pad_maximum_fusion.3.refs_4_), channel_id=1, source_target_pairs={{0,2},{2,0},{4,6},{6,4},{8,10},{10,8},{12,14},{14,12},{16,18},{18,... | collective-permute-start | bytes 835592 | tf_op jit(solution)/shard_map/ppermute | solution.py:594
  403.3 25.6 %collective-permute-start.64 = (bf16[272,512]{1,0:T(8,128)(2,1)S(1)}, bf16[272,512]{1,0:T(8,128)(2,1)S(1)}, u32[]{:S(2)}, u32[]{:S(2)}) collective-permute-start(bf16[272,512]{1,0:T(8,128)(2,1)S(1)} %pad_maximum_fusion.3.refs_4_), channel_id=1, source_target_pairs={{0,4},{2,6},{4,0},{6,2},{8,12},{10,14},{12,8},{14,10},{16,20},{18,... | collective-permute-start | bytes 835592 | tf_op jit(solution)/shard_map/ppermute | solution.py:594
  404.7 24.2 %collective-permute-start.65 = (bf16[272,512]{1,0:T(8,128)(2,1)S(1)}, bf16[272,512]{1,0:T(8,128)(2,1)S(1)}, u32[]{:S(2)}, u32[]{:S(2)}) collective-permute-start(bf16[272,512]{1,0:T(8,128)(2,1)S(1)} %pad_maximum_fusion.3.refs_4_), channel_id=1, source_target_pairs={{0,6},{2,4},{4,2},{6,0},{8,14},{10,12},{12,10},{14,8},{16,22},{18,... | collective-permute-start | bytes 835592 | tf_op jit(solution)/shard_map/ppermute | solution.py:594
  (93 other events, 488.2 us)

commit v5 on v4

--- a/solution.py
+++ b/solution.py
@@ -714,6 +714,9 @@
         k = len(slots)
         slots.append([held[k]] + [hop(held[k], s) for s in range(1, n_tensor)])
 
+    def add(a, b):
+        return (a.astype(F32) + b.astype(F32)).astype(BF16)
+
     def weight_pieces(k, fence=()):
         parts = list(saved[k].values())
         if fence:
@@ -729,13 +732,13 @@
 
     def weight_total(k):
         grads = weight_pieces(k)
-        return total_of(grads, hop_back(grads))
+        return total_of(grads, hop_back(grads)).astype(BF16)
 
     def send_on(k, moving):
         total = totals[k]
         if moving is not None:
-            total = total + moving.astype(F32)
-        return ring(total.astype(BF16)) if k else total
+            total = add(total, moving)
+        return ring(total)
 
     for _ in range(1, group):
         add_slot()
@@ -836,9 +839,6 @@
         stay, go = part(a, upper(bit), rows), part(a, 1 - upper(bit), rows)
         return stay, go if tail is None else jnp.concatenate([go, tail], axis=0)
 
-    def add(a, b):
-        return (a.astype(F32) + b.astype(F32)).astype(BF16)
-
     def z_join(a, got, bit):
         return jnp.where(upper(bit) == 0, jnp.concatenate([a, got], 0), jnp.concatenate([got, a], 0))
 
@@ -937,12 +937,15 @@
     second, block_out, first_all, ring_on[0], late[0] = after((second, block_out, first_all, ring_on[0], late[0]))
     late_got = hop_back(late[0])
     second_all = [second] + [plane(second, m) for m in range(1, PLANE)]
-    final = [a + b.astype(F32) for a, b in zip(total_of(late[0], late_got), ring_on)]
-    final[2] = final[2].T
+    own = total_of(late[0], late_got)
+    final = [own[c] + ring_on[c].astype(F32) for c in range(2)]
     second_all, final = after((second_all, final))
     gains = functools.reduce(jnp.add, [v[rows : rows + gain_rows].astype(F32) for v in second_all]).reshape(-1)
     cuts = [w.shape[1] // parts for w in (w_query, key_matrix, value_matrix)]
-    grad_query, grad_key, grad_value, grad_out = lay_out(p_at.reshape(1), first_all, second_all, parts, cuts)
+    laid = lay_out(p_at.reshape(1), first_all, second_all, parts, cuts)
+    grad_query, grad_key, grad_value, grad_out = laid
+    grad_query, down_arrived = after((grad_query, ring_on[2]))
+    final.append((own[2] + down_arrived.astype(F32)).T)
     return (
         block_out,
         grad_tokens,

time: 440 us -> 434 us (0.986)
  waiting for transfers between devices: 70.1 us -> 63.8 us
    ppermute x10, waiting for transfers between devices: 28.8 us -> 21.4 us  [ring(): return jax.tree.map(lambda a: lax.ppermute(a, 'expert', pairs), x)]
  transfers between devices with their start and end apart: 69 -> 69, of which waited for: 20 -> 21; matrix products, arithmetic and copies ran while one was open for 13% -> 14% of each run, Pallas kernels for 42% -> 44%
where the time goes in v5:
time: 434 us; the launch traced here: 429 us
  Pallas kernels  207 us (48%)
  waiting for transfers between devices  63.8 us (15%)
  starting transfers between devices  59.9 us (14%)
  other arithmetic  48.1 us (11%)
  local copies, waits for them, and re-layouts  36.1 us (8%)
  matrix products  12 us (3%)
    pallas_call x8, Pallas kernels, expert_data(): pl.pallas_call(functools.partial(data_kernel, first, last, blocks, tiles,...  110 us
    pallas_call x4, Pallas kernels, expert_weight(): pl.pallas_call(functools.partial(weight_kernel, tuple(shape), pieces), gr...  48.6 us
    ppermute x34, starting transfers between devices, plane(): return jax.tree.map(lambda a: lax.ppermute(a, 'expert', pairs), x)  38.4 us
    unnamed x180, local copies, waits for them, and re-layouts  27 us
    ppermute x8, waiting for transfers between devices, swap(): return lax.ppermute(a, 'expert', pairs)  23.2 us
    ppermute x10, waiting for transfers between devices, ring(): return jax.tree.map(lambda a: lax.ppermute(a, 'expert', pairs), x)  21.4 us
    pallas_call x2, Pallas kernels, attn_backward(): pl.pallas_call(functools.partial(attn_bwd_kernel, block), grid=(count,),...  20 us
    ppermute x10, starting transfers between devices, ring(): return jax.tree.map(lambda a: lax.ppermute(a, 'expert', pairs), x)  12.5 us
  transfers between devices with their start and end apart: 69, of which 21 were waited for; matrix products, arithmetic and copies ran while one was open for 14% of the time, Pallas kernels for 44%

profile of v5, /device:TPU:0, one launch (start us, length us, event | category | flops | bytes accessed | tf_op | source)
XLA Modules:
  0.0 429.1 jit_solution(12362802946439843256)
XLA Ops:
  6.0 2.0 copy.97
  8.5 2.7 pad_maximum_fusion.refs_4_
  11.8 1.7 maximum_select_fusion.1
  13.6 2.7 collective-permute-start.2
  16.3 1.5 collective-permute-start.3
  18.3 1.9 collective-permute-start.9
  24.8 5.3 %attn_forward.3 = (bf16[256,1024]{1,0:T(8,128)(2,1)S(1)}, bf16[128,1024]{1,0:T(8,128)(2,1)S(1)}, bf16[256,1024]{1,0:T(8,128)(2,1)S(1)}, f32[2,2,1024]{2,1,0:T(2,128)S(1)}) custom-call(f32[512,1024]{1,0:T(8,128)S(1)} %convolution_bitcast_fusion.q_ref, f32[256,1024]{1,0:T(8,128)S(1)} %convolution_bitcast_fusion.1.k_ref, bf16[256,1024]{1,0:T(8,128)(2,1)S(1)} %fusion.6.v_ref, ...), custom_call_target="tpu_custom_call" | custom-call | flops 2147483648 | bytes 2097152 | tf_op jit(solution)/shard_map/attn_forward/pallas_call | solution.py:122
  32.2 5.2 %attn_forward.2 = (bf16[256,1024]{1,0:T(8,128)(2,1)S(1)}, bf16[128,1024]{1,0:T(8,128)(2,1)S(1)}, bf16[256,1024]{1,0:T(8,128)(2,1)S(1)}, f32[2,2,1024]{2,1,0:T(2,128)S(1)}) custom-call(f32[512,1024]{1,0:T(8,128)S(1)} %convolution_bitcast_fusion.q_ref, f32[256,1024]{1,0:T(8,128)S(1)} %convolution_bitcast_fusion.1.k_ref, bf16[256,1024]{1,0:T(8,128)(2,1)S(1)} %fusion.6.v_ref, ...), custom_call_target="tpu_custom_call" | custom-call | flops 2147483648 | bytes 2097152 | tf_op jit(solution)/shard_map/attn_forward/pallas_call | solution.py:122
  37.5 5.3 %collective-permute-done.2.refs_2_.refs_8_.refs_14_ = bf16[512,1152]{1,0:T(8,128)(2,1)S(1)} collective-permute-done((bf16[512,1152]{1,0:T(8,128)(2,1)S(1)}, bf16[512,1152]{1,0:T(8,128)(2,1)S(1)}, u32[]{:S(2)}, u32[]{:S(2)}) %collective-permute-start.2) | collective-permute-done | bytes 1179680 | tf_op jit(solution)/shard_map/ppermute | solution.py:594
  44.3 1.6 collective-permute-start.7
  50.5 3.9 join_heads.1
  54.4 2.5 collective-permute-done.9.refs_6_
  56.9 2.0 collective-permute-done.7.refs_2_.refs_20_
  60.2 2.1 collective-permute-start.17
  62.3 1.5 collective-permute-done.10.refs_7_
  66.4 1.6 collective-permute-start.16
  68.7 12.8 %expert_data.8 = (bf16[512,1024]{1,0:T(8,128)(2,1)}, bf16[512,1024]{1,0:T(8,128)(2,1)}, f32[512,128]{1,0:T(8,128)}, bf16[512,1024]{1,0:T(8,128)(2,1)}, bf16[512,...) custom-call(s32[2]{0:T(128)} %get-tuple-element.633.expert_ref, bf16[256,1024]{1,0:T(8,128)(2,1)} %copy-done.4, ...), custom_call_target="tpu_custom_call" | custom-call | flops 1610612736 | bytes 12582912 | tf_op jit(solution)/shard_map/expert_data/pallas_call | solution.py:295
  82.3 12.8 %expert_data.9 = (bf16[512,1024]{1,0:T(8,128)(2,1)}, bf16[512,1024]{1,0:T(8,128)(2,1)}, f32[512,128]{1,0:T(8,128)}, bf16[512,1024]{1,0:T(8,128)(2,1)}, bf16[512,...) custom-call(s32[2]{0:T(128)} %get-tuple-element.633.expert_ref, ...), custom_call_target="tpu_custom_call" | custom-call | flops 1610612736 | bytes 12582912 | tf_op jit(solution)/shard_map/expert_data/pallas_call | solution.py:295
  95.0 4.7 %collective-permute-done.17.refs_4_ = bf16[3,1024,256]{2,1,0:T(8,128)(2,1)} collective-permute-done((bf16[3,1024,256]{2,1,0:T(8,128)(2,1)}, bf16[3,1024,256]{2,1,0:T(8,128)(2,1)}, u32[]{:S(2)}, u32[]{:S(2)}) %collective-permute-start.17) | collective-permute-done | bytes 1572896 | tf_op jit(solution)/shard_map/ppermute | solution.py:598
  101.1 12.9 %expert_data.10 = (bf16[512,1024]{1,0:T(8,128)(2,1)}, bf16[512,1024]{1,0:T(8,128)(2,1)}, f32[512,128]{1,0:T(8,128)}, bf16[512,1024]{1,0:T(8,128)(2,1)}, bf16[512...) custom-call(s32[2]{0:T(128)} %get-tuple-element.633.expert_ref, ...), custom_call_target="tpu_custom_call" | custom-call | flops 1610612736 | bytes 12582912 | tf_op jit(solution)/shard_map/expert_data/pallas_call | solution.py:295
  114.8 12.7 %expert_data.11 = (bf16[512,1024]{1,0:T(8,128)(2,1)}, bf16[512,1024]{1,0:T(8,128)(2,1)}, f32[512,128]{1,0:T(8,128)}, bf16[512,1024]{1,0:T(8,128)(2,1)}, bf16[512...) custom-call(s32[2]{0:T(128)} %get-tuple-element.633.expert_ref, ...), custom_call_target="tpu_custom_call" | custom-call | flops 1610612736 | bytes 12582912 | tf_op jit(solution)/shard_map/expert_data/pallas_call | solution.py:295
  127.6 12.1 %expert_weight.4 = (bf16[3,1024,256]{2,1,0:T(8,128)(2,1)}, bf16[3,1024,256]{2,1,0:T(8,128)(2,1)}) custom-call(bf16[256,1024]{1,0:T(8,128)(2,1)} %copy-done.4, bf16[256,1024]{1,0:T(8,128)(2,1)} %copy-done.5, bf16[512,1152]{1,0:T(8,128)(2,1)} %copy-done.2, bf16[512,1152]{1,0:T(8,128)(2,1)} %copy-done.2, bf16[512,1024]{1,0:T(8,128)(2,1)} %get-tuple-element.327.refs_4_, ...), custom_call_target="tpu_custom_call" | custom-call | flops 1073741824 | bytes 17825792 | tf_op jit(solution)/shard_map/expert_weight/pallas_call | solution.py:351
  140.4 4.4 %collective-permute-done.21 = bf16[3,1024,256]{2,1,0:T(8,128)(2,1)S(1)} collective-permute-done((bf16[3,1024,256]{2,1,0:T(8,128)(2,1)}, bf16[3,1024,256]{2,1,0:T(8,128)(2,1)S(1)}, u32[]{:S(2)}, u32[]{:S(2)}) %collective-permute-start.21) | collective-permute-done | bytes 1572896 | tf_op jit(solution)/shard_map/ppermute | solution.py:590
  144.7 2.9 add_convert_fusion.2
  148.8 14.8 %expert_data.12 = (bf16[256,1024]{1,0:T(8,128)(2,1)}, bf16[256,1024]{1,0:T(8,128)(2,1)}, bf16[256,1152]{1,0:T(8,128)(2,1)}, bf16[256,1152]{1,0:T(8,128)(2,1)}, b...) custom-call(s32[2]{0:T(128)} %get-tuple-element.368.expert_ref, ...), custom_call_target="tpu_custom_call" | custom-call | flops 1610612736 | bytes 12582912 | tf_op jit(solution)/shard_map/expert_data/pallas_call | solution.py:295
  165.1 1.5 collective-permute-start.23
  167.9 14.6 %expert_data.13 = (bf16[256,1024]{1,0:T(8,128)(2,1)}, bf16[256,1024]{1,0:T(8,128)(2,1)}, bf16[256,1152]{1,0:T(8,128)(2,1)}, bf16[256,1152]{1,0:T(8,128)(2,1)}, b...) custom-call(s32[2]{0:T(128)} %get-tuple-element.368.expert_ref, ...), custom_call_target="tpu_custom_call" | custom-call | flops 1610612736 | bytes 12582912 | tf_op jit(solution)/shard_map/expert_data/pallas_call | solution.py:295
  183.7 14.6 %expert_data.14 = (bf16[256,1024]{1,0:T(8,128)(2,1)}, bf16[256,1024]{1,0:T(8,128)(2,1)}, bf16[256,1152]{1,0:T(8,128)(2,1)}, bf16[256,1152]{1,0:T(8,128)(2,1)}, b...) custom-call(s32[2]{0:T(128)} %get-tuple-element.368.expert_ref, ...), custom_call_target="tpu_custom_call" | custom-call | flops 1610612736 | bytes 12582912 | tf_op jit(solution)/shard_map/expert_data/pallas_call | solution.py:295
  198.3 2.1 add_convert_fusion.3
  204.3 15.0 %expert_data.15 = (bf16[256,1024]{1,0:T(8,128)(2,1)}, bf16[256,1024]{1,0:T(8,128)(2,1)}, bf16[256,1152]{1,0:T(8,128)(2,1)}, bf16[256,1152]{1,0:T(8,128)(2,1)}, b...) custom-call(s32[2]{0:T(128)} %get-tuple-element.368.expert_ref, ...), custom_call_target="tpu_custom_call" | custom-call | flops 1610612736 | bytes 12582912 | tf_op jit(solution)/shard_map/expert_data/pallas_call | solution.py:295
  221.5 4.2 turn_back.1
  226.8 12.1 %expert_weight.5 = (bf16[3,1024,256]{2,1,0:T(8,128)(2,1)}, bf16[3,1024,256]{2,1,0:T(8,128)(2,1)}) custom-call(bf16[256,1024]{1,0:T(8,128)(2,1)} %copy-done.62, bf16[256,1024]{1,0:T(8,128)(2,1)} %collective-permute-done.14.refs_1_.refs_19_, bf16[256,1152]{1,0:T(8,128)(2,1)} %copy-done.59, bf16[256,1152]{1,0:T(8,128)(2,1)} %copy-done.60, ...), custom_call_target="tpu_custom_call" | custom-call | flops 1073741824 | bytes 17825792 | tf_op jit(solution)/shard_map/expert_weight/pallas_call | solution.py:351
  238.9 3.7 maximum_select_fusion
  245.1 1.5 collective-permute-start.33
  246.6 2.9 fusion.4.do_ref
  252.2 10.0 %attn_backward.2 = (bf16[256,1024]{1,0:T(8,128)(2,1)S(1)}, bf16[128,1024]{1,0:T(8,128)(2,1)S(1)}, bf16[128,1024]{1,0:T(8,128)(2,1)S(1)}) custom-call(bf16[256,1024]{1,0:T(8,128)(2,1)S(1)} %copy-done.39, bf16[128,1024]{1,0:T(8,128)(2,1)S(1)} %copy-done.43, bf16[256,1024]{1,0:T(8,128)(2,1)S(1)} %copy-done.29, bf16[512,1024]{1,0:T(8,128)(2,1)S(1)} %fusion.4.do_ref, ...), custom_call_target="tpu_custom_call" | custom-call | flops 2147483648 | bytes 2097152 | tf_op jit(solution)/shard_map/attn_backward/pallas_call | solution.py:141
  266.7 3.0 add_convert_fusion.1
  272.0 2.4 collective-permute-start.37
  275.6 1.6 collective-permute-start.38
  277.2 2.1 collective-permute-start.39
  280.2 10.0 %attn_backward.3 = (bf16[256,1024]{1,0:T(8,128)(2,1)S(1)}, bf16[128,1024]{1,0:T(8,128)(2,1)S(1)}, bf16[128,1024]{1,0:T(8,128)(2,1)S(1)}) custom-call(bf16[256,1024]{1,0:T(8,128)(2,1)S(1)} %copy-done.37, bf16[128,1024]{1,0:T(8,128)(2,1)S(1)} %copy-done.41, bf16[256,1024]{1,0:T(8,128)(2,1)S(1)} %copy-done.29, bf16[512,1024]{1,0:T(8,128)(2,1)S(1)} %copy-done.35, ...), custom_call_target="tpu_custom_call" | custom-call | flops 2147483648 | bytes 2097152 | tf_op jit(solution)/shard_map/attn_backward/pallas_call | solution.py:141
  290.3 12.2 %expert_weight.6 = (bf16[3,1024,256]{2,1,0:T(8,128)(2,1)}, bf16[3,1024,256]{2,1,0:T(8,128)(2,1)}) custom-call(bf16[256,1024]{1,0:T(8,128)(2,1)} %copy-done.62, bf16[256,1024]{1,0:T(8,128)(2,1)} %collective-permute-done.14.refs_1_.refs_19_, bf16[256,1152]{1,0:T(8,128)(2,1)} %copy-done.59, bf16[256,1152]{1,0:T(8,128)(2,1)} %copy-done.60, ...), custom_call_target="tpu_custom_call" | custom-call | flops 1073741824 | bytes 17825792 | tf_op jit(solution)/shard_map/expert_weight/pallas_call | solution.py:351
  302.8 2.0 add_convert_fusion.7
  311.2 2.1 collective-permute-start.42
  313.3 3.6 collective-permute-done.44
  321.9 6.3 %input_terms.1 = (f32[1024,512]{1,0:T(8,128)}, bf16[1024,512]{1,0:T(8,128)(2,1)S(1)}, f32[1024,1]{1,0:T(8,128)S(1)}) custom-call(s32[1]{0:T(128)} %bitcast.9.at_ref, bf16[1024,1024]{1,0:T(8,128)(2,1)} %x_ref.1, f32[1,1024]{1,0:T(1,128)S(1)} %bitcast.91, bf16[256,1024]{1,0:T(8,128)(2,1)S(1)} %copy-done.33, bf16[128,1024]{1,0:T(8,128)(2,1)S(1)} %copy-done.25, ...), custom_call_target="tpu_custom_call" | custom-call | flops 2147483648 | bytes 8388608 | tf_op jit(solution)/shard_map/input_terms/pallas_call | solution.py:448
  331.8 2.4 add_convert_fusion.6
  336.0 7.8 %collective-permute-done.46 = bf16[64,1024]{1,0:T(8,128)(2,1)S(1)} collective-permute-done((bf16[64,1024]{1,0:T(8,128)(2,1)S(1)}, bf16[64,1024]{1,0:T(8,128)(2,1)S(1)}, u32[]{:S(2)}, u32[]{:S(2)}) %collective-permute-start.46) | collective-permute-done | bytes 131104 | tf_op jit(solution)/shard_map/ppermute | solution.py:830
  345.3 3.9 multiply_add_fusion
  350.0 1.5 collective-permute-start.50
  351.5 6.8 %collective-permute-done.50 = bf16[64,1024]{1,0:T(8,128)(2,1)} collective-permute-done((bf16[64,1024]{1,0:T(8,128)(2,1)S(1)}, bf16[64,1024]{1,0:T(8,128)(2,1)}, u32[]{:S(2)}, u32[]{:S(2)}) %collective-permute-start.50) | collective-permute-done | bytes 131104 | tf_op jit(solution)/shard_map/ppermute | solution.py:830
  361.0 2.5 add_convert_fusion
  363.5 1.6 collective-permute-done.53
  365.1 2.0 collective-permute-done.54
  374.2 2.1 collective-permute-done.55
  378.5 2.9 collective-permute-done.56
  383.8 12.1 %expert_weight.7 = (bf16[3,1024,256]{2,1,0:T(8,128)(2,1)}, bf16[3,1024,256]{2,1,0:T(8,128)(2,1)}) custom-call(bf16[256,1024]{1,0:T(8,128)(2,1)} %copy-done.4, bf16[256,1024]{1,0:T(8,128)(2,1)} %copy-done.5, bf16[512,1152]{1,0:T(8,128)(2,1)} %copy-done.2, bf16[512,1152]{1,0:T(8,128)(2,1)} %copy-done.2, bf16[512,1024]{1,0:T(8,128)(2,1)} %get-tuple-element.508.refs_4_, ...), custom_call_target="tpu_custom_call" | custom-call | flops 1073741824 | bytes 17825792 | tf_op jit(solution)/shard_map/expert_weight/pallas_call | solution.py:351
  396.0 2.6 maximum_select_fusion.2
  400.9 1.6 collective-permute-done.62
  407.8 2.2 convert_add_fusion
  410.0 6.6 %collective-permute-done.67 = bf16[1024,256]{1,0:T(8,128)(2,1)} collective-permute-done((bf16[1024,256]{1,0:T(8,128)(2,1)}, bf16[1024,256]{1,0:T(8,128)(2,1)}, u32[]{:S(2)}, u32[]{:S(2)}) %collective-permute-start.67) | collective-permute-done | bytes 524320 | tf_op jit(solution)/shard_map/ppermute | solution.py:598
  416.6 2.6 fusion.11
  419.6 3.1 lay_out.1
  422.7 4.1 collective-permute-done.68
  (370 shorter events, 97.2 us)
Async XLA Ops:
  5.2 6.6 %collective-permute-start = (bf16[512,512]{1,0:T(8,128)(2,1)}, bf16[512,512]{1,0:T(8,128)(2,1)}, u32[]{:S(2)}, u32[]{:S(2)}) collective-permute-start(bf16[512,512]{1,0:T(8,128)(2,1)} %get-tuple-element.277), channel_id=1, source_target_pairs={{0,1},{1,0},{2,3},{3,2},{4,5},{5,4},{6,7},{7,6},{8,9},{9,8},{10,11... | collective-permute-start | bytes 1572872 | tf_op jit(solution)/shard_map/ppermute | solution.py:590
  5.6 41.0 %collective-permute-start.6 = (bf16[512,1024]{1,0:T(8,128)(2,1)S(1)}, bf16[512,1024]{1,0:T(8,128)(2,1)S(1)}, u32[]{:S(2)}, u32[]{:S(2)}) collective-permute-start(bf16[512,1024]{1,0:T(8,128)(2,1)S(1)} %copy-done.6), channel_id=1, source_target_pairs={{0,1},{1,0},{2,3},{3,2},{4,5},{5,4},{6,7},{7,6},{8,9},{9,8},{10,11... | collective-permute-start | bytes 3145736 | tf_op jit(solution)/shard_map/ppermute | solution.py:590
  13.6 29.2 %collective-permute-start.2 = (bf16[512,1152]{1,0:T(8,128)(2,1)S(1)}, bf16[512,1152]{1,0:T(8,128)(2,1)S(1)}, u32[]{:S(2)}, u32[]{:S(2)}) collective-permute-start(bf16[512,1152]{1,0:T(8,128)(2,1)S(1)} %pad_maximum_fusion.1.refs_2_.refs_3_.grad_ref.refs_20_.refs_21_), channel_id=1, source_target_pairs={{0,2},{2,0},{4,6},{6,4},{8,10},{10,8},{12,14},{14,12},{16,18},{18,... | collective-permute-start | bytes 3538952 | tf_op jit(solution)/shard_map/ppermute | solution.py:594
  16.3 27.9 %collective-permute-start.3 = (bf16[512,1152]{1,0:T(8,128)(2,1)S(1)}, bf16[512,1152]{1,0:T(8,128)(2,1)S(1)}, u32[]{:S(2)}, u32[]{:S(2)}) collective-permute-start(bf16[512,1152]{1,0:T(8,128)(2,1)S(1)} %pad_maximum_fusion.1.refs_2_.refs_3_.grad_ref.refs_20_.refs_21_), channel_id=1, source_target_pairs={{0,4},{2,6},{4,0},{6,2},{8,12},{10,14},{12,8},{14,10},{16,20},{18,... | collective-permute-start | bytes 3538952 | tf_op jit(solution)/shard_map/ppermute | solution.py:594
  18.3 38.6 %collective-permute-start.9 = (bf16[3,1024,256]{2,1,0:T(8,128)(2,1)}, bf16[3,1024,256]{2,1,0:T(8,128)(2,1)}, u32[]{:S(2)}, u32[]{:S(2)}) collective-permute-start(bf16[3,1024,256]{2,1,0:T(8,128)(2,1)} %pad_maximum_fusion.refs_4_), channel_id=1, source_target_pairs={{0,8},{2,10},{4,12},{6,14},{8,16},{10,18},{12,20},{14,22},{16,24},... | collective-permute-start | bytes 4718600 | tf_op jit(solution)/shard_map/ppermute | solution.py:598
  44.3 14.6 %collective-permute-start.7 = (bf16[256,1152]{1,0:T(8,128)(2,1)S(1)}, bf16[256,1152]{1,0:T(8,128)(2,1)S(1)}, u32[]{:S(2)}, u32[]{:S(2)}) collective-permute-start(bf16[256,1152]{1,0:T(8,128)(2,1)S(1)} %slice.81), channel_id=1, source_target_pairs={{0,4},{2,6},{4,0},{6,2},{8,12},{10,14},{12,8},{14,10},{16,20},{18,... | collective-permute-start | bytes 1769480 | tf_op jit(solution)/shard_map/ppermute | solution.py:594
  45.9 14.3 %collective-permute-start.8 = (bf16[256,1152]{1,0:T(8,128)(2,1)S(1)}, bf16[256,1152]{1,0:T(8,128)(2,1)S(1)}, u32[]{:S(2)}, u32[]{:S(2)}) collective-permute-start(bf16[256,1152]{1,0:T(8,128)(2,1)S(1)} %slice.82), channel_id=1, source_target_pairs={{0,2},{2,0},{4,6},{6,4},{8,10},{10,8},{12,14},{14,12},{16,18},{18,... | collective-permute-start | bytes 1769480 | tf_op jit(solution)/shard_map/ppermute | solution.py:594
  48.1 14.2 %collective-permute-start.1 = (bf16[3,1024,256]{2,1,0:T(8,128)(2,1)}, bf16[3,1024,256]{2,1,0:T(8,128)(2,1)S(1)}, u32[]{:S(2)}, u32[]{:S(2)}) collective-permute-start(bf16[3,1024,256]{2,1,0:T(8,128)(2,1)} %pad_maximum_fusion.refs_4_), channel_id=1, source_target_pairs={{0,1},{1,0},{2,3},{3,2},{4,5},{5,4},{6,7},{7,6},{8,9},{9,8},{10,11... | collective-permute-start | bytes 4718600 | tf_op jit(solution)/shard_map/ppermute | solution.py:590
  60.2 39.5 %collective-permute-start.17 = (bf16[3,1024,256]{2,1,0:T(8,128)(2,1)}, bf16[3,1024,256]{2,1,0:T(8,128)(2,1)}, u32[]{:S(2)}, u32[]{:S(2)}) collective-permute-start(bf16[3,1024,256]{2,1,0:T(8,128)(2,1)} %collective-permute-done.9.refs_6_), channel_id=1, source_target_pairs={{0,8},{2,10},{4,12},{6,14},{8,16},{10,18},{12,20},{14,22},{16,24},... | collective-permute-start | bytes 4718600 | tf_op jit(solution)/shard_map/ppermute | solution.py:598
  63.9 17.6 %collective-permute-start.11 = (bf16[256,1024]{1,0:T(8,128)(2,1)S(1)}, bf16[256,1024]{1,0:T(8,128)(2,1)S(1)}, u32[]{:S(2)}, u32[]{:S(2)}) collective-permute-start(bf16[256,1024]{1,0:T(8,128)(2,1)S(1)} %get-tuple-element.298.refs_0_.refs_18_), channel_id=1, source_target_pairs={{0,2},{2,0},{4,6},{6,4},{8,10},{10,8},{12,14},{14,12},{16,18},{18,... | collective-permute-start | bytes 1572872 | tf_op jit(solution)/shard_map/ppermute | solution.py:594
  64.5 17.0 %collective-permute-start.12 = (bf16[256,1024]{1,0:T(8,128)(2,1)S(1)}, bf16[256,1024]{1,0:T(8,128)(2,1)}, u32[]{:S(2)}, u32[]{:S(2)}) collective-permute-start(bf16[256,1024]{1,0:T(8,128)(2,1)S(1)} %get-tuple-element.299.refs_1_.refs_19_), channel_id=1, source_target_pairs={{0,4},{2,6},{4,0},{6,2},{8,12},{10,14},{12,8},{14,10},{16,20},{18,... | collective-permute-start | bytes 1572872 | tf_op jit(solution)/shard_map/ppermute | solution.py:594
  65.0 34.7 %collective-permute-start.15 = (bf16[256,1024]{1,0:T(8,128)(2,1)S(1)}, bf16[256,1024]{1,0:T(8,128)(2,1)}, u32[]{:S(2)}, u32[]{:S(2)}) collective-permute-start(bf16[256,1024]{1,0:T(8,128)(2,1)S(1)} %get-tuple-element.299.refs_1_.refs_19_), channel_id=1, source_target_pairs={{0,2},{2,0},{4,6},{6,4},{8,10},{10,8},{12,14},{14,12},{16,18},{18,... | collective-permute-start | bytes 1572872 | tf_op jit(solution)/shard_map/ppermute | solution.py:594
  66.4 33.3 %collective-permute-start.16 = (bf16[256,1024]{1,0:T(8,128)(2,1)S(1)}, bf16[256,1024]{1,0:T(8,128)(2,1)}, u32[]{:S(2)}, u32[]{:S(2)}) collective-permute-start(bf16[256,1024]{1,0:T(8,128)(2,1)S(1)} %get-tuple-element.298.refs_0_.refs_18_), channel_id=1, source_target_pairs={{0,4},{2,6},{4,0},{6,2},{8,12},{10,14},{12,8},{14,10},{16,20},{18,... | collective-permute-start | bytes 1572872 | tf_op jit(solution)/shard_map/ppermute | solution.py:594
  99.7 40.5 %collective-permute-start.19 = (bf16[3,1024,256]{2,1,0:T(8,128)(2,1)}, bf16[3,1024,256]{2,1,0:T(8,128)(2,1)S(1)}, u32[]{:S(2)}, u32[]{:S(2)}) collective-permute-start(bf16[3,1024,256]{2,1,0:T(8,128)(2,1)} %collective-permute-done.17.refs_4_), channel_id=1, source_target_pairs={{0,8},{2,10},{4,12},{6,14},{8,16},{10,18},{12,20},{14,22},{16,24},... | collective-permute-start | bytes 4718600 | tf_op jit(solution)/shard_map/ppermute | solution.py:598
  99.9 14.1 %collective-permute-start.13 = (bf16[256,1024]{1,0:T(8,128)(2,1)}, bf16[256,1024]{1,0:T(8,128)(2,1)S(1)}, u32[]{:S(2)}, u32[]{:S(2)}) collective-permute-start(bf16[256,1024]{1,0:T(8,128)(2,1)} %copy-done.61), channel_id=1, source_target_pairs={{0,4},{2,6},{4,0},{6,2},{8,12},{10,14},{12,8},{14,10},{16,20},{18,... | collective-permute-start | bytes 1572872 | tf_op jit(solution)/shard_map/ppermute | solution.py:594
  100.5 13.7 %collective-permute-start.14 = (bf16[256,1024]{1,0:T(8,128)(2,1)}, bf16[256,1024]{1,0:T(8,128)(2,1)}, u32[]{:S(2)}, u32[]{:S(2)}) collective-permute-start(bf16[256,1024]{1,0:T(8,128)(2,1)} %collective-permute-done.12.refs_1_.refs_7_), channel_id=1, source_target_pairs={{0,2},{2,0},{4,6},{6,4},{8,10},{10,8},{12,14},{14,12},{16,18},{18,... | collective-permute-start | bytes 1572872 | tf_op jit(solution)/shard_map/ppermute | solution.py:594
  101.1 39.3 %collective-permute-start.18 = (bf16[3,1024,256]{2,1,0:T(8,128)(2,1)}, bf16[3,1024,256]{2,1,0:T(8,128)(2,1)}, u32[]{:S(2)}, u32[]{:S(2)}) collective-permute-start(bf16[3,1024,256]{2,1,0:T(8,128)(2,1)} %collective-permute-done.17.refs_4_), channel_id=1, source_target_pairs={{0,1},{1,0},{2,3},{3,2},{4,5},{5,4},{6,7},{7,6},{8,9},{9,8},{10,11... | collective-permute-start | bytes 4718600 | tf_op jit(solution)/shard_map/ppermute | solution.py:590
  139.7 5.0 %collective-permute-start.21 = (bf16[3,1024,256]{2,1,0:T(8,128)(2,1)}, bf16[3,1024,256]{2,1,0:T(8,128)(2,1)S(1)}, u32[]{:S(2)}, u32[]{:S(2)}) collective-permute-start(bf16[3,1024,256]{2,1,0:T(8,128)(2,1)} %get-tuple-element.336), channel_id=1, source_target_pairs={{0,1},{1,0},{2,3},{3,2},{4,5},{5,4},{6,7},{7,6},{8,9},{9,8},{10,11... | collective-permute-start | bytes 4718600 | tf_op jit(solution)/shard_map/ppermute | solution.py:590
  140.3 7.4 %collective-permute-start.20 = (bf16[3,1024,256]{2,1,0:T(8,128)(2,1)S(1)}, bf16[3,1024,256]{2,1,0:T(8,128)(2,1)S(1)}, u32[]{:S(2)}, u32[]{:S(2)}) collective-permute-start(bf16[3,1024,256]{2,1,0:T(8,128)(2,1)S(1)} %collective-permute-done.19.refs_6_), channel_id=1, source_target_pairs={{0,1},{1,0},{2,3},{3,2},{4,5},{5,4},{6,7},{7,6},{8,9},{9,8},{10,11... | collective-permute-start | bytes 4718600 | tf_op jit(solution)/shard_map/ppermute | solution.py:590
  163.6 18.8 %collective-permute-start.22 = (bf16[256,1152]{1,0:T(8,128)(2,1)}, bf16[256,1152]{1,0:T(8,128)(2,1)S(1)}, u32[]{:S(2)}, u32[]{:S(2)}) collective-permute-start(bf16[256,1152]{1,0:T(8,128)(2,1)} %get-tuple-element.344), channel_id=1, source_target_pairs={{0,2},{2,0},{4,6},{6,4},{8,10},{10,8},{12,14},{14,12},{16,18},{18,... | collective-permute-start | bytes 1769480 | tf_op jit(solution)/shard_map/ppermute | solution.py:594
  165.1 17.4 %collective-permute-start.23 = (bf16[256,1152]{1,0:T(8,128)(2,1)}, bf16[256,1152]{1,0:T(8,128)(2,1)S(1)}, u32[]{:S(2)}, u32[]{:S(2)}) collective-permute-start(bf16[256,1152]{1,0:T(8,128)(2,1)} %get-tuple-element.345), channel_id=1, source_target_pairs={{0,4},{2,6},{4,0},{6,2},{8,12},{10,14},{12,8},{14,10},{16,20},{18,... | collective-permute-start | bytes 1769480 | tf_op jit(solution)/shard_map/ppermute | solution.py:594
  166.6 52.7 %collective-permute-start.28 = (bf16[3,1024,256]{2,1,0:T(8,128)(2,1)}, bf16[3,1024,256]{2,1,0:T(8,128)(2,1)}, u32[]{:S(2)}, u32[]{:S(2)}) collective-permute-start(bf16[3,1024,256]{2,1,0:T(8,128)(2,1)} %add_convert_fusion.2), channel_id=1, source_target_pairs={{0,8},{2,10},{4,12},{6,14},{8,16},{10,18},{12,20},{14,22},{16,24},... | collective-permute-start | bytes 4718600 | tf_op jit(solution)/shard_map/ppermute | solution.py:598
  182.5 18.8 %collective-permute-start.24 = (bf16[256,1152]{1,0:T(8,128)(2,1)}, bf16[256,1152]{1,0:T(8,128)(2,1)S(1)}, u32[]{:S(2)}, u32[]{:S(2)}) collective-permute-start(bf16[256,1152]{1,0:T(8,128)(2,1)} %get-tuple-element.354), channel_id=1, source_target_pairs={{0,2},{2,0},{4,6},{6,4},{8,10},{10,8},{12,14},{14,12},{16,18},{18,... | collective-permute-start | bytes 1769480 | tf_op jit(solution)/shard_map/ppermute | solution.py:594
  183.2 18.2 %collective-permute-start.25 = (bf16[256,1152]{1,0:T(8,128)(2,1)}, bf16[256,1152]{1,0:T(8,128)(2,1)}, u32[]{:S(2)}, u32[]{:S(2)}) collective-permute-start(bf16[256,1152]{1,0:T(8,128)(2,1)} %get-tuple-element.355), channel_id=1, source_target_pairs={{0,4},{2,6},{4,0},{6,2},{8,12},{10,14},{12,8},{14,10},{16,20},{18,... | collective-permute-start | bytes 1769480 | tf_op jit(solution)/shard_map/ppermute | solution.py:594
  201.3 18.0 %collective-permute-start.26 = (bf16[256,1152]{1,0:T(8,128)(2,1)}, bf16[256,1152]{1,0:T(8,128)(2,1)}, u32[]{:S(2)}, u32[]{:S(2)}) collective-permute-start(bf16[256,1152]{1,0:T(8,128)(2,1)} %add_convert_fusion.4), channel_id=1, source_target_pairs={{0,2},{2,0},{4,6},{6,4},{8,10},{10,8},{12,14},{14,12},{16,18},{18,... | collective-permute-start | bytes 1769480 | tf_op jit(solution)/shard_map/ppermute | solution.py:594
  202.8 16.5 %collective-permute-start.27 = (bf16[256,1152]{1,0:T(8,128)(2,1)}, bf16[256,1152]{1,0:T(8,128)(2,1)}, u32[]{:S(2)}, u32[]{:S(2)}) collective-permute-start(bf16[256,1152]{1,0:T(8,128)(2,1)} %add_convert_fusion.3), channel_id=1, source_target_pairs={{0,4},{2,6},{4,0},{6,2},{8,12},{10,14},{12,8},{14,10},{16,20},{18,... | collective-permute-start | bytes 1769480 | tf_op jit(solution)/shard_map/ppermute | solution.py:594
  225.7 13.2 %collective-permute-start.29 = (bf16[512,1024]{1,0:T(8,128)(2,1)}, bf16[512,1024]{1,0:T(8,128)(2,1)S(1)}, u32[]{:S(2)}, u32[]{:S(2)}) collective-permute-start(bf16[512,1024]{1,0:T(8,128)(2,1)} %get-tuple-element.385), channel_id=1, source_target_pairs={{0,1},{1,0},{2,3},{3,2},{4,5},{5,4},{6,7},{7,6},{8,9},{9,8},{10,11... | collective-permute-start | bytes 3145736 | tf_op jit(solution)/shard_map/ppermute | solution.py:590
  225.7 17.0 %collective-permute-start.30 = (bf16[256,1024]{1,0:T(8,128)(2,1)}, bf16[256,1024]{1,0:T(8,128)(2,1)S(1)}, u32[]{:S(2)}, u32[]{:S(2)}) collective-permute-start(bf16[256,1024]{1,0:T(8,128)(2,1)} %get-tuple-element.397), channel_id=1, source_target_pairs={{0,2},{2,0},{4,6},{6,4},{8,10},{10,8},{12,14},{14,12},{16,18},{18,... | collective-permute-start | bytes 1572872 | tf_op jit(solution)/shard_map/ppermute | solution.py:594
  226.3 16.4 %collective-permute-start.31 = (bf16[256,1024]{1,0:T(8,128)(2,1)}, bf16[256,1024]{1,0:T(8,128)(2,1)S(1)}, u32[]{:S(2)}, u32[]{:S(2)}) collective-permute-start(bf16[256,1024]{1,0:T(8,128)(2,1)} %get-tuple-element.398), channel_id=1, source_target_pairs={{0,4},{2,6},{4,0},{6,2},{8,12},{10,14},{12,8},{14,10},{16,20},{18,... | collective-permute-start | bytes 1572872 | tf_op jit(solution)/shard_map/ppermute | solution.py:594
  243.6 18.6 %collective-permute-start.34 = (bf16[3,1024,256]{2,1,0:T(8,128)(2,1)}, bf16[3,1024,256]{2,1,0:T(8,128)(2,1)S(1)}, u32[]{:S(2)}, u32[]{:S(2)}) collective-permute-start(bf16[3,1024,256]{2,1,0:T(8,128)(2,1)} %get-tuple-element.405), channel_id=1, source_target_pairs={{0,1},{1,0},{2,3},{3,2},{4,5},{5,4},{6,7},{7,6},{8,9},{9,8},{10,11... | collective-permute-start | bytes 4718600 | tf_op jit(solution)/shard_map/ppermute | solution.py:590
  243.6 18.6 %collective-permute-start.32 = (bf16[256,1024]{1,0:T(8,128)(2,1)}, bf16[256,1024]{1,0:T(8,128)(2,1)S(1)}, u32[]{:S(2)}, u32[]{:S(2)}) collective-permute-start(bf16[256,1024]{1,0:T(8,128)(2,1)} %get-tuple-element.356), channel_id=1, source_target_pairs={{0,2},{2,0},{4,6},{6,4},{8,10},{10,8},{12,14},{14,12},{16,18},{18,... | collective-permute-start | bytes 1572872 | tf_op jit(solution)/shard_map/ppermute | solution.py:594
  245.1 17.2 %collective-permute-start.33 = (bf16[256,1024]{1,0:T(8,128)(2,1)}, bf16[256,1024]{1,0:T(8,128)(2,1)S(1)}, u32[]{:S(2)}, u32[]{:S(2)}) collective-permute-start(bf16[256,1024]{1,0:T(8,128)(2,1)} %get-tuple-element.357), channel_id=1, source_target_pairs={{0,4},{2,6},{4,0},{6,2},{8,12},{10,14},{12,8},{14,10},{16,20},{18,... | collective-permute-start | bytes 1572872 | tf_op jit(solution)/shard_map/ppermute | solution.py:594
  270.9 31.6 %collective-permute-start.35 = (bf16[256,1024]{1,0:T(8,128)(2,1)}, bf16[256,1024]{1,0:T(8,128)(2,1)}, u32[]{:S(2)}, u32[]{:S(2)}) collective-permute-start(bf16[256,1024]{1,0:T(8,128)(2,1)} %get-tuple-element.608), channel_id=1, source_target_pairs={{0,2},{2,0},{4,6},{6,4},{8,10},{10,8},{12,14},{14,12},{16,18},{18,... | collective-permute-start | bytes 1572872 | tf_op jit(solution)/shard_map/ppermute | solution.py:594
  271.5 31.2 %collective-permute-start.36 = (bf16[256,1024]{1,0:T(8,128)(2,1)}, bf16[256,1024]{1,0:T(8,128)(2,1)}, u32[]{:S(2)}, u32[]{:S(2)}) collective-permute-start(bf16[256,1024]{1,0:T(8,128)(2,1)} %get-tuple-element.607), channel_id=1, source_target_pairs={{0,4},{2,6},{4,0},{6,2},{8,12},{10,14},{12,8},{14,10},{16,20},{18,... | collective-permute-start | bytes 1572872 | tf_op jit(solution)/shard_map/ppermute | solution.py:594
  272.0 30.7 %collective-permute-start.37 = (bf16[256,1024]{1,0:T(8,128)(2,1)}, bf16[256,1024]{1,0:T(8,128)(2,1)}, u32[]{:S(2)}, u32[]{:S(2)}) collective-permute-start(bf16[256,1024]{1,0:T(8,128)(2,1)} %get-tuple-element.606), channel_id=1, source_target_pairs={{0,6},{2,4},{4,2},{6,0},{8,14},{10,12},{12,10},{14,8},{16,22},{18,... | collective-permute-start | bytes 1572872 | tf_op jit(solution)/shard_map/ppermute | solution.py:594
  275.6 27.0 %collective-permute-start.38 = (bf16[1024,256]{1,0:T(8,128)(2,1)}, bf16[1024,256]{1,0:T(8,128)(2,1)}, u32[]{:S(2)}, u32[]{:S(2)}) collective-permute-start(bf16[1024,256]{1,0:T(8,128)(2,1)} %get-tuple-element.614), channel_id=1, source_target_pairs={{0,8},{2,10},{4,12},{6,14},{8,16},{10,18},{12,20},{14,22},{16,24},... | collective-permute-start | bytes 1572872 | tf_op jit(solution)/shard_map/ppermute | solution.py:598
  277.2 25.5 %collective-permute-start.39 = (bf16[1024,256]{1,0:T(8,128)(2,1)}, bf16[1024,256]{1,0:T(8,128)(2,1)}, u32[]{:S(2)}, u32[]{:S(2)}) collective-permute-start(bf16[1024,256]{1,0:T(8,128)(2,1)} %get-tuple-element.613), channel_id=1, source_target_pairs={{0,8},{2,10},{4,12},{6,14},{8,16},{10,18},{12,20},{14,22},{16,24},... | collective-permute-start | bytes 1572872 | tf_op jit(solution)/shard_map/ppermute | solution.py:598
  302.5 14.4 %collective-permute-start.44 = (bf16[1024,256]{1,0:T(8,128)(2,1)}, bf16[1024,256]{1,0:T(8,128)(2,1)S(1)}, u32[]{:S(2)}, u32[]{:S(2)}) collective-permute-start(bf16[1024,256]{1,0:T(8,128)(2,1)} %get-tuple-element.612), channel_id=1, source_target_pairs={{0,8},{2,10},{4,12},{6,14},{8,16},{10,18},{12,20},{14,22},{16,24},... | collective-permute-start | bytes 1572872 | tf_op jit(solution)/shard_map/ppermute | solution.py:598
  302.7 26.8 %collective-permute-start.45 = (bf16[3,1024,256]{2,1,0:T(8,128)(2,1)}, bf16[3,1024,256]{2,1,0:T(8,128)(2,1)}, u32[]{:S(2)}, u32[]{:S(2)}) collective-permute-start(bf16[3,1024,256]{2,1,0:T(8,128)(2,1)} %get-tuple-element.459), channel_id=1, source_target_pairs={{0,1},{1,0},{2,3},{3,2},{4,5},{5,4},{6,7},{7,6},{8,9},{9,8},{10,11... | collective-permute-start | bytes 4718600 | tf_op jit(solution)/shard_map/ppermute | solution.py:590
  309.8 19.6 %collective-permute-start.40 = (bf16[256,512]{1,0:T(8,128)(2,1)}, bf16[256,512]{1,0:T(8,128)(2,1)}, u32[]{:S(2)}, u32[]{:S(2)}) collective-permute-start(bf16[256,512]{1,0:T(8,128)(2,1)} %get-tuple-element.619), channel_id=1, source_target_pairs={{0,2},{2,0},{4,6},{6,4},{8,10},{10,8},{12,14},{14,12},{16,18},{18,... | collective-permute-start | bytes 786440 | tf_op jit(solution)/shard_map/ppermute | solution.py:594
  310.4 19.0 %collective-permute-start.41 = (bf16[256,512]{1,0:T(8,128)(2,1)}, bf16[256,512]{1,0:T(8,128)(2,1)}, u32[]{:S(2)}, u32[]{:S(2)}) collective-permute-start(bf16[256,512]{1,0:T(8,128)(2,1)} %get-tuple-element.618), channel_id=1, source_target_pairs={{0,4},{2,6},{4,0},{6,2},{8,12},{10,14},{12,8},{14,10},{16,20},{18,... | collective-permute-start | bytes 786440 | tf_op jit(solution)/shard_map/ppermute | solution.py:594
  311.2 18.2 %collective-permute-start.42 = (bf16[256,512]{1,0:T(8,128)(2,1)}, bf16[256,512]{1,0:T(8,128)(2,1)}, u32[]{:S(2)}, u32[]{:S(2)}) collective-permute-start(bf16[256,512]{1,0:T(8,128)(2,1)} %get-tuple-element.617), channel_id=1, source_target_pairs={{0,6},{2,4},{4,2},{6,0},{8,14},{10,12},{12,10},{14,8},{16,22},{18,... | collective-permute-start | bytes 786440 | tf_op jit(solution)/shard_map/ppermute | solution.py:594
  316.9 12.5 %collective-permute-start.43 = (bf16[128,1024]{1,0:T(8,128)(2,1)}, bf16[128,1024]{1,0:T(8,128)(2,1)}, u32[]{:S(2)}, u32[]{:S(2)}) collective-permute-start(bf16[128,1024]{1,0:T(8,128)(2,1)} %get-tuple-element.448), channel_id=1, source_target_pairs={{0,8},{2,10},{4,12},{6,14},{8,0},{10,2},{12,4},{14,6},{16,24},{18,... | collective-permute-start | bytes 786440 | tf_op jit(solution)/shard_map/ppermute | solution.py:830
  330.7 13.2 %collective-permute-start.47 = (bf16[1024,512]{1,0:T(8,128)(2,1)}, bf16[1024,512]{1,0:T(8,128)(2,1)S(1)}, u32[]{:S(2)}, u32[]{:S(2)}) collective-permute-start(bf16[1024,512]{1,0:T(8,128)(2,1)} %copy-done.21), channel_id=1, source_target_pairs={{0,1},{1,0},{2,3},{3,2},{4,5},{5,4},{6,7},{7,6},{8,9},{9,8},{10,11... | collective-permute-start | bytes 3145736 | tf_op jit(solution)/shard_map/ppermute | solution.py:590
  334.7 9.2 %collective-permute-start.46 = (bf16[64,1024]{1,0:T(8,128)(2,1)S(1)}, bf16[64,1024]{1,0:T(8,128)(2,1)S(1)}, u32[]{:S(2)}, u32[]{:S(2)}) collective-permute-start(bf16[64,1024]{1,0:T(8,128)(2,1)S(1)} %get-tuple-element.464), channel_id=1, source_target_pairs={{0,16},{2,18},{4,20},{6,22},{8,24},{10,26},{12,28},{14,30},{16,0},... | collective-permute-start | bytes 393224 | tf_op jit(solution)/shard_map/ppermute | solution.py:830
  343.9 14.4 %collective-permute-start.51 = (bf16[256,1024]{1,0:T(8,128)(2,1)}, bf16[256,1024]{1,0:T(8,128)(2,1)S(1)}, u32[]{:S(2)}, u32[]{:S(2)}) collective-permute-start(bf16[256,1024]{1,0:T(8,128)(2,1)} %add_convert_fusion.6), channel_id=1, source_target_pairs={{0,2},{2,0},{4,6},{6,4},{8,10},{10,8},{12,14},{14,12},{16,18},{18,... | collective-permute-start | bytes 1572872 | tf_op jit(solution)/shard_map/ppermute | solution.py:594
  344.5 13.8 %collective-permute-start.52 = (bf16[256,1024]{1,0:T(8,128)(2,1)}, bf16[256,1024]{1,0:T(8,128)(2,1)}, u32[]{:S(2)}, u32[]{:S(2)}) collective-permute-start(bf16[256,1024]{1,0:T(8,128)(2,1)} %add_convert_fusion.5), channel_id=1, source_target_pairs={{0,4},{2,6},{4,0},{6,2},{8,12},{10,14},{12,8},{14,10},{16,20},{18,... | collective-permute-start | bytes 1572872 | tf_op jit(solution)/shard_map/ppermute | solution.py:594
  349.9 8.4 %collective-permute-start.49 = (bf16[144,512]{1,0:T(8,128)(2,1)}, bf16[144,512]{1,0:T(8,128)(2,1)S(1)}, u32[]{:S(2)}, u32[]{:S(2)}) collective-permute-start(bf16[144,512]{1,0:T(8,128)(2,1)} %pad_maximum_fusion.4), channel_id=1, source_target_pairs={{0,8},{2,10},{4,12},{6,14},{8,0},{10,2},{12,4},{14,6},{16,24},{18,... | collective-permute-start | bytes 442376 | tf_op jit(solution)/shard_map/ppermute | solution.py:830
  350.0 8.3 %collective-permute-start.50 = (bf16[64,1024]{1,0:T(8,128)(2,1)S(1)}, bf16[64,1024]{1,0:T(8,128)(2,1)}, u32[]{:S(2)}, u32[]{:S(2)}) collective-permute-start(bf16[64,1024]{1,0:T(8,128)(2,1)S(1)} %add_convert_fusion.11), channel_id=1, source_target_pairs={{0,16},{2,18},{4,20},{6,22},{8,24},{10,26},{12,28},{14,30},{16,0},... | collective-permute-start | bytes 393224 | tf_op jit(solution)/shard_map/ppermute | solution.py:830
  359.5 7.6 %collective-permute-start.54 = (bf16[128,1024]{1,0:T(8,128)(2,1)S(1)}, bf16[128,1024]{1,0:T(8,128)(2,1)S(1)}, u32[]{:S(2)}, u32[]{:S(2)}) collective-permute-start(bf16[128,1024]{1,0:T(8,128)(2,1)S(1)} %maximum_select_fusion.4), channel_id=1, source_target_pairs={{0,8},{2,10},{4,12},{6,14},{8,0},{10,2},{12,4},{14,6},{16,24},{18,... | collective-permute-start | bytes 786440 | tf_op jit(solution)/shard_map/ppermute | solution.py:830
  359.5 5.6 %collective-permute-start.53 = (bf16[80,512]{1,0:T(8,128)(2,1)S(1)}, bf16[80,512]{1,0:T(8,128)(2,1)S(1)}, u32[]{:S(2)}, u32[]{:S(2)}) collective-permute-start(bf16[80,512]{1,0:T(8,128)(2,1)S(1)} %pad_maximum_fusion.5), channel_id=1, source_target_pairs={{0,16},{2,18},{4,20},{6,22},{8,24},{10,26},{12,28},{14,30},{16,0},... | collective-permute-start | bytes 245768 | tf_op jit(solution)/shard_map/ppermute | solution.py:830
  367.2 31.3 %collective-permute-start.58 = (bf16[256,1024]{1,0:T(8,128)(2,1)S(1)}, bf16[256,1024]{1,0:T(8,128)(2,1)S(1)}, u32[]{:S(2)}, u32[]{:S(2)}) collective-permute-start(bf16[256,1024]{1,0:T(8,128)(2,1)S(1)} %maximum_select_fusion.3.refs_0_), channel_id=1, source_target_pairs={{0,2},{2,0},{4,6},{6,4},{8,10},{10,8},{12,14},{14,12},{16,18},{18,... | collective-permute-start | bytes 1572872 | tf_op jit(solution)/shard_map/ppermute | solution.py:594
  368.7 29.8 %collective-permute-start.59 = (bf16[256,1024]{1,0:T(8,128)(2,1)S(1)}, bf16[256,1024]{1,0:T(8,128)(2,1)S(1)}, u32[]{:S(2)}, u32[]{:S(2)}) collective-permute-start(bf16[256,1024]{1,0:T(8,128)(2,1)S(1)} %maximum_select_fusion.3.refs_0_), channel_id=1, source_target_pairs={{0,4},{2,6},{4,0},{6,2},{8,12},{10,14},{12,8},{14,10},{16,20},{18,... | collective-permute-start | bytes 1572872 | tf_op jit(solution)/shard_map/ppermute | solution.py:594
  369.9 28.6 %collective-permute-start.60 = (bf16[256,1024]{1,0:T(8,128)(2,1)S(1)}, bf16[256,1024]{1,0:T(8,128)(2,1)S(1)}, u32[]{:S(2)}, u32[]{:S(2)}) collective-permute-start(bf16[256,1024]{1,0:T(8,128)(2,1)S(1)} %maximum_select_fusion.3.refs_0_), channel_id=1, source_target_pairs={{0,6},{2,4},{4,2},{6,0},{8,14},{10,12},{12,10},{14,8},{16,22},{18,... | collective-permute-start | bytes 1572872 | tf_op jit(solution)/shard_map/ppermute | solution.py:594
  370.8 5.6 %collective-permute-start.55 = (bf16[64,512]{1,0:T(8,128)(2,1)S(1)}, bf16[64,512]{1,0:T(8,128)(2,1)S(1)}, u32[]{:S(2)}, u32[]{:S(2)}) collective-permute-start(bf16[64,512]{1,0:T(8,128)(2,1)S(1)} %add_convert_fusion.12), channel_id=1, source_target_pairs={{0,16},{2,18},{4,20},{6,22},{8,24},{10,26},{12,28},{14,30},{16,0},... | collective-permute-start | bytes 196616 | tf_op jit(solution)/shard_map/ppermute | solution.py:830
  376.4 5.0 %collective-permute-start.56 = (bf16[128,512]{1,0:T(8,128)(2,1)S(1)}, bf16[128,512]{1,0:T(8,128)(2,1)S(1)}, u32[]{:S(2)}, u32[]{:S(2)}) collective-permute-start(bf16[128,512]{1,0:T(8,128)(2,1)S(1)} %maximum_select_fusion.6), channel_id=1, source_target_pairs={{0,8},{2,10},{4,12},{6,14},{8,0},{10,2},{12,4},{14,6},{16,24},{18,... | collective-permute-start | bytes 393224 | tf_op jit(solution)/shard_map/ppermute | solution.py:830
  378.5 17.5 %collective-permute-start.57 = (bf16[512,512]{1,0:T(8,128)(2,1)}, bf16[512,512]{1,0:T(8,128)(2,1)}, u32[]{:S(2)}, u32[]{:S(2)}) collective-permute-start(bf16[512,512]{1,0:T(8,128)(2,1)} %get-tuple-element.616), channel_id=1, source_target_pairs={{0,1},{1,0},{2,3},{3,2},{4,5},{5,4},{6,7},{7,6},{8,9},{9,8},{10,11... | collective-permute-start | bytes 1572872 | tf_op jit(solution)/shard_map/ppermute | solution.py:590
  382.7 15.9 %collective-permute-start.61 = (bf16[1024,256]{1,0:T(8,128)(2,1)}, bf16[1024,256]{1,0:T(8,128)(2,1)S(1)}, u32[]{:S(2)}, u32[]{:S(2)}) collective-permute-start(bf16[1024,256]{1,0:T(8,128)(2,1)} %get-tuple-element.611), channel_id=1, source_target_pairs={{0,8},{2,10},{4,12},{6,14},{8,16},{10,18},{12,20},{14,22},{16,24},... | collective-permute-start | bytes 1572872 | tf_op jit(solution)/shard_map/ppermute | solution.py:598
  398.6 8.3 %collective-permute-start.66 = (bf16[3,1024,256]{2,1,0:T(8,128)(2,1)}, bf16[3,1024,256]{2,1,0:T(8,128)(2,1)}, u32[]{:S(2)}, u32[]{:S(2)}) collective-permute-start(bf16[3,1024,256]{2,1,0:T(8,128)(2,1)} %get-tuple-element.522), channel_id=1, source_target_pairs={{0,1},{1,0},{2,3},{3,2},{4,5},{5,4},{6,7},{7,6},{8,9},{9,8},{10,11... | collective-permute-start | bytes 4718600 | tf_op jit(solution)/shard_map/ppermute | solution.py:590
  399.7 16.9 %collective-permute-start.67 = (bf16[1024,256]{1,0:T(8,128)(2,1)}, bf16[1024,256]{1,0:T(8,128)(2,1)}, u32[]{:S(2)}, u32[]{:S(2)}) collective-permute-start(bf16[1024,256]{1,0:T(8,128)(2,1)} %get-tuple-element.610), channel_id=1, source_target_pairs={{0,8},{2,10},{4,12},{6,14},{8,16},{10,18},{12,20},{14,22},{16,24},... | collective-permute-start | bytes 1572872 | tf_op jit(solution)/shard_map/ppermute | solution.py:598
  403.2 23.6 %collective-permute-start.68 = (bf16[1024,256]{1,0:T(8,128)(2,1)}, bf16[1024,256]{1,0:T(8,128)(2,1)S(1)}, u32[]{:S(2)}, u32[]{:S(2)}) collective-permute-start(bf16[1024,256]{1,0:T(8,128)(2,1)} %get-tuple-element.609), channel_id=1, source_target_pairs={{0,8},{2,10},{4,12},{6,14},{8,16},{10,18},{12,20},{14,22},{16,24},... | collective-permute-start | bytes 1572872 | tf_op jit(solution)/shard_map/ppermute | solution.py:598
  404.3 14.9 %collective-permute-start.63 = (bf16[272,512]{1,0:T(8,128)(2,1)S(1)}, bf16[272,512]{1,0:T(8,128)(2,1)S(1)}, u32[]{:S(2)}, u32[]{:S(2)}) collective-permute-start(bf16[272,512]{1,0:T(8,128)(2,1)S(1)} %pad_maximum_fusion.3.refs_4_), channel_id=1, source_target_pairs={{0,2},{2,0},{4,6},{6,4},{8,10},{10,8},{12,14},{14,12},{16,18},{18,... | collective-permute-start | bytes 835592 | tf_op jit(solution)/shard_map/ppermute | solution.py:594
  405.5 14.1 %collective-permute-start.64 = (bf16[272,512]{1,0:T(8,128)(2,1)S(1)}, bf16[272,512]{1,0:T(8,128)(2,1)S(1)}, u32[]{:S(2)}, u32[]{:S(2)}) collective-permute-start(bf16[272,512]{1,0:T(8,128)(2,1)S(1)} %pad_maximum_fusion.3.refs_4_), channel_id=1, source_target_pairs={{0,4},{2,6},{4,0},{6,2},{8,12},{10,14},{12,8},{14,10},{16,20},{18,... | collective-permute-start | bytes 835592 | tf_op jit(solution)/shard_map/ppermute | solution.py:594
  406.9 12.7 %collective-permute-start.65 = (bf16[272,512]{1,0:T(8,128)(2,1)S(1)}, bf16[272,512]{1,0:T(8,128)(2,1)S(1)}, u32[]{:S(2)}, u32[]{:S(2)}) collective-permute-start(bf16[272,512]{1,0:T(8,128)(2,1)S(1)} %pad_maximum_fusion.3.refs_4_), channel_id=1, source_target_pairs={{0,6},{2,4},{4,2},{6,0},{8,14},{10,12},{12,10},{14,8},{16,22},{18,... | collective-permute-start | bytes 835592 | tf_op jit(solution)/shard_map/ppermute | solution.py:594
  (93 other events, 485.0 us)

commit v6 on v5

--- a/solution.py
+++ b/solution.py
@@ -730,10 +730,6 @@
     def total_of(grads, got):
         return functools.reduce(jnp.add, [v.astype(F32) for v in [grads[0], *got]])
 
-    def weight_total(k):
-        grads = weight_pieces(k)
-        return total_of(grads, hop_back(grads)).astype(BF16)
-
     def send_on(k, moving):
         total = totals[k]
         if moving is not None:
@@ -768,17 +764,19 @@
     totals = {}
     order = list(range(1, depth)) + [0]
     early = order[: depth - group - 1]
-    for k in early:
-        totals[k] = weight_total(k)
+    early_grads = {k: weight_pieces(k) for k in early}
     while len(slots) < depth:
         add_slot()
-    slots[-1], totals = after((slots[-1], totals))
+    slots[-1], early_grads = after((slots[-1], early_grads))
+    rest = order[len(early) :]
+
+    early_got = {k: hop_back(early_grads[k]) for k in early}
+    run("diag", last)
+    carry["diag"], early_grads, early_got = after((carry["diag"], early_grads, early_got))
     moving = None
     for k in early:
+        totals[k] = total_of(early_grads[k], early_got[k]).astype(BF16)
         moving = send_on(k, moving)
-    rest = order[len(early) :]
-
-    run("diag", last)
     back_parts = [plane(v, m) for v, m in zip(carry["diag"][1], (1, 2))]
     run("one", last, [carry["diag"]])
     back_parts, carry["one"] = after((back_parts, carry["one"]))

time: 434 us -> 466 us (1.074)
  waiting for transfers between devices: 63.8 us -> 95.8 us
    ppermute x10, waiting for transfers between devices: 21.4 us -> 56 us  [ring(): return jax.tree.map(lambda a: lax.ppermute(a, 'expert', pairs), x)]
  transfers between devices with their start and end apart: 69 -> 69, of which waited for: 21 -> 21; matrix products, arithmetic and copies ran while one was open for 14% -> 13% of each run, Pallas kernels for 44% -> 44%
where the time goes in v6:
time: 466 us; the launch traced here: 461 us
  Pallas kernels  207 us (44%)
  waiting for transfers between devices  95.8 us (21%)
  starting transfers between devices  60.9 us (13%)
  other arithmetic  49.2 us (11%)
  local copies, waits for them, and re-layouts  34 us (7%)
  matrix products  12 us (3%)
    pallas_call x8, Pallas kernels, expert_data(): pl.pallas_call(functools.partial(data_kernel, first, last, blocks, tiles,...  110 us
    ppermute x10, waiting for transfers between devices, ring(): return jax.tree.map(lambda a: lax.ppermute(a, 'expert', pairs), x)  56 us
    pallas_call x4, Pallas kernels, expert_weight(): pl.pallas_call(functools.partial(weight_kernel, tuple(shape), pieces), gr...  48.6 us
    ppermute x34, starting transfers between devices, plane(): return jax.tree.map(lambda a: lax.ppermute(a, 'expert', pairs), x)  38.1 us
    unnamed x180, local copies, waits for them, and re-layouts  25 us
    ppermute x8, waiting for transfers between devices, swap(): return lax.ppermute(a, 'expert', pairs)  23.8 us
    pallas_call x2, Pallas kernels, attn_backward(): pl.pallas_call(functools.partial(attn_bwd_kernel, block), grid=(count,),...  20 us
    ppermute x10, starting transfers between devices, ring(): return jax.tree.map(lambda a: lax.ppermute(a, 'expert', pairs), x)  11.9 us
  transfers between devices with their start and end apart: 69, of which 21 were waited for; matrix products, arithmetic and copies ran while one was open for 13% of the time, Pallas kernels for 44%

profile of v6, /device:TPU:0, one launch (start us, length us, event | category | flops | bytes accessed | tf_op | source)
XLA Modules:
  0.0 461.3 jit_solution(1322566824089163422)
XLA Ops:
  6.0 2.0 copy.97
  8.5 2.7 pad_maximum_fusion.refs_4_
  11.8 1.7 maximum_select_fusion.1
  13.6 2.7 collective-permute-start.2
  16.3 1.5 collective-permute-start.3
  18.3 1.9 collective-permute-start.9
  24.8 5.3 %attn_forward.3 = (bf16[256,1024]{1,0:T(8,128)(2,1)S(1)}, bf16[128,1024]{1,0:T(8,128)(2,1)S(1)}, bf16[256,1024]{1,0:T(8,128)(2,1)S(1)}, f32[2,2,1024]{2,1,0:T(2,128)S(1)}) custom-call(f32[512,1024]{1,0:T(8,128)S(1)} %convolution_bitcast_fusion.q_ref, f32[256,1024]{1,0:T(8,128)S(1)} %convolution_bitcast_fusion.1.k_ref, bf16[256,1024]{1,0:T(8,128)(2,1)S(1)} %fusion.6.v_ref, ...), custom_call_target="tpu_custom_call" | custom-call | flops 2147483648 | bytes 2097152 | tf_op jit(solution)/shard_map/attn_forward/pallas_call | solution.py:122
  32.2 5.2 %attn_forward.2 = (bf16[256,1024]{1,0:T(8,128)(2,1)S(1)}, bf16[128,1024]{1,0:T(8,128)(2,1)S(1)}, bf16[256,1024]{1,0:T(8,128)(2,1)S(1)}, f32[2,2,1024]{2,1,0:T(2,128)S(1)}) custom-call(f32[512,1024]{1,0:T(8,128)S(1)} %convolution_bitcast_fusion.q_ref, f32[256,1024]{1,0:T(8,128)S(1)} %convolution_bitcast_fusion.1.k_ref, bf16[256,1024]{1,0:T(8,128)(2,1)S(1)} %fusion.6.v_ref, ...), custom_call_target="tpu_custom_call" | custom-call | flops 2147483648 | bytes 2097152 | tf_op jit(solution)/shard_map/attn_forward/pallas_call | solution.py:122
  37.5 5.3 %collective-permute-done.2.refs_2_.refs_8_.refs_14_ = bf16[512,1152]{1,0:T(8,128)(2,1)S(1)} collective-permute-done((bf16[512,1152]{1,0:T(8,128)(2,1)S(1)}, bf16[512,1152]{1,0:T(8,128)(2,1)S(1)}, u32[]{:S(2)}, u32[]{:S(2)}) %collective-permute-start.2) | collective-permute-done | bytes 1179680 | tf_op jit(solution)/shard_map/ppermute | solution.py:594
  44.3 1.6 collective-permute-start.7
  50.5 3.9 join_heads.1
  54.4 2.5 collective-permute-done.9.refs_6_
  56.9 2.0 collective-permute-done.7.refs_2_.refs_20_
  60.2 2.1 collective-permute-start.17
  62.3 1.5 collective-permute-done.10.refs_7_
  66.4 1.6 collective-permute-start.16
  68.7 12.8 %expert_data.8 = (bf16[512,1024]{1,0:T(8,128)(2,1)}, bf16[512,1024]{1,0:T(8,128)(2,1)}, f32[512,128]{1,0:T(8,128)}, bf16[512,1024]{1,0:T(8,128)(2,1)}, bf16[512,...) custom-call(s32[2]{0:T(128)} %get-tuple-element.647.expert_ref, bf16[256,1024]{1,0:T(8,128)(2,1)} %copy-done.4, ...), custom_call_target="tpu_custom_call" | custom-call | flops 1610612736 | bytes 12582912 | tf_op jit(solution)/shard_map/expert_data/pallas_call | solution.py:295
  82.3 12.8 %expert_data.9 = (bf16[512,1024]{1,0:T(8,128)(2,1)}, bf16[512,1024]{1,0:T(8,128)(2,1)}, f32[512,128]{1,0:T(8,128)}, bf16[512,1024]{1,0:T(8,128)(2,1)}, bf16[512,...) custom-call(s32[2]{0:T(128)} %get-tuple-element.647.expert_ref, ...), custom_call_target="tpu_custom_call" | custom-call | flops 1610612736 | bytes 12582912 | tf_op jit(solution)/shard_map/expert_data/pallas_call | solution.py:295
  95.0 4.7 %collective-permute-done.17.refs_4_ = bf16[3,1024,256]{2,1,0:T(8,128)(2,1)} collective-permute-done((bf16[3,1024,256]{2,1,0:T(8,128)(2,1)}, bf16[3,1024,256]{2,1,0:T(8,128)(2,1)}, u32[]{:S(2)}, u32[]{:S(2)}) %collective-permute-start.17) | collective-permute-done | bytes 1572896 | tf_op jit(solution)/shard_map/ppermute | solution.py:598
  99.9 38.1 %collective-permute-done.19.refs_6_ = bf16[3,1024,256]{2,1,0:T(8,128)(2,1)S(1)} collective-permute-done((bf16[3,1024,256]{2,1,0:T(8,128)(2,1)}, bf16[3,1024,256]{2,1,0:T(8,128)(2,1)S(1)}, u32[]{:S(2)}, u32[]{:S(2)}) %collective-permute-start.19) | collective-permute-done | bytes 1572896 | tf_op jit(solution)/shard_map/ppermute | solution.py:598
  139.0 12.8 %expert_data.10 = (bf16[512,1024]{1,0:T(8,128)(2,1)}, bf16[512,1024]{1,0:T(8,128)(2,1)}, f32[512,128]{1,0:T(8,128)}, bf16[512,1024]{1,0:T(8,128)(2,1)}, bf16[512...) custom-call(s32[2]{0:T(128)} %get-tuple-element.647.expert_ref, ...), custom_call_target="tpu_custom_call" | custom-call | flops 1610612736 | bytes 12582912 | tf_op jit(solution)/shard_map/expert_data/pallas_call | solution.py:295
  153.4 12.7 %expert_data.11 = (bf16[512,1024]{1,0:T(8,128)(2,1)}, bf16[512,1024]{1,0:T(8,128)(2,1)}, f32[512,128]{1,0:T(8,128)}, bf16[512,1024]{1,0:T(8,128)(2,1)}, bf16[512...) custom-call(s32[2]{0:T(128)} %get-tuple-element.647.expert_ref, ...), custom_call_target="tpu_custom_call" | custom-call | flops 1610612736 | bytes 12582912 | tf_op jit(solution)/shard_map/expert_data/pallas_call | solution.py:295
  166.1 12.1 %expert_weight.4 = (bf16[3,1024,256]{2,1,0:T(8,128)(2,1)}, bf16[3,1024,256]{2,1,0:T(8,128)(2,1)}) custom-call(bf16[256,1024]{1,0:T(8,128)(2,1)} %copy-done.4, bf16[256,1024]{1,0:T(8,128)(2,1)} %copy-done.5, bf16[512,1152]{1,0:T(8,128)(2,1)} %copy-done.2, bf16[512,1152]{1,0:T(8,128)(2,1)} %copy-done.2, bf16[512,1024]{1,0:T(8,128)(2,1)} %get-tuple-element.334.refs_4_, ...), custom_call_target="tpu_custom_call" | custom-call | flops 1073741824 | bytes 17825792 | tf_op jit(solution)/shard_map/expert_weight/pallas_call | solution.py:351
  178.3 15.1 %expert_data.12 = (bf16[256,1024]{1,0:T(8,128)(2,1)}, bf16[256,1024]{1,0:T(8,128)(2,1)}, bf16[256,1152]{1,0:T(8,128)(2,1)}, bf16[256,1152]{1,0:T(8,128)(2,1)}, b...) custom-call(s32[2]{0:T(128)} %get-tuple-element.381.expert_ref, ...), custom_call_target="tpu_custom_call" | custom-call | flops 1610612736 | bytes 12582912 | tf_op jit(solution)/shard_map/expert_data/pallas_call | solution.py:295
  194.7 1.5 collective-permute-start.23
  196.2 2.9 add_convert_fusion.2
  199.2 14.6 %expert_data.13 = (bf16[256,1024]{1,0:T(8,128)(2,1)}, bf16[256,1024]{1,0:T(8,128)(2,1)}, bf16[256,1152]{1,0:T(8,128)(2,1)}, bf16[256,1152]{1,0:T(8,128)(2,1)}, b...) custom-call(s32[2]{0:T(128)} %get-tuple-element.381.expert_ref, ...), custom_call_target="tpu_custom_call" | custom-call | flops 1610612736 | bytes 12582912 | tf_op jit(solution)/shard_map/expert_data/pallas_call | solution.py:295
  215.1 14.6 %expert_data.14 = (bf16[256,1024]{1,0:T(8,128)(2,1)}, bf16[256,1024]{1,0:T(8,128)(2,1)}, bf16[256,1152]{1,0:T(8,128)(2,1)}, bf16[256,1152]{1,0:T(8,128)(2,1)}, b...) custom-call(s32[2]{0:T(128)} %get-tuple-element.381.expert_ref, ...), custom_call_target="tpu_custom_call" | custom-call | flops 1610612736 | bytes 12582912 | tf_op jit(solution)/shard_map/expert_data/pallas_call | solution.py:295
  229.7 2.3 add_convert_fusion.3
  232.0 2.1 add_convert_fusion.4
  235.4 1.5 collective-permute-start.27
  236.9 15.0 %expert_data.15 = (bf16[256,1024]{1,0:T(8,128)(2,1)}, bf16[256,1024]{1,0:T(8,128)(2,1)}, bf16[256,1152]{1,0:T(8,128)(2,1)}, bf16[256,1152]{1,0:T(8,128)(2,1)}, b...) custom-call(s32[2]{0:T(128)} %get-tuple-element.381.expert_ref, ...), custom_call_target="tpu_custom_call" | custom-call | flops 1610612736 | bytes 12582912 | tf_op jit(solution)/shard_map/expert_data/pallas_call | solution.py:295
  254.1 4.2 turn_back.1
  259.6 12.1 %expert_weight.5 = (bf16[3,1024,256]{2,1,0:T(8,128)(2,1)}, bf16[3,1024,256]{2,1,0:T(8,128)(2,1)}) custom-call(bf16[256,1024]{1,0:T(8,128)(2,1)} %copy-done.61, bf16[256,1024]{1,0:T(8,128)(2,1)} %collective-permute-done.14.refs_1_.refs_19_, bf16[256,1152]{1,0:T(8,128)(2,1)} %copy-done.58, bf16[256,1152]{1,0:T(8,128)(2,1)} %copy-done.59, ...), custom_call_target="tpu_custom_call" | custom-call | flops 1073741824 | bytes 17825792 | tf_op jit(solution)/shard_map/expert_weight/pallas_call | solution.py:351
  271.8 3.8 maximum_select_fusion
  279.3 2.9 fusion.4.do_ref
  284.9 10.0 %attn_backward.2 = (bf16[256,1024]{1,0:T(8,128)(2,1)S(1)}, bf16[128,1024]{1,0:T(8,128)(2,1)S(1)}, bf16[128,1024]{1,0:T(8,128)(2,1)S(1)}) custom-call(bf16[256,1024]{1,0:T(8,128)(2,1)S(1)} %copy-done.39, bf16[128,1024]{1,0:T(8,128)(2,1)S(1)} %copy-done.43, bf16[256,1024]{1,0:T(8,128)(2,1)S(1)} %copy-done.29, bf16[512,1024]{1,0:T(8,128)(2,1)S(1)} %fusion.4.do_ref, ...), custom_call_target="tpu_custom_call" | custom-call | flops 2147483648 | bytes 2097152 | tf_op jit(solution)/shard_map/attn_backward/pallas_call | solution.py:141
  299.4 3.0 add_convert_fusion.1
  304.8 2.2 collective-permute-start.37
  310.2 10.0 %attn_backward.3 = (bf16[256,1024]{1,0:T(8,128)(2,1)S(1)}, bf16[128,1024]{1,0:T(8,128)(2,1)S(1)}, bf16[128,1024]{1,0:T(8,128)(2,1)S(1)}) custom-call(bf16[256,1024]{1,0:T(8,128)(2,1)S(1)} %copy-done.37, bf16[128,1024]{1,0:T(8,128)(2,1)S(1)} %copy-done.41, bf16[256,1024]{1,0:T(8,128)(2,1)S(1)} %copy-done.29, bf16[512,1024]{1,0:T(8,128)(2,1)S(1)} %copy-done.35, ...), custom_call_target="tpu_custom_call" | custom-call | flops 2147483648 | bytes 2097152 | tf_op jit(solution)/shard_map/attn_backward/pallas_call | solution.py:141
  320.2 12.2 %expert_weight.6 = (bf16[3,1024,256]{2,1,0:T(8,128)(2,1)}, bf16[3,1024,256]{2,1,0:T(8,128)(2,1)}) custom-call(bf16[256,1024]{1,0:T(8,128)(2,1)} %copy-done.61, bf16[256,1024]{1,0:T(8,128)(2,1)} %collective-permute-done.14.refs_1_.refs_19_, bf16[256,1152]{1,0:T(8,128)(2,1)} %copy-done.58, bf16[256,1152]{1,0:T(8,128)(2,1)} %copy-done.59, ...), custom_call_target="tpu_custom_call" | custom-call | flops 1073741824 | bytes 17825792 | tf_op jit(solution)/shard_map/expert_weight/pallas_call | solution.py:351
  332.5 4.0 collective-permute-start.44
  336.6 1.9 add_convert_fusion.7
  344.8 2.2 collective-permute-start.42
  347.0 2.0 collective-permute-start.43
  353.2 6.3 %input_terms.1 = (f32[1024,512]{1,0:T(8,128)}, bf16[1024,512]{1,0:T(8,128)(2,1)S(1)}, f32[1024,1]{1,0:T(8,128)S(1)}) custom-call(s32[1]{0:T(128)} %bitcast.9.at_ref, bf16[1024,1024]{1,0:T(8,128)(2,1)} %x_ref.1, f32[1,1024]{1,0:T(1,128)S(1)} %bitcast.91, bf16[256,1024]{1,0:T(8,128)(2,1)S(1)} %copy-done.33, bf16[128,1024]{1,0:T(8,128)(2,1)S(1)} %copy-done.25, ...), custom_call_target="tpu_custom_call" | custom-call | flops 2147483648 | bytes 8388608 | tf_op jit(solution)/shard_map/input_terms/pallas_call | solution.py:448
  363.1 2.4 add_convert_fusion.6
  367.9 7.3 %collective-permute-done.46 = bf16[64,1024]{1,0:T(8,128)(2,1)S(1)} collective-permute-done((bf16[64,1024]{1,0:T(8,128)(2,1)S(1)}, bf16[64,1024]{1,0:T(8,128)(2,1)S(1)}, u32[]{:S(2)}, u32[]{:S(2)}) %collective-permute-start.46) | collective-permute-done | bytes 131104 | tf_op jit(solution)/shard_map/ppermute | solution.py:828
  376.6 3.9 multiply_add_fusion
  381.3 1.8 collective-permute-start.50
  383.1 6.8 %collective-permute-done.50 = bf16[64,1024]{1,0:T(8,128)(2,1)} collective-permute-done((bf16[64,1024]{1,0:T(8,128)(2,1)S(1)}, bf16[64,1024]{1,0:T(8,128)(2,1)}, u32[]{:S(2)}, u32[]{:S(2)}) %collective-permute-start.50) | collective-permute-done | bytes 131104 | tf_op jit(solution)/shard_map/ppermute | solution.py:828
  392.6 2.5 add_convert_fusion
  395.1 2.2 collective-permute-done.53
  397.3 2.0 collective-permute-done.54
  406.3 2.4 collective-permute-done.55
  410.7 3.0 collective-permute-done.56
  416.0 12.1 %expert_weight.7 = (bf16[3,1024,256]{2,1,0:T(8,128)(2,1)}, bf16[3,1024,256]{2,1,0:T(8,128)(2,1)}) custom-call(bf16[256,1024]{1,0:T(8,128)(2,1)} %copy-done.4, bf16[256,1024]{1,0:T(8,128)(2,1)} %copy-done.5, bf16[512,1152]{1,0:T(8,128)(2,1)} %copy-done.2, bf16[512,1152]{1,0:T(8,128)(2,1)} %copy-done.2, bf16[512,1024]{1,0:T(8,128)(2,1)} %get-tuple-element.522.refs_4_, ...), custom_call_target="tpu_custom_call" | custom-call | flops 1073741824 | bytes 17825792 | tf_op jit(solution)/shard_map/expert_weight/pallas_call | solution.py:351
  428.2 2.6 maximum_select_fusion.2
  432.8 1.8 collective-permute-done.62
  439.7 2.2 convert_add_fusion
  442.0 6.8 %collective-permute-done.67 = bf16[1024,256]{1,0:T(8,128)(2,1)} collective-permute-done((bf16[1024,256]{1,0:T(8,128)(2,1)}, bf16[1024,256]{1,0:T(8,128)(2,1)}, u32[]{:S(2)}, u32[]{:S(2)}) %collective-permute-start.67) | collective-permute-done | bytes 524320 | tf_op jit(solution)/shard_map/ppermute | solution.py:598
  448.8 2.6 fusion.11
  451.9 3.1 lay_out.1
  455.0 4.0 collective-permute-done.68
  (370 shorter events, 93.5 us)
Async XLA Ops:
  5.2 6.6 %collective-permute-start = (bf16[512,512]{1,0:T(8,128)(2,1)}, bf16[512,512]{1,0:T(8,128)(2,1)}, u32[]{:S(2)}, u32[]{:S(2)}) collective-permute-start(bf16[512,512]{1,0:T(8,128)(2,1)} %get-tuple-element.284), channel_id=1, source_target_pairs={{0,1},{1,0},{2,3},{3,2},{4,5},{5,4},{6,7},{7,6},{8,9},{9,8},{10,11... | collective-permute-start | bytes 1572872 | tf_op jit(solution)/shard_map/ppermute | solution.py:590
  5.6 41.0 %collective-permute-start.6 = (bf16[512,1024]{1,0:T(8,128)(2,1)S(1)}, bf16[512,1024]{1,0:T(8,128)(2,1)S(1)}, u32[]{:S(2)}, u32[]{:S(2)}) collective-permute-start(bf16[512,1024]{1,0:T(8,128)(2,1)S(1)} %copy-done.6), channel_id=1, source_target_pairs={{0,1},{1,0},{2,3},{3,2},{4,5},{5,4},{6,7},{7,6},{8,9},{9,8},{10,11... | collective-permute-start | bytes 3145736 | tf_op jit(solution)/shard_map/ppermute | solution.py:590
  13.6 29.2 %collective-permute-start.2 = (bf16[512,1152]{1,0:T(8,128)(2,1)S(1)}, bf16[512,1152]{1,0:T(8,128)(2,1)S(1)}, u32[]{:S(2)}, u32[]{:S(2)}) collective-permute-start(bf16[512,1152]{1,0:T(8,128)(2,1)S(1)} %pad_maximum_fusion.1.refs_2_.refs_3_.grad_ref.refs_20_.refs_21_), channel_id=1, source_target_pairs={{0,2},{2,0},{4,6},{6,4},{8,10},{10,8},{12,14},{14,12},{16,18},{18,... | collective-permute-start | bytes 3538952 | tf_op jit(solution)/shard_map/ppermute | solution.py:594
  16.3 27.9 %collective-permute-start.3 = (bf16[512,1152]{1,0:T(8,128)(2,1)S(1)}, bf16[512,1152]{1,0:T(8,128)(2,1)S(1)}, u32[]{:S(2)}, u32[]{:S(2)}) collective-permute-start(bf16[512,1152]{1,0:T(8,128)(2,1)S(1)} %pad_maximum_fusion.1.refs_2_.refs_3_.grad_ref.refs_20_.refs_21_), channel_id=1, source_target_pairs={{0,4},{2,6},{4,0},{6,2},{8,12},{10,14},{12,8},{14,10},{16,20},{18,... | collective-permute-start | bytes 3538952 | tf_op jit(solution)/shard_map/ppermute | solution.py:594
  18.3 38.6 %collective-permute-start.9 = (bf16[3,1024,256]{2,1,0:T(8,128)(2,1)}, bf16[3,1024,256]{2,1,0:T(8,128)(2,1)}, u32[]{:S(2)}, u32[]{:S(2)}) collective-permute-start(bf16[3,1024,256]{2,1,0:T(8,128)(2,1)} %pad_maximum_fusion.refs_4_), channel_id=1, source_target_pairs={{0,8},{2,10},{4,12},{6,14},{8,16},{10,18},{12,20},{14,22},{16,24},... | collective-permute-start | bytes 4718600 | tf_op jit(solution)/shard_map/ppermute | solution.py:598
  44.3 14.6 %collective-permute-start.7 = (bf16[256,1152]{1,0:T(8,128)(2,1)S(1)}, bf16[256,1152]{1,0:T(8,128)(2,1)S(1)}, u32[]{:S(2)}, u32[]{:S(2)}) collective-permute-start(bf16[256,1152]{1,0:T(8,128)(2,1)S(1)} %slice.81), channel_id=1, source_target_pairs={{0,4},{2,6},{4,0},{6,2},{8,12},{10,14},{12,8},{14,10},{16,20},{18,... | collective-permute-start | bytes 1769480 | tf_op jit(solution)/shard_map/ppermute | solution.py:594
  45.9 14.3 %collective-permute-start.8 = (bf16[256,1152]{1,0:T(8,128)(2,1)S(1)}, bf16[256,1152]{1,0:T(8,128)(2,1)S(1)}, u32[]{:S(2)}, u32[]{:S(2)}) collective-permute-start(bf16[256,1152]{1,0:T(8,128)(2,1)S(1)} %slice.82), channel_id=1, source_target_pairs={{0,2},{2,0},{4,6},{6,4},{8,10},{10,8},{12,14},{14,12},{16,18},{18,... | collective-permute-start | bytes 1769480 | tf_op jit(solution)/shard_map/ppermute | solution.py:594
  48.1 14.2 %collective-permute-start.1 = (bf16[3,1024,256]{2,1,0:T(8,128)(2,1)}, bf16[3,1024,256]{2,1,0:T(8,128)(2,1)S(1)}, u32[]{:S(2)}, u32[]{:S(2)}) collective-permute-start(bf16[3,1024,256]{2,1,0:T(8,128)(2,1)} %pad_maximum_fusion.refs_4_), channel_id=1, source_target_pairs={{0,1},{1,0},{2,3},{3,2},{4,5},{5,4},{6,7},{7,6},{8,9},{9,8},{10,11... | collective-permute-start | bytes 4718600 | tf_op jit(solution)/shard_map/ppermute | solution.py:590
  60.2 39.5 %collective-permute-start.17 = (bf16[3,1024,256]{2,1,0:T(8,128)(2,1)}, bf16[3,1024,256]{2,1,0:T(8,128)(2,1)}, u32[]{:S(2)}, u32[]{:S(2)}) collective-permute-start(bf16[3,1024,256]{2,1,0:T(8,128)(2,1)} %collective-permute-done.9.refs_6_), channel_id=1, source_target_pairs={{0,8},{2,10},{4,12},{6,14},{8,16},{10,18},{12,20},{14,22},{16,24},... | collective-permute-start | bytes 4718600 | tf_op jit(solution)/shard_map/ppermute | solution.py:598
  63.9 17.6 %collective-permute-start.11 = (bf16[256,1024]{1,0:T(8,128)(2,1)S(1)}, bf16[256,1024]{1,0:T(8,128)(2,1)S(1)}, u32[]{:S(2)}, u32[]{:S(2)}) collective-permute-start(bf16[256,1024]{1,0:T(8,128)(2,1)S(1)} %get-tuple-element.305.refs_0_.refs_18_), channel_id=1, source_target_pairs={{0,2},{2,0},{4,6},{6,4},{8,10},{10,8},{12,14},{14,12},{16,18},{18,... | collective-permute-start | bytes 1572872 | tf_op jit(solution)/shard_map/ppermute | solution.py:594
  64.5 17.0 %collective-permute-start.12 = (bf16[256,1024]{1,0:T(8,128)(2,1)S(1)}, bf16[256,1024]{1,0:T(8,128)(2,1)}, u32[]{:S(2)}, u32[]{:S(2)}) collective-permute-start(bf16[256,1024]{1,0:T(8,128)(2,1)S(1)} %get-tuple-element.306.refs_1_.refs_19_), channel_id=1, source_target_pairs={{0,4},{2,6},{4,0},{6,2},{8,12},{10,14},{12,8},{14,10},{16,20},{18,... | collective-permute-start | bytes 1572872 | tf_op jit(solution)/shard_map/ppermute | solution.py:594
  65.0 34.7 %collective-permute-start.15 = (bf16[256,1024]{1,0:T(8,128)(2,1)S(1)}, bf16[256,1024]{1,0:T(8,128)(2,1)}, u32[]{:S(2)}, u32[]{:S(2)}) collective-permute-start(bf16[256,1024]{1,0:T(8,128)(2,1)S(1)} %get-tuple-element.306.refs_1_.refs_19_), channel_id=1, source_target_pairs={{0,2},{2,0},{4,6},{6,4},{8,10},{10,8},{12,14},{14,12},{16,18},{18,... | collective-permute-start | bytes 1572872 | tf_op jit(solution)/shard_map/ppermute | solution.py:594
  66.4 33.3 %collective-permute-start.16 = (bf16[256,1024]{1,0:T(8,128)(2,1)S(1)}, bf16[256,1024]{1,0:T(8,128)(2,1)}, u32[]{:S(2)}, u32[]{:S(2)}) collective-permute-start(bf16[256,1024]{1,0:T(8,128)(2,1)S(1)} %get-tuple-element.305.refs_0_.refs_18_), channel_id=1, source_target_pairs={{0,4},{2,6},{4,0},{6,2},{8,12},{10,14},{12,8},{14,10},{16,20},{18,... | collective-permute-start | bytes 1572872 | tf_op jit(solution)/shard_map/ppermute | solution.py:594
  99.7 38.3 %collective-permute-start.19 = (bf16[3,1024,256]{2,1,0:T(8,128)(2,1)}, bf16[3,1024,256]{2,1,0:T(8,128)(2,1)S(1)}, u32[]{:S(2)}, u32[]{:S(2)}) collective-permute-start(bf16[3,1024,256]{2,1,0:T(8,128)(2,1)} %collective-permute-done.17.refs_4_), channel_id=1, source_target_pairs={{0,8},{2,10},{4,12},{6,14},{8,16},{10,18},{12,20},{14,22},{16,24},... | collective-permute-start | bytes 4718600 | tf_op jit(solution)/shard_map/ppermute | solution.py:598
  138.0 40.2 %collective-permute-start.20 = (bf16[3,1024,256]{2,1,0:T(8,128)(2,1)S(1)}, bf16[3,1024,256]{2,1,0:T(8,128)(2,1)}, u32[]{:S(2)}, u32[]{:S(2)}) collective-permute-start(bf16[3,1024,256]{2,1,0:T(8,128)(2,1)S(1)} %collective-permute-done.19.refs_6_), channel_id=1, source_target_pairs={{0,1},{1,0},{2,3},{3,2},{4,5},{5,4},{6,7},{7,6},{8,9},{9,8},{10,11... | collective-permute-start | bytes 4718600 | tf_op jit(solution)/shard_map/ppermute | solution.py:590
  138.0 14.5 %collective-permute-start.13 = (bf16[256,1024]{1,0:T(8,128)(2,1)}, bf16[256,1024]{1,0:T(8,128)(2,1)S(1)}, u32[]{:S(2)}, u32[]{:S(2)}) collective-permute-start(bf16[256,1024]{1,0:T(8,128)(2,1)} %copy-done.60), channel_id=1, source_target_pairs={{0,4},{2,6},{4,0},{6,2},{8,12},{10,14},{12,8},{14,10},{16,20},{18,... | collective-permute-start | bytes 1572872 | tf_op jit(solution)/shard_map/ppermute | solution.py:594
  138.5 14.4 %collective-permute-start.14 = (bf16[256,1024]{1,0:T(8,128)(2,1)}, bf16[256,1024]{1,0:T(8,128)(2,1)}, u32[]{:S(2)}, u32[]{:S(2)}) collective-permute-start(bf16[256,1024]{1,0:T(8,128)(2,1)} %collective-permute-done.12.refs_1_.refs_7_), channel_id=1, source_target_pairs={{0,2},{2,0},{4,6},{6,4},{8,10},{10,8},{12,14},{14,12},{16,18},{18,... | collective-permute-start | bytes 1572872 | tf_op jit(solution)/shard_map/ppermute | solution.py:594
  139.0 39.3 %collective-permute-start.18 = (bf16[3,1024,256]{2,1,0:T(8,128)(2,1)}, bf16[3,1024,256]{2,1,0:T(8,128)(2,1)}, u32[]{:S(2)}, u32[]{:S(2)}) collective-permute-start(bf16[3,1024,256]{2,1,0:T(8,128)(2,1)} %collective-permute-done.17.refs_4_), channel_id=1, source_target_pairs={{0,1},{1,0},{2,3},{3,2},{4,5},{5,4},{6,7},{7,6},{8,9},{9,8},{10,11... | collective-permute-start | bytes 4718600 | tf_op jit(solution)/shard_map/ppermute | solution.py:590
  178.2 15.2 %collective-permute-start.21 = (bf16[3,1024,256]{2,1,0:T(8,128)(2,1)}, bf16[3,1024,256]{2,1,0:T(8,128)(2,1)}, u32[]{:S(2)}, u32[]{:S(2)}) collective-permute-start(bf16[3,1024,256]{2,1,0:T(8,128)(2,1)} %get-tuple-element.354), channel_id=1, source_target_pairs={{0,1},{1,0},{2,3},{3,2},{4,5},{5,4},{6,7},{7,6},{8,9},{9,8},{10,11... | collective-permute-start | bytes 4718600 | tf_op jit(solution)/shard_map/ppermute | solution.py:590
  193.4 20.3 %collective-permute-start.22 = (bf16[256,1152]{1,0:T(8,128)(2,1)}, bf16[256,1152]{1,0:T(8,128)(2,1)}, u32[]{:S(2)}, u32[]{:S(2)}) collective-permute-start(bf16[256,1152]{1,0:T(8,128)(2,1)} %get-tuple-element.357), channel_id=1, source_target_pairs={{0,2},{2,0},{4,6},{6,4},{8,10},{10,8},{12,14},{14,12},{16,18},{18,... | collective-permute-start | bytes 1769480 | tf_op jit(solution)/shard_map/ppermute | solution.py:594
  194.7 19.1 %collective-permute-start.23 = (bf16[256,1152]{1,0:T(8,128)(2,1)}, bf16[256,1152]{1,0:T(8,128)(2,1)}, u32[]{:S(2)}, u32[]{:S(2)}) collective-permute-start(bf16[256,1152]{1,0:T(8,128)(2,1)} %get-tuple-element.358), channel_id=1, source_target_pairs={{0,4},{2,6},{4,0},{6,2},{8,12},{10,14},{12,8},{14,10},{16,20},{18,... | collective-permute-start | bytes 1769480 | tf_op jit(solution)/shard_map/ppermute | solution.py:594
  199.1 52.7 %collective-permute-start.28 = (bf16[3,1024,256]{2,1,0:T(8,128)(2,1)}, bf16[3,1024,256]{2,1,0:T(8,128)(2,1)}, u32[]{:S(2)}, u32[]{:S(2)}) collective-permute-start(bf16[3,1024,256]{2,1,0:T(8,128)(2,1)} %add_convert_fusion.2), channel_id=1, source_target_pairs={{0,8},{2,10},{4,12},{6,14},{8,16},{10,18},{12,20},{14,22},{16,24},... | collective-permute-start | bytes 4718600 | tf_op jit(solution)/shard_map/ppermute | solution.py:598
  213.8 20.3 %collective-permute-start.24 = (bf16[256,1152]{1,0:T(8,128)(2,1)}, bf16[256,1152]{1,0:T(8,128)(2,1)S(1)}, u32[]{:S(2)}, u32[]{:S(2)}) collective-permute-start(bf16[256,1152]{1,0:T(8,128)(2,1)} %get-tuple-element.367), channel_id=1, source_target_pairs={{0,2},{2,0},{4,6},{6,4},{8,10},{10,8},{12,14},{14,12},{16,18},{18,... | collective-permute-start | bytes 1769480 | tf_op jit(solution)/shard_map/ppermute | solution.py:594
  214.4 19.6 %collective-permute-start.25 = (bf16[256,1152]{1,0:T(8,128)(2,1)}, bf16[256,1152]{1,0:T(8,128)(2,1)}, u32[]{:S(2)}, u32[]{:S(2)}) collective-permute-start(bf16[256,1152]{1,0:T(8,128)(2,1)} %get-tuple-element.368), channel_id=1, source_target_pairs={{0,4},{2,6},{4,0},{6,2},{8,12},{10,14},{12,8},{14,10},{16,20},{18,... | collective-permute-start | bytes 1769480 | tf_op jit(solution)/shard_map/ppermute | solution.py:594
  234.1 17.8 %collective-permute-start.26 = (bf16[256,1152]{1,0:T(8,128)(2,1)}, bf16[256,1152]{1,0:T(8,128)(2,1)}, u32[]{:S(2)}, u32[]{:S(2)}) collective-permute-start(bf16[256,1152]{1,0:T(8,128)(2,1)} %add_convert_fusion.4), channel_id=1, source_target_pairs={{0,2},{2,0},{4,6},{6,4},{8,10},{10,8},{12,14},{14,12},{16,18},{18,... | collective-permute-start | bytes 1769480 | tf_op jit(solution)/shard_map/ppermute | solution.py:594
  235.4 16.5 %collective-permute-start.27 = (bf16[256,1152]{1,0:T(8,128)(2,1)}, bf16[256,1152]{1,0:T(8,128)(2,1)}, u32[]{:S(2)}, u32[]{:S(2)}) collective-permute-start(bf16[256,1152]{1,0:T(8,128)(2,1)} %add_convert_fusion.3), channel_id=1, source_target_pairs={{0,4},{2,6},{4,0},{6,2},{8,12},{10,14},{12,8},{14,10},{16,20},{18,... | collective-permute-start | bytes 1769480 | tf_op jit(solution)/shard_map/ppermute | solution.py:594
  258.3 13.5 %collective-permute-start.29 = (bf16[512,1024]{1,0:T(8,128)(2,1)}, bf16[512,1024]{1,0:T(8,128)(2,1)S(1)}, u32[]{:S(2)}, u32[]{:S(2)}) collective-permute-start(bf16[512,1024]{1,0:T(8,128)(2,1)} %get-tuple-element.399), channel_id=1, source_target_pairs={{0,1},{1,0},{2,3},{3,2},{4,5},{5,4},{6,7},{7,6},{8,9},{9,8},{10,11... | collective-permute-start | bytes 3145736 | tf_op jit(solution)/shard_map/ppermute | solution.py:590
  258.3 17.2 %collective-permute-start.30 = (bf16[256,1024]{1,0:T(8,128)(2,1)}, bf16[256,1024]{1,0:T(8,128)(2,1)S(1)}, u32[]{:S(2)}, u32[]{:S(2)}) collective-permute-start(bf16[256,1024]{1,0:T(8,128)(2,1)} %get-tuple-element.411), channel_id=1, source_target_pairs={{0,2},{2,0},{4,6},{6,4},{8,10},{10,8},{12,14},{14,12},{16,18},{18,... | collective-permute-start | bytes 1572872 | tf_op jit(solution)/shard_map/ppermute | solution.py:594
  258.9 16.6 %collective-permute-start.31 = (bf16[256,1024]{1,0:T(8,128)(2,1)}, bf16[256,1024]{1,0:T(8,128)(2,1)S(1)}, u32[]{:S(2)}, u32[]{:S(2)}) collective-permute-start(bf16[256,1024]{1,0:T(8,128)(2,1)} %get-tuple-element.412), channel_id=1, source_target_pairs={{0,4},{2,6},{4,0},{6,2},{8,12},{10,14},{12,8},{14,10},{16,20},{18,... | collective-permute-start | bytes 1572872 | tf_op jit(solution)/shard_map/ppermute | solution.py:594
  276.5 18.4 %collective-permute-start.34 = (bf16[3,1024,256]{2,1,0:T(8,128)(2,1)}, bf16[3,1024,256]{2,1,0:T(8,128)(2,1)S(1)}, u32[]{:S(2)}, u32[]{:S(2)}) collective-permute-start(bf16[3,1024,256]{2,1,0:T(8,128)(2,1)} %get-tuple-element.419), channel_id=1, source_target_pairs={{0,1},{1,0},{2,3},{3,2},{4,5},{5,4},{6,7},{7,6},{8,9},{9,8},{10,11... | collective-permute-start | bytes 4718600 | tf_op jit(solution)/shard_map/ppermute | solution.py:590
  276.5 18.4 %collective-permute-start.32 = (bf16[256,1024]{1,0:T(8,128)(2,1)}, bf16[256,1024]{1,0:T(8,128)(2,1)S(1)}, u32[]{:S(2)}, u32[]{:S(2)}) collective-permute-start(bf16[256,1024]{1,0:T(8,128)(2,1)} %get-tuple-element.369), channel_id=1, source_target_pairs={{0,2},{2,0},{4,6},{6,4},{8,10},{10,8},{12,14},{14,12},{16,18},{18,... | collective-permute-start | bytes 1572872 | tf_op jit(solution)/shard_map/ppermute | solution.py:594
  277.7 17.2 %collective-permute-start.33 = (bf16[256,1024]{1,0:T(8,128)(2,1)}, bf16[256,1024]{1,0:T(8,128)(2,1)S(1)}, u32[]{:S(2)}, u32[]{:S(2)}) collective-permute-start(bf16[256,1024]{1,0:T(8,128)(2,1)} %get-tuple-element.370), channel_id=1, source_target_pairs={{0,4},{2,6},{4,0},{6,2},{8,12},{10,14},{12,8},{14,10},{16,20},{18,... | collective-permute-start | bytes 1572872 | tf_op jit(solution)/shard_map/ppermute | solution.py:594
  303.5 28.9 %collective-permute-start.35 = (bf16[256,1024]{1,0:T(8,128)(2,1)}, bf16[256,1024]{1,0:T(8,128)(2,1)}, u32[]{:S(2)}, u32[]{:S(2)}) collective-permute-start(bf16[256,1024]{1,0:T(8,128)(2,1)} %get-tuple-element.622), channel_id=1, source_target_pairs={{0,2},{2,0},{4,6},{6,4},{8,10},{10,8},{12,14},{14,12},{16,18},{18,... | collective-permute-start | bytes 1572872 | tf_op jit(solution)/shard_map/ppermute | solution.py:594
  304.1 32.4 %collective-permute-start.36 = (bf16[256,1024]{1,0:T(8,128)(2,1)}, bf16[256,1024]{1,0:T(8,128)(2,1)}, u32[]{:S(2)}, u32[]{:S(2)}) collective-permute-start(bf16[256,1024]{1,0:T(8,128)(2,1)} %get-tuple-element.621), channel_id=1, source_target_pairs={{0,4},{2,6},{4,0},{6,2},{8,12},{10,14},{12,8},{14,10},{16,20},{18,... | collective-permute-start | bytes 1572872 | tf_op jit(solution)/shard_map/ppermute | solution.py:594
  304.8 31.7 %collective-permute-start.37 = (bf16[256,1024]{1,0:T(8,128)(2,1)}, bf16[256,1024]{1,0:T(8,128)(2,1)}, u32[]{:S(2)}, u32[]{:S(2)}) collective-permute-start(bf16[256,1024]{1,0:T(8,128)(2,1)} %get-tuple-element.620), channel_id=1, source_target_pairs={{0,6},{2,4},{4,2},{6,0},{8,14},{10,12},{12,10},{14,8},{16,22},{18,... | collective-permute-start | bytes 1572872 | tf_op jit(solution)/shard_map/ppermute | solution.py:594
  308.2 28.3 %collective-permute-start.38 = (bf16[1024,256]{1,0:T(8,128)(2,1)}, bf16[1024,256]{1,0:T(8,128)(2,1)}, u32[]{:S(2)}, u32[]{:S(2)}) collective-permute-start(bf16[1024,256]{1,0:T(8,128)(2,1)} %get-tuple-element.628), channel_id=1, source_target_pairs={{0,8},{2,10},{4,12},{6,14},{8,16},{10,18},{12,20},{14,22},{16,24},... | collective-permute-start | bytes 1572872 | tf_op jit(solution)/shard_map/ppermute | solution.py:598
  308.2 28.3 %collective-permute-start.39 = (bf16[1024,256]{1,0:T(8,128)(2,1)}, bf16[1024,256]{1,0:T(8,128)(2,1)}, u32[]{:S(2)}, u32[]{:S(2)}) collective-permute-start(bf16[1024,256]{1,0:T(8,128)(2,1)} %get-tuple-element.627), channel_id=1, source_target_pairs={{0,8},{2,10},{4,12},{6,14},{8,16},{10,18},{12,20},{14,22},{16,24},... | collective-permute-start | bytes 1572872 | tf_op jit(solution)/shard_map/ppermute | solution.py:598
  332.5 14.6 %collective-permute-start.44 = (bf16[1024,256]{1,0:T(8,128)(2,1)}, bf16[1024,256]{1,0:T(8,128)(2,1)S(1)}, u32[]{:S(2)}, u32[]{:S(2)}) collective-permute-start(bf16[1024,256]{1,0:T(8,128)(2,1)} %get-tuple-element.626), channel_id=1, source_target_pairs={{0,8},{2,10},{4,12},{6,14},{8,16},{10,18},{12,20},{14,22},{16,24},... | collective-permute-start | bytes 1572872 | tf_op jit(solution)/shard_map/ppermute | solution.py:598
  336.5 24.3 %collective-permute-start.45 = (bf16[3,1024,256]{2,1,0:T(8,128)(2,1)}, bf16[3,1024,256]{2,1,0:T(8,128)(2,1)}, u32[]{:S(2)}, u32[]{:S(2)}) collective-permute-start(bf16[3,1024,256]{2,1,0:T(8,128)(2,1)} %get-tuple-element.473), channel_id=1, source_target_pairs={{0,1},{1,0},{2,3},{3,2},{4,5},{5,4},{6,7},{7,6},{8,9},{9,8},{10,11... | collective-permute-start | bytes 4718600 | tf_op jit(solution)/shard_map/ppermute | solution.py:590
  343.5 17.2 %collective-permute-start.40 = (bf16[256,512]{1,0:T(8,128)(2,1)}, bf16[256,512]{1,0:T(8,128)(2,1)}, u32[]{:S(2)}, u32[]{:S(2)}) collective-permute-start(bf16[256,512]{1,0:T(8,128)(2,1)} %get-tuple-element.633), channel_id=1, source_target_pairs={{0,2},{2,0},{4,6},{6,4},{8,10},{10,8},{12,14},{14,12},{16,18},{18,... | collective-permute-start | bytes 786440 | tf_op jit(solution)/shard_map/ppermute | solution.py:594
  344.1 16.6 %collective-permute-start.41 = (bf16[256,512]{1,0:T(8,128)(2,1)}, bf16[256,512]{1,0:T(8,128)(2,1)}, u32[]{:S(2)}, u32[]{:S(2)}) collective-permute-start(bf16[256,512]{1,0:T(8,128)(2,1)} %get-tuple-element.632), channel_id=1, source_target_pairs={{0,4},{2,6},{4,0},{6,2},{8,12},{10,14},{12,8},{14,10},{16,20},{18,... | collective-permute-start | bytes 786440 | tf_op jit(solution)/shard_map/ppermute | solution.py:594
  344.8 15.9 %collective-permute-start.42 = (bf16[256,512]{1,0:T(8,128)(2,1)}, bf16[256,512]{1,0:T(8,128)(2,1)}, u32[]{:S(2)}, u32[]{:S(2)}) collective-permute-start(bf16[256,512]{1,0:T(8,128)(2,1)} %get-tuple-element.631), channel_id=1, source_target_pairs={{0,6},{2,4},{4,2},{6,0},{8,14},{10,12},{12,10},{14,8},{16,22},{18,... | collective-permute-start | bytes 786440 | tf_op jit(solution)/shard_map/ppermute | solution.py:594
  347.0 13.8 %collective-permute-start.43 = (bf16[128,1024]{1,0:T(8,128)(2,1)}, bf16[128,1024]{1,0:T(8,128)(2,1)}, u32[]{:S(2)}, u32[]{:S(2)}) collective-permute-start(bf16[128,1024]{1,0:T(8,128)(2,1)} %get-tuple-element.462), channel_id=1, source_target_pairs={{0,8},{2,10},{4,12},{6,14},{8,0},{10,2},{12,4},{14,6},{16,24},{18,... | collective-permute-start | bytes 786440 | tf_op jit(solution)/shard_map/ppermute | solution.py:828
  362.0 13.2 %collective-permute-start.47 = (bf16[1024,512]{1,0:T(8,128)(2,1)}, bf16[1024,512]{1,0:T(8,128)(2,1)S(1)}, u32[]{:S(2)}, u32[]{:S(2)}) collective-permute-start(bf16[1024,512]{1,0:T(8,128)(2,1)} %copy-done.21), channel_id=1, source_target_pairs={{0,1},{1,0},{2,3},{3,2},{4,5},{5,4},{6,7},{7,6},{8,9},{9,8},{10,11... | collective-permute-start | bytes 3145736 | tf_op jit(solution)/shard_map/ppermute | solution.py:590
  366.0 9.2 %collective-permute-start.46 = (bf16[64,1024]{1,0:T(8,128)(2,1)S(1)}, bf16[64,1024]{1,0:T(8,128)(2,1)S(1)}, u32[]{:S(2)}, u32[]{:S(2)}) collective-permute-start(bf16[64,1024]{1,0:T(8,128)(2,1)S(1)} %get-tuple-element.478), channel_id=1, source_target_pairs={{0,16},{2,18},{4,20},{6,22},{8,24},{10,26},{12,28},{14,30},{16,0},... | collective-permute-start | bytes 393224 | tf_op jit(solution)/shard_map/ppermute | solution.py:828
  375.2 14.7 %collective-permute-start.51 = (bf16[256,1024]{1,0:T(8,128)(2,1)}, bf16[256,1024]{1,0:T(8,128)(2,1)S(1)}, u32[]{:S(2)}, u32[]{:S(2)}) collective-permute-start(bf16[256,1024]{1,0:T(8,128)(2,1)} %add_convert_fusion.6), channel_id=1, source_target_pairs={{0,2},{2,0},{4,6},{6,4},{8,10},{10,8},{12,14},{14,12},{16,18},{18,... | collective-permute-start | bytes 1572872 | tf_op jit(solution)/shard_map/ppermute | solution.py:594
  375.9 14.1 %collective-permute-start.52 = (bf16[256,1024]{1,0:T(8,128)(2,1)}, bf16[256,1024]{1,0:T(8,128)(2,1)}, u32[]{:S(2)}, u32[]{:S(2)}) collective-permute-start(bf16[256,1024]{1,0:T(8,128)(2,1)} %add_convert_fusion.5), channel_id=1, source_target_pairs={{0,4},{2,6},{4,0},{6,2},{8,12},{10,14},{12,8},{14,10},{16,20},{18,... | collective-permute-start | bytes 1572872 | tf_op jit(solution)/shard_map/ppermute | solution.py:594
  381.3 8.7 %collective-permute-start.49 = (bf16[144,512]{1,0:T(8,128)(2,1)}, bf16[144,512]{1,0:T(8,128)(2,1)S(1)}, u32[]{:S(2)}, u32[]{:S(2)}) collective-permute-start(bf16[144,512]{1,0:T(8,128)(2,1)} %pad_maximum_fusion.4), channel_id=1, source_target_pairs={{0,8},{2,10},{4,12},{6,14},{8,0},{10,2},{12,4},{14,6},{16,24},{18,... | collective-permute-start | bytes 442376 | tf_op jit(solution)/shard_map/ppermute | solution.py:828
  381.3 8.6 %collective-permute-start.50 = (bf16[64,1024]{1,0:T(8,128)(2,1)S(1)}, bf16[64,1024]{1,0:T(8,128)(2,1)}, u32[]{:S(2)}, u32[]{:S(2)}) collective-permute-start(bf16[64,1024]{1,0:T(8,128)(2,1)S(1)} %add_convert_fusion.11), channel_id=1, source_target_pairs={{0,16},{2,18},{4,20},{6,22},{8,24},{10,26},{12,28},{14,30},{16,0},... | collective-permute-start | bytes 393224 | tf_op jit(solution)/shard_map/ppermute | solution.py:828
  391.1 8.2 %collective-permute-start.54 = (bf16[128,1024]{1,0:T(8,128)(2,1)S(1)}, bf16[128,1024]{1,0:T(8,128)(2,1)S(1)}, u32[]{:S(2)}, u32[]{:S(2)}) collective-permute-start(bf16[128,1024]{1,0:T(8,128)(2,1)S(1)} %maximum_select_fusion.4), channel_id=1, source_target_pairs={{0,8},{2,10},{4,12},{6,14},{8,0},{10,2},{12,4},{14,6},{16,24},{18,... | collective-permute-start | bytes 786440 | tf_op jit(solution)/shard_map/ppermute | solution.py:828
  391.2 6.1 %collective-permute-start.53 = (bf16[80,512]{1,0:T(8,128)(2,1)S(1)}, bf16[80,512]{1,0:T(8,128)(2,1)S(1)}, u32[]{:S(2)}, u32[]{:S(2)}) collective-permute-start(bf16[80,512]{1,0:T(8,128)(2,1)S(1)} %pad_maximum_fusion.5), channel_id=1, source_target_pairs={{0,16},{2,18},{4,20},{6,22},{8,24},{10,26},{12,28},{14,30},{16,0},... | collective-permute-start | bytes 245768 | tf_op jit(solution)/shard_map/ppermute | solution.py:828
  399.5 31.3 %collective-permute-start.58 = (bf16[256,1024]{1,0:T(8,128)(2,1)S(1)}, bf16[256,1024]{1,0:T(8,128)(2,1)S(1)}, u32[]{:S(2)}, u32[]{:S(2)}) collective-permute-start(bf16[256,1024]{1,0:T(8,128)(2,1)S(1)} %maximum_select_fusion.3.refs_0_), channel_id=1, source_target_pairs={{0,2},{2,0},{4,6},{6,4},{8,10},{10,8},{12,14},{14,12},{16,18},{18,... | collective-permute-start | bytes 1572872 | tf_op jit(solution)/shard_map/ppermute | solution.py:594
  401.0 29.8 %collective-permute-start.59 = (bf16[256,1024]{1,0:T(8,128)(2,1)S(1)}, bf16[256,1024]{1,0:T(8,128)(2,1)S(1)}, u32[]{:S(2)}, u32[]{:S(2)}) collective-permute-start(bf16[256,1024]{1,0:T(8,128)(2,1)S(1)} %maximum_select_fusion.3.refs_0_), channel_id=1, source_target_pairs={{0,4},{2,6},{4,0},{6,2},{8,12},{10,14},{12,8},{14,10},{16,20},{18,... | collective-permute-start | bytes 1572872 | tf_op jit(solution)/shard_map/ppermute | solution.py:594
  401.8 29.0 %collective-permute-start.60 = (bf16[256,1024]{1,0:T(8,128)(2,1)S(1)}, bf16[256,1024]{1,0:T(8,128)(2,1)S(1)}, u32[]{:S(2)}, u32[]{:S(2)}) collective-permute-start(bf16[256,1024]{1,0:T(8,128)(2,1)S(1)} %maximum_select_fusion.3.refs_0_), channel_id=1, source_target_pairs={{0,6},{2,4},{4,2},{6,0},{8,14},{10,12},{12,10},{14,8},{16,22},{18,... | collective-permute-start | bytes 1572872 | tf_op jit(solution)/shard_map/ppermute | solution.py:594
  403.1 5.6 %collective-permute-start.55 = (bf16[64,512]{1,0:T(8,128)(2,1)S(1)}, bf16[64,512]{1,0:T(8,128)(2,1)S(1)}, u32[]{:S(2)}, u32[]{:S(2)}) collective-permute-start(bf16[64,512]{1,0:T(8,128)(2,1)S(1)} %add_convert_fusion.12), channel_id=1, source_target_pairs={{0,16},{2,18},{4,20},{6,22},{8,24},{10,26},{12,28},{14,30},{16,0},... | collective-permute-start | bytes 196616 | tf_op jit(solution)/shard_map/ppermute | solution.py:828
  408.7 5.0 %collective-permute-start.56 = (bf16[128,512]{1,0:T(8,128)(2,1)S(1)}, bf16[128,512]{1,0:T(8,128)(2,1)S(1)}, u32[]{:S(2)}, u32[]{:S(2)}) collective-permute-start(bf16[128,512]{1,0:T(8,128)(2,1)S(1)} %maximum_select_fusion.6), channel_id=1, source_target_pairs={{0,8},{2,10},{4,12},{6,14},{8,0},{10,2},{12,4},{14,6},{16,24},{18,... | collective-permute-start | bytes 393224 | tf_op jit(solution)/shard_map/ppermute | solution.py:828
  410.7 17.5 %collective-permute-start.57 = (bf16[512,512]{1,0:T(8,128)(2,1)}, bf16[512,512]{1,0:T(8,128)(2,1)}, u32[]{:S(2)}, u32[]{:S(2)}) collective-permute-start(bf16[512,512]{1,0:T(8,128)(2,1)} %get-tuple-element.630), channel_id=1, source_target_pairs={{0,1},{1,0},{2,3},{3,2},{4,5},{5,4},{6,7},{7,6},{8,9},{9,8},{10,11... | collective-permute-start | bytes 1572872 | tf_op jit(solution)/shard_map/ppermute | solution.py:590
  415.0 15.8 %collective-permute-start.61 = (bf16[1024,256]{1,0:T(8,128)(2,1)}, bf16[1024,256]{1,0:T(8,128)(2,1)S(1)}, u32[]{:S(2)}, u32[]{:S(2)}) collective-permute-start(bf16[1024,256]{1,0:T(8,128)(2,1)} %get-tuple-element.625), channel_id=1, source_target_pairs={{0,8},{2,10},{4,12},{6,14},{8,16},{10,18},{12,20},{14,22},{16,24},... | collective-permute-start | bytes 1572872 | tf_op jit(solution)/shard_map/ppermute | solution.py:598
  430.8 8.1 %collective-permute-start.66 = (bf16[3,1024,256]{2,1,0:T(8,128)(2,1)}, bf16[3,1024,256]{2,1,0:T(8,128)(2,1)}, u32[]{:S(2)}, u32[]{:S(2)}) collective-permute-start(bf16[3,1024,256]{2,1,0:T(8,128)(2,1)} %get-tuple-element.536), channel_id=1, source_target_pairs={{0,1},{1,0},{2,3},{3,2},{4,5},{5,4},{6,7},{7,6},{8,9},{9,8},{10,11... | collective-permute-start | bytes 4718600 | tf_op jit(solution)/shard_map/ppermute | solution.py:590
  431.9 16.9 %collective-permute-start.67 = (bf16[1024,256]{1,0:T(8,128)(2,1)}, bf16[1024,256]{1,0:T(8,128)(2,1)}, u32[]{:S(2)}, u32[]{:S(2)}) collective-permute-start(bf16[1024,256]{1,0:T(8,128)(2,1)} %get-tuple-element.624), channel_id=1, source_target_pairs={{0,8},{2,10},{4,12},{6,14},{8,16},{10,18},{12,20},{14,22},{16,24},... | collective-permute-start | bytes 1572872 | tf_op jit(solution)/shard_map/ppermute | solution.py:598
  435.4 23.6 %collective-permute-start.68 = (bf16[1024,256]{1,0:T(8,128)(2,1)}, bf16[1024,256]{1,0:T(8,128)(2,1)S(1)}, u32[]{:S(2)}, u32[]{:S(2)}) collective-permute-start(bf16[1024,256]{1,0:T(8,128)(2,1)} %get-tuple-element.623), channel_id=1, source_target_pairs={{0,8},{2,10},{4,12},{6,14},{8,16},{10,18},{12,20},{14,22},{16,24},... | collective-permute-start | bytes 1572872 | tf_op jit(solution)/shard_map/ppermute | solution.py:598
  436.3 15.1 %collective-permute-start.63 = (bf16[272,512]{1,0:T(8,128)(2,1)S(1)}, bf16[272,512]{1,0:T(8,128)(2,1)S(1)}, u32[]{:S(2)}, u32[]{:S(2)}) collective-permute-start(bf16[272,512]{1,0:T(8,128)(2,1)S(1)} %pad_maximum_fusion.3.refs_4_), channel_id=1, source_target_pairs={{0,2},{2,0},{4,6},{6,4},{8,10},{10,8},{12,14},{14,12},{16,18},{18,... | collective-permute-start | bytes 835592 | tf_op jit(solution)/shard_map/ppermute | solution.py:594
  437.8 14.1 %collective-permute-start.64 = (bf16[272,512]{1,0:T(8,128)(2,1)S(1)}, bf16[272,512]{1,0:T(8,128)(2,1)S(1)}, u32[]{:S(2)}, u32[]{:S(2)}) collective-permute-start(bf16[272,512]{1,0:T(8,128)(2,1)S(1)} %pad_maximum_fusion.3.refs_4_), channel_id=1, source_target_pairs={{0,4},{2,6},{4,0},{6,2},{8,12},{10,14},{12,8},{14,10},{16,20},{18,... | collective-permute-start | bytes 835592 | tf_op jit(solution)/shard_map/ppermute | solution.py:594
  438.9 13.0 %collective-permute-start.65 = (bf16[272,512]{1,0:T(8,128)(2,1)S(1)}, bf16[272,512]{1,0:T(8,128)(2,1)S(1)}, u32[]{:S(2)}, u32[]{:S(2)}) collective-permute-start(bf16[272,512]{1,0:T(8,128)(2,1)S(1)} %pad_maximum_fusion.3.refs_4_), channel_id=1, source_target_pairs={{0,6},{2,4},{4,2},{6,0},{8,14},{10,12},{12,10},{14,8},{16,22},{18,... | collective-permute-start | bytes 835592 | tf_op jit(solution)/shard_map/ppermute | solution.py:594
  (93 other events, 504.4 us)
